TPU v7x, 32 devices: a whole 2x2x4 slice. The times are simulated.
32 devices in a mesh: expert: 8 (over y, x, core), wshard: 4 (over z).
Axes of the slice: x: 2, y: 2, z: 4, core: 2. Of those that a mesh axis runs over, the one named last changes fastest.
Arguments:
- tokens: bfloat16 [4096, 2048], P(('expert', 'wshard')), may hold values from -6 to 6
- segment_ids: int32 [4096], P('expert'), may hold values from 0 to 15, never falling along the last dimension, each value on 1 to 512 neighbouring positions
- routes: int32 [4096, 8], P(('expert', 'wshard')), may hold values from 0 to 15, all different within a row; in each aligned block of 128 rows (0 to 127, 128 to 255, ...) at most 128 rows name the same one
- pair_order: int32 [32768], P(('expert', 'wshard')), may hold values from 0 to 32767, each once
- attn_gain: bfloat16 [2048], P(('expert', 'wshard')), may hold values from 0.5 to 1.5
- w_query: bfloat16 [2048, 2048], P(('expert', 'wshard')), may hold values from -0.125 to 0.125
- w_key: bfloat16 [2048, 2048], P(('expert', 'wshard')), may hold values from -0.125 to 0.125
- w_value: bfloat16 [2048, 2048], P(('expert', 'wshard')), may hold values from -0.125 to 0.125
- query_gain: bfloat16 [128], P(('expert', 'wshard')), may hold values from 0.5 to 1.5
- key_gain: bfloat16 [128], P(('expert', 'wshard')), may hold values from 0.5 to 1.5
- w_out: bfloat16 [2048, 2048], P(('expert', 'wshard')), may hold values from -1 to 1
- ffn_gain: bfloat16 [2048], P(('expert', 'wshard')), may hold values from 0.5 to 1.5
- w_router: bfloat16 [2048, 16], P(('expert', 'wshard')), may hold values from -0.0625 to 0.0625
- w_gate: bfloat16 [16, 2048, 1024], P('expert', 'wshard'), may hold values from -0.125 to 0.125
- w_up: bfloat16 [16, 2048, 1024], P('expert', 'wshard'), may hold values from -0.125 to 0.125
- w_down: bfloat16 [16, 1024, 2048], P('expert', None, 'wshard'), may hold values from -1.5 to 1.5
- out_grad: bfloat16 [4096, 2048], P(('expert', 'wshard')), may hold values from -6 to 6
Outputs:
- mixed_out: bfloat16 [4096, 2048], P(('expert', 'wshard'))
- tokens_grad: bfloat16 [4096, 2048], P(('expert', 'wshard'))
- attn_gain_grad: float32 [2048], P(('expert', 'wshard'))
- w_query_grad: float32 [2048, 2048], P(('expert', 'wshard'))
- w_key_grad: float32 [2048, 2048], P(('expert', 'wshard'))
- w_value_grad: float32 [2048, 2048], P(('expert', 'wshard'))
- query_gain_grad: float32 [128], P(('expert', 'wshard'))
- key_gain_grad: float32 [128], P(('expert', 'wshard'))
- w_out_grad: float32 [2048, 2048], P(('expert', 'wshard'))
- ffn_gain_grad: float32 [2048], P(('expert', 'wshard'))
- w_router_grad: float32 [2048, 16], P(('expert', 'wshard'))
- w_gate_grad: float32 [16, 2048, 1024], P('expert', 'wshard')
- w_up_grad: float32 [16, 2048, 1024], P('expert', 'wshard')
- w_down_grad: float32 [16, 1024, 2048], P('expert', None, 'wshard')
Inputs may be any that keep to these rules, and one draw needn't show every extreme that they name: `routes`: each row names 8 different experts; in each aligned block of 128 rows (the rows of one device) no expert is named by more than 128 rows, and some expert reaches 128. `pair_order`: each number once. `segment_ids`: never falling; each document has 1 to 512 tokens, one has exactly 512.
All inputs are finite; a program needn't handle non-finite values.
Results may differ from a plain program's by a relative error of at most 0.019.
Values may be sent and summed in bfloat16 or wider, within the bound.
A program may use at most 384 MiB of HBM per device.

v0:
```python
import jax
import jax.numpy as jnp
from jax import lax
from jax.sharding import PartitionSpec as P

HEADS = 16
HD = 128


EPSILON = 1e-06
THETA = 10000.0


def matmul(left, right):
    return jnp.dot(left, right, preferred_element_type=jnp.float32)


def matmul_tn(left, right):
    return lax.dot_general(
        left, right, (((0,), (0,)), ((), ())), preferred_element_type=jnp.float32
    )


def matmul_nt(left, right):
    return lax.dot_general(
        left, right, (((1,), (1,)), ((), ())), preferred_element_type=jnp.float32
    )


def rms_scale(values, scale_gain):
    factor = lax.rsqrt(jnp.mean(values * values, axis=-1, keepdims=True) + EPSILON)
    return values * factor * scale_gain


def rope_tables(positions):
    exponent = jnp.arange(HD // 2, dtype=jnp.float32) * (2.0 / HD)
    frequency = jnp.power(jnp.float32(THETA), -exponent)
    angles = positions.astype(jnp.float32)[:, None] * frequency[None, :]
    return (jnp.cos(angles), jnp.sin(angles))


def rotate(values, cosine, sine):
    first_half = values[..., : HD // 2]
    second_half = values[..., HD // 2 :]
    cos_part = cosine[:, None, :]
    sin_part = sine[:, None, :]
    return jnp.concatenate(
        [
            first_half * cos_part - second_half * sin_part,
            second_half * cos_part + first_half * sin_part,
        ],
        axis=-1,
    )


def padded_rows(rows):
    return jnp.concatenate([jnp.zeros((1,) + rows.shape[1:], rows.dtype), rows], axis=0)


def masked_scores(query_rot, key_rot, query_segment, key_segment):
    scores = jnp.einsum("qhd,khd->hqk", query_rot, key_rot, preferred_element_type=jnp.float32)
    allowed = query_segment[:, None] == key_segment[None, :]
    return jnp.where(allowed[None], scores, -1e30)


def swiglu_fn(gate_in, up_in):
    return jax.nn.silu(gate_in) * up_in


def local(
    tokens,
    segment_ids,
    routes,
    pair_order,
    attn_gain,
    w_query,
    w_key,
    w_value,
    query_gain,
    key_gain,
    w_out,
    ffn_gain,
    w_router,
    w_gate,
    w_up,
    w_down,
    out_grad,
):
    tok_rows, width = tokens.shape
    top_count = routes.shape[1]
    expert_devs = lax.axis_size("expert")
    shard_devs = lax.axis_size("wshard")
    local_experts = w_gate.shape[0]
    expert_count = local_experts * expert_devs
    most_rows = 2 * tok_rows * top_count // expert_count
    capacity = 5 * tok_rows * top_count // (4 * local_experts)
    seq_length = segment_ids.shape[0]
    device_expert = lax.axis_index("expert")
    device_shard = lax.axis_index("wshard")
    low_type = jnp.bfloat16
    wide_type = jnp.float32
    gathered = (
        lax.all_gather(attn_gain, ("expert", "wshard"), axis=0, tiled=True),
        lax.all_gather(w_query, ("expert", "wshard"), axis=0, tiled=True),
        lax.all_gather(w_key, ("expert", "wshard"), axis=0, tiled=True),
        lax.all_gather(w_value, ("expert", "wshard"), axis=0, tiled=True),
        lax.all_gather(query_gain, ("expert", "wshard"), axis=0, tiled=True),
        lax.all_gather(key_gain, ("expert", "wshard"), axis=0, tiled=True),
        lax.all_gather(w_out, ("expert", "wshard"), axis=0, tiled=True),
        lax.all_gather(ffn_gain, ("expert", "wshard"), axis=0, tiled=True),
        lax.all_gather(w_router, ("expert", "wshard"), axis=0, tiled=True),
    )
    attn_scale = gathered[0].astype(wide_type)
    query_w, key_w, value_w = (gathered[1], gathered[2], gathered[3])
    query_scale = gathered[4].astype(wide_type)
    key_scale = gathered[5].astype(wide_type)
    out_w = gathered[6]
    ffn_scale = gathered[7].astype(wide_type)
    router_w = gathered[8]
    inputs = tokens.astype(wide_type)
    normed, norm_one_pull = jax.vjp(rms_scale, inputs, attn_scale)
    normed_low = normed.astype(low_type)
    query_raw = matmul(normed_low, query_w)
    key_raw = matmul(normed_low, key_w)
    value_low = matmul(normed_low, value_w).astype(low_type)
    positions = device_shard * tok_rows + jnp.arange(tok_rows, dtype=jnp.int32)
    cosine, sine = rope_tables(positions)

    def prepare(query_in, key_in, query_g, key_g):
        query_heads = rms_scale(query_in.reshape(tok_rows, HEADS, HD), query_g)
        key_heads = rms_scale(key_in.reshape(tok_rows, HEADS, HD), key_g)
        return (rotate(query_heads, cosine, sine) * HD ** (-0.5), rotate(key_heads, cosine, sine))

    rotated, prepare_pull = jax.vjp(prepare, query_raw, key_raw, query_scale, key_scale)
    query_low = rotated[0].astype(low_type)
    key_low = rotated[1].astype(low_type).reshape(tok_rows, width)
    seq_keys, seq_values = (
        lax.all_gather(key_low, "wshard", axis=0, tiled=True),
        lax.all_gather(value_low, "wshard", axis=0, tiled=True),
    )
    query_segment = lax.dynamic_slice_in_dim(segment_ids, device_shard * tok_rows, tok_rows)
    scores = masked_scores(
        query_low, seq_keys.reshape(seq_length, HEADS, HD), query_segment, segment_ids
    )
    row_max = jnp.max(scores, axis=-1, keepdims=True)
    shifted = jnp.exp(scores - row_max)
    totals = jnp.sum(shifted, axis=-1, keepdims=True)
    log_total = row_max + jnp.log(totals)
    probs_low = (shifted / totals).astype(low_type)
    mixed = jnp.einsum(
        "hqk,khd->qhd",
        probs_low,
        seq_values.reshape(seq_length, HEADS, HD),
        preferred_element_type=wide_type,
    )
    mixed_low = mixed.reshape(tok_rows, width).astype(low_type)
    hidden = inputs + matmul(mixed_low, out_w)
    normed_two, norm_two_pull = jax.vjp(rms_scale, hidden, ffn_scale)
    normed_two_low = normed_two.astype(low_type)
    logits = matmul(normed_two_low, router_w)

    def router_weights(logit_values):
        return jnp.take_along_axis(jax.nn.softmax(logit_values, axis=-1), routes, axis=1)

    route_weight, route_pull = jax.vjp(router_weights, logits)
    group_routes, group_order = (
        lax.all_gather(routes, "expert", axis=0, tiled=True),
        lax.all_gather(pair_order, "expert", axis=0, tiled=True),
    )
    per_source = tok_rows * top_count
    group_pairs = per_source * expert_devs
    expert_of = group_routes.reshape(-1)
    pair_index = jnp.arange(group_pairs, dtype=jnp.int32)
    source_of = pair_index // per_source
    expert_ids = jnp.arange(expert_count, dtype=jnp.int32)
    onehot = (expert_of.reshape(expert_devs, per_source, 1) == expert_ids).astype(jnp.int32)
    position_of = (jnp.sum(jnp.cumsum(onehot, axis=1) * onehot, axis=-1) - 1).reshape(-1)
    order_span = group_pairs * shard_devs
    sort_keys = expert_of * order_span + group_order
    sorted_pairs = jnp.argsort(sort_keys)
    placement = jnp.zeros((group_pairs,), jnp.int32).at[sorted_pairs].set(pair_index)
    expert_counts = jnp.sum(onehot, axis=(0, 1))
    expert_start = jnp.cumsum(expert_counts) - expert_counts
    start_of = jnp.sum(onehot.reshape(group_pairs, expert_count) * expert_start[None, :], axis=-1)
    slot_rank = placement - start_of
    retained = slot_rank < capacity
    own_expert = routes.reshape(-1)
    own_position = lax.dynamic_slice_in_dim(position_of, device_expert * per_source, per_source)
    send_slot = own_expert * most_rows + own_position
    send_pair = (
        jnp.zeros((expert_count * most_rows,), jnp.int32)
        .at[send_slot]
        .set(jnp.arange(per_source, dtype=jnp.int32) + 1)
    )
    send_token = jnp.where(send_pair > 0, (send_pair - 1) // top_count + 1, 0)
    owner_local = expert_of % local_experts
    is_mine = expert_of // local_experts == device_expert
    recv_row = source_of * (local_experts * most_rows) + owner_local * most_rows + position_of
    slot_target = jnp.where(
        is_mine & retained, owner_local * capacity + slot_rank, local_experts * capacity
    )
    slot_source = (
        jnp.zeros((local_experts * capacity,), jnp.int32)
        .at[slot_target]
        .set(recv_row + 1, mode="drop")
    )
    back_room = expert_devs * local_experts * most_rows
    back_target = jnp.where(is_mine, recv_row, back_room)
    back_source = (
        jnp.zeros((back_room,), jnp.int32)
        .at[back_target]
        .set(jnp.where(retained, owner_local * capacity + slot_rank + 1, 0), mode="drop")
    )
    send_rows = padded_rows(normed_two_low)[send_token].reshape(
        expert_devs, local_experts * most_rows, width
    )
    recv_rows = lax.all_to_all(
        send_rows, "expert", split_axis=0, concat_axis=0, tiled=True
    ).reshape(-1, width)
    slot_rows = padded_rows(recv_rows)[slot_source].reshape(local_experts, capacity, width)
    full_gate, full_up, full_down = (
        lax.all_gather(w_gate, "wshard", axis=1, tiled=True),
        lax.all_gather(w_up, "wshard", axis=1, tiled=True),
        lax.all_gather(w_down, "wshard", axis=2, tiled=True),
    )
    gate_act = jnp.einsum("ecd,edf->ecf", slot_rows, full_gate, preferred_element_type=wide_type)
    up_act = jnp.einsum("ecd,edf->ecf", slot_rows, full_up, preferred_element_type=wide_type)
    swiglu_out, swiglu_pull = jax.vjp(swiglu_fn, gate_act, up_act)
    swiglu_low = swiglu_out.astype(low_type)
    expert_out = jnp.einsum(
        "ecf,efd->ecd", swiglu_low, full_down, preferred_element_type=wide_type
    ).astype(low_type)
    back_rows = padded_rows(expert_out.reshape(-1, width))[back_source].reshape(
        expert_devs, local_experts * most_rows, width
    )
    returned = lax.all_to_all(back_rows, "expert", split_axis=0, concat_axis=0, tiled=True).reshape(
        -1, width
    )
    pair_rows = returned[send_slot].reshape(tok_rows, top_count, width)
    combined = jnp.einsum("tk,tkd->td", route_weight, pair_rows, preferred_element_type=wide_type)
    mixed_out = (hidden + combined).astype(low_type)
    result_grad = out_grad.astype(wide_type)
    weight_grad = jnp.einsum("td,tkd->tk", result_grad, pair_rows, preferred_element_type=wide_type)
    pair_grad = (
        (route_weight[:, :, None] * result_grad[:, None, :])
        .astype(low_type)
        .reshape(per_source, width)
    )
    send_grad = padded_rows(pair_grad)[send_pair].reshape(
        expert_devs, local_experts * most_rows, width
    )
    recv_grad = lax.all_to_all(
        send_grad, "expert", split_axis=0, concat_axis=0, tiled=True
    ).reshape(-1, width)
    slot_grad = padded_rows(recv_grad)[slot_source].reshape(local_experts, capacity, width)
    act_grad = jnp.einsum("ecd,efd->ecf", slot_grad, full_down, preferred_element_type=wide_type)
    down_grad = jnp.einsum("ecf,ecd->efd", swiglu_low, slot_grad, preferred_element_type=wide_type)
    gate_grad, up_grad = swiglu_pull(act_grad)
    gate_low = gate_grad.astype(low_type)
    up_low = up_grad.astype(low_type)
    gate_w_grad = jnp.einsum("ecd,ecf->edf", slot_rows, gate_low, preferred_element_type=wide_type)
    up_w_grad = jnp.einsum("ecd,ecf->edf", slot_rows, up_low, preferred_element_type=wide_type)
    slot_in_grad = jnp.einsum("ecf,edf->ecd", gate_low, full_gate, preferred_element_type=wide_type)
    slot_in_grad = (
        slot_in_grad + jnp.einsum("ecf,edf->ecd", up_low, full_up, preferred_element_type=wide_type)
    ).astype(low_type)
    gate_shard, up_shard, down_shard = (
        lax.psum_scatter(
            gate_w_grad.astype(jnp.bfloat16), "wshard", scatter_dimension=1, tiled=True
        ).astype(jnp.float32),
        lax.psum_scatter(
            up_w_grad.astype(jnp.bfloat16), "wshard", scatter_dimension=1, tiled=True
        ).astype(jnp.float32),
        lax.psum_scatter(
            down_grad.astype(jnp.bfloat16), "wshard", scatter_dimension=2, tiled=True
        ).astype(jnp.float32),
    )
    back_grad = padded_rows(slot_in_grad.reshape(-1, width))[back_source].reshape(
        expert_devs, local_experts * most_rows, width
    )
    returned_grad = lax.all_to_all(
        back_grad, "expert", split_axis=0, concat_axis=0, tiled=True
    ).reshape(-1, width)
    expert_in_grad = jnp.sum(
        returned_grad[send_slot].reshape(tok_rows, top_count, width).astype(wide_type), axis=1
    )
    logit_grad = route_pull(weight_grad)[0]
    logit_low = logit_grad.astype(low_type)
    router_grad = matmul_tn(normed_two_low, logit_low)
    normed_two_grad = expert_in_grad + matmul_nt(logit_low, router_w)
    hidden_norm_grad, ffn_scale_grad = norm_two_pull(normed_two_grad)
    hidden_grad = result_grad + hidden_norm_grad
    attn_low = hidden_grad.astype(low_type)
    out_w_grad = matmul_tn(mixed_low, attn_low)
    mixed_grad = matmul_nt(attn_low, out_w).astype(low_type).reshape(tok_rows, HEADS, HD)
    back_keys, back_values = (seq_keys, seq_values)
    key_heads = back_keys.reshape(seq_length, HEADS, HD)
    value_heads = back_values.reshape(seq_length, HEADS, HD)
    scores_again = masked_scores(query_low, key_heads, query_segment, segment_ids)
    probs_again = jnp.exp(scores_again - log_total)
    probs_again_low = probs_again.astype(low_type)
    prob_grad = jnp.einsum(
        "qhd,khd->hqk", mixed_grad, value_heads, preferred_element_type=wide_type
    )
    value_part = jnp.einsum(
        "hqk,qhd->khd", probs_again_low, mixed_grad, preferred_element_type=wide_type
    )
    row_inner = jnp.sum(probs_again * prob_grad, axis=-1, keepdims=True)
    score_low = (probs_again * (prob_grad - row_inner)).astype(low_type)
    query_rot_grad = jnp.einsum(
        "hqk,khd->qhd", score_low, key_heads, preferred_element_type=wide_type
    )
    key_part = jnp.einsum("hqk,qhd->khd", score_low, query_low, preferred_element_type=wide_type)
    key_rot_grad, value_grad = (
        lax.psum_scatter(
            key_part.reshape(seq_length, width).astype(jnp.bfloat16),
            "wshard",
            scatter_dimension=0,
            tiled=True,
        ).astype(jnp.float32),
        lax.psum_scatter(
            value_part.reshape(seq_length, width).astype(jnp.bfloat16),
            "wshard",
            scatter_dimension=0,
            tiled=True,
        ).astype(jnp.float32),
    )
    query_raw_grad, key_raw_grad, query_scale_grad, key_scale_grad = prepare_pull(
        (query_rot_grad, key_rot_grad.reshape(tok_rows, HEADS, HD))
    )
    query_grad_low = query_raw_grad.astype(low_type)
    key_grad_low = key_raw_grad.astype(low_type)
    value_grad_low = value_grad.astype(low_type)
    query_w_grad = matmul_tn(normed_low, query_grad_low)
    key_w_grad = matmul_tn(normed_low, key_grad_low)
    value_w_grad = matmul_tn(normed_low, value_grad_low)
    normed_grad = (
        matmul_nt(query_grad_low, query_w)
        + matmul_nt(key_grad_low, key_w)
        + matmul_nt(value_grad_low, value_w)
    )
    input_norm_grad, attn_scale_grad = norm_one_pull(normed_grad)
    input_grad = (hidden_grad + input_norm_grad).astype(low_type)
    summed = (
        lax.psum_scatter(attn_scale_grad, ("expert", "wshard"), scatter_dimension=0, tiled=True),
        lax.psum_scatter(query_w_grad, ("expert", "wshard"), scatter_dimension=0, tiled=True),
        lax.psum_scatter(key_w_grad, ("expert", "wshard"), scatter_dimension=0, tiled=True),
        lax.psum_scatter(value_w_grad, ("expert", "wshard"), scatter_dimension=0, tiled=True),
        lax.psum_scatter(query_scale_grad, ("expert", "wshard"), scatter_dimension=0, tiled=True),
        lax.psum_scatter(key_scale_grad, ("expert", "wshard"), scatter_dimension=0, tiled=True),
        lax.psum_scatter(out_w_grad, ("expert", "wshard"), scatter_dimension=0, tiled=True),
        lax.psum_scatter(ffn_scale_grad, ("expert", "wshard"), scatter_dimension=0, tiled=True),
        lax.psum_scatter(router_grad, ("expert", "wshard"), scatter_dimension=0, tiled=True),
    )
    return (
        mixed_out,
        input_grad,
        summed[0],
        summed[1],
        summed[2],
        summed[3],
        summed[4],
        summed[5],
        summed[6],
        summed[7],
        summed[8],
        gate_shard,
        up_shard,
        down_shard,
    )


def solution(mesh):
    return jax.shard_map(
        local,
        mesh=mesh,
        in_specs=(
            P(("expert", "wshard"), None),
            P("expert"),
            P(("expert", "wshard"), None),
            P(("expert", "wshard")),
            P(("expert", "wshard")),
            P(("expert", "wshard"), None),
            P(("expert", "wshard"), None),
            P(("expert", "wshard"), None),
            P(("expert", "wshard")),
            P(("expert", "wshard")),
            P(("expert", "wshard"), None),
            P(("expert", "wshard")),
            P(("expert", "wshard"), None),
            P("expert", "wshard", None),
            P("expert", "wshard", None),
            P("expert", None, "wshard"),
            P(("expert", "wshard"), None),
        ),
        out_specs=(
            P(("expert", "wshard"), None),
            P(("expert", "wshard"), None),
            P(("expert", "wshard")),
            P(("expert", "wshard"), None),
            P(("expert", "wshard"), None),
            P(("expert", "wshard"), None),
            P(("expert", "wshard")),
            P(("expert", "wshard")),
            P(("expert", "wshard"), None),
            P(("expert", "wshard")),
            P(("expert", "wshard"), None),
            P("expert", "wshard", None),
            P("expert", "wshard", None),
            P("expert", None, "wshard"),
        ),
        check_vma=False,
    )
```

profile of v0, /device:TPU:0, one launch (start us, length us, event | category | flops | bytes accessed | tf_op | source)
XLA Modules:
  0.0 3316.4 jit_solution(16856127144819950626)
XLA Ops:
  12.9 42.5 %all-reduce.19 = (bf16[2048]{0:T(1024)(128)(2,1)S(1)}, bf16[128]{0:T(256)(128)(2,1)S(1)}, bf16[128]{0:T(256)(128)(2,1)S(1)}, bf16[2048]{0:T(1024)(128)(2,1)S(1)}) all-reduce(bf16[2048]{0:T(1024)(128)(2,1)S(1)} %dynamic-update-slice, bf16[128]{0:T(256)(128)(2,1)S(1)} %dynamic-update-slice.1, ...), channel_id=1, replica_groups=mesh['expert'=8,'wshard'=4] {'expert','wshard'}, use_global_device_ids=true, to_apply=%add.10 | all-reduce | flops 4352 | bytes 17408
  57.6 33.8 %all-gather.17.cloned.1.call-done = bf16[2048,2048]{1,0:T(8,128)(2,1)} async-done(((bf16[64,2048]{1,0:T(8,128)(2,1)}), bf16[2048,2048]{1,0:T(8,128)(2,1)}) %all-gather.17.cloned.1.call-update) | async-done | bytes 8388624 | tf_op jit(solution)/shard_map/all_gather | solution.py:105
  91.4 4.9 fusion.102
  96.9 73.5 %all-gather.15.cloned.1.call-done = bf16[2048,2048]{1,0:T(8,128)(2,1)} async-done(((bf16[64,2048]{1,0:T(8,128)(2,1)}), bf16[2048,2048]{1,0:T(8,128)(2,1)}) %all-gather.15.cloned.1.call-update) | async-done | bytes 8388624 | tf_op jit(solution)/shard_map/all_gather | solution.py:104
  179.5 69.8 %all-gather.11.cloned.1.call-done = bf16[2048,2048]{1,0:T(8,128)(2,1)} async-done(((bf16[64,2048]{1,0:T(8,128)(2,1)}), bf16[2048,2048]{1,0:T(8,128)(2,1)}) %all-gather.11.cloned.1.call-update) | async-done | bytes 8388624 | tf_op jit(solution)/shard_map/all_gather | solution.py:106
  249.3 5.5 convolution_convert_fusion.5
  256.9 9.0 all_gather.59
  267.7 69.2 %all-gather = bf16[32,64,16]{1,2,0:T(8,128)(2,1)S(1)} all-gather(bf16[1,64,16]{1,2,0:T(8,128)(2,1)S(1)} %bitcast.250), channel_id=1, replica_groups=mesh['expert'=8,'wshard'=4] {'expert','wshard'}, dimensions={0}, use_global_device_ids=true | all-gather | bytes 67584 | tf_op jit(solution)/shard_map/all_gather | solution.py:111
  338.0 62.0 %reduce-window.18 = s32[8,16,8,128]{3,2,1,0:T(8,128)S(1)} reduce-window(s32[8,16,8,128]{3,2,1,0:T(8,128)} %fusion.49, s32[]{:T(128)} %constant.135.clone.1), window={size=1x1x1x128 pad=0_0x0_0x0_0x127_0}, to_apply=%region_8.9 | reduce-window | flops 16646144 | bytes 1048580 | tf_op jit(solution)/shard_map/reduce-window
  432.4 7.0 gather_fusion.8
  444.0 19.1 gather_fusion.4
  463.1 5.4 all-to-all-start.2
  469.4 11.0 gather_fusion
  480.3 82.2 %all-to-all-done.2 = bf16[8,256,2048]{2,1,0:T(8,128)(2,1)} async-done(((bf16[8,256,2048]{2,1,0:T(8,128)(2,1)}), bf16[8,256,2048]{2,1,0:T(8,128)(2,1)}, u32[]{:S(2)}, u32[]{:S(2)}) %all-to-all-start.2) | async-done | bytes 8388640 | tf_op jit(solution)/shard_map/all_to_all | solution.py:252
  562.5 5.1 all-to-all-start
  568.5 96.4 %all_gather.60 = s32[8192]{0:T(1024)S(1)} all-gather(s32[1024]{0:T(1024)S(1)} %copy-done.70), channel_id=1, replica_groups=mesh['expert'=8,'wshard'=4] {'expert'}, dimensions={0}, use_global_device_ids=true | all-gather | bytes 36864 | tf_op jit(solution)/shard_map/all_gather | solution.py:168
  664.8 6.8 sort.17
  671.6 30.5 scatter_custom_fusion.1
  702.4 30.4 scatter_custom_fusion.2
  733.2 30.4 scatter_custom_fusion.3
  763.7 9.9 concatenate.31
  773.5 15.5 gather_fusion.5
  789.1 9.9 concatenate.28
  798.9 15.3 gather_fusion.1
  814.3 11.5 fusion.110
  825.7 11.5 fusion.109
  837.2 37.6 %all-gather.27.cloned.1.call-done = bf16[2,1024,2048]{2,1,0:T(8,128)(2,1)} async-done(((bf16[2,1024,512]{2,1,0:T(8,128)(2,1)}), bf16[2,1024,2048]{2,1,0:T(8,128)(2,1)}) %all-gather.27.cloned.1.call-update) | async-done | bytes 8388624 | tf_op jit(solution)/shard_map/all_gather | solution.py:224
  874.8 14.4 multiply_convert_fusion
  889.2 14.0 fusion.111
  903.2 12.3 add_convert_fusion
  915.6 6.6 concatenate.32
  922.2 19.9 gather_fusion.6
  942.1 5.0 all-to-all-start.3
  947.1 9.2 convolution_convert_fusion.3
  960.0 19.5 gather_fusion.2
  979.5 61.6 %all-to-all-done.3 = bf16[8,256,2048]{2,1,0:T(8,128)(2,1)} async-done(((bf16[8,256,2048]{2,1,0:T(8,128)(2,1)}), bf16[8,256,2048]{2,1,0:T(8,128)(2,1)}, u32[]{:S(2)}, u32[]{:S(2)}) %all-to-all-start.3) | async-done | bytes 8388640 | tf_op jit(solution)/shard_map/all_to_all | solution.py:281
  1041.2 5.1 all-to-all-start.1
  1047.0 13.4 gather_fusion.7
  1060.4 5.0 convert_reduce_fusion
  1065.5 74.9 %all-to-all-done.1 = bf16[8,256,2048]{2,1,0:T(8,128)(2,1)} async-done(((bf16[8,256,2048]{2,1,0:T(8,128)(2,1)}), bf16[8,256,2048]{2,1,0:T(8,128)(2,1)}, u32[]{:S(2)}, u32[]{:S(2)}) %all-to-all-start.1) | async-done | bytes 8388640 | tf_op jit(solution)/shard_map/all_to_all | solution.py:236
  1140.4 13.3 gather_fusion.3
  1153.8 5.0 fusion.5
  1160.2 6.6 scatter_custom_fusion.4
  1171.0 6.3 convolution_convert_fusion.4
  1183.4 5.0 multiply_reduce_fusion
  1197.1 11.9 convolution_convert_fusion
  1209.5 12.1 convolution_convert_fusion.2
  1221.7 11.9 convolution_convert_fusion.1
  1234.6 9.3 fusion.50
  1245.0 9.2 fusion.96
  1257.7 12.3 reduce-scatter.31.cloned.1.call-done
  1279.7 8.2 fusion.98
  1295.7 8.2 fusion.100
  1303.9 103.4 %reduce-scatter.35.cloned.1.call-done = f32[64,16]{1,0:T(8,128)} async-done(((f32[2048,16]{1,0:T(8,128)}), f32[64,16]{1,0:T(8,128)}) %reduce-scatter.35.cloned.1.call-update) | async-done | bytes 4112
  1408.7 6.7 fusion.112
  1415.4 6.4 convolution_add_fusion.2
  1425.1 40.8 %all-reduce.18 = (f32[2048]{0:T(1024)S(1)}, f32[128]{0:T(128)S(1)}, f32[128]{0:T(128)S(1)}, f32[2048]{0:T(1024)S(1)}) all-reduce(f32[2048]{0:T(1024)S(1)} %get-tuple-element.22, f32[128]{0:T(128)S(1)} %get-tuple-element.18, f32[128]{0:T(128)S(1)} %get-tuple-element.16, ...), channel_id=4, replica_groups=mesh['expert'=8,'wshard'=4] {'expert','wshard'}, use_global_device_ids=true, to_apply=%region_30.31.clone | all-reduce | flops 4352 | bytes 34816
  1469.4 82.1 %reduce-scatter.29.cloned.1.call-done = bf16[2,1024,512]{2,1,0:T(8,128)(2,1)} async-done(((bf16[2,1024,2048]{2,1,0:T(8,128)(2,1)}), bf16[2,1024,512]{2,1,0:T(8,128)(2,1)}) %reduce-scatter.29.cloned.1.call-update) | async-done | bytes 2097168 | tf_op jit(solution)/shard_map/reduce_scatter | solution.py:274
  1555.7 143.4 %reduce-scatter.25.cloned.1.call-done = bf16[2,512,1024]{2,1,0:T(8,128)(2,1)} async-done(((bf16[2,2048,1024]{2,1,0:T(8,128)(2,1)}), bf16[2,512,1024]{2,1,0:T(8,128)(2,1)}) %reduce-scatter.25.cloned.1.call-update) | async-done | bytes 2097168 | tf_op jit(solution)/shard_map/reduce_scatter | solution.py:268
  1703.2 143.5 %reduce-scatter.27.cloned.1.call-done = bf16[2,512,1024]{2,1,0:T(8,128)(2,1)} async-done(((bf16[2,2048,1024]{2,1,0:T(8,128)(2,1)}), bf16[2,512,1024]{2,1,0:T(8,128)(2,1)}) %reduce-scatter.27.cloned.1.call-update) | async-done | bytes 2097168 | tf_op jit(solution)/shard_map/reduce_scatter | solution.py:271
  1850.7 363.7 %reduce-scatter.23.cloned.1.call-done = f32[64,2048]{1,0:T(8,128)} async-done(((f32[2048,2048]{1,0:T(8,128)}), f32[64,2048]{1,0:T(8,128)}) %reduce-scatter.23.cloned.1.call-update) | async-done | bytes 524304 | tf_op jit(solution)/shard_map/reduce_scatter | solution.py:351
  2214.4 365.0 %reduce-scatter.21.cloned.1.call-done = f32[64,2048]{1,0:T(8,128)} async-done(((f32[2048,2048]{1,0:T(8,128)}), f32[64,2048]{1,0:T(8,128)}) %reduce-scatter.21.cloned.1.call-update) | async-done | bytes 524304 | tf_op jit(solution)/shard_map/reduce_scatter | solution.py:348
  2579.5 365.0 %reduce-scatter.19.cloned.1.call-done = f32[64,2048]{1,0:T(8,128)} async-done(((f32[2048,2048]{1,0:T(8,128)}), f32[64,2048]{1,0:T(8,128)}) %reduce-scatter.19.cloned.1.call-update) | async-done | bytes 524304 | tf_op jit(solution)/shard_map/reduce_scatter | solution.py:347
  2944.5 365.1 %reduce-scatter.17.cloned.1.call-done = f32[64,2048]{1,0:T(8,128)} async-done(((f32[2048,2048]{1,0:T(8,128)}), f32[64,2048]{1,0:T(8,128)}) %reduce-scatter.17.cloned.1.call-update) | async-done | bytes 524304 | tf_op jit(solution)/shard_map/reduce_scatter | solution.py:346
  (352 shorter events, 129.5 us)
Async XLA Ops:
  7.2 84.2 %all-gather.17.cloned.1.call-start = ((), (), s32[]{:S(2)}) async-start(), calls=%async_computation.17 | async-start | bytes 8650752 | tf_op jit(solution)/shard_map/all_gather | solution.py:105
  7.9 162.4 %all-gather.15.cloned.1.call-start = ((), (), s32[]{:S(2)}) async-start(), calls=%async_computation.16 | async-start | bytes 8650752 | tf_op jit(solution)/shard_map/all_gather | solution.py:104
  8.7 240.6 %all-gather.11.cloned.1.call-start = ((), (), s32[]{:S(2)}) async-start(), calls=%async_computation.14 | async-start | bytes 8650752 | tf_op jit(solution)/shard_map/all_gather | solution.py:106
  9.4 403.4 %all-gather.19.cloned.1.call-start = ((), (), s32[]{:S(2)}) async-start(), calls=%async_computation.18 | async-start | bytes 2621440 | tf_op jit(solution)/shard_map/all_gather | solution.py:138
  55.4 120.3 %copy-start.65 = (f32[128]{0:T(128)}, f32[128]{0:T(128)S(1)}, u32[]{:S(2)}) copy-start(f32[128]{0:T(128)S(1)} %convert_element_type.163) | copy-start | bytes 1540
  55.4 120.3 %copy-start.67 = (f32[128]{0:T(128)}, f32[128]{0:T(128)S(1)}, u32[]{:S(2)}) copy-start(f32[128]{0:T(128)S(1)} %convert_element_type.166) | copy-start | bytes 1540
  55.4 193.9 %copy-start.23 = (f32[2048]{0:T(1024)}, f32[2048]{0:T(1024)S(1)}, u32[]{:S(2)}) copy-start(f32[2048]{0:T(1024)S(1)} %convert_element_type.160) | copy-start | bytes 24580
  57.3 192.0 %copy-start.44 = (f32[128]{0:T(128)}, f32[128]{0:T(128)S(1)}, u32[]{:S(2)}) copy-start(f32[128]{0:T(128)S(1)} %fusion.92) | copy-start | bytes 1540
  57.6 118.9 %copy-start.30 = (f32[128,64]{1,0:T(8,128)}, f32[128,64]{1,0:T(8,128)S(1)}, u32[]{:S(2)}) copy-start(f32[128,64]{1,0:T(8,128)S(1)} %get-tuple-element.64) | copy-start | bytes 98308
  57.6 118.9 %copy-start.32 = (f32[128,64]{1,0:T(8,128)}, f32[128,64]{1,0:T(8,128)S(1)}, u32[]{:S(2)}) copy-start(f32[128,64]{1,0:T(8,128)S(1)} %get-tuple-element.65) | copy-start | bytes 98308
  57.6 112.8 %copy-start.2 = (bf16[128,2048]{1,0:T(8,128)(2,1)S(1)}, bf16[128,2048]{1,0:T(8,128)(2,1)}, u32[]{:S(2)}) copy-start(bf16[128,2048]{1,0:T(8,128)(2,1)} %param.17) | copy-start | bytes 1572868
  96.3 79.4 %copy-start.6 = (f32[128,2048]{1,0:T(8,128)}, f32[128,2048]{1,0:T(8,128)S(1)}, u32[]{:S(2)}) copy-start(f32[128,2048]{1,0:T(8,128)S(1)} %fusion.102) | copy-start | bytes 3145732
  96.9 78.8 %copy-start.50 = (f32[128,16]{0,1:T(8,128)}, f32[128,16]{0,1:T(8,128)S(1)}, u32[]{:S(2)}) copy-start(f32[128,16]{0,1:T(8,128)S(1)} %copy.214) | copy-start | bytes 24580
  179.5 77.4 %copy-start.52 = (s32[128,8]{0,1:T(8,128)S(1)}, s32[128,8]{0,1:T(8,128)}, u32[]{:S(2)}) copy-start(s32[128,8]{0,1:T(8,128)} %param.19) | copy-start | bytes 12292
  179.5 239.2 %all-gather.13.cloned.1.call-start = ((), (), s32[]{:S(2)}) async-start(), calls=%async_computation.15 | async-start | bytes 2621440 | tf_op jit(solution)/shard_map/all_gather | solution.py:139
  254.8 12.9 copy-start.69
  254.8 171.2 %all-gather.21.cloned.1.call-start = ((), (), s32[]{:S(2)}) async-start(), calls=%async_computation.19 | async-start | bytes 8650752 | tf_op jit(solution)/shard_map/all_gather | solution.py:109
  255.4 558.9 %all-gather.25.cloned.1.call-start = ((), (), s32[]{:S(2)}) async-start(), calls=%async_computation.21 | async-start | bytes 10485760 | tf_op jit(solution)/shard_map/all_gather | solution.py:223
  256.1 148.8 %copy-start.27 = (bf16[128,2048]{1,0:T(8,128)(2,1)S(1)}, bf16[128,2048]{1,0:T(8,128)(2,1)}, u32[]{:S(2)}) copy-start(bf16[128,2048]{1,0:T(8,128)(2,1)} %param.33) | copy-start | bytes 1572868
  256.2 569.6 %all-gather.23.cloned.1.call-start = ((), (), s32[]{:S(2)}) async-start(), calls=%async_computation.20 | async-start | bytes 10485760 | tf_op jit(solution)/shard_map/all_gather | solution.py:222
  266.0 140.0 %copy-start.71 = (s32[512]{0:T(512)S(1)}, s32[512]{0:T(512)}, u32[]{:S(2)}) copy-start(s32[512]{0:T(512)} %param.18) | copy-start | bytes 6148
  266.7 164.1 %copy-start.42 = (f32[2048]{0:T(1024)}, f32[2048]{0:T(1024)S(1)}, u32[]{:S(2)}) copy-start(f32[2048]{0:T(1024)S(1)} %convert_element_type.172) | copy-start | bytes 24580
  337.1 94.4 %copy-start.34 = (bf16[2048,16]{0,1:T(8,128)(2,1)}, bf16[2048,16]{0,1:T(8,128)(2,1)S(1)}, u32[]{:S(2)}) copy-start(bf16[2048,16]{0,1:T(8,128)(2,1)S(1)} %reshape.696) | copy-start | bytes 196612
  411.1 7.6 copy-start.25
  415.4 8.0 copy-start.46
  423.3 7.4 copy-start.20
  430.7 8.7 copy-start.72
  431.5 37.7 %copy-start.16 = (bf16[128,2048]{1,0:T(8,128)(2,1)}, bf16[128,2048]{1,0:T(8,128)(2,1)S(1)}, u32[]{:S(2)}) copy-start(bf16[128,2048]{1,0:T(8,128)(2,1)S(1)} %multiply_convert_fusion.3) | copy-start | bytes 1572868
  431.8 7.7 copy-start.59
  432.4 7.1 copy-start.63
  432.4 7.4 copy-start.22
  463.1 99.5 %all-to-all-start.2 = ((bf16[8,256,2048]{2,1,0:T(8,128)(2,1)}), bf16[8,256,2048]{2,1,0:T(8,128)(2,1)}, u32[]{:S(2)}, u32[]{:S(2)}) async-start(bf16[8,256,2048]{2,1,0:T(8,128)(2,1)} %bitcast.216), calls=%async_computation.2 | async-start | bytes 16777216 | tf_op jit(solution)/shard_map/all_to_all | solution.py:252
  468.5 406.3 %all-gather.27.cloned.1.call-start = ((), (), s32[]{:S(2)}) async-start(), calls=%async_computation.22 | async-start | bytes 10485760 | tf_op jit(solution)/shard_map/all_gather | solution.py:224
  562.5 226.5 %all-to-all-start = ((bf16[8,256,2048]{2,1,0:T(8,128)(2,1)}), bf16[8,256,2048]{2,1,0:T(8,128)(2,1)}, u32[]{:S(2)}, u32[]{:S(2)}) async-start(bf16[8,256,2048]{2,1,0:T(8,128)(2,1)} %bitcast.214), calls=%async_computation | async-start | bytes 16777216 | tf_op jit(solution)/shard_map/all_to_all | solution.py:217
  889.2 14.0 copy-start.78
  889.2 57.9 %copy-start.13 = (bf16[2,640,1024]{2,1,0:T(8,128)(2,1)}, bf16[2,640,1024]{2,1,0:T(8,128)(2,1)S(1)}, u32[]{:S(2)}) copy-start(bf16[2,640,1024]{2,1,0:T(8,128)(2,1)S(1)} %get-tuple-element.40) | copy-start | bytes 7864324
  942.1 99.0 %all-to-all-start.3 = ((bf16[8,256,2048]{2,1,0:T(8,128)(2,1)}), bf16[8,256,2048]{2,1,0:T(8,128)(2,1)}, u32[]{:S(2)}, u32[]{:S(2)}) async-start(bf16[8,256,2048]{2,1,0:T(8,128)(2,1)} %bitcast.217), calls=%async_computation.3 | async-start | bytes 16777216 | tf_op jit(solution)/shard_map/all_to_all | solution.py:281
  1041.2 99.2 %all-to-all-start.1 = ((bf16[8,256,2048]{2,1,0:T(8,128)(2,1)}), bf16[8,256,2048]{2,1,0:T(8,128)(2,1)}, u32[]{:S(2)}, u32[]{:S(2)}) async-start(bf16[8,256,2048]{2,1,0:T(8,128)(2,1)} %bitcast.215), calls=%async_computation.1 | async-start | bytes 16777216 | tf_op jit(solution)/shard_map/all_to_all | solution.py:236
  1046.3 197.7 %reduce-scatter.33.cloned.1.call-start = ((), (), s32[]{:S(2)}) async-start(), calls=%async_computation.31 | async-start | bytes 2621440
  1140.4 13.3 copy-start.28
  1153.7 13.1 copy-start.37
  1153.7 13.1 copy-start.60
  1153.7 13.1 copy-start.12
  1153.7 13.1 copy-start.35
  1153.7 13.1 copy-start.43
  1153.8 13.1 copy-start.62
  1158.8 8.6 copy-start.73
  1171.0 6.6 copy-start.26
  1183.4 86.7 %reduce-scatter.31.cloned.1.call-start = ((), (), s32[]{:S(2)}) async-start(), calls=%async_computation.30 | async-start | bytes 2621440
  1195.7 211.6 %reduce-scatter.35.cloned.1.call-start = ((), (), s32[]{:S(2)}) async-start(), calls=%async_computation.32 | async-start | bytes 1081344
  1197.1 354.4 %reduce-scatter.29.cloned.1.call-start = ((), (), s32[]{:S(2)}) async-start(), calls=%async_computation.29 | async-start | bytes 10485760 | tf_op jit(solution)/shard_map/reduce_scatter | solution.py:274
  1209.0 490.1 %reduce-scatter.25.cloned.1.call-start = ((), (), s32[]{:S(2)}) async-start(), calls=%async_computation.27 | async-start | bytes 10485760 | tf_op jit(solution)/shard_map/reduce_scatter | solution.py:268
  1221.6 625.0 %reduce-scatter.27.cloned.1.call-start = ((), (), s32[]{:S(2)}) async-start(), calls=%async_computation.28 | async-start | bytes 10485760 | tf_op jit(solution)/shard_map/reduce_scatter | solution.py:271
  1233.6 980.9 %reduce-scatter.23.cloned.1.call-start = ((), (), s32[]{:S(2)}) async-start(), calls=%async_computation.26 | async-start | bytes 17301504 | tf_op jit(solution)/shard_map/reduce_scatter | solution.py:351
  1243.9 1335.5 %reduce-scatter.21.cloned.1.call-start = ((), (), s32[]{:S(2)}) async-start(), calls=%async_computation.25 | async-start | bytes 17301504 | tf_op jit(solution)/shard_map/reduce_scatter | solution.py:348
  1254.2 19.9 copy-start.31
  1254.2 19.9 copy-start.33
  1254.2 1690.3 %reduce-scatter.19.cloned.1.call-start = ((), (), s32[]{:S(2)}) async-start(), calls=%async_computation.24 | async-start | bytes 17301504 | tf_op jit(solution)/shard_map/reduce_scatter | solution.py:347
  1257.7 16.4 copy-start.14
  1288.0 2021.7 %reduce-scatter.17.cloned.1.call-start = ((), (), s32[]{:S(2)}) async-start(), calls=%async_computation.23 | async-start | bytes 17301504 | tf_op jit(solution)/shard_map/reduce_scatter | solution.py:346
  1408.7 13.2 slice-start
  1415.4 6.5 slice-start.1
  1421.9 46.3 %copy-start.75 = (f32[128]{0:T(128)S(1)}, f32[128]{0:T(128)}, u32[]{:S(2)}) copy-start(f32[128]{0:T(128)} %copy-done.74) | copy-start | bytes 1540
  1421.9 46.3 %copy-start.10 = (f32[128,2048]{1,0:T(8,128)S(1)}, f32[128,2048]{1,0:T(8,128)}, u32[]{:S(2)}) copy-start(f32[128,2048]{1,0:T(8,128)} %copy-done.9) | copy-start | bytes 3145732
  (40 other events, 132.6 us)
Sparse Core Ops, SparseCore 0:
  10.9 80.4 all-gather.16
  94.3 75.9 all-gather.14
  173.3 75.9 all-gather.10
  251.3 45.9 all-gather.18
  299.2 47.6 all-gather.12
  349.8 76.1 all-gather.20
  427.6 148.2 all-gather.24
  577.4 147.9 all-gather.22
  726.9 147.8 all-gather.26
  1183.5 40.3 reduce-scatter.32
  1226.8 43.1 reduce-scatter.30
  1272.2 135.0 reduce-scatter.34
  1409.7 141.6 reduce-scatter.28
  1553.8 145.2 reduce-scatter.24
  1701.4 145.1 reduce-scatter.26
  1849.5 364.9 reduce-scatter.22
  2217.3 362.1 reduce-scatter.20
  2582.3 362.1 reduce-scatter.18
  2947.5 362.1 reduce-scatter.16
where the time goes:
time: 3330 us; the launch traced here: 3320 us
  waiting for transfers between devices  2380 us (71%)
  local copies, waits for them, and re-layouts  299 us (9%)
  blocking collectives  258 us (8%)
  matrix products  215 us (6%)
  other arithmetic  122 us (4%)
    reduce_scatter x1, waiting for transfers between devices, local(): lax.psum_scatter(query_w_grad, ('expert', 'wshard'), scatter_dimension=0,...  365 us
    reduce_scatter x1, waiting for transfers between devices, local(): lax.psum_scatter(key_w_grad, ('expert', 'wshard'), scatter_dimension=0, t...  365 us
    reduce_scatter x1, waiting for transfers between devices, local(): lax.psum_scatter(value_w_grad, ('expert', 'wshard'), scatter_dimension=0,...  365 us
    reduce_scatter x1, waiting for transfers between devices, local(): lax.psum_scatter(out_w_grad, ('expert', 'wshard'), scatter_dimension=0, t...  364 us
    reduce_scatter x1, waiting for transfers between devices, local(): lax.psum_scatter(up_w_grad.astype(jnp.bfloat16), 'wshard', scatter_dimens...  143 us
    reduce_scatter x1, waiting for transfers between devices, local(): lax.psum_scatter(gate_w_grad.astype(jnp.bfloat16), 'wshard', scatter_dime...  143 us
    unnamed x22, waiting for transfers between devices  121 us
    all_gather x1, blocking collectives, local(): lax.all_gather(pair_order, 'expert', axis=0, tiled=True)  96.4 us
  transfers between devices with their start and end apart: 23, of which 17 were waited for; matrix products, arithmetic and copies ran while one was open for 16% of the time, Pallas kernels for 0%

commit v1 on v0

v1 whole, which is shorter than its diff:
```python
import functools

import jax
import jax.numpy as jnp
import numpy as np
from jax import lax
from jax.experimental import pallas as pl
from jax.experimental.pallas import tpu as pltpu
from jax.sharding import PartitionSpec as P

HEADS = 16
HD = 128


EXPERT = "expert"
SHARD = "wshard"
BOTH = (EXPERT, SHARD)

SUM_QHD_KHD_HQK = "qhd,khd->hqk"
SUM_HQK_KHD_QHD = "hqk,khd->qhd"
SUM_ECD_EDF_ECF = "ecd,edf->ecf"
SUM_ECF_EFD_ECD = "ecf,efd->ecd"
SUM_TK_TKD_TD = "tk,tkd->td"
SUM_TD_TKD_TK = "td,tkd->tk"
SUM_ECD_EFD_ECF = "ecd,efd->ecf"
SUM_ECF_ECD_EFD = "ecf,ecd->efd"
SUM_ECD_ECF_EDF = "ecd,ecf->edf"
SUM_ECF_EDF_ECD = "ecf,edf->ecd"
SUM_HQK_QHD_KHD = "hqk,qhd->khd"
EPSILON = 1e-06
THETA = 10000.0


def matmul(left, right):
    return jnp.dot(left, right, preferred_element_type=jnp.float32)


def matmul_tn(left, right):
    return lax.dot_general(
        left, right, (((0,), (0,)), ((), ())), preferred_element_type=jnp.float32
    )


def matmul_nt(left, right):
    return lax.dot_general(
        left, right, (((1,), (1,)), ((), ())), preferred_element_type=jnp.float32
    )


def rms_scale(values, scale_gain):
    factor = lax.rsqrt(jnp.mean(values * values, axis=-1, keepdims=True) + EPSILON)
    return values * factor * scale_gain


def rope_tables(positions):
    exponent = jnp.arange(HD // 2, dtype=jnp.float32) * (2.0 / HD)
    frequency = jnp.power(jnp.float32(THETA), -exponent)
    angles = positions.astype(jnp.float32)[:, None] * frequency[None, :]
    return (jnp.cos(angles), jnp.sin(angles))


def rotate(values, cosine, sine):
    first_half = values[..., : HD // 2]
    second_half = values[..., HD // 2 :]
    cos_part = cosine[:, None, :]
    sin_part = sine[:, None, :]
    return jnp.concatenate(
        [
            first_half * cos_part - second_half * sin_part,
            second_half * cos_part + first_half * sin_part,
        ],
        axis=-1,
    )


def padded_rows(rows):
    return jnp.concatenate([jnp.zeros((1,) + rows.shape[1:], rows.dtype), rows], axis=0)


def masked_scores(query_rot, key_rot, query_segment, key_segment):
    scores = jnp.einsum(SUM_QHD_KHD_HQK, query_rot, key_rot, preferred_element_type=jnp.float32)
    allowed = query_segment[:, None] == key_segment[None, :]
    return jnp.where(allowed[None], scores, -1e30)


def swiglu_fn(gate_in, up_in):
    return jax.nn.silu(gate_in) * up_in


def general_local(
    tokens,
    segment_ids,
    routes,
    pair_order,
    attn_gain,
    w_query,
    w_key,
    w_value,
    query_gain,
    key_gain,
    w_out,
    ffn_gain,
    w_router,
    w_gate,
    w_up,
    w_down,
    out_grad,
):
    tok_rows, width = tokens.shape
    top_count = routes.shape[1]
    expert_devs = lax.axis_size(EXPERT)
    shard_devs = lax.axis_size(SHARD)
    local_experts = w_gate.shape[0]
    expert_count = local_experts * expert_devs
    most_rows = 2 * tok_rows * top_count // expert_count
    capacity = 5 * tok_rows * top_count // (4 * local_experts)
    seq_length = segment_ids.shape[0]
    device_expert = lax.axis_index(EXPERT)
    device_shard = lax.axis_index(SHARD)
    low_type = jnp.bfloat16
    wide_type = jnp.float32
    gathered = (
        lax.all_gather(attn_gain, BOTH, axis=0, tiled=True),
        lax.all_gather(w_query, BOTH, axis=0, tiled=True),
        lax.all_gather(w_key, BOTH, axis=0, tiled=True),
        lax.all_gather(w_value, BOTH, axis=0, tiled=True),
        lax.all_gather(query_gain, BOTH, axis=0, tiled=True),
        lax.all_gather(key_gain, BOTH, axis=0, tiled=True),
        lax.all_gather(w_out, BOTH, axis=0, tiled=True),
        lax.all_gather(ffn_gain, BOTH, axis=0, tiled=True),
        lax.all_gather(w_router, BOTH, axis=0, tiled=True),
    )
    attn_scale = gathered[0].astype(wide_type)
    query_w, key_w, value_w = (gathered[1], gathered[2], gathered[3])
    query_scale = gathered[4].astype(wide_type)
    key_scale = gathered[5].astype(wide_type)
    out_w = gathered[6]
    ffn_scale = gathered[7].astype(wide_type)
    router_w = gathered[8]
    inputs = tokens.astype(wide_type)
    normed, norm_one_pull = jax.vjp(rms_scale, inputs, attn_scale)
    normed_low = normed.astype(low_type)
    query_raw = matmul(normed_low, query_w)
    key_raw = matmul(normed_low, key_w)
    value_low = matmul(normed_low, value_w).astype(low_type)
    positions = device_shard * tok_rows + jnp.arange(tok_rows, dtype=jnp.int32)
    cosine, sine = rope_tables(positions)

    def prepare(query_in, key_in, query_g, key_g):
        query_heads = rms_scale(query_in.reshape(tok_rows, HEADS, HD), query_g)
        key_heads = rms_scale(key_in.reshape(tok_rows, HEADS, HD), key_g)
        return (rotate(query_heads, cosine, sine) * HD ** (-0.5), rotate(key_heads, cosine, sine))

    rotated, prepare_pull = jax.vjp(prepare, query_raw, key_raw, query_scale, key_scale)
    query_low = rotated[0].astype(low_type)
    key_low = rotated[1].astype(low_type).reshape(tok_rows, width)
    seq_keys, seq_values = (
        lax.all_gather(key_low, SHARD, axis=0, tiled=True),
        lax.all_gather(value_low, SHARD, axis=0, tiled=True),
    )
    query_segment = lax.dynamic_slice_in_dim(segment_ids, device_shard * tok_rows, tok_rows)
    scores = masked_scores(
        query_low, seq_keys.reshape(seq_length, HEADS, HD), query_segment, segment_ids
    )
    row_max = jnp.max(scores, axis=-1, keepdims=True)
    shifted = jnp.exp(scores - row_max)
    totals = jnp.sum(shifted, axis=-1, keepdims=True)
    log_total = row_max + jnp.log(totals)
    probs_low = (shifted / totals).astype(low_type)
    mixed = jnp.einsum(
        SUM_HQK_KHD_QHD,
        probs_low,
        seq_values.reshape(seq_length, HEADS, HD),
        preferred_element_type=wide_type,
    )
    mixed_low = mixed.reshape(tok_rows, width).astype(low_type)
    hidden = inputs + matmul(mixed_low, out_w)
    normed_two, norm_two_pull = jax.vjp(rms_scale, hidden, ffn_scale)
    normed_two_low = normed_two.astype(low_type)
    logits = matmul(normed_two_low, router_w)

    def router_weights(logit_values):
        return jnp.take_along_axis(jax.nn.softmax(logit_values, axis=-1), routes, axis=1)

    route_weight, route_pull = jax.vjp(router_weights, logits)
    group_routes, group_order = (
        lax.all_gather(routes, EXPERT, axis=0, tiled=True),
        lax.all_gather(pair_order, EXPERT, axis=0, tiled=True),
    )
    per_source = tok_rows * top_count
    group_pairs = per_source * expert_devs
    expert_of = group_routes.reshape(-1)
    pair_index = jnp.arange(group_pairs, dtype=jnp.int32)
    source_of = pair_index // per_source
    expert_ids = jnp.arange(expert_count, dtype=jnp.int32)
    onehot = (expert_of.reshape(expert_devs, per_source, 1) == expert_ids).astype(jnp.int32)
    position_of = (jnp.sum(jnp.cumsum(onehot, axis=1) * onehot, axis=-1) - 1).reshape(-1)
    order_span = group_pairs * shard_devs
    sort_keys = expert_of * order_span + group_order
    sorted_pairs = jnp.argsort(sort_keys)
    placement = jnp.zeros((group_pairs,), jnp.int32).at[sorted_pairs].set(pair_index)
    expert_counts = jnp.sum(onehot, axis=(0, 1))
    expert_start = jnp.cumsum(expert_counts) - expert_counts
    start_of = jnp.sum(onehot.reshape(group_pairs, expert_count) * expert_start[None, :], axis=-1)
    slot_rank = placement - start_of
    retained = slot_rank < capacity
    own_expert = routes.reshape(-1)
    own_position = lax.dynamic_slice_in_dim(position_of, device_expert * per_source, per_source)
    send_slot = own_expert * most_rows + own_position
    send_pair = (
        jnp.zeros((expert_count * most_rows,), jnp.int32)
        .at[send_slot]
        .set(jnp.arange(per_source, dtype=jnp.int32) + 1)
    )
    send_token = jnp.where(send_pair > 0, (send_pair - 1) // top_count + 1, 0)
    owner_local = expert_of % local_experts
    is_mine = expert_of // local_experts == device_expert
    recv_row = source_of * (local_experts * most_rows) + owner_local * most_rows + position_of
    slot_target = jnp.where(
        is_mine & retained, owner_local * capacity + slot_rank, local_experts * capacity
    )
    slot_source = (
        jnp.zeros((local_experts * capacity,), jnp.int32)
        .at[slot_target]
        .set(recv_row + 1, mode="drop")
    )
    back_room = expert_devs * local_experts * most_rows
    back_target = jnp.where(is_mine, recv_row, back_room)
    back_source = (
        jnp.zeros((back_room,), jnp.int32)
        .at[back_target]
        .set(jnp.where(retained, owner_local * capacity + slot_rank + 1, 0), mode="drop")
    )
    send_rows = padded_rows(normed_two_low)[send_token].reshape(
        expert_devs, local_experts * most_rows, width
    )
    recv_rows = lax.all_to_all(
        send_rows, EXPERT, split_axis=0, concat_axis=0, tiled=True
    ).reshape(-1, width)
    slot_rows = padded_rows(recv_rows)[slot_source].reshape(local_experts, capacity, width)
    full_gate, full_up, full_down = (
        lax.all_gather(w_gate, SHARD, axis=1, tiled=True),
        lax.all_gather(w_up, SHARD, axis=1, tiled=True),
        lax.all_gather(w_down, SHARD, axis=2, tiled=True),
    )
    gate_act = jnp.einsum(SUM_ECD_EDF_ECF, slot_rows, full_gate, preferred_element_type=wide_type)
    up_act = jnp.einsum(SUM_ECD_EDF_ECF, slot_rows, full_up, preferred_element_type=wide_type)
    swiglu_out, swiglu_pull = jax.vjp(swiglu_fn, gate_act, up_act)
    swiglu_low = swiglu_out.astype(low_type)
    expert_out = jnp.einsum(
        SUM_ECF_EFD_ECD, swiglu_low, full_down, preferred_element_type=wide_type
    ).astype(low_type)
    back_rows = padded_rows(expert_out.reshape(-1, width))[back_source].reshape(
        expert_devs, local_experts * most_rows, width
    )
    returned = lax.all_to_all(back_rows, EXPERT, split_axis=0, concat_axis=0, tiled=True).reshape(
        -1, width
    )
    pair_rows = returned[send_slot].reshape(tok_rows, top_count, width)
    combined = jnp.einsum(SUM_TK_TKD_TD, route_weight, pair_rows, preferred_element_type=wide_type)
    mixed_out = (hidden + combined).astype(low_type)
    result_grad = out_grad.astype(wide_type)
    weight_grad = jnp.einsum(SUM_TD_TKD_TK, result_grad, pair_rows, preferred_element_type=wide_type)
    pair_grad = (
        (route_weight[:, :, None] * result_grad[:, None, :])
        .astype(low_type)
        .reshape(per_source, width)
    )
    send_grad = padded_rows(pair_grad)[send_pair].reshape(
        expert_devs, local_experts * most_rows, width
    )
    recv_grad = lax.all_to_all(
        send_grad, EXPERT, split_axis=0, concat_axis=0, tiled=True
    ).reshape(-1, width)
    slot_grad = padded_rows(recv_grad)[slot_source].reshape(local_experts, capacity, width)
    act_grad = jnp.einsum(SUM_ECD_EFD_ECF, slot_grad, full_down, preferred_element_type=wide_type)
    down_grad = jnp.einsum(SUM_ECF_ECD_EFD, swiglu_low, slot_grad, preferred_element_type=wide_type)
    gate_grad, up_grad = swiglu_pull(act_grad)
    gate_low = gate_grad.astype(low_type)
    up_low = up_grad.astype(low_type)
    gate_w_grad = jnp.einsum(SUM_ECD_ECF_EDF, slot_rows, gate_low, preferred_element_type=wide_type)
    up_w_grad = jnp.einsum(SUM_ECD_ECF_EDF, slot_rows, up_low, preferred_element_type=wide_type)
    slot_in_grad = jnp.einsum(SUM_ECF_EDF_ECD, gate_low, full_gate, preferred_element_type=wide_type)
    slot_in_grad = (
        slot_in_grad + jnp.einsum(SUM_ECF_EDF_ECD, up_low, full_up, preferred_element_type=wide_type)
    ).astype(low_type)
    gate_shard, up_shard, down_shard = (
        lax.psum_scatter(
            gate_w_grad.astype(jnp.bfloat16), SHARD, scatter_dimension=1, tiled=True
        ).astype(jnp.float32),
        lax.psum_scatter(
            up_w_grad.astype(jnp.bfloat16), SHARD, scatter_dimension=1, tiled=True
        ).astype(jnp.float32),
        lax.psum_scatter(
            down_grad.astype(jnp.bfloat16), SHARD, scatter_dimension=2, tiled=True
        ).astype(jnp.float32),
    )
    back_grad = padded_rows(slot_in_grad.reshape(-1, width))[back_source].reshape(
        expert_devs, local_experts * most_rows, width
    )
    returned_grad = lax.all_to_all(
        back_grad, EXPERT, split_axis=0, concat_axis=0, tiled=True
    ).reshape(-1, width)
    expert_in_grad = jnp.sum(
        returned_grad[send_slot].reshape(tok_rows, top_count, width).astype(wide_type), axis=1
    )
    logit_grad = route_pull(weight_grad)[0]
    logit_low = logit_grad.astype(low_type)
    router_grad = matmul_tn(normed_two_low, logit_low)
    normed_two_grad = expert_in_grad + matmul_nt(logit_low, router_w)
    hidden_norm_grad, ffn_scale_grad = norm_two_pull(normed_two_grad)
    hidden_grad = result_grad + hidden_norm_grad
    attn_low = hidden_grad.astype(low_type)
    out_w_grad = matmul_tn(mixed_low, attn_low)
    mixed_grad = matmul_nt(attn_low, out_w).astype(low_type).reshape(tok_rows, HEADS, HD)
    back_keys, back_values = (seq_keys, seq_values)
    key_heads = back_keys.reshape(seq_length, HEADS, HD)
    value_heads = back_values.reshape(seq_length, HEADS, HD)
    scores_again = masked_scores(query_low, key_heads, query_segment, segment_ids)
    probs_again = jnp.exp(scores_again - log_total)
    probs_again_low = probs_again.astype(low_type)
    prob_grad = jnp.einsum(
        SUM_QHD_KHD_HQK, mixed_grad, value_heads, preferred_element_type=wide_type
    )
    value_part = jnp.einsum(
        SUM_HQK_QHD_KHD, probs_again_low, mixed_grad, preferred_element_type=wide_type
    )
    row_inner = jnp.sum(probs_again * prob_grad, axis=-1, keepdims=True)
    score_low = (probs_again * (prob_grad - row_inner)).astype(low_type)
    query_rot_grad = jnp.einsum(
        SUM_HQK_KHD_QHD, score_low, key_heads, preferred_element_type=wide_type
    )
    key_part = jnp.einsum(SUM_HQK_QHD_KHD, score_low, query_low, preferred_element_type=wide_type)
    key_rot_grad, value_grad = (
        lax.psum_scatter(
            key_part.reshape(seq_length, width).astype(jnp.bfloat16),
            SHARD,
            scatter_dimension=0,
            tiled=True,
        ).astype(jnp.float32),
        lax.psum_scatter(
            value_part.reshape(seq_length, width).astype(jnp.bfloat16),
            SHARD,
            scatter_dimension=0,
            tiled=True,
        ).astype(jnp.float32),
    )
    query_raw_grad, key_raw_grad, query_scale_grad, key_scale_grad = prepare_pull(
        (query_rot_grad, key_rot_grad.reshape(tok_rows, HEADS, HD))
    )
    query_grad_low = query_raw_grad.astype(low_type)
    key_grad_low = key_raw_grad.astype(low_type)
    value_grad_low = value_grad.astype(low_type)
    query_w_grad = matmul_tn(normed_low, query_grad_low)
    key_w_grad = matmul_tn(normed_low, key_grad_low)
    value_w_grad = matmul_tn(normed_low, value_grad_low)
    normed_grad = (
        matmul_nt(query_grad_low, query_w)
        + matmul_nt(key_grad_low, key_w)
        + matmul_nt(value_grad_low, value_w)
    )
    input_norm_grad, attn_scale_grad = norm_one_pull(normed_grad)
    input_grad = (hidden_grad + input_norm_grad).astype(low_type)
    summed = (
        lax.psum_scatter(attn_scale_grad, BOTH, scatter_dimension=0, tiled=True),
        lax.psum_scatter(query_w_grad, BOTH, scatter_dimension=0, tiled=True),
        lax.psum_scatter(key_w_grad, BOTH, scatter_dimension=0, tiled=True),
        lax.psum_scatter(value_w_grad, BOTH, scatter_dimension=0, tiled=True),
        lax.psum_scatter(query_scale_grad, BOTH, scatter_dimension=0, tiled=True),
        lax.psum_scatter(key_scale_grad, BOTH, scatter_dimension=0, tiled=True),
        lax.psum_scatter(out_w_grad, BOTH, scatter_dimension=0, tiled=True),
        lax.psum_scatter(ffn_scale_grad, BOTH, scatter_dimension=0, tiled=True),
        lax.psum_scatter(router_grad, BOTH, scatter_dimension=0, tiled=True),
    )
    return (
        mixed_out,
        input_grad,
        summed[0],
        summed[1],
        summed[2],
        summed[3],
        summed[4],
        summed[5],
        summed[6],
        summed[7],
        summed[8],
        gate_shard,
        up_shard,
        down_shard,
    )


MIB = 1 << 20


def nt_dot(left, right):
    return lax.dot_general(
        left, right, (((1,), (1,)), ((), ())), preferred_element_type=jnp.float32
    )


def tn_dot(left, right):
    return lax.dot_general(
        left, right, (((0,), (0,)), ((), ())), preferred_element_type=jnp.float32
    )


def vmem_params(mib):
    return pltpu.CompilerParams(vmem_limit_bytes=mib * MIB)


def turn_tables(length):
    exponent = np.arange(HD // 2, dtype=np.float32) * np.float32(2.0 / HD)
    frequency = np.power(np.float32(THETA), -exponent).astype(np.float32)
    angles = np.arange(length, dtype=np.float32)[:, None] * frequency[None, :]
    cosine, sine = np.cos(angles), np.sin(angles)
    return (
        jnp.asarray(np.concatenate([cosine, cosine], axis=1), jnp.float32),
        jnp.asarray(np.concatenate([-sine, sine], axis=1), jnp.float32),
    )


def norm_factor(values):
    return lax.rsqrt(jnp.mean(values * values, axis=-1, keepdims=True) + EPSILON)


def attend_kernel(
    tokens, gain, weight, query_gain, key_gain, cosine, sine, seg_row, seg_col,
    normed_out, raw_out, low_out, mixed_out, total_out, qkv,
):
    part = mixed_out.shape[1]
    values = tokens[...].astype(jnp.float32)
    normed = (values * norm_factor(values) * gain[...]).astype(jnp.bfloat16)
    normed_out[...] = normed
    qkv[...] = jnp.dot(normed, weight[...], preferred_element_type=jnp.float32)
    raw_out[...] = qkv[:, : 2 * part]
    low_out[:, 2 * part :] = qkv[:, 2 * part :].astype(jnp.bfloat16)
    allowed = seg_col[...] == seg_row[...]
    for head in range(part // HD):
        span = pl.ds(head * HD, HD)
        for offset, scale_gain, scale in ((0, query_gain, HD ** (-0.5)), (part, key_gain, 1.0)):
            raw = qkv[:, pl.ds(offset + head * HD, HD)]
            unit = raw * norm_factor(raw) * scale_gain[...]
            turned = unit * cosine[...] + pltpu.roll(unit, HD // 2, 1) * sine[...]
            low_out[:, pl.ds(offset + head * HD, HD)] = (turned * scale).astype(jnp.bfloat16)
        query, key = low_out[:, span], low_out[:, pl.ds(part + head * HD, HD)]
        scores = jnp.where(allowed, nt_dot(query, key), -1e30)
        top = jnp.max(scores, axis=-1, keepdims=True)
        shifted = jnp.exp(scores - top)
        total = jnp.sum(shifted, axis=-1, keepdims=True)
        probs = (shifted / total).astype(jnp.bfloat16)
        mixed = jnp.dot(
            probs, low_out[:, pl.ds(2 * part + head * HD, HD)], preferred_element_type=jnp.float32
        )
        mixed_out[:, span] = mixed.astype(jnp.bfloat16)
        total_out[:, head : head + 1] = top + jnp.log(total)


def attend_call(tokens, gain, weight, query_gain, key_gain, tables, seg_row, seg_col):
    seq, width = tokens.shape
    part = weight.shape[1] // 3
    return pl.pallas_call(
        attend_kernel,
        out_shape=(
            jax.ShapeDtypeStruct((seq, width), jnp.bfloat16),
            jax.ShapeDtypeStruct((seq, 2 * part), jnp.float32),
            jax.ShapeDtypeStruct((seq, 3 * part), jnp.bfloat16),
            jax.ShapeDtypeStruct((seq, part), jnp.bfloat16),
            jax.ShapeDtypeStruct((seq, 128), jnp.float32),
        ),
        scratch_shapes=[pltpu.VMEM((seq, 3 * part), jnp.float32)],
        compiler_params=vmem_params(52),
        cost_estimate=pl.CostEstimate(
            flops=2 * seq * width * 3 * part, bytes_accessed=16 * MIB, transcendentals=seq * seq * 4
        ),
    )(tokens, gain, weight, query_gain, key_gain, *tables, seg_row, seg_col)


def join_kernel(mixed, weight, tokens, gain, hidden_out, normed_out):
    shards, _, part = mixed.shape
    total = tokens[...].astype(jnp.float32)
    for shard in range(shards):
        total = total + jnp.dot(
            mixed[shard], weight[pl.ds(shard * part, part), :], preferred_element_type=jnp.float32
        )
    hidden_out[...] = total
    normed_out[...] = (total * norm_factor(total) * gain[...]).astype(jnp.bfloat16)


def join_call(mixed, weight, tokens, gain):
    shards, seq, part = mixed.shape
    width = weight.shape[1]
    tile = seq // 2
    return pl.pallas_call(
        join_kernel,
        grid=(2,),
        in_specs=[
            pl.BlockSpec((shards, tile, part), lambda i: (0, i, 0)),
            pl.BlockSpec(weight.shape, lambda i: (0, 0), pipeline_mode=pl.Buffered(1)),
            pl.BlockSpec((tile, width), lambda i: (i, 0)),
            pl.BlockSpec((1, width), lambda i: (0, 0)),
        ],
        out_specs=[
            pl.BlockSpec((tile, width), lambda i: (i, 0)),
            pl.BlockSpec((tile, width), lambda i: (i, 0)),
        ],
        out_shape=(
            jax.ShapeDtypeStruct((seq, width), jnp.float32),
            jax.ShapeDtypeStruct((seq, width), jnp.bfloat16),
        ),
        compiler_params=vmem_params(40),
        cost_estimate=pl.CostEstimate(
            flops=2 * seq * width * width, bytes_accessed=18 * MIB, transcendentals=0
        ),
    )(mixed, weight, tokens, gain)


def expert_kernel(
    first, experts, blocks, x, g, keep, wide_w, router_w, down_w, hot, *refs
):
    del blocks
    if first:
        out, grad, wide_sum, router_sum, down_sum, acc, racc, dacc, sems = refs
    else:
        wide_in, router_in, down_in, out, grad, wide_sum, router_sum, down_sum = refs[:8]
        acc, racc, dacc, sems = refs[8:]
    step, steps = pl.program_id(0), pl.num_programs(0)

    @pl.when(step == 0)
    def _():
        if first:
            acc[...] = jnp.zeros_like(acc)
            racc[...] = jnp.zeros_like(racc)
            dacc[...] = jnp.zeros_like(dacc)
        else:
            pltpu.make_async_copy(wide_in, acc, sems.at[0]).start()
            pltpu.make_async_copy(router_in, racc, sems.at[1]).start()
            pltpu.make_async_copy(down_in, dacc, sems.at[2]).start()

    shards, units, part = down_w.shape
    own = keep.shape[1]
    each = units // own
    wide = jnp.dot(x[...], wide_w[...], preferred_element_type=jnp.float32)
    logits = jnp.dot(x[...], router_w[...], preferred_element_type=jnp.float32)
    back = nt_dot(g[:, :part], down_w[0])
    for shard in range(1, shards):
        back = back + nt_dot(g[:, shard * part : (shard + 1) * part], down_w[shard])
    lane = lax.broadcasted_iota(jnp.int32, logits.shape, 1)
    logits = jnp.where(lane < experts, logits, -1e30)
    shifted = jnp.exp(logits - jnp.max(logits, axis=-1, keepdims=True))
    probs = shifted / jnp.sum(shifted, axis=-1, keepdims=True)
    dense = jnp.zeros_like(probs)
    acts, gates, ups = [], [], []
    for index in range(own):
        mark = hot[index : index + 1, :]
        kept = keep[:, index : index + 1]
        route = jnp.sum(probs * mark, axis=-1, keepdims=True) * kept
        gate = wide[:, index * each : (index + 1) * each]
        up = wide[:, units + index * each : units + (index + 1) * each]
        behind = back[:, index * each : (index + 1) * each]
        sigma = 1.0 / (1.0 + jnp.exp(-gate))
        silu = gate * sigma
        act = silu * up
        dense = dense + jnp.sum(act * behind, axis=-1, keepdims=True) * kept * mark
        acts.append((act * route).astype(jnp.bfloat16))
        act_grad = behind * route
        gates.append((act_grad * up * sigma * (1.0 + gate * (1.0 - sigma))).astype(jnp.bfloat16))
        ups.append((act_grad * silu).astype(jnp.bfloat16))
    logit_grad = probs * (dense - jnp.sum(probs * dense, axis=-1, keepdims=True))
    logit_low = logit_grad.astype(jnp.bfloat16)
    act_low = jnp.concatenate(acts, axis=1)
    wide_low = jnp.concatenate(gates + ups, axis=1)
    for shard in range(shards):
        out[:, shard * part : (shard + 1) * part] = jnp.dot(
            act_low, down_w[shard], preferred_element_type=jnp.float32
        ).astype(jnp.bfloat16)
    grad[...] = (nt_dot(wide_low, wide_w[...]) + nt_dot(logit_low, router_w[...])).astype(
        jnp.bfloat16
    )
    if not first:

        @pl.when(step == 0)
        def _():
            pltpu.make_async_copy(wide_in, acc, sems.at[0]).wait()
            pltpu.make_async_copy(router_in, racc, sems.at[1]).wait()
            pltpu.make_async_copy(down_in, dacc, sems.at[2]).wait()

    acc[...] += tn_dot(x[...], wide_low)
    racc[...] += tn_dot(x[...], logit_low)
    for shard in range(shards):
        dacc[shard] += tn_dot(act_low, g[:, shard * part : (shard + 1) * part])

    @pl.when(step == steps - 1)
    def _():
        copies = [
            pltpu.make_async_copy(acc, wide_sum, sems.at[0]),
            pltpu.make_async_copy(racc, router_sum, sems.at[1]),
            pltpu.make_async_copy(dacc, down_sum, sems.at[2]),
        ]
        for copy in copies:
            copy.start()
        for copy in copies:
            copy.wait()


def expert_call(blocks, x_all, g_all, keep, wide_w, router_w, down_w, hot, experts, sums):
    _, rows, width = x_all.shape
    count = blocks.shape[0]
    tile = 256
    per = rows // tile
    hbm = pl.BlockSpec(memory_space=pl.ANY)

    def whole(value):
        zeros = (0,) * value.ndim
        return pl.BlockSpec(value.shape, lambda i, b: zeros, pipeline_mode=pl.Buffered(1))

    def chosen(lanes):
        return pl.BlockSpec((None, tile, lanes), lambda i, b: (b[i // per], i % per, 0))

    rowwise = pl.BlockSpec((None, tile, width), lambda i, b: (i // per, i % per, 0))
    shapes = (
        jax.ShapeDtypeStruct(wide_w.shape, jnp.float32),
        jax.ShapeDtypeStruct(router_w.shape, jnp.float32),
        jax.ShapeDtypeStruct(down_w.shape, jnp.float32),
    )
    first = sums is None
    result = pl.pallas_call(
        functools.partial(expert_kernel, first, experts),
        grid_spec=pltpu.PrefetchScalarGridSpec(
            num_scalar_prefetch=1,
            grid=(count * per,),
            in_specs=[
                chosen(width),
                chosen(width),
                chosen(keep.shape[2]),
                whole(wide_w),
                whole(router_w),
                whole(down_w),
                whole(hot),
            ]
            + ([] if first else [hbm] * 3),
            out_specs=[rowwise, rowwise, hbm, hbm, hbm],
            scratch_shapes=[
                pltpu.VMEM(wide_w.shape, jnp.float32),
                pltpu.VMEM(router_w.shape, jnp.float32),
                pltpu.VMEM(down_w.shape, jnp.float32),
                pltpu.SemaphoreType.DMA((3,)),
            ],
        ),
        out_shape=(
            jax.ShapeDtypeStruct((count, rows, width), jnp.bfloat16),
            jax.ShapeDtypeStruct((count, rows, width), jnp.bfloat16),
        )
        + shapes,
        input_output_aliases={} if first else {8: 2, 9: 3, 10: 4},
        compiler_params=vmem_params(56),
        cost_estimate=pl.CostEstimate(
            flops=2 * count * rows * width * (3 * wide_w.shape[1] + 3 * down_w.shape[1]),
            bytes_accessed=40 * MIB,
            transcendentals=count * rows * down_w.shape[1],
        ),
    )(blocks, x_all, g_all, keep, wide_w, router_w, down_w, hot, *(() if first else sums))
    return result[0], result[1], result[2:]


def turn_back_kernel(
    hidden, grad, out_grad, gain, weight, hidden_grad_out, low_out, message_out, gain_grad_out
):
    shards, _, part = message_out.shape
    factor = norm_factor(hidden[...])
    gain_grad_out[...] = jnp.sum(grad[...] * hidden[...] * factor, axis=0, keepdims=True)
    scaled = grad[...] * gain[...]
    inner = jnp.mean(scaled * hidden[...], axis=-1, keepdims=True)
    total = out_grad[...].astype(jnp.float32) + factor * scaled
    total = total - hidden[...] * (factor * factor * factor) * inner
    hidden_grad_out[...] = total
    low = total.astype(jnp.bfloat16)
    low_out[...] = low
    for shard in range(shards):
        message_out[shard] = nt_dot(low, weight[pl.ds(shard * part, part), :]).astype(jnp.bfloat16)


def turn_back_call(hidden, grad, out_grad, gain, weight, shards):
    rows, width = hidden.shape
    return pl.pallas_call(
        turn_back_kernel,
        out_shape=(
            jax.ShapeDtypeStruct((rows, width), jnp.float32),
            jax.ShapeDtypeStruct((rows, width), jnp.bfloat16),
            jax.ShapeDtypeStruct((shards, rows, width // shards), jnp.bfloat16),
            jax.ShapeDtypeStruct((1, width), jnp.float32),
        ),
        compiler_params=vmem_params(40),
        cost_estimate=pl.CostEstimate(
            flops=2 * rows * width * width, bytes_accessed=12 * MIB, transcendentals=0
        ),
    )(hidden, grad, out_grad, gain, weight)


def attend_back_kernel(
    mixed_grad, raw, low, total, weight, query_gain, key_gain, cosine, sine, seg_row, seg_col,
    qkv_grad_out, normed_grad_out, query_gain_out, key_gain_out,
):
    part = mixed_grad.shape[1]
    allowed = seg_col[...] == seg_row[...]
    gain_sums = [None, None]
    for head in range(part // HD):
        span = pl.ds(head * HD, HD)
        query, key = low[:, span], low[:, pl.ds(part + head * HD, HD)]
        value = low[:, pl.ds(2 * part + head * HD, HD)]
        out_grad = mixed_grad[:, span]
        scores = jnp.where(allowed, nt_dot(query, key), -1e30)
        probs = jnp.exp(scores - total[:, head : head + 1])
        prob_grad = nt_dot(out_grad, value)
        value_grad = tn_dot(probs.astype(jnp.bfloat16), out_grad)
        qkv_grad_out[:, pl.ds(2 * part + head * HD, HD)] = value_grad.astype(jnp.bfloat16)
        inner = jnp.sum(probs * prob_grad, axis=-1, keepdims=True)
        score_grad = (probs * (prob_grad - inner)).astype(jnp.bfloat16)
        rotated = (
            jnp.dot(score_grad, key, preferred_element_type=jnp.float32) * HD ** (-0.5),
            tn_dot(score_grad, query),
        )
        for which, (offset, scale_gain) in enumerate(((0, query_gain), (part, key_gain))):
            grad = rotated[which]
            grad = grad * cosine[...] - pltpu.roll(grad, HD // 2, 1) * sine[...]
            source = raw[:, pl.ds(offset + head * HD, HD)]
            factor = norm_factor(source)
            gain_sum = jnp.sum(grad * source * factor, axis=0, keepdims=True)
            gain_sums[which] = gain_sum if head == 0 else gain_sums[which] + gain_sum
            scaled = grad * scale_gain[...]
            inner = jnp.mean(scaled * source, axis=-1, keepdims=True)
            result = factor * scaled - source * (factor * factor * factor) * inner
            qkv_grad_out[:, pl.ds(offset + head * HD, HD)] = result.astype(jnp.bfloat16)
    query_gain_out[...] = gain_sums[0]
    key_gain_out[...] = gain_sums[1]
    normed_grad_out[...] = nt_dot(qkv_grad_out[...], weight[...]).astype(jnp.bfloat16)


def attend_back_call(
    mixed_grad, raw, low, total, weight, query_gain, key_gain, tables, seg_row, seg_col
):
    seq = mixed_grad.shape[0]
    width = weight.shape[0]
    return pl.pallas_call(
        attend_back_kernel,
        out_shape=(
            jax.ShapeDtypeStruct(low.shape, jnp.bfloat16),
            jax.ShapeDtypeStruct((seq, width), jnp.bfloat16),
            jax.ShapeDtypeStruct((1, HD), jnp.float32),
            jax.ShapeDtypeStruct((1, HD), jnp.float32),
        ),
        compiler_params=vmem_params(52),
        cost_estimate=pl.CostEstimate(
            flops=2 * seq * width * low.shape[1], bytes_accessed=16 * MIB, transcendentals=seq * seq * 4
        ),
    )(mixed_grad, raw, low, total, weight, query_gain, key_gain, *tables, seg_row, seg_col)


def finish_kernel(pieces, tokens, hidden_grad, gain, grad_out, gain_grad_out):
    grad = pieces[0].astype(jnp.float32)
    for shard in range(1, pieces.shape[0]):
        grad = grad + pieces[shard].astype(jnp.float32)
    values = tokens[...].astype(jnp.float32)
    factor = norm_factor(values)
    gain_grad_out[...] = jnp.sum(grad * values * factor, axis=0, keepdims=True)
    scaled = grad * gain[...]
    inner = jnp.mean(scaled * values, axis=-1, keepdims=True)
    total = hidden_grad[...] + factor * scaled - values * (factor * factor * factor) * inner
    grad_out[...] = total.astype(jnp.bfloat16)


def finish_call(pieces, tokens, hidden_grad, gain):
    rows, width = tokens.shape
    return pl.pallas_call(
        finish_kernel,
        out_shape=(
            jax.ShapeDtypeStruct((rows, width), jnp.bfloat16),
            jax.ShapeDtypeStruct((1, width), jnp.float32),
        ),
        compiler_params=vmem_params(24),
    )(pieces, tokens, hidden_grad, gain)


def copy_kernel(*refs):
    half = len(refs) // 2
    for source, result in zip(refs[:half], refs[half:], strict=True):
        result[...] = source[...].reshape(result.shape).astype(result.dtype)


def unpack_units(wide, narrow, own):
    shards, part, count = wide.shape
    each = count // (2 * own)
    gate = pl.BlockSpec((1, part, each), lambda e, s: (s, 0, e))
    up = pl.BlockSpec((1, part, each), lambda e, s: (s, 0, own + e))
    result = pl.BlockSpec((1, part, each), lambda e, s: (e, 0, s))
    shape = jax.ShapeDtypeStruct((own, part, shards * each), jnp.float32)
    gate_grad, up_grad = pl.pallas_call(
        copy_kernel,
        grid=(own, shards),
        in_specs=[gate, up],
        out_specs=[result, result],
        out_shape=[shape, shape],
        compiler_params=vmem_params(16),
    )(wide, wide)
    down_grad = pl.pallas_call(
        copy_kernel,
        grid=(own, shards),
        in_specs=[pl.BlockSpec((1, each, part), lambda e, s: (s, e, 0))],
        out_specs=[pl.BlockSpec((1, each, part), lambda e, s: (e, s, 0))],
        out_shape=[jax.ShapeDtypeStruct((own, shards * each, part), jnp.float32)],
        compiler_params=vmem_params(16),
    )(narrow)[0]
    return gate_grad, up_grad, down_grad


CORE, XBIT, YBIT = 1, 2, 4


MESH = pl.DeviceIdType.MESH


class Wires:
    def __init__(self, send, recv):
        self.send, self.recv, self.used = send, recv, 0
        self.device, self.shard = lax.axis_index(EXPERT), lax.axis_index(SHARD)

    def slot(self):
        self.used += 1
        return self.used - 1

    def peer(self, bits=0, step=0, shards=1):
        shard = lax.rem(self.shard + step, shards) if step else self.shard
        return (self.device ^ bits, shard)

    def copy(self, source, target, slot, peer):
        return pltpu.make_async_remote_copy(
            src_ref=source,
            dst_ref=target,
            send_sem=self.send.at[slot],
            recv_sem=self.recv.at[slot],
            device_id=peer,
            device_id_type=MESH,
        )


def greet(peers):
    barrier = pltpu.get_barrier_semaphore()
    for peer in peers:
        pl.semaphore_signal(barrier, inc=1, device_id=peer, device_id_type=MESH)
    pl.semaphore_wait(barrier, len(peers))


class Relay:
    def __init__(self, wires, shards, views):
        self.wires, self.shards, self.views = wires, shards, views
        self.slots = [[[wires.slot() for _ in views] for _ in range(shards - 1)] for _ in range(2)]

    def copies(self, way, step, block):
        wires = self.wires
        peer = (wires.device, wires.shard + (1 if way == 0 else -1))
        return [
            wires.copy(view(block), view(block), slot, peer)
            for view, slot in zip(self.views, self.slots[way][step], strict=True)
        ]

    def has(self, way, step):
        shard = self.wires.shard
        return shard - step >= 0 if way == 0 else shard + step < self.shards

    def sends(self, way, step):
        shard = self.wires.shard
        edge = shard < self.shards - 1 if way == 0 else shard > 0
        return jnp.logical_and(edge, self.has(way, step))

    def block(self, way, step):
        return self.wires.shard + (-step if way == 0 else step)

    def run(self, step, first=None):
        for way in range(2):
            if step > 0:

                @pl.when(self.has(way, step))
                def _(way=way):
                    for copy in self.copies(way, step - 1, self.block(way, step)):
                        copy.wait_recv()

            if step < self.shards - 1:

                @pl.when(self.sends(way, step))
                def _(way=way):
                    if first is None:
                        copies = self.copies(way, step, self.block(way, step))
                    else:
                        wires = self.wires
                        peer = (wires.device, wires.shard + (1 if way == 0 else -1))
                        block = self.block(way, step)
                        copies = [
                            wires.copy(source, view(block), slot, peer)
                            for source, view, slot in zip(
                                first, self.views, self.slots[way][step], strict=True
                            )
                        ]
                    for copy in copies:
                        copy.start()

    def drain(self):
        for way in range(2):
            for step in range(self.shards - 1):

                @pl.when(self.sends(way, step))
                def _(way=way, step=step):
                    for copy in self.copies(way, step, self.block(way, step)):
                        copy.wait_send()


class Plane:
    def __init__(self, wires, views, whole):
        self.wires, self.views, self.whole = wires, views, whole
        count = len(views)
        self.first = [[wires.slot() for _ in range(count)] for _ in range(2)]
        self.second = [[[wires.slot() for _ in range(count)] for _ in range(2)] for _ in range(2)]
        self.last = [[wires.slot() for _ in range(count)] for _ in range(4)]
        self.sent = []

    def start(self, copies):
        for copy in copies:
            copy.start()
        self.sent += copies

    def one(self, owner, half, bits, slots):
        wires = self.wires
        return [
            wires.copy(view(owner, half), view(owner, half), slot, wires.peer(bits))
            for view, slot in zip(self.views, slots, strict=True)
        ]

    def step_one(self):
        me = self.wires.device
        for half, bits in enumerate((XBIT, YBIT)):
            self.start(self.one(me, half, bits, self.first[half]))

    def step_two(self):
        me = self.wires.device
        for half, bits in enumerate((XBIT, YBIT)):
            for copy in self.one(me ^ bits, half, bits, self.first[half]):
                copy.wait_recv()
        for half, bits in enumerate((XBIT, YBIT)):
            other = (XBIT | YBIT) ^ bits
            self.start(self.one(me, half, other, self.second[half][0]))
            self.start(self.one(me ^ bits, half, other, self.second[half][1]))

    def cores(self, index):
        wires = self.wires
        owner = wires.device ^ (0, XBIT, YBIT, XBIT | YBIT)[index]
        return [
            wires.copy(place(owner), place(owner), slot, wires.peer(CORE))
            for place, slot in zip(self.whole, self.last[index], strict=True)
        ]

    def step_three(self):
        me = self.wires.device
        for half, bits in enumerate((XBIT, YBIT)):
            other = (XBIT | YBIT) ^ bits
            for owner, slots in ((me ^ other, 0), (me ^ other ^ bits, 1)):
                for copy in self.one(owner, half, other, self.second[half][slots]):
                    copy.wait_recv()
        for index in range(1, 4):
            self.start(self.cores(index))

    def finish(self):
        for index, bits in enumerate((0, XBIT, YBIT, XBIT | YBIT)):
            owner = self.wires.device ^ CORE ^ bits
            for place, slot in zip(self.whole, self.last[index], strict=True):
                self.wires.copy(
                    place(owner), place(owner), slot, self.wires.peer(CORE)
                ).wait_recv()
        for copy in self.sent:
            copy.wait_send()


def opening_kernel(
    shards, small, w_query, w_key, w_value, tokens, w_out, out_grad,
    small_all, qkv_w, tokens_all, out_block, grad_seq, send, recv, local,
):
    wires = Wires(send, recv)
    device, shard = wires.device, wires.shard
    weights = (w_query, w_key, w_value)
    block, width = w_query.shape
    rows = tokens.shape[0]
    part = width // shards
    greet(
        [wires.peer(step=step, shards=shards) for step in range(1, shards)]
        + [wires.peer(XBIT), wires.peer(YBIT), wires.peer(CORE)]
    )

    def place(source_shard, which):
        start = pl.multiple_of((device * shards + source_shard) * block, block)
        return qkv_w.at[pl.ds(start, block), pl.ds(which * part, part)]

    def cut(which, target):
        return weights[which].at[:, pl.ds(pl.multiple_of(target * part, part), part)]

    exchange = [[wires.slot() for _ in range(4)] for _ in range(1, shards)]
    sent = []
    for step in range(1, shards):
        peer = wires.peer(step=step, shards=shards)
        copies = [
            wires.copy(small, small_all.at[device * shards + shard], exchange[step - 1][3], peer)
        ] + [
            wires.copy(cut(which, peer[1]), place(shard, which), exchange[step - 1][which], peer)
            for which in range(3)
        ]
        for copy in copies:
            copy.start()
        sent += copies
    own = [
        pltpu.make_async_copy(cut(which, shard), place(shard, which), local.at[which])
        for which in range(3)
    ]
    own += [
        pltpu.make_async_copy(small, small_all.at[device * shards + shard], local.at[3]),
        pltpu.make_async_copy(
            tokens, tokens_all.at[pl.ds(pl.multiple_of(shard * rows, rows), rows)], local.at[4]
        ),
        pltpu.make_async_copy(
            w_out, out_block.at[pl.ds(pl.multiple_of(shard * block, block), block)], local.at[5]
        ),
        pltpu.make_async_copy(
            out_grad, grad_seq.at[pl.ds(pl.multiple_of(shard * rows, rows), rows)], local.at[6]
        ),
    ]
    for copy in own:
        copy.start()
    line = Relay(
        wires,
        shards,
        [
            lambda b: tokens_all.at[pl.ds(pl.multiple_of(b * rows, rows), rows)],
            lambda b: out_block.at[pl.ds(pl.multiple_of(b * block, block), block)],
            lambda b: grad_seq.at[pl.ds(pl.multiple_of(b * rows, rows), rows)],
        ],
    )
    line.run(0, (tokens, w_out, out_grad))
    for copy in own:
        copy.wait()
    for step in range(1, shards):
        peer = wires.peer(step=shards - step, shards=shards)
        source = peer[1]
        slots = exchange[step - 1]
        wires.copy(small, small_all.at[device * shards + source], slots[3], peer).wait_recv()
        for which in range(3):
            wires.copy(place(source, which), place(source, which), slots[which], peer).wait_recv()

    each = shards * block // 2

    def rows_of(owner, half):
        return qkv_w.at[pl.ds(pl.multiple_of((owner * 2 + half) * each, each), each)]

    def small_of(owner, half):
        return small_all.at[pl.ds((owner * 2 + half) * (shards // 2), shards // 2)]

    plane = Plane(
        wires,
        [rows_of, small_of],
        [
            lambda owner: qkv_w.at[pl.ds(pl.multiple_of(owner * 2 * each, 2 * each), 2 * each)],
            lambda owner: small_all.at[pl.ds(owner * shards, shards)],
        ],
    )
    plane.step_one()
    plane.start(plane.cores(0))
    plane.step_two()
    line.run(1)
    line.run(2)
    plane.step_three()
    for step in range(3, shards):
        line.run(step)
    plane.finish()
    for copy in sent:
        copy.wait_send()
    line.drain()


def opening_call(small, w_query, w_key, w_value, tokens, w_out, out_grad, planes, shards):
    block, width = w_query.shape
    rows = tokens.shape[0]
    hbm = pl.BlockSpec(memory_space=pl.ANY)
    slots = 64
    return pl.pallas_call(
        functools.partial(opening_kernel, shards),
        in_specs=[hbm] * 7,
        out_specs=[hbm] * 5,
        out_shape=(
            jax.ShapeDtypeStruct((planes * shards,) + small.shape, small.dtype),
            jax.ShapeDtypeStruct((planes * shards * block, 3 * width // shards), w_query.dtype),
            jax.ShapeDtypeStruct((shards * rows, width), tokens.dtype),
            jax.ShapeDtypeStruct((shards * block, width), w_out.dtype),
            jax.ShapeDtypeStruct((shards * rows, width), out_grad.dtype),
        ),
        scratch_shapes=[
            pltpu.SemaphoreType.DMA((slots,)),
            pltpu.SemaphoreType.DMA((slots,)),
            pltpu.SemaphoreType.DMA((7,)),
        ],
        compiler_params=pltpu.CompilerParams(
            collective_id=1, has_side_effects=True, vmem_limit_bytes=4 * MIB
        ),
        cost_estimate=pl.CostEstimate(flops=0, bytes_accessed=200 * MIB, transcendentals=0),
    )(small, w_query, w_key, w_value, tokens, w_out, out_grad)


def middle_kernel(shards, mixed, out_block, mixed_all, out_w, send, recv, local):
    wires = Wires(send, recv)
    device, shard = wires.device, wires.shard
    greet(
        [wires.peer(step=step, shards=shards) for step in range(1, shards)]
        + [wires.peer(XBIT), wires.peer(YBIT), wires.peer(CORE)]
    )
    each = out_block.shape[0] // 2
    line = Relay(wires, shards, [lambda b: mixed_all.at[b]])
    line.run(0, (mixed,))
    own = [
        pltpu.make_async_copy(
            out_block,
            out_w.at[pl.ds(pl.multiple_of(device * 2 * each, 2 * each), 2 * each)],
            local.at[0],
        ),
        pltpu.make_async_copy(mixed, mixed_all.at[shard], local.at[1]),
    ]
    for copy in own:
        copy.start()
    for copy in own:
        copy.wait()
    plane = Plane(
        wires,
        [lambda owner, half: out_w.at[pl.ds(pl.multiple_of((owner * 2 + half) * each, each), each)]],
        [lambda owner: out_w.at[pl.ds(pl.multiple_of(owner * 2 * each, 2 * each), 2 * each)]],
    )
    plane.step_one()
    plane.start(plane.cores(0))
    line.run(1)
    plane.step_two()
    line.run(2)
    for step in range(3, shards):
        line.run(step)
    plane.step_three()
    plane.finish()
    line.drain()


def middle_call(mixed, out_block, planes, shards):
    hbm = pl.BlockSpec(memory_space=pl.ANY)
    slots = 32
    return pl.pallas_call(
        functools.partial(middle_kernel, shards),
        in_specs=[hbm] * 2,
        out_specs=[hbm] * 2,
        out_shape=(
            jax.ShapeDtypeStruct((shards,) + mixed.shape, mixed.dtype),
            jax.ShapeDtypeStruct((planes * out_block.shape[0], out_block.shape[1]), mixed.dtype),
        ),
        scratch_shapes=[
            pltpu.SemaphoreType.DMA((slots,)),
            pltpu.SemaphoreType.DMA((slots,)),
            pltpu.SemaphoreType.DMA((2,)),
        ],
        compiler_params=pltpu.CompilerParams(
            collective_id=2, has_side_effects=True, vmem_limit_bytes=4 * MIB
        ),
        cost_estimate=pl.CostEstimate(flops=0, bytes_accessed=150 * MIB, transcendentals=0),
    )(mixed, out_block)


def meeting_kernel(
    shards, normed, grad_seq, gate, up, down,
    normed_all, grad_all, wide_w, down_w, send, recv, local,
):
    wires = Wires(send, recv)
    device, shard = wires.device, wires.shard
    own, part, hidden_units = gate.shape
    each = hidden_units // shards
    half = normed.shape[0] // 2
    greet(
        [wires.peer(step=step, shards=shards) for step in range(1, shards)]
        + [wires.peer(XBIT), wires.peer(YBIT), wires.peer(CORE)]
    )

    def wide_pair(source, target):
        lanes = pl.ds(pl.multiple_of(target * each, each), each)
        pairs = []
        for which, weight in enumerate((gate, up)):
            for index in range(own):
                place = wide_w.at[source, :, pl.ds((which * own + index) * each, each)]
                pairs.append((weight.at[index, :, lanes], place))
        return pairs

    def down_pair(source, target):
        lines = pl.ds(pl.multiple_of(target * each, each), each)
        return [
            (down.at[index, lines, :], down_w.at[source, pl.ds(index * each, each), :])
            for index in range(own)
        ]

    sent, pending = [], []
    token_plane = Plane(
        wires, [lambda owner, part_of: normed_all.at[owner, pl.ds(part_of * half, half)]],
        [lambda owner: normed_all.at[owner]],
    )
    grad_plane = Plane(
        wires, [lambda owner, part_of: grad_all.at[owner, pl.ds(part_of * half, half)]],
        [lambda owner: grad_all.at[owner]],
    )
    own_copies = [
        pltpu.make_async_copy(normed, normed_all.at[device], local.at[0]),
        pltpu.make_async_copy(grad_seq, grad_all.at[device], local.at[1]),
    ]
    for index, (source, place) in enumerate(wide_pair(shard, shard) + down_pair(shard, shard)):
        own_copies.append(pltpu.make_async_copy(source, place, local.at[2 + index]))
    for copy in own_copies:
        copy.start()
    for pair in (wide_pair, down_pair):
        for step in range(1, shards):
            peer = wires.peer(step=step, shards=shards)
            back = wires.peer(step=shards - step, shards=shards)
            for (source, place), (_, mine) in zip(
                pair(shard, peer[1]), pair(back[1], shard), strict=True
            ):
                slot = wires.slot()
                copy = wires.copy(source, place, slot, peer)
                copy.start()
                sent.append(copy)
                pending.append((mine, slot, back))
    for copy in own_copies:
        copy.wait()
    token_plane.step_one()
    token_plane.start(token_plane.cores(0))
    grad_plane.start(grad_plane.cores(0))
    token_plane.step_two()
    grad_plane.step_one()
    token_plane.step_three()
    grad_plane.step_two()
    grad_plane.step_three()
    token_plane.finish()
    grad_plane.finish()
    for mine, slot, back in pending:
        wires.copy(mine, mine, slot, back).wait_recv()
    for copy in sent:
        copy.wait_send()


def meeting_call(normed, grad_seq, gate, up, down, planes, shards):
    hbm = pl.BlockSpec(memory_space=pl.ANY)
    own, part, hidden_units = gate.shape
    count = own * hidden_units // shards
    slots = 48
    return pl.pallas_call(
        functools.partial(meeting_kernel, shards),
        in_specs=[hbm] * 5,
        out_specs=[hbm] * 4,
        out_shape=(
            jax.ShapeDtypeStruct((planes,) + normed.shape, normed.dtype),
            jax.ShapeDtypeStruct((planes,) + grad_seq.shape, grad_seq.dtype),
            jax.ShapeDtypeStruct((shards, part, 2 * count), gate.dtype),
            jax.ShapeDtypeStruct((shards, count, part), down.dtype),
        ),
        scratch_shapes=[
            pltpu.SemaphoreType.DMA((slots,)),
            pltpu.SemaphoreType.DMA((slots,)),
            pltpu.SemaphoreType.DMA((2 + 3 * own,)),
        ],
        compiler_params=pltpu.CompilerParams(
            collective_id=3, has_side_effects=True, vmem_limit_bytes=4 * MIB
        ),
        cost_estimate=pl.CostEstimate(flops=0, bytes_accessed=300 * MIB, transcendentals=0),
    )(normed, grad_seq, gate, up, down)


LOW = jnp.bfloat16
WIDE = jnp.float32


def swap(value, bits):
    count = lax.axis_size(EXPERT)
    return lax.ppermute(value, EXPERT, [(i, i ^ bits) for i in range(count)])


def shard_exchange(pieces, shard):
    size = lax.axis_size(SHARD)
    result = pieces
    for step in range(1, size):
        target = (shard + step) % size
        sent = lax.dynamic_index_in_dim(pieces, target, 0, keepdims=True)
        got = lax.ppermute(sent, SHARD, [(i, (i + step) % size) for i in range(size)])
        result = lax.dynamic_update_slice_in_dim(result, got, (shard - step) % size, 0)
    return result


def plane_scatter(parts, device):
    shape = parts.shape[1:]
    core, xbit, ybit = device & 1, (device >> 1) & 1, (device >> 2) & 1
    cube = parts.reshape((2, 2, 2) + shape)
    keep = lax.dynamic_index_in_dim(cube, core, 2, keepdims=False)
    give = lax.dynamic_index_in_dim(cube, 1 - core, 2, keepdims=False)
    cube = keep.astype(WIDE) + swap(give.astype(LOW), CORE).astype(WIDE)
    half = shape[0] // 2

    def halves(value, first, second, first_bit, second_bit, axis):
        keep = lax.dynamic_index_in_dim(value, first, axis, keepdims=False)
        give = lax.dynamic_index_in_dim(value, 1 - first, axis, keepdims=False)
        value = keep + swap(give.astype(LOW), first_bit).astype(WIDE)
        keep = lax.dynamic_index_in_dim(value, second, 0, keepdims=False)
        give = lax.dynamic_index_in_dim(value, 1 - second, 0, keepdims=False)
        return keep + swap(give.astype(LOW), second_bit).astype(WIDE)

    low_half = halves(cube[:, :, :half], xbit, ybit, XBIT, YBIT, 1)
    high_half = halves(cube[:, :, half:], ybit, xbit, YBIT, XBIT, 0)
    return jnp.concatenate([low_half, high_half], axis=0)


def tiny_scatter(table, device, shard):
    planes, shards = lax.axis_size(EXPERT), lax.axis_size(SHARD)
    cube = table.reshape(2, 2, 2, shards, -1)
    for axis, bits in ((2, CORE), (1, XBIT), (0, YBIT)):
        mine = (device // bits) & 1
        keep = lax.dynamic_index_in_dim(cube, mine, axis, keepdims=True)
        give = lax.dynamic_index_in_dim(cube, 1 - mine, axis, keepdims=True)
        cube = keep + swap(give, bits)
    return jnp.sum(shard_exchange(cube.reshape(shards, -1), shard), axis=0)


def fast_local(
    tokens,
    segment_ids,
    routes,
    pair_order,
    attn_gain,
    w_query,
    w_key,
    w_value,
    query_gain,
    key_gain,
    w_out,
    ffn_gain,
    w_router,
    w_gate,
    w_up,
    w_down,
    out_grad,
):
    rows, width = tokens.shape
    top_count = routes.shape[1]
    planes = lax.axis_size(EXPERT)
    shards = lax.axis_size(SHARD)
    own_experts = w_gate.shape[0]
    experts = own_experts * planes
    capacity = 5 * rows * top_count // (4 * own_experts)
    seq = segment_ids.shape[0]
    device = lax.axis_index(EXPERT)
    shard = lax.axis_index(SHARD)
    part = width // shards
    both = BOTH

    order = pair_order.reshape(rows, top_count)
    expert_ids = jnp.arange(experts, dtype=jnp.int32)
    chosen = routes[:, :, None] == expert_ids[None, None, :]
    dense_order = jnp.sum(jnp.where(chosen, order[:, :, None] + 1, 0), axis=1)
    small = jnp.concatenate(
        [
            (dense_order // 256).astype(LOW).reshape(-1),
            (dense_order % 256).astype(LOW).reshape(-1),
            w_router.reshape(-1),
            attn_gain,
            ffn_gain,
            query_gain,
            key_gain,
        ]
    )
    used = small.shape[0]
    lines = -(-used // (128 * 16)) * 16
    small = jnp.pad(small, (0, lines * 128 - used)).reshape(lines, 128)
    small, qkv_w, tokens_seq, out_block, grad_seq = opening_call(
        small, w_query, w_key, w_value, tokens, w_out, out_grad, planes, shards
    )
    small = small.reshape(planes, shards, -1)[:, :, :used]
    cuts = [rows * experts, rows * experts, w_router.size, attn_gain.size, ffn_gain.size]
    cuts += [query_gain.size, key_gain.size]
    fields, at = [], 0
    for size in cuts:
        fields.append(small[:, :, at : at + size])
        at += size
    all_order = fields[0].astype(jnp.int32) * 256 + fields[1].astype(jnp.int32)
    all_order = all_order.reshape(planes, shards, rows, experts)
    router_w = fields[2].reshape(width, experts)
    attn_scale = fields[3].reshape(width).astype(WIDE)
    ffn_scale = fields[4].reshape(width).astype(WIDE)
    query_scale = fields[5].reshape(HD).astype(WIDE)
    key_scale = fields[6].reshape(HD).astype(WIDE)

    attn_row, ffn_row = attn_scale.reshape(1, width), ffn_scale.reshape(1, width)
    query_row, key_row = query_scale.reshape(1, HD), key_scale.reshape(1, HD)
    tables = turn_tables(seq)
    seg_row, seg_col = segment_ids.reshape(1, seq), segment_ids.reshape(seq, 1)
    normed_low, raw, low, mixed_own, total = attend_call(
        tokens_seq, attn_row, qkv_w, query_row, key_row, tables, seg_row, seg_col
    )
    mixed, out_w = middle_call(mixed_own, out_block, planes, shards)
    hidden_seq, normed_seq = join_call(mixed, out_w, tokens_seq, ffn_row)

    token_all, grad_all, wide_w, down_w = meeting_call(
        normed_seq, grad_seq, w_gate, w_up, w_down, planes, shards
    )
    wide_w = wide_w.reshape(width, -1)
    extra = 128
    router_pad = jnp.pad(router_w, ((0, 0), (0, extra - experts)))
    own_ids = device * own_experts + jnp.arange(own_experts, dtype=jnp.int32)
    own_hot = (own_ids[:, None] == jnp.arange(extra, dtype=jnp.int32)[None, :]).astype(WIDE)
    mine = jnp.stack(
        [lax.dynamic_index_in_dim(all_order, own_ids[i], 3, keepdims=False) for i in range(own_experts)]
    )
    mine = mine.transpose(0, 2, 1, 3).reshape(own_experts, shards, planes * rows)
    smaller = (mine[:, :, None, :] < mine[:, :, :, None]) & (mine[:, :, None, :] > 0)
    rank = jnp.sum(smaller.astype(jnp.int32), axis=-1)
    kept = ((mine > 0) & (rank < capacity)).astype(WIDE)
    kept = kept.reshape(own_experts, shards, planes, rows).transpose(2, 1, 3, 0)
    kept = kept.reshape(planes, seq, own_experts)

    sums = None
    out_parts, in_parts = [None] * 4, [None] * 4
    for chip in (3, 1, 2, 0):
        blocks = jnp.stack([device ^ (2 * chip), device ^ (2 * chip + 1)])
        out_parts[chip], in_parts[chip], sums = expert_call(
            blocks, token_all, grad_all, kept, wide_w, router_pad, down_w, own_hot, experts, sums
        )
    wide_grad, router_grad, down_grad = sums

    def combine(parts):
        total = None
        for chip, bits in enumerate((0, XBIT, YBIT, XBIT | YBIT)):
            value = parts[chip]
            value = value[0].astype(WIDE) + swap(value[1], CORE).astype(WIDE)
            if bits:
                value = swap(value.astype(LOW), bits).astype(WIDE)
            total = value if total is None else total + value
        pieces = shard_exchange(total.astype(LOW).reshape(shards, rows, width), shard)
        return jnp.sum(pieces.astype(WIDE), axis=0)

    normed_two_grad = combine(in_parts)
    out_parts, _ = lax.optimization_barrier((out_parts, normed_two_grad))
    expert_sum = combine(out_parts)
    hidden = lax.dynamic_slice_in_dim(hidden_seq, shard * rows, rows)
    mixed_out = (hidden + expert_sum).astype(LOW)

    hidden_grad, attn_low, message, ffn_scale_grad = turn_back_call(
        hidden, normed_two_grad, out_grad, ffn_row, out_w, shards
    )
    mixed_grad = shard_exchange(message, shard).reshape(seq, part)
    qkv_grad, normed_grad, query_scale_grad, key_scale_grad = attend_back_call(
        mixed_grad, raw, low, total, qkv_w, query_row, key_row, tables, seg_row, seg_col
    )
    pieces = shard_exchange(normed_grad.reshape(shards, rows, width), shard)
    input_grad, attn_scale_grad = finish_call(pieces, tokens, hidden_grad, attn_row)

    qkv_w_grad = matmul_tn(normed_low, qkv_grad).reshape(planes, -1, 3 * part)
    qkv_w_grad = plane_scatter(qkv_w_grad, device).astype(LOW)
    qkv_w_grad = shard_exchange(qkv_w_grad.reshape(shards, -1, 3 * part), shard).astype(WIDE)
    qkv_w_grad = qkv_w_grad.reshape(shards, -1, 3, part).transpose(2, 1, 0, 3)
    qkv_w_grad = qkv_w_grad.reshape(3, -1, width)

    own_mixed = lax.dynamic_slice_in_dim(mixed, shard * rows, rows, 1)
    own_mixed = own_mixed.transpose(1, 0, 2).reshape(rows, width)
    out_w_grad = matmul_tn(own_mixed, attn_low).reshape(planes, -1, width)
    out_w_grad = plane_scatter(out_w_grad, device).astype(LOW)
    out_w_grad = shard_exchange(out_w_grad.reshape(shards, -1, width), shard)
    out_w_grad = jnp.sum(out_w_grad.astype(WIDE), axis=0)

    wide_pieces = shard_exchange(wide_grad.astype(LOW).reshape(shards, part, -1), shard)
    down_pieces = shard_exchange(down_grad.astype(LOW), shard)
    gate_grad, up_grad, down_grad = unpack_units(wide_pieces, down_pieces, own_experts)

    devices = planes * shards
    tiny = [router_grad[:, :experts], ffn_scale_grad, attn_scale_grad, query_scale_grad, key_scale_grad]
    tiny = [value.reshape(devices, -1) for value in tiny]
    sizes = [value.shape[1] for value in tiny]
    summed = tiny_scatter(jnp.concatenate(tiny, axis=1), device, shard)
    fields, at = [], 0
    for size in sizes:
        fields.append(summed[at : at + size])
        at += size
    return (
        mixed_out,
        input_grad,
        fields[2],
        qkv_w_grad[0],
        qkv_w_grad[1],
        qkv_w_grad[2],
        fields[3],
        fields[4],
        out_w_grad,
        fields[1],
        fields[0].reshape(-1, experts),
        gate_grad,
        up_grad,
        down_grad,
    )


def solution(mesh):
    local = fast_local if mesh.shape[EXPERT] == 8 else general_local
    return jax.shard_map(
        local,
        mesh=mesh,
        in_specs=(
            P(BOTH, None),
            P(EXPERT),
            P(BOTH, None),
            P(BOTH),
            P(BOTH),
            P(BOTH, None),
            P(BOTH, None),
            P(BOTH, None),
            P(BOTH),
            P(BOTH),
            P(BOTH, None),
            P(BOTH),
            P(BOTH, None),
            P(EXPERT, SHARD, None),
            P(EXPERT, SHARD, None),
            P(EXPERT, None, SHARD),
            P(BOTH, None),
        ),
        out_specs=(
            P(BOTH, None),
            P(BOTH, None),
            P(BOTH),
            P(BOTH, None),
            P(BOTH, None),
            P(BOTH, None),
            P(BOTH),
            P(BOTH),
            P(BOTH, None),
            P(BOTH),
            P(BOTH, None),
            P(EXPERT, SHARD, None),
            P(EXPERT, SHARD, None),
            P(EXPERT, None, SHARD),
        ),
        check_vma=False,
    )
```

time: 3330 us -> 1230 us (0.37)
  waiting for transfers between devices: 2380 us -> 391 us
  Pallas kernels: 0 us -> 503 us
  blocking collectives: 258 us -> 0 us
  matrix products: 215 us -> 17.5 us
  local copies, waits for them, and re-layouts: 299 us -> 140 us
  starting transfers between devices: 21.9 us -> 105 us
  other arithmetic: 122 us -> 56.6 us
    reduce_scatter x7 -> x0, waiting for transfers between devices: 1830 us -> none  [the longest x1 365 us: local(): lax.psum_scatter(query_w_grad, ('expert', 'wshard'), scatter_dimension=0,...]
    pallas_call x0 -> x14, Pallas kernels: none -> 503 us  [the longest x1 152 us: meeting_call(): pl.pallas_call(functools.partial(meeting_kernel, shards), in_specs=[hbm]...]
    ppermute x0 -> x54, waiting for transfers between devices: none -> 391 us  [the longest x27 208 us: swap(): return lax.ppermute(value, EXPERT, [(i, i ^ bits) for i in range(count)])]
    all_to_all x4 -> x0, waiting for transfers between devices: 219 us -> none  [the longest x1 82.2 us: local(): lax.all_to_all(send_grad, 'expert', split_axis=0, concat_axis=0, tiled=True)]
    all_gather x9 -> x0, waiting for transfers between devices: 217 us -> none  [the longest x1 73.5 us: local(): lax.all_gather(w_query, ('expert', 'wshard'), axis=0, tiled=True)]
    dot_general x27 -> x0, matrix products: 179 us -> none  [the longest x5 23.1 us: matmul_nt(): lax.dot_general(left, right, (((1,), (1,)), ((), ())), preferred_element_...]
    all_gather x3 -> x0, blocking collectives: 175 us -> none  [the longest x1 96.4 us: local(): lax.all_gather(pair_order, 'expert', axis=0, tiled=True)]
    gather x14 -> x0, local copies, waits for them, and re-layouts: 135 us -> none  [the longest x1 19.9 us: local(): padded_rows(slot_in_grad.reshape(-1, width))[back_source]]
  transfers between devices with their start and end apart: 23 -> 54, of which waited for: 17 -> 21; matrix products, arithmetic and copies ran while one was open for 16% -> 10% of each run, Pallas kernels for 0% -> 12%
where the time goes in v1:
time: 1230 us; the launch traced here: 1220 us
  Pallas kernels  503 us (41%)
  waiting for transfers between devices  391 us (32%)
  local copies, waits for them, and re-layouts  140 us (11%)
  starting transfers between devices  105 us (9%)
  other arithmetic  56.6 us (5%)
  matrix products  17.5 us (1%)
    ppermute x27, waiting for transfers between devices, swap(): return lax.ppermute(value, EXPERT, [(i, i ^ bits) for i in range(count)])  208 us
    ppermute x27, waiting for transfers between devices, shard_exchange(): lax.ppermute(sent, SHARD, [(i, (i + step) % size) for i in range(size)])  183 us
    pallas_call x1, Pallas kernels, meeting_call(): pl.pallas_call(functools.partial(meeting_kernel, shards), in_specs=[hbm]...  152 us
    pallas_call x4, Pallas kernels, expert_call(): pl.pallas_call(functools.partial(expert_kernel, first, experts), grid_spe...  146 us
    pallas_call x1, Pallas kernels, opening_call(): pl.pallas_call(functools.partial(opening_kernel, shards), in_specs=[hbm]...  110 us
    ppermute x27, starting transfers between devices, shard_exchange(): lax.ppermute(sent, SHARD, [(i, (i + step) % size) for i in range(size)])  85.2 us
    unnamed x117, local copies, waits for them, and re-layouts  47.7 us
    pallas_call x1, Pallas kernels, middle_call(): pl.pallas_call(functools.partial(middle_kernel, shards), in_specs=[hbm] *...  43.7 us
  transfers between devices with their start and end apart: 54, of which 21 were waited for; matrix products, arithmetic and copies ran while one was open for 10% of the time, Pallas kernels for 12%

profile of v1, /device:TPU:0, one launch (start us, length us, event | category | flops | bytes accessed | tf_op | source)
XLA Modules:
  0.0 1219.2 jit_solution(2739331580644146132)
XLA Ops:
  7.1 2.8 concatenate.25
  15.8 110.0 %shard_map.290 = (bf16[32,48,128]{2,1,0:T(8,128)(2,1)S(1)}, bf16[2048,1536]{1,0:T(8,128)(2,1)S(1)}, bf16[512,2048]{1,0:T(8,128)(2,1)S(1)}, bf16[256,2048]{1,0:T(8,128)(2,1)S(1)}, bf16[512,2048]{1,0:T(8,128)(2,1)S(1)}) custom-call(bf16[48,128]{1,0:T(8,128)(2,1)S(1)} %pad_bitcast_fusion.small, bf16[64,2048]{1,0:T(8,128)(2,1)S(1)} %copy-done.15, ...), custom_call_target="tpu_custom_call" | custom-call | bytes 209715200 | tf_op jit(solution)/shard_map/pallas_call | solution.py:1089
  125.8 2.6 copy-done.23
  139.9 3.0 reshape.239
  144.1 4.5 dynamic-slice_reduce_fusion.1
  148.7 6.3 convert_reduce_fusion
  160.8 10.4 shard_map.291
  171.3 43.7 %shard_map.292 = (bf16[4,512,512]{2,1,0:T(8,128)(2,1)S(1)}, bf16[2048,2048]{1,0:T(8,128)(2,1)S(1)}) custom-call(bf16[512,512]{1,0:T(8,128)(2,1)S(1)} %get-tuple-element.71.mixed, bf16[256,2048]{1,0:T(8,128)(2,1)S(1)} %get-tuple-element.72.out_block), custom_call_target="tpu_custom_call" | custom-call | bytes 157286400 | tf_op jit(solution)/shard_map/pallas_call | solution.py:1154
  215.0 3.3 copy-done
  218.3 2.3 copy-done.26
  220.6 8.8 shard_map.293
  232.0 152.1 %shard_map.294 = (bf16[8,512,2048]{2,1,0:T(8,128)(2,1)S(1)}, bf16[8,512,2048]{2,1,0:T(8,128)(2,1)S(1)}, bf16[4,512,1024]{2,1,0:T(8,128)(2,1)S(1)}, bf16[4,512,512]{2,1,0:T(8,128)(2,1)S(1)}) custom-call(bf16[512,2048]{1,0:T(8,128)(2,1)S(1)} %get-tuple-element.76.normed, bf16[512,2048]{1,0:T(8,128)(2,1)S(1)} %get-tuple-element.77.grad_seq, ...), custom_call_target="tpu_custom_call" | custom-call | bytes 314572800 | tf_op jit(solution)/shard_map/pallas_call | solution.py:1256
  384.0 5.8 copy-done.21
  389.9 5.7 copy-done.22
  398.9 36.1 %shard_map.295 = (bf16[2,512,2048]{2,1,0:T(8,128)(2,1)}, bf16[2,512,2048]{2,1,0:T(8,128)(2,1)}, f32[2048,1024]{1,0:T(8,128)}, f32[2048,128]{1,0:T(8,128)}, f32[4,512,512]{2,1,0:T(8,128)}) custom-call(s32[2]{0:T(128)} %get-tuple-element.233.blocks, bf16[8,512,2048]{2,1,0:T(8,128)(2,1)} %copy-done.21, bf16[8,512,2048]{2,1,0:T(8,128)(2,1)} %copy-done.22, ...), custom_call_target="tpu_custom_call" | custom-call | flops 19327352832 | bytes 41943040 | tf_op jit(solution)/shard_map/pallas_call | solution.py:627
  435.0 3.1 slice_bitcast_fusion.4
  438.5 36.6 %shard_map.296 = (bf16[2,512,2048]{2,1,0:T(8,128)(2,1)}, bf16[2,512,2048]{2,1,0:T(8,128)(2,1)}, f32[2048,1024]{1,0:T(8,128)}, f32[2048,128]{1,0:T(8,128)}, f32[4,512,512]{2,1,0:T(8,128)}) custom-call(s32[2]{0:T(128)} %get-tuple-element.232.blocks, bf16[8,512,2048]{2,1,0:T(8,128)(2,1)} %copy-done.21, ...), custom_call_target="tpu_custom_call", output_to_operand_aliasing={{2}: (8, {}), {3}: (9, {}), {4}: (10, {})} | custom-call | flops 19327352832 | bytes 41943040 | tf_op jit(solution)/shard_map/pallas_call | solution.py:627
  475.1 3.2 slice_bitcast_fusion.6
  479.0 36.4 %shard_map.297 = (bf16[2,512,2048]{2,1,0:T(8,128)(2,1)}, bf16[2,512,2048]{2,1,0:T(8,128)(2,1)}, f32[2048,1024]{1,0:T(8,128)}, f32[2048,128]{1,0:T(8,128)}, f32[4,512,512]{2,1,0:T(8,128)}) custom-call(s32[2]{0:T(128)} %get-tuple-element.231.blocks, bf16[8,512,2048]{2,1,0:T(8,128)(2,1)} %copy-done.21, ...), custom_call_target="tpu_custom_call", output_to_operand_aliasing={{2}: (8, {}), {3}: (9, {}), {4}: (10, {})} | custom-call | flops 19327352832 | bytes 41943040 | tf_op jit(solution)/shard_map/pallas_call | solution.py:627
  517.8 36.6 %shard_map.298 = (bf16[2,512,2048]{2,1,0:T(8,128)(2,1)}, bf16[2,512,2048]{2,1,0:T(8,128)(2,1)}, f32[2048,1024]{1,0:T(8,128)}, f32[2048,128]{1,0:T(8,128)}, f32[4,512,512]{2,1,0:T(8,128)}) custom-call(s32[2]{0:T(128)} %get-tuple-element.230.blocks, bf16[8,512,2048]{2,1,0:T(8,128)(2,1)} %copy-done.21, ...), custom_call_target="tpu_custom_call", output_to_operand_aliasing={{2}: (8, {}), {3}: (9, {}), {4}: (10, {})} | custom-call | flops 19327352832 | bytes 41943040 | tf_op jit(solution)/shard_map/pallas_call | solution.py:627
  554.4 3.3 slice_bitcast_fusion.7
  561.4 2.4 fusion.10
  568.0 41.7 %collective-permute-done.6 = bf16[512,2048]{1,0:T(8,128)(2,1)} collective-permute-done((bf16[512,2048]{1,0:T(8,128)(2,1)}, bf16[512,2048]{1,0:T(8,128)(2,1)}, u32[]{:S(2)}, u32[]{:S(2)}) %collective-permute-start.6) | collective-permute-done | bytes 2097184 | tf_op jit(solution)/shard_map/ppermute | solution.py:1284
  609.7 43.6 %collective-permute-done.2 = bf16[512,2048]{1,0:T(8,128)(2,1)} collective-permute-done((bf16[512,2048]{1,0:T(8,128)(2,1)S(1)}, bf16[512,2048]{1,0:T(8,128)(2,1)}, u32[]{:S(2)}, u32[]{:S(2)}) %collective-permute-start.2) | collective-permute-done | bytes 2097184 | tf_op jit(solution)/shard_map/ppermute | solution.py:1284
  654.0 6.4 fusion.14
  661.1 15.1 %collective-permute-done.7 = bf16[1,128,2048]{2,1,0:T(8,128)(2,1)S(1)} collective-permute-done((bf16[1,128,2048]{2,1,0:T(8,128)(2,1)S(1)}, bf16[1,128,2048]{2,1,0:T(8,128)(2,1)S(1)}, u32[]{:S(2)}, u32[]{:S(2)}) %collective-permute-start.7) | collective-permute-done | bytes 524320 | tf_op jit(solution)/shard_map/ppermute | solution.py:1293
  678.6 22.3 %collective-permute-done.8 = bf16[1,128,2048]{2,1,0:T(8,128)(2,1)} collective-permute-done((bf16[1,128,2048]{2,1,0:T(8,128)(2,1)}, bf16[1,128,2048]{2,1,0:T(8,128)(2,1)}, u32[]{:S(2)}, u32[]{:S(2)}) %collective-permute-start.8) | collective-permute-done | bytes 524320 | tf_op jit(solution)/shard_map/ppermute | solution.py:1293
  717.7 42.0 %collective-permute-done.16 = bf16[512,2048]{1,0:T(8,128)(2,1)S(1)} collective-permute-done((bf16[512,2048]{1,0:T(8,128)(2,1)S(1)}, bf16[512,2048]{1,0:T(8,128)(2,1)S(1)}, u32[]{:S(2)}, u32[]{:S(2)}) %collective-permute-start.16) | collective-permute-done | bytes 2097184 | tf_op jit(solution)/shard_map/ppermute | solution.py:1284
  759.6 44.5 %collective-permute-done.14 = bf16[512,2048]{1,0:T(8,128)(2,1)S(1)} collective-permute-done((bf16[512,2048]{1,0:T(8,128)(2,1)S(1)}, bf16[512,2048]{1,0:T(8,128)(2,1)S(1)}, u32[]{:S(2)}, u32[]{:S(2)}) %collective-permute-start.14) | collective-permute-done | bytes 2097184 | tf_op jit(solution)/shard_map/ppermute | solution.py:1284
  804.1 3.9 fusion.7
  808.1 10.5 collective-permute-start.17
  818.6 14.9 %collective-permute-done.17 = bf16[1,128,2048]{2,1,0:T(8,128)(2,1)S(1)} collective-permute-done((bf16[1,128,2048]{2,1,0:T(8,128)(2,1)S(1)}, bf16[1,128,2048]{2,1,0:T(8,128)(2,1)S(1)}, u32[]{:S(2)}, u32[]{:S(2)}) %collective-permute-start.17) | collective-permute-done | bytes 524320 | tf_op jit(solution)/shard_map/ppermute | solution.py:1293
  838.1 2.8 convert_element_type.399
  845.1 15.8 %collective-permute-done.18 = bf16[1,128,2048]{2,1,0:T(8,128)(2,1)} collective-permute-done((bf16[1,128,2048]{2,1,0:T(8,128)(2,1)}, bf16[1,128,2048]{2,1,0:T(8,128)(2,1)}, u32[]{:S(2)}, u32[]{:S(2)}) %collective-permute-start.18) | collective-permute-done | bytes 524320 | tf_op jit(solution)/shard_map/ppermute | solution.py:1293
  862.8 31.9 %collective-permute-done.19 = bf16[1,128,2048]{2,1,0:T(8,128)(2,1)} collective-permute-done((bf16[1,128,2048]{2,1,0:T(8,128)(2,1)}, bf16[1,128,2048]{2,1,0:T(8,128)(2,1)}, u32[]{:S(2)}, u32[]{:S(2)}) %collective-permute-start.19) | collective-permute-done | bytes 524320 | tf_op jit(solution)/shard_map/ppermute | solution.py:1293
  900.9 3.4 copy-done.1
  904.2 3.3 shard_map.299
  907.6 11.6 collective-permute-start.20
  923.1 2.7 collective-permute-start.22
  927.2 3.6 constant_dynamic-slice_fusion.3
  932.3 56.9 %collective-permute-done.21 = bf16[1,128,512]{2,1,0:T(8,128)(2,1)S(1)} collective-permute-done((bf16[1,128,512]{2,1,0:T(8,128)(2,1)S(1)}, bf16[1,128,512]{2,1,0:T(8,128)(2,1)S(1)}, u32[]{:S(2)}, u32[]{:S(2)}) %collective-permute-start.21) | collective-permute-done | bytes 131104 | tf_op jit(solution)/shard_map/ppermute | solution.py:1293
  989.2 16.6 %shard_map.300 = (bf16[512,1536]{1,0:T(8,128)(2,1)}, bf16[512,2048]{1,0:T(8,128)(2,1)}, f32[1,128]{1,0:T(1,128)S(1)}, f32[1,128]{1,0:T(1,128)S(1)}) custom-call(bf16[512,512]{1,0:T(8,128)(2,1)S(1)} %bitcast.171, f32[512,1024]{1,0:T(8,128)} %get-tuple-element.104.raw, bf16[512,1536]{1,0:T(8,128)(2,1)} %get-tuple-element.105.low, f32[512,128]{1,0:T(8,128)S(1)} %copy-done.33, ...), custom_call_target="tpu_custom_call" | custom-call | flops 3221225472 | bytes 16777216 | tf_op jit(solution)/shard_map/pallas_call | solution.py:744
  1013.7 3.5 shard_map.303
  1017.3 3.8 collective-permute-start.50
  1021.1 2.3 constant_dynamic-update-slice_fusion.4
  1026.8 27.7 %collective-permute-start.25 = (bf16[1,128,2048]{2,1,0:T(8,128)(2,1)S(1)}, bf16[1,128,2048]{2,1,0:T(8,128)(2,1)}, u32[]{:S(2)}, u32[]{:S(2)}) collective-permute-start(bf16[1,128,2048]{2,1,0:T(8,128)(2,1)S(1)} %get-tuple-element.195), channel_id=1, source_target_pairs={{0,3},{1,0},{2,1},{3,2},{4,7},{5,4},{6,5},{7,6},{8,11},{9,8},{10,9... | collective-permute-start | bytes 1572872 | tf_op jit(solution)/shard_map/ppermute | solution.py:1293
  1054.5 5.1 collective-permute-start.24
  1059.6 8.1 fusion.45
  1069.3 9.0 collective-permute-done.24
  1083.4 3.3 fusion.15
  1088.5 9.4 fusion.26
  1099.0 6.0 fusion
  1111.4 2.3 constant_dynamic-update-slice_fusion.3.refs_0_.refs_1_
  1113.7 7.3 shard_map.302
  1125.5 4.6 collective-permute-done.35
  1133.9 10.1 collective-permute-done.33
  1146.5 5.9 bitcast_add_fusion
  1158.0 2.9 collective-permute-start.37
  1161.0 15.4 %collective-permute-done.43 = bf16[2,128,2048]{2,1,0:T(8,128)(2,1)S(1)} collective-permute-done((bf16[2,128,2048]{2,1,0:T(8,128)(2,1)S(1)}, bf16[2,128,2048]{2,1,0:T(8,128)(2,1)S(1)}, u32[]{:S(2)}, u32[]{:S(2)}) %collective-permute-start.43) | collective-permute-done | bytes 1048608 | tf_op jit(solution)/shard_map/ppermute | solution.py:1284
  1181.4 3.2 collective-permute-start.39
  1185.7 2.6 collective-permute-done.44
  1191.7 8.0 collective-permute-done.38
  1201.0 2.7 reshape.268
  1209.1 8.8 collective-permute-done.46
  (328 shorter events, 149.2 us)
Async XLA Ops:
  0.6 134.8 %copy-start.20 = (s32[512]{0:T(512)S(1)}, s32[512]{0:T(512)}, u32[]{:S(2)}) copy-start(s32[512]{0:T(512)} %param.20) | copy-start | bytes 6148
  171.2 47.0 %copy-start.32 = (f32[512,128]{1,0:T(8,128)}, f32[512,128]{1,0:T(8,128)S(1)}, u32[]{:S(2)}) copy-start(f32[512,128]{1,0:T(8,128)S(1)} %get-tuple-element.106.total) | copy-start | bytes 786436
  438.1 119.7 %collective-permute-start.5 = (bf16[512,2048]{1,0:T(8,128)(2,1)}, bf16[512,2048]{1,0:T(8,128)(2,1)S(1)}, u32[]{:S(2)}, u32[]{:S(2)}) collective-permute-start(bf16[512,2048]{1,0:T(8,128)(2,1)} %slice_bitcast_fusion.4), channel_id=1, source_target_pairs={{0,4},{4,0},{8,12},{12,8},{16,20},{20,16},{24,28},{28,24},{1,5},{5... | collective-permute-start | bytes 6291464 | tf_op jit(solution)/shard_map/ppermute | solution.py:1284
  478.3 83.1 %collective-permute-start.1 = (bf16[512,2048]{1,0:T(8,128)(2,1)}, bf16[512,2048]{1,0:T(8,128)(2,1)}, u32[]{:S(2)}, u32[]{:S(2)}) collective-permute-start(bf16[512,2048]{1,0:T(8,128)(2,1)} %slice_bitcast_fusion.6), channel_id=1, source_target_pairs={{0,4},{4,0},{8,12},{12,8},{16,20},{20,16},{24,28},{28,24},{1,5},{5... | collective-permute-start | bytes 6291464 | tf_op jit(solution)/shard_map/ppermute | solution.py:1284
  517.3 47.2 %collective-permute-start.3 = (bf16[512,2048]{1,0:T(8,128)(2,1)S(1)}, bf16[512,2048]{1,0:T(8,128)(2,1)S(1)}, u32[]{:S(2)}, u32[]{:S(2)}) collective-permute-start(bf16[512,2048]{1,0:T(8,128)(2,1)S(1)} %slice_bitcast_fusion.5), channel_id=1, source_target_pairs={{0,4},{4,0},{8,12},{12,8},{16,20},{20,16},{24,28},{28,24},{1,5},{5... | collective-permute-start | bytes 6291464 | tf_op jit(solution)/shard_map/ppermute | solution.py:1284
  557.7 10.3 collective-permute-start
  560.0 49.7 %collective-permute-start.6 = (bf16[512,2048]{1,0:T(8,128)(2,1)}, bf16[512,2048]{1,0:T(8,128)(2,1)}, u32[]{:S(2)}, u32[]{:S(2)}) collective-permute-start(bf16[512,2048]{1,0:T(8,128)(2,1)} %fusion.8), channel_id=1, source_target_pairs={{0,24},{4,28},{8,16},{12,20},{16,8},{20,12},{24,0},{28,4},{1,25},{... | collective-permute-start | bytes 6291464 | tf_op jit(solution)/shard_map/ppermute | solution.py:1284
  563.8 89.5 %collective-permute-start.2 = (bf16[512,2048]{1,0:T(8,128)(2,1)S(1)}, bf16[512,2048]{1,0:T(8,128)(2,1)}, u32[]{:S(2)}, u32[]{:S(2)}) collective-permute-start(bf16[512,2048]{1,0:T(8,128)(2,1)S(1)} %fusion.10), channel_id=1, source_target_pairs={{0,8},{4,12},{8,0},{12,4},{16,24},{20,28},{24,16},{28,20},{1,9},{5... | collective-permute-start | bytes 6291464 | tf_op jit(solution)/shard_map/ppermute | solution.py:1284
  566.6 87.4 %collective-permute-start.4 = (bf16[512,2048]{1,0:T(8,128)(2,1)}, bf16[512,2048]{1,0:T(8,128)(2,1)}, u32[]{:S(2)}, u32[]{:S(2)}) collective-permute-start(bf16[512,2048]{1,0:T(8,128)(2,1)} %fusion.9), channel_id=1, source_target_pairs={{0,16},{4,20},{8,24},{12,28},{16,0},{20,4},{24,8},{28,12},{1,17},{... | collective-permute-start | bytes 6291464 | tf_op jit(solution)/shard_map/ppermute | solution.py:1284
  660.5 15.7 %collective-permute-start.7 = (bf16[1,128,2048]{2,1,0:T(8,128)(2,1)S(1)}, bf16[1,128,2048]{2,1,0:T(8,128)(2,1)S(1)}, u32[]{:S(2)}, u32[]{:S(2)}) collective-permute-start(bf16[1,128,2048]{2,1,0:T(8,128)(2,1)S(1)} %constant_dynamic-slice_fusion.30), channel_id=1, source_target_pairs={{0,1},{1,2},{2,3},{3,0},{4,5},{5,6},{6,7},{7,4},{8,9},{9,10},{10,1... | collective-permute-start | bytes 1572872 | tf_op jit(solution)/shard_map/ppermute | solution.py:1293
  677.1 23.8 %collective-permute-start.8 = (bf16[1,128,2048]{2,1,0:T(8,128)(2,1)}, bf16[1,128,2048]{2,1,0:T(8,128)(2,1)}, u32[]{:S(2)}, u32[]{:S(2)}) collective-permute-start(bf16[1,128,2048]{2,1,0:T(8,128)(2,1)} %get-tuple-element.202), channel_id=1, source_target_pairs={{0,2},{1,3},{2,0},{3,1},{4,6},{5,7},{6,4},{7,5},{8,10},{9,11},{10,... | collective-permute-start | bytes 1572872 | tf_op jit(solution)/shard_map/ppermute | solution.py:1293
  677.1 24.9 %collective-permute-start.9 = (bf16[1,128,2048]{2,1,0:T(8,128)(2,1)S(1)}, bf16[1,128,2048]{2,1,0:T(8,128)(2,1)S(1)}, u32[]{:S(2)}, u32[]{:S(2)}) collective-permute-start(bf16[1,128,2048]{2,1,0:T(8,128)(2,1)S(1)} %get-tuple-element.201), channel_id=1, source_target_pairs={{0,3},{1,0},{2,1},{3,2},{4,7},{5,4},{6,5},{7,6},{8,11},{9,8},{10,9... | collective-permute-start | bytes 1572872 | tf_op jit(solution)/shard_map/ppermute | solution.py:1293
  704.4 5.0 collective-permute-start.15
  706.6 5.1 collective-permute-start.13
  708.0 6.7 collective-permute-start.11
  709.3 8.3 collective-permute-start.10
  710.2 49.4 %collective-permute-start.16 = (bf16[512,2048]{1,0:T(8,128)(2,1)S(1)}, bf16[512,2048]{1,0:T(8,128)(2,1)S(1)}, u32[]{:S(2)}, u32[]{:S(2)}) collective-permute-start(bf16[512,2048]{1,0:T(8,128)(2,1)S(1)} %fusion.1), channel_id=1, source_target_pairs={{0,24},{4,28},{8,16},{12,20},{16,8},{20,12},{24,0},{28,4},{1,25},{... | collective-permute-start | bytes 6291464 | tf_op jit(solution)/shard_map/ppermute | solution.py:1284
  712.6 91.6 %collective-permute-start.14 = (bf16[512,2048]{1,0:T(8,128)(2,1)S(1)}, bf16[512,2048]{1,0:T(8,128)(2,1)S(1)}, u32[]{:S(2)}, u32[]{:S(2)}) collective-permute-start(bf16[512,2048]{1,0:T(8,128)(2,1)S(1)} %fusion.2), channel_id=1, source_target_pairs={{0,16},{4,20},{8,24},{12,28},{16,0},{20,4},{24,8},{28,12},{1,17},{... | collective-permute-start | bytes 6291464 | tf_op jit(solution)/shard_map/ppermute | solution.py:1284
  714.7 123.4 %slice-start = ((s8[8388608]{0:T(1024)(128)(4,1)}), s8[4194304]{0:T(1024)(128)(4,1)S(1)}, s32[]{:S(2)}) async-start(s8[8388608]{0:T(1024)(128)(4,1)} %bitcast.183), calls=%async_computation | async-start | bytes 8388608
  715.5 122.6 %slice-start.1 = ((s8[8388608]{0:T(1024)(128)(4,1)}), s8[4194304]{0:T(1024)(128)(4,1)S(1)}, s32[]{:S(2)}) async-start(s8[8388608]{0:T(1024)(128)(4,1)} %bitcast.183), calls=%async_computation.1 | async-start | bytes 8388608
  715.5 88.7 %collective-permute-start.12 = (bf16[512,2048]{1,0:T(8,128)(2,1)S(1)}, bf16[512,2048]{1,0:T(8,128)(2,1)S(1)}, u32[]{:S(2)}, u32[]{:S(2)}) collective-permute-start(bf16[512,2048]{1,0:T(8,128)(2,1)S(1)} %fusion.3), channel_id=1, source_target_pairs={{0,8},{4,12},{8,0},{12,4},{16,24},{20,28},{24,16},{28,20},{1,9},{5... | collective-permute-start | bytes 6291464 | tf_op jit(solution)/shard_map/ppermute | solution.py:1284
  759.6 44.5 %copy-start.49 = (bf16[512,2048]{1,0:T(8,128)(2,1)}, bf16[512,2048]{1,0:T(8,128)(2,1)S(1)}, u32[]{:S(2)}) copy-start(bf16[512,2048]{1,0:T(8,128)(2,1)S(1)} %collective-permute-done.16) | copy-start | bytes 6291460
  808.0 28.4 %copy-start.46 = (f32[4,512,512]{2,1,0:T(8,128)S(1)}, f32[4,512,512]{2,1,0:T(8,128)}, u32[]{:S(2)}) copy-start(f32[4,512,512]{2,1,0:T(8,128)} %get-tuple-element.121) | copy-start | bytes 12582916
  808.1 25.4 %collective-permute-start.17 = (bf16[1,128,2048]{2,1,0:T(8,128)(2,1)S(1)}, bf16[1,128,2048]{2,1,0:T(8,128)(2,1)S(1)}, u32[]{:S(2)}, u32[]{:S(2)}) collective-permute-start(bf16[1,128,2048]{2,1,0:T(8,128)(2,1)S(1)} %constant_dynamic-slice_fusion.27), channel_id=1, source_target_pairs={{0,1},{1,2},{2,3},{3,0},{4,5},{5,6},{6,7},{7,4},{8,9},{9,10},{10,1... | collective-permute-start | bytes 1572872 | tf_op jit(solution)/shard_map/ppermute | solution.py:1293
  834.7 26.3 %collective-permute-start.18 = (bf16[1,128,2048]{2,1,0:T(8,128)(2,1)}, bf16[1,128,2048]{2,1,0:T(8,128)(2,1)}, u32[]{:S(2)}, u32[]{:S(2)}) collective-permute-start(bf16[1,128,2048]{2,1,0:T(8,128)(2,1)} %get-tuple-element.199), channel_id=1, source_target_pairs={{0,2},{1,3},{2,0},{3,1},{4,6},{5,7},{6,4},{7,5},{8,10},{9,11},{10,... | collective-permute-start | bytes 1572872 | tf_op jit(solution)/shard_map/ppermute | solution.py:1293
  834.7 60.0 %collective-permute-start.19 = (bf16[1,128,2048]{2,1,0:T(8,128)(2,1)}, bf16[1,128,2048]{2,1,0:T(8,128)(2,1)}, u32[]{:S(2)}, u32[]{:S(2)}) collective-permute-start(bf16[1,128,2048]{2,1,0:T(8,128)(2,1)} %get-tuple-element.198), channel_id=1, source_target_pairs={{0,3},{1,0},{2,1},{3,2},{4,7},{5,4},{6,5},{7,6},{8,11},{9,8},{10,9... | collective-permute-start | bytes 1572872 | tf_op jit(solution)/shard_map/ppermute | solution.py:1293
  837.5 81.7 %collective-permute-start.51 = (bf16[1,512,512]{2,1,0:T(8,128)(2,1)}, bf16[1,512,512]{2,1,0:T(8,128)(2,1)}, u32[]{:S(2)}, u32[]{:S(2)}) collective-permute-start(bf16[1,512,512]{2,1,0:T(8,128)(2,1)} %constant_dynamic-slice_fusion.2), channel_id=1, source_target_pairs={{0,1},{1,2},{2,3},{3,0},{4,5},{5,6},{6,7},{7,4},{8,9},{9,10},{10,1... | collective-permute-start | bytes 1572872 | tf_op jit(solution)/shard_map/ppermute | solution.py:1293
  843.1 84.0 %collective-permute-start.48 = (bf16[1,512,1024]{2,1,0:T(8,128)(2,1)}, bf16[1,512,1024]{2,1,0:T(8,128)(2,1)}, u32[]{:S(2)}, u32[]{:S(2)}) collective-permute-start(bf16[1,512,1024]{2,1,0:T(8,128)(2,1)} %constant_dynamic-slice_fusion.5), channel_id=1, source_target_pairs={{0,1},{1,2},{2,3},{3,0},{4,5},{5,6},{6,7},{7,4},{8,9},{9,10},{10,1... | collective-permute-start | bytes 3145736 | tf_op jit(solution)/shard_map/ppermute | solution.py:1293
  907.6 15.4 %collective-permute-start.20 = (bf16[1,128,512]{2,1,0:T(8,128)(2,1)S(1)}, bf16[1,128,512]{2,1,0:T(8,128)(2,1)S(1)}, u32[]{:S(2)}, u32[]{:S(2)}) collective-permute-start(bf16[1,128,512]{2,1,0:T(8,128)(2,1)S(1)} %constant_dynamic-slice_fusion.24), channel_id=1, source_target_pairs={{0,1},{1,2},{2,3},{3,0},{4,5},{5,6},{6,7},{7,4},{8,9},{9,10},{10,1... | collective-permute-start | bytes 393224 | tf_op jit(solution)/shard_map/ppermute | solution.py:1293
  921.1 91.5 %collective-permute-start.53 = (bf16[1,512,512]{2,1,0:T(8,128)(2,1)S(1)}, bf16[1,512,512]{2,1,0:T(8,128)(2,1)}, u32[]{:S(2)}, u32[]{:S(2)}) collective-permute-start(bf16[1,512,512]{2,1,0:T(8,128)(2,1)S(1)} %get-tuple-element.189), channel_id=1, source_target_pairs={{0,3},{1,0},{2,1},{3,2},{4,7},{5,4},{6,5},{7,6},{8,11},{9,8},{10,9... | collective-permute-start | bytes 1572872 | tf_op jit(solution)/shard_map/ppermute | solution.py:1293
  921.1 90.4 %collective-permute-start.52 = (bf16[1,512,512]{2,1,0:T(8,128)(2,1)}, bf16[1,512,512]{2,1,0:T(8,128)(2,1)}, u32[]{:S(2)}, u32[]{:S(2)}) collective-permute-start(bf16[1,512,512]{2,1,0:T(8,128)(2,1)} %get-tuple-element.190), channel_id=1, source_target_pairs={{0,2},{1,3},{2,0},{3,1},{4,6},{5,7},{6,4},{7,5},{8,10},{9,11},{10,... | collective-permute-start | bytes 1572872 | tf_op jit(solution)/shard_map/ppermute | solution.py:1293
  923.1 66.1 %collective-permute-start.22 = (bf16[1,128,512]{2,1,0:T(8,128)(2,1)S(1)}, bf16[1,128,512]{2,1,0:T(8,128)(2,1)S(1)}, u32[]{:S(2)}, u32[]{:S(2)}) collective-permute-start(bf16[1,128,512]{2,1,0:T(8,128)(2,1)S(1)} %get-tuple-element.210), channel_id=1, source_target_pairs={{0,3},{1,0},{2,1},{3,2},{4,7},{5,4},{6,5},{7,6},{8,11},{9,8},{10,9... | collective-permute-start | bytes 393224 | tf_op jit(solution)/shard_map/ppermute | solution.py:1293
  925.8 63.4 %copy-start.29 = (f32[512,128]{1,0:T(8,128)S(1)}, f32[512,128]{1,0:T(8,128)}, u32[]{:S(2)}) copy-start(f32[512,128]{1,0:T(8,128)} %constant.384.clone.sine) | copy-start | bytes 786436
  925.8 63.4 %copy-start.31 = (f32[512,128]{1,0:T(8,128)S(1)}, f32[512,128]{1,0:T(8,128)}, u32[]{:S(2)}) copy-start(f32[512,128]{1,0:T(8,128)} %constant.383.clone.cosine) | copy-start | bytes 786436
  925.8 63.4 %copy-start.33 = (f32[512,128]{1,0:T(8,128)S(1)}, f32[512,128]{1,0:T(8,128)}, u32[]{:S(2)}) copy-start(f32[512,128]{1,0:T(8,128)} %copy-done.32) | copy-start | bytes 786436
  925.8 63.3 %collective-permute-start.21 = (bf16[1,128,512]{2,1,0:T(8,128)(2,1)S(1)}, bf16[1,128,512]{2,1,0:T(8,128)(2,1)S(1)}, u32[]{:S(2)}, u32[]{:S(2)}) collective-permute-start(bf16[1,128,512]{2,1,0:T(8,128)(2,1)S(1)} %get-tuple-element.211), channel_id=1, source_target_pairs={{0,2},{1,3},{2,0},{3,1},{4,6},{5,7},{6,4},{7,5},{8,10},{9,11},{10,... | collective-permute-start | bytes 393224 | tf_op jit(solution)/shard_map/ppermute | solution.py:1293
  930.7 90.4 %collective-permute-start.49 = (bf16[1,512,1024]{2,1,0:T(8,128)(2,1)}, bf16[1,512,1024]{2,1,0:T(8,128)(2,1)}, u32[]{:S(2)}, u32[]{:S(2)}) collective-permute-start(bf16[1,512,1024]{2,1,0:T(8,128)(2,1)} %get-tuple-element.187), channel_id=1, source_target_pairs={{0,2},{1,3},{2,0},{3,1},{4,6},{5,7},{6,4},{7,5},{8,10},{9,11},{10,... | collective-permute-start | bytes 3145736 | tf_op jit(solution)/shard_map/ppermute | solution.py:1293
  1007.7 17.0 %collective-permute-start.23 = (bf16[1,128,2048]{2,1,0:T(8,128)(2,1)}, bf16[1,128,2048]{2,1,0:T(8,128)(2,1)}, u32[]{:S(2)}, u32[]{:S(2)}) collective-permute-start(bf16[1,128,2048]{2,1,0:T(8,128)(2,1)} %constant_dynamic-slice_fusion.21), channel_id=1, source_target_pairs={{0,1},{1,2},{2,3},{3,0},{4,5},{5,6},{6,7},{7,4},{8,9},{9,10},{10,1... | collective-permute-start | bytes 1572872 | tf_op jit(solution)/shard_map/ppermute | solution.py:1293
  1017.3 93.1 %collective-permute-start.50 = (bf16[1,512,1024]{2,1,0:T(8,128)(2,1)}, bf16[1,512,1024]{2,1,0:T(8,128)(2,1)}, u32[]{:S(2)}, u32[]{:S(2)}) collective-permute-start(bf16[1,512,1024]{2,1,0:T(8,128)(2,1)} %get-tuple-element.186), channel_id=1, source_target_pairs={{0,3},{1,0},{2,1},{3,2},{4,7},{5,4},{6,5},{7,6},{8,11},{9,8},{10,9... | collective-permute-start | bytes 3145736 | tf_op jit(solution)/shard_map/ppermute | solution.py:1293
  1024.6 35.0 %copy-start.50 = (bf16[512,1536]{1,0:T(8,128)(2,1)S(1)}, bf16[512,1536]{1,0:T(8,128)(2,1)}, u32[]{:S(2)}) copy-start(bf16[512,1536]{1,0:T(8,128)(2,1)} %get-tuple-element.116) | copy-start | bytes 4718596
  1026.8 52.6 %collective-permute-start.25 = (bf16[1,128,2048]{2,1,0:T(8,128)(2,1)S(1)}, bf16[1,128,2048]{2,1,0:T(8,128)(2,1)}, u32[]{:S(2)}, u32[]{:S(2)}) collective-permute-start(bf16[1,128,2048]{2,1,0:T(8,128)(2,1)S(1)} %get-tuple-element.195), channel_id=1, source_target_pairs={{0,3},{1,0},{2,1},{3,2},{4,7},{5,4},{6,5},{7,6},{8,11},{9,8},{10,9... | collective-permute-start | bytes 1572872 | tf_op jit(solution)/shard_map/ppermute | solution.py:1293
  1054.5 23.8 %collective-permute-start.24 = (bf16[1,128,2048]{2,1,0:T(8,128)(2,1)}, bf16[1,128,2048]{2,1,0:T(8,128)(2,1)}, u32[]{:S(2)}, u32[]{:S(2)}) collective-permute-start(bf16[1,128,2048]{2,1,0:T(8,128)(2,1)} %get-tuple-element.196), channel_id=1, source_target_pairs={{0,2},{1,3},{2,0},{3,1},{4,6},{5,7},{6,4},{7,5},{8,10},{9,11},{10,... | collective-permute-start | bytes 1572872 | tf_op jit(solution)/shard_map/ppermute | solution.py:1293
  1083.3 3.9 collective-permute-start.26
  1086.7 20.5 %collective-permute-start.32 = (bf16[2,2,256,1536]{3,2,1,0:T(8,128)(2,1)S(1)}, bf16[2,2,256,1536]{3,2,1,0:T(8,128)(2,1)S(1)}, u32[]{:S(2)}, u32[]{:S(2)}) collective-permute-start(bf16[2,2,256,1536]{3,2,1,0:T(8,128)(2,1)S(1)} %fusion.15), channel_id=1, source_target_pairs={{0,4},{4,0},{8,12},{12,8},{16,20},{20,16},{24,28},{28,24},{1,5},{5... | collective-permute-start | bytes 9437192 | tf_op jit(solution)/shard_map/ppermute | solution.py:1284
  1087.3 10.6 collective-permute-start.27
  1097.9 7.0 collective-permute-start.28
  1105.0 41.5 %collective-permute-start.40 = (bf16[2,2,256,2048]{3,2,1,0:T(8,128)(2,1)}, bf16[2,2,256,2048]{3,2,1,0:T(8,128)(2,1)}, u32[]{:S(2)}, u32[]{:S(2)}) collective-permute-start(bf16[2,2,256,2048]{3,2,1,0:T(8,128)(2,1)} %fusion), channel_id=1, source_target_pairs={{0,4},{4,0},{8,12},{12,8},{16,20},{20,16},{24,28},{28,24},{1,5},{5... | collective-permute-start | bytes 12582920 | tf_op jit(solution)/shard_map/ppermute | solution.py:1284
  1105.0 16.2 %collective-permute-start.31 = (f32[1,1160]{1,0:T(1,128)S(1)}, f32[1,1160]{1,0:T(1,128)S(1)}, u32[]{:S(2)}, u32[]{:S(2)}) collective-permute-start(f32[1,1160]{1,0:T(1,128)S(1)} %get-tuple-element.219), channel_id=1, source_target_pairs={{0,3},{1,0},{2,1},{3,2},{4,7},{5,4},{6,5},{7,6},{8,11},{9,8},{10,9... | collective-permute-start | bytes 13928 | tf_op jit(solution)/shard_map/ppermute | solution.py:1293
  1107.1 14.0 %collective-permute-start.30 = (f32[1,1160]{1,0:T(1,128)S(1)}, f32[1,1160]{1,0:T(1,128)S(1)}, u32[]{:S(2)}, u32[]{:S(2)}) collective-permute-start(f32[1,1160]{1,0:T(1,128)S(1)} %get-tuple-element.220), channel_id=1, source_target_pairs={{0,2},{1,3},{2,0},{3,1},{4,6},{5,7},{6,4},{7,5},{8,10},{9,11},{10,... | collective-permute-start | bytes 13928 | tf_op jit(solution)/shard_map/ppermute | solution.py:1293
  1107.2 13.8 %collective-permute-start.29 = (f32[1,1160]{1,0:T(1,128)S(1)}, f32[1,1160]{1,0:T(1,128)S(1)}, u32[]{:S(2)}, u32[]{:S(2)}) collective-permute-start(f32[1,1160]{1,0:T(1,128)S(1)} %get-tuple-element.221), channel_id=1, source_target_pairs={{0,1},{1,2},{2,3},{3,0},{4,5},{5,6},{6,7},{7,4},{8,9},{9,10},{10,1... | collective-permute-start | bytes 13928 | tf_op jit(solution)/shard_map/ppermute | solution.py:1293
  1110.4 19.7 %collective-permute-start.35 = (bf16[2,128,1536]{2,1,0:T(8,128)(2,1)}, bf16[2,128,1536]{2,1,0:T(8,128)(2,1)}, u32[]{:S(2)}, u32[]{:S(2)}) collective-permute-start(bf16[2,128,1536]{2,1,0:T(8,128)(2,1)} %fusion.20), channel_id=1, source_target_pairs={{0,16},{4,20},{8,24},{12,28},{16,0},{20,4},{24,8},{28,12},{1,17},{... | collective-permute-start | bytes 2359304 | tf_op jit(solution)/shard_map/ppermute | solution.py:1284
  1123.2 20.8 %collective-permute-start.33 = (bf16[2,128,1536]{2,1,0:T(8,128)(2,1)}, bf16[2,128,1536]{2,1,0:T(8,128)(2,1)}, u32[]{:S(2)}, u32[]{:S(2)}) collective-permute-start(bf16[2,128,1536]{2,1,0:T(8,128)(2,1)} %fusion.21), channel_id=1, source_target_pairs={{0,8},{4,12},{8,0},{12,4},{16,24},{20,28},{24,16},{28,20},{1,9},{5... | collective-permute-start | bytes 2359304 | tf_op jit(solution)/shard_map/ppermute | solution.py:1284
  1132.8 23.1 %collective-permute-start.36 = (bf16[128,1536]{1,0:T(8,128)(2,1)}, bf16[128,1536]{1,0:T(8,128)(2,1)S(1)}, u32[]{:S(2)}, u32[]{:S(2)}) collective-permute-start(bf16[128,1536]{1,0:T(8,128)(2,1)} %fusion.29), channel_id=1, source_target_pairs={{0,8},{4,12},{8,0},{12,4},{16,24},{20,28},{24,16},{28,20},{1,9},{5... | collective-permute-start | bytes 1179656 | tf_op jit(solution)/shard_map/ppermute | solution.py:1284
  1145.4 10.7 collective-permute-start.34
  1153.6 22.7 %collective-permute-start.43 = (bf16[2,128,2048]{2,1,0:T(8,128)(2,1)S(1)}, bf16[2,128,2048]{2,1,0:T(8,128)(2,1)S(1)}, u32[]{:S(2)}, u32[]{:S(2)}) collective-permute-start(bf16[2,128,2048]{2,1,0:T(8,128)(2,1)S(1)} %fusion.16), channel_id=1, source_target_pairs={{0,16},{4,20},{8,24},{12,28},{16,0},{20,4},{24,8},{28,12},{1,17},{... | collective-permute-start | bytes 3145736 | tf_op jit(solution)/shard_map/ppermute | solution.py:1284
  1154.8 23.2 %collective-permute-start.41 = (bf16[2,128,2048]{2,1,0:T(8,128)(2,1)S(1)}, bf16[2,128,2048]{2,1,0:T(8,128)(2,1)S(1)}, u32[]{:S(2)}, u32[]{:S(2)}) collective-permute-start(bf16[2,128,2048]{2,1,0:T(8,128)(2,1)S(1)} %fusion.17), channel_id=1, source_target_pairs={{0,8},{4,12},{8,0},{12,4},{16,24},{20,28},{24,16},{28,20},{1,9},{5... | collective-permute-start | bytes 3145736 | tf_op jit(solution)/shard_map/ppermute | solution.py:1284
  1158.0 21.6 %collective-permute-start.37 = (bf16[1,64,1536]{2,1,0:T(8,128)(2,1)S(1)}, bf16[1,64,1536]{2,1,0:T(8,128)(2,1)S(1)}, u32[]{:S(2)}, u32[]{:S(2)}) collective-permute-start(bf16[1,64,1536]{2,1,0:T(8,128)(2,1)S(1)} %constant_dynamic-slice_fusion.11), channel_id=1, source_target_pairs={{0,1},{1,2},{2,3},{3,0},{4,5},{5,6},{6,7},{7,4},{8,9},{9,10},{10,1... | collective-permute-start | bytes 589832 | tf_op jit(solution)/shard_map/ppermute | solution.py:1293
  1176.7 11.6 collective-permute-start.44
  1178.4 10.0 collective-permute-start.42
  1181.4 18.9 %collective-permute-start.39 = (bf16[1,64,1536]{2,1,0:T(8,128)(2,1)S(1)}, bf16[1,64,1536]{2,1,0:T(8,128)(2,1)S(1)}, u32[]{:S(2)}, u32[]{:S(2)}) collective-permute-start(bf16[1,64,1536]{2,1,0:T(8,128)(2,1)S(1)} %get-tuple-element.207), channel_id=1, source_target_pairs={{0,3},{1,0},{2,1},{3,2},{4,7},{5,4},{6,5},{7,6},{8,11},{9,8},{10,9... | collective-permute-start | bytes 589832 | tf_op jit(solution)/shard_map/ppermute | solution.py:1293
  1184.5 15.1 %collective-permute-start.38 = (bf16[1,64,1536]{2,1,0:T(8,128)(2,1)S(1)}, bf16[1,64,1536]{2,1,0:T(8,128)(2,1)S(1)}, u32[]{:S(2)}, u32[]{:S(2)}) collective-permute-start(bf16[1,64,1536]{2,1,0:T(8,128)(2,1)S(1)} %get-tuple-element.208), channel_id=1, source_target_pairs={{0,2},{1,3},{2,0},{3,1},{4,6},{5,7},{6,4},{7,5},{8,10},{9,11},{10,... | collective-permute-start | bytes 589832 | tf_op jit(solution)/shard_map/ppermute | solution.py:1293
  1189.4 14.4 %collective-permute-start.45 = (bf16[1,64,2048]{2,1,0:T(8,128)(2,1)}, bf16[1,64,2048]{2,1,0:T(8,128)(2,1)S(1)}, u32[]{:S(2)}, u32[]{:S(2)}) collective-permute-start(bf16[1,64,2048]{2,1,0:T(8,128)(2,1)} %constant_dynamic-slice_fusion.8), channel_id=1, source_target_pairs={{0,1},{1,2},{2,3},{3,0},{4,5},{5,6},{6,7},{7,4},{8,9},{9,10},{10,1... | collective-permute-start | bytes 786440 | tf_op jit(solution)/shard_map/ppermute | solution.py:1293
  1203.9 14.1 %collective-permute-start.47 = (bf16[1,64,2048]{2,1,0:T(8,128)(2,1)S(1)}, bf16[1,64,2048]{2,1,0:T(8,128)(2,1)S(1)}, u32[]{:S(2)}, u32[]{:S(2)}) collective-permute-start(bf16[1,64,2048]{2,1,0:T(8,128)(2,1)S(1)} %get-tuple-element.204), channel_id=1, source_target_pairs={{0,3},{1,0},{2,1},{3,2},{4,7},{5,4},{6,5},{7,6},{8,11},{9,8},{10,9... | collective-permute-start | bytes 786440 | tf_op jit(solution)/shard_map/ppermute | solution.py:1293
  1203.9 14.0 %collective-permute-start.46 = (bf16[1,64,2048]{2,1,0:T(8,128)(2,1)S(1)}, bf16[1,64,2048]{2,1,0:T(8,128)(2,1)S(1)}, u32[]{:S(2)}, u32[]{:S(2)}) collective-permute-start(bf16[1,64,2048]{2,1,0:T(8,128)(2,1)S(1)} %get-tuple-element.205), channel_id=1, source_target_pairs={{0,2},{1,3},{2,0},{3,1},{4,6},{5,7},{6,4},{7,5},{8,10},{9,11},{10,... | collective-permute-start | bytes 786440 | tf_op jit(solution)/shard_map/ppermute | solution.py:1293
  (46 other events, 270.1 us)

commit v2 on v1

--- a/solution.py
+++ b/solution.py
@@ -516,26 +516,16 @@
 
 
 def expert_kernel(
-    first, experts, blocks, x, g, keep, wide_w, router_w, down_w, hot, *refs
+    experts, x, g, keep, wide_w, router_w, down_w, hot,
+    out, grad, wide_sum, router_sum, down_sum, acc, racc, dacc, wide_out, down_out, sems,
 ):
-    del blocks
-    if first:
-        out, grad, wide_sum, router_sum, down_sum, acc, racc, dacc, sems = refs
-    else:
-        wide_in, router_in, down_in, out, grad, wide_sum, router_sum, down_sum = refs[:8]
-        acc, racc, dacc, sems = refs[8:]
     step, steps = pl.program_id(0), pl.num_programs(0)
 
     @pl.when(step == 0)
     def _():
-        if first:
-            acc[...] = jnp.zeros_like(acc)
-            racc[...] = jnp.zeros_like(racc)
-            dacc[...] = jnp.zeros_like(dacc)
-        else:
-            pltpu.make_async_copy(wide_in, acc, sems.at[0]).start()
-            pltpu.make_async_copy(router_in, racc, sems.at[1]).start()
-            pltpu.make_async_copy(down_in, dacc, sems.at[2]).start()
+        acc[...] = jnp.zeros_like(acc)
+        racc[...] = jnp.zeros_like(racc)
+        dacc[...] = jnp.zeros_like(dacc)
 
     shards, units, part = down_w.shape
     own = keep.shape[1]
@@ -577,14 +567,6 @@
     grad[...] = (nt_dot(wide_low, wide_w[...]) + nt_dot(logit_low, router_w[...])).astype(
         jnp.bfloat16
     )
-    if not first:
-
-        @pl.when(step == 0)
-        def _():
-            pltpu.make_async_copy(wide_in, acc, sems.at[0]).wait()
-            pltpu.make_async_copy(router_in, racc, sems.at[1]).wait()
-            pltpu.make_async_copy(down_in, dacc, sems.at[2]).wait()
-
     acc[...] += tn_dot(x[...], wide_low)
     racc[...] += tn_dot(x[...], logit_low)
     for shard in range(shards):
@@ -592,109 +574,67 @@
 
     @pl.when(step == steps - 1)
     def _():
-        copies = [
-            pltpu.make_async_copy(acc, wide_sum, sems.at[0]),
-            pltpu.make_async_copy(racc, router_sum, sems.at[1]),
-            pltpu.make_async_copy(dacc, down_sum, sems.at[2]),
-        ]
-        for copy in copies:
-            copy.start()
-        for copy in copies:
-            copy.wait()
-
-
-def expert_call(blocks, x_all, g_all, keep, wide_w, router_w, down_w, hot, experts, sums):
-    _, rows, width = x_all.shape
-    count = blocks.shape[0]
+        router_copy = pltpu.make_async_copy(racc, router_sum, sems.at[1])
+        router_copy.start()
+        wide_out[...] = acc[...].astype(jnp.bfloat16)
+        wide_copy = pltpu.make_async_copy(wide_out, wide_sum, sems.at[0])
+        wide_copy.start()
+        down_out[...] = dacc[...].astype(jnp.bfloat16)
+        down_copy = pltpu.make_async_copy(down_out, down_sum, sems.at[2])
+        down_copy.start()
+        router_copy.wait()
+        wide_copy.wait()
+        down_copy.wait()
+
+
+def expert_call(x_all, g_all, keep, wide_w, router_w, down_w, hot, experts):
+    planes, rows, width = x_all.shape
     tile = 256
     per = rows // tile
-    hbm = pl.BlockSpec(memory_space=pl.ANY)
+    hbm = pl.BlockSpec(memory_space=pltpu.HBM)
 
     def whole(value):
         zeros = (0,) * value.ndim
-        return pl.BlockSpec(value.shape, lambda i, b: zeros, pipeline_mode=pl.Buffered(1))
-
-    def chosen(lanes):
-        return pl.BlockSpec((None, tile, lanes), lambda i, b: (b[i // per], i % per, 0))
-
-    rowwise = pl.BlockSpec((None, tile, width), lambda i, b: (i // per, i % per, 0))
-    shapes = (
-        jax.ShapeDtypeStruct(wide_w.shape, jnp.float32),
-        jax.ShapeDtypeStruct(router_w.shape, jnp.float32),
-        jax.ShapeDtypeStruct(down_w.shape, jnp.float32),
-    )
-    first = sums is None
-    result = pl.pallas_call(
-        functools.partial(expert_kernel, first, experts),
-        grid_spec=pltpu.PrefetchScalarGridSpec(
-            num_scalar_prefetch=1,
-            grid=(count * per,),
-            in_specs=[
-                chosen(width),
-                chosen(width),
-                chosen(keep.shape[2]),
-                whole(wide_w),
-                whole(router_w),
-                whole(down_w),
-                whole(hot),
-            ]
-            + ([] if first else [hbm] * 3),
-            out_specs=[rowwise, rowwise, hbm, hbm, hbm],
-            scratch_shapes=[
-                pltpu.VMEM(wide_w.shape, jnp.float32),
-                pltpu.VMEM(router_w.shape, jnp.float32),
-                pltpu.VMEM(down_w.shape, jnp.float32),
-                pltpu.SemaphoreType.DMA((3,)),
-            ],
-        ),
+        return pl.BlockSpec(value.shape, lambda i: zeros, pipeline_mode=pl.Buffered(1))
+
+    def rowwise(lanes):
+        return pl.BlockSpec((None, tile, lanes), lambda i: (i // per, i % per, 0))
+
+    return pl.pallas_call(
+        functools.partial(expert_kernel, experts),
+        grid=(planes * per,),
+        in_specs=[
+            rowwise(width),
+            rowwise(width),
+            rowwise(keep.shape[2]),
+            whole(wide_w),
+            whole(router_w),
+            whole(down_w),
+            whole(hot),
+        ],
+        out_specs=[rowwise(width), rowwise(width), hbm, hbm, hbm],
+        scratch_shapes=[
+            pltpu.VMEM(wide_w.shape, jnp.float32),
+            pltpu.VMEM(router_w.shape, jnp.float32),
+            pltpu.VMEM(down_w.shape, jnp.float32),
+            pltpu.VMEM(wide_w.shape, jnp.bfloat16),
+            pltpu.VMEM(down_w.shape, jnp.bfloat16),
+            pltpu.SemaphoreType.DMA((3,)),
+        ],
         out_shape=(
-            jax.ShapeDtypeStruct((count, rows, width), jnp.bfloat16),
-            jax.ShapeDtypeStruct((count, rows, width), jnp.bfloat16),
-        )
-        + shapes,
-        input_output_aliases={} if first else {8: 2, 9: 3, 10: 4},
+            jax.ShapeDtypeStruct((planes, rows, width), jnp.bfloat16),
+            jax.ShapeDtypeStruct((planes, rows, width), jnp.bfloat16),
+            jax.ShapeDtypeStruct(wide_w.shape, jnp.bfloat16),
+            jax.ShapeDtypeStruct(router_w.shape, jnp.float32),
+            jax.ShapeDtypeStruct(down_w.shape, jnp.bfloat16),
+        ),
         compiler_params=vmem_params(56),
         cost_estimate=pl.CostEstimate(
-            flops=2 * count * rows * width * (3 * wide_w.shape[1] + 3 * down_w.shape[1]),
-            bytes_accessed=40 * MIB,
-            transcendentals=count * rows * down_w.shape[1],
-        ),
-    )(blocks, x_all, g_all, keep, wide_w, router_w, down_w, hot, *(() if first else sums))
-    return result[0], result[1], result[2:]
-
-
-def turn_back_kernel(
-    hidden, grad, out_grad, gain, weight, hidden_grad_out, low_out, message_out, gain_grad_out
-):
-    shards, _, part = message_out.shape
-    factor = norm_factor(hidden[...])
-    gain_grad_out[...] = jnp.sum(grad[...] * hidden[...] * factor, axis=0, keepdims=True)
-    scaled = grad[...] * gain[...]
-    inner = jnp.mean(scaled * hidden[...], axis=-1, keepdims=True)
-    total = out_grad[...].astype(jnp.float32) + factor * scaled
-    total = total - hidden[...] * (factor * factor * factor) * inner
-    hidden_grad_out[...] = total
-    low = total.astype(jnp.bfloat16)
-    low_out[...] = low
-    for shard in range(shards):
-        message_out[shard] = nt_dot(low, weight[pl.ds(shard * part, part), :]).astype(jnp.bfloat16)
-
-
-def turn_back_call(hidden, grad, out_grad, gain, weight, shards):
-    rows, width = hidden.shape
-    return pl.pallas_call(
-        turn_back_kernel,
-        out_shape=(
-            jax.ShapeDtypeStruct((rows, width), jnp.float32),
-            jax.ShapeDtypeStruct((rows, width), jnp.bfloat16),
-            jax.ShapeDtypeStruct((shards, rows, width // shards), jnp.bfloat16),
-            jax.ShapeDtypeStruct((1, width), jnp.float32),
-        ),
-        compiler_params=vmem_params(40),
-        cost_estimate=pl.CostEstimate(
-            flops=2 * rows * width * width, bytes_accessed=12 * MIB, transcendentals=0
-        ),
-    )(hidden, grad, out_grad, gain, weight)
+            flops=2 * planes * rows * width * (3 * wide_w.shape[1] + 3 * down_w.shape[1]),
+            bytes_accessed=100 * MIB,
+            transcendentals=planes * rows * down_w.shape[1],
+        ),
+    )(x_all, g_all, keep, wide_w, router_w, down_w, hot)
 
 
 def attend_back_kernel(
@@ -756,31 +696,6 @@
     )(mixed_grad, raw, low, total, weight, query_gain, key_gain, *tables, seg_row, seg_col)
 
 
-def finish_kernel(pieces, tokens, hidden_grad, gain, grad_out, gain_grad_out):
-    grad = pieces[0].astype(jnp.float32)
-    for shard in range(1, pieces.shape[0]):
-        grad = grad + pieces[shard].astype(jnp.float32)
-    values = tokens[...].astype(jnp.float32)
-    factor = norm_factor(values)
-    gain_grad_out[...] = jnp.sum(grad * values * factor, axis=0, keepdims=True)
-    scaled = grad * gain[...]
-    inner = jnp.mean(scaled * values, axis=-1, keepdims=True)
-    total = hidden_grad[...] + factor * scaled - values * (factor * factor * factor) * inner
-    grad_out[...] = total.astype(jnp.bfloat16)
-
-
-def finish_call(pieces, tokens, hidden_grad, gain):
-    rows, width = tokens.shape
-    return pl.pallas_call(
-        finish_kernel,
-        out_shape=(
-            jax.ShapeDtypeStruct((rows, width), jnp.bfloat16),
-            jax.ShapeDtypeStruct((1, width), jnp.float32),
-        ),
-        compiler_params=vmem_params(24),
-    )(pieces, tokens, hidden_grad, gain)
-
-
 def copy_kernel(*refs):
     half = len(refs) // 2
     for source, result in zip(refs[:half], refs[half:], strict=True):
@@ -813,6 +728,36 @@
     return gate_grad, up_grad, down_grad
 
 
+def keep_kernel(capacity, bits, shards, high, low, keep_out):
+    own, _, rows = high.shape
+    for index in range(own):
+        order = high[index].astype(jnp.float32) * 256.0 + low[index].astype(jnp.float32)
+        there = order > 0.0
+        row = lax.broadcasted_iota(jnp.int32, order.shape, 0)
+        group = lax.rem(row, shards)
+        bound = jnp.zeros_like(order)
+        for bit in reversed(range(bits)):
+            trial = bound + float(1 << bit)
+            within = jnp.where(there & (order <= trial), 1.0, 0.0)
+            for shard in range(shards):
+                here = group == shard
+                count = jnp.sum(jnp.where(here, within, 0.0), keepdims=True)
+                bound = jnp.where(here & (count <= float(capacity)), trial, bound)
+        kept = jnp.where(there & (order <= bound), 1.0, 0.0).T
+        for block in range(order.shape[0]):
+            place = keep_out.at[block // shards, pl.ds(block % shards * rows, rows)]
+            place[:, index : index + 1] = kept[:, block : block + 1]
+
+
+def keep_call(high, low, capacity, most, planes, shards):
+    own, _, rows = high.shape
+    return pl.pallas_call(
+        functools.partial(keep_kernel, capacity, most.bit_length(), shards),
+        out_shape=jax.ShapeDtypeStruct((planes, shards * rows, own), jnp.float32),
+        compiler_params=vmem_params(24),
+    )(high, low)
+
+
 CORE, XBIT, YBIT = 1, 2, 4
 
 
@@ -979,8 +924,8 @@
 
 
 def opening_kernel(
-    shards, small, w_query, w_key, w_value, tokens, w_out, out_grad,
-    small_all, qkv_w, tokens_all, out_block, grad_seq, send, recv, local,
+    shards, experts, routes, order, gains, router, w_query, w_key, w_value, tokens, w_out, out_grad,
+    small_all, router_all, qkv_w, tokens_all, out_block, grad_seq, small, send, recv, local,
 ):
     wires = Wires(send, recv)
     device, shard = wires.device, wires.shard
@@ -1000,14 +945,14 @@
     def cut(which, target):
         return weights[which].at[:, pl.ds(pl.multiple_of(target * part, part), part)]
 
-    exchange = [[wires.slot() for _ in range(4)] for _ in range(1, shards)]
+    mine = device * shards + shard
+    exchange = [[wires.slot() for _ in range(5)] for _ in range(1, shards)]
     sent = []
     for step in range(1, shards):
         peer = wires.peer(step=step, shards=shards)
-        copies = [
-            wires.copy(small, small_all.at[device * shards + shard], exchange[step - 1][3], peer)
-        ] + [
-            wires.copy(cut(which, peer[1]), place(shard, which), exchange[step - 1][which], peer)
+        slots = exchange[step - 1]
+        copies = [wires.copy(router, router_all.at[mine], slots[4], peer)] + [
+            wires.copy(cut(which, peer[1]), place(shard, which), slots[which], peer)
             for which in range(3)
         ]
         for copy in copies:
@@ -1018,7 +963,7 @@
         for which in range(3)
     ]
     own += [
-        pltpu.make_async_copy(small, small_all.at[device * shards + shard], local.at[3]),
+        pltpu.make_async_copy(router, router_all.at[mine], local.at[3]),
         pltpu.make_async_copy(
             tokens, tokens_all.at[pl.ds(pl.multiple_of(shard * rows, rows), rows)], local.at[4]
         ),
@@ -1041,6 +986,23 @@
         ],
     )
     line.run(0, (tokens, w_out, out_grad))
+    column = lax.broadcasted_iota(jnp.int32, (rows, 128), 1)
+    dense = jnp.zeros((rows, 128), jnp.int32)
+    for choice in range(routes.shape[1]):
+        named = routes[:, choice : choice + 1] == column
+        dense = dense + jnp.where(named, order[:, choice : choice + 1] + 1, 0)
+    high = lax.shift_right_logical(dense, 8)
+    for start, digits in ((0, high), (experts, dense - high * 256)):
+        turned = digits.astype(jnp.float32).T
+        small[pl.ds(start, experts), :] = turned[:experts, :].astype(small.dtype)
+    small[pl.ds(2 * experts, gains.shape[0]), :] = gains[...]
+    for step in range(1, shards):
+        peer = wires.peer(step=step, shards=shards)
+        copy = wires.copy(small, small_all.at[mine], exchange[step - 1][3], peer)
+        copy.start()
+        sent.append(copy)
+    own.append(pltpu.make_async_copy(small, small_all.at[mine], local.at[7]))
+    own[-1].start()
     for copy in own:
         copy.wait()
     for step in range(1, shards):
@@ -1048,6 +1010,7 @@
         source = peer[1]
         slots = exchange[step - 1]
         wires.copy(small, small_all.at[device * shards + source], slots[3], peer).wait_recv()
+        wires.copy(router, router_all.at[device * shards + source], slots[4], peer).wait_recv()
         for which in range(3):
             wires.copy(place(source, which), place(source, which), slots[which], peer).wait_recv()
 
@@ -1059,12 +1022,16 @@
     def small_of(owner, half):
         return small_all.at[pl.ds((owner * 2 + half) * (shards // 2), shards // 2)]
 
+    def router_of(owner, half):
+        return router_all.at[pl.ds((owner * 2 + half) * (shards // 2), shards // 2)]
+
     plane = Plane(
         wires,
-        [rows_of, small_of],
+        [rows_of, small_of, router_of],
         [
             lambda owner: qkv_w.at[pl.ds(pl.multiple_of(owner * 2 * each, 2 * each), 2 * each)],
             lambda owner: small_all.at[pl.ds(owner * shards, shards)],
+            lambda owner: router_all.at[pl.ds(owner * shards, shards)],
         ],
     )
     plane.step_one()
@@ -1081,32 +1048,38 @@
     line.drain()
 
 
-def opening_call(small, w_query, w_key, w_value, tokens, w_out, out_grad, planes, shards):
+def opening_call(
+    routes, order, gains, router, w_query, w_key, w_value, tokens, w_out, out_grad, experts, planes, shards
+):
     block, width = w_query.shape
     rows = tokens.shape[0]
-    hbm = pl.BlockSpec(memory_space=pl.ANY)
-    slots = 64
+    hbm = pl.BlockSpec(memory_space=pltpu.HBM)
+    vmem = pl.BlockSpec(memory_space=pltpu.VMEM)
+    slots = 72
+    small = (2 * experts + gains.shape[0], 128)
     return pl.pallas_call(
-        functools.partial(opening_kernel, shards),
-        in_specs=[hbm] * 7,
-        out_specs=[hbm] * 5,
+        functools.partial(opening_kernel, shards, experts),
+        in_specs=[vmem] * 3 + [hbm] * 7,
+        out_specs=[hbm] * 6,
         out_shape=(
-            jax.ShapeDtypeStruct((planes * shards,) + small.shape, small.dtype),
+            jax.ShapeDtypeStruct((planes * shards,) + small, gains.dtype),
+            jax.ShapeDtypeStruct((planes * shards,) + router.shape, router.dtype),
             jax.ShapeDtypeStruct((planes * shards * block, 3 * width // shards), w_query.dtype),
             jax.ShapeDtypeStruct((shards * rows, width), tokens.dtype),
             jax.ShapeDtypeStruct((shards * block, width), w_out.dtype),
             jax.ShapeDtypeStruct((shards * rows, width), out_grad.dtype),
         ),
         scratch_shapes=[
+            pltpu.VMEM(small, gains.dtype),
             pltpu.SemaphoreType.DMA((slots,)),
             pltpu.SemaphoreType.DMA((slots,)),
-            pltpu.SemaphoreType.DMA((7,)),
+            pltpu.SemaphoreType.DMA((8,)),
         ],
         compiler_params=pltpu.CompilerParams(
             collective_id=1, has_side_effects=True, vmem_limit_bytes=4 * MIB
         ),
         cost_estimate=pl.CostEstimate(flops=0, bytes_accessed=200 * MIB, transcendentals=0),
-    )(small, w_query, w_key, w_value, tokens, w_out, out_grad)
+    )(routes, order, gains, router, w_query, w_key, w_value, tokens, w_out, out_grad)
 
 
 def middle_kernel(shards, mixed, out_block, mixed_all, out_w, send, recv, local):
@@ -1149,7 +1122,7 @@
 
 
 def middle_call(mixed, out_block, planes, shards):
-    hbm = pl.BlockSpec(memory_space=pl.ANY)
+    hbm = pl.BlockSpec(memory_space=pltpu.HBM)
     slots = 32
     return pl.pallas_call(
         functools.partial(middle_kernel, shards),
@@ -1249,7 +1222,7 @@
 
 
 def meeting_call(normed, grad_seq, gate, up, down, planes, shards):
-    hbm = pl.BlockSpec(memory_space=pl.ANY)
+    hbm = pl.BlockSpec(memory_space=pltpu.HBM)
     own, part, hidden_units = gate.shape
     count = own * hidden_units // shards
     slots = 48
@@ -1275,6 +1248,469 @@
     )(normed, grad_seq, gate, up, down)
 
 
+def add_rows(target, sources, lines):
+    rows = target.shape[0]
+
+    def body(index, carry):
+        span = pl.ds(pl.multiple_of(index * lines, lines), lines)
+        total = target[span, :].astype(jnp.float32)
+        for source in sources:
+            total = total + source[span, :].astype(jnp.float32)
+        target[span, :] = total.astype(target.dtype)
+        return carry
+
+    lax.fori_loop(0, rows // lines, body, 0)
+
+
+class PlaneSum:
+    def __init__(self, wires, part, held, came, diag, side, local, base):
+        self.wires, self.part, self.local, self.base = wires, part, local, base
+        self.held, self.came, self.diag, self.side = held, came, diag, side
+        self.half = held.shape[1] // 2
+        self.core = [wires.slot() for _ in range(4)]
+        self.corner = [wires.slot() for _ in range(2)]
+        self.edge = [wires.slot() for _ in range(2)]
+        self.sent = []
+
+    def start(self, copy):
+        copy.start()
+        self.sent.append(copy)
+
+    def load(self, chip):
+        return pltpu.make_async_copy(
+            self.part(chip, 0), self.held.at[chip], self.local.at[self.base + chip]
+        )
+
+    def begin(self):
+        for chip in (3, 1, 2, 0):
+            self.load(chip).start()
+            self.start(
+                self.wires.copy(
+                    self.part(chip, 1), self.came.at[chip], self.core[chip], self.wires.peer(CORE)
+                )
+            )
+
+    def add_core(self, chip):
+        self.load(chip).wait()
+        place = self.came.at[chip]
+        self.wires.copy(place, place, self.core[chip], self.wires.peer(CORE)).wait_recv()
+        add_rows(self.held.at[chip], [place], 64)
+
+    def part_of_corner(self, which):
+        return self.held.at[3, pl.ds(which * self.half, self.half)]
+
+    def send_corner(self):
+        self.add_core(3)
+        for which, bits in enumerate((XBIT, YBIT)):
+            self.start(
+                self.wires.copy(
+                    self.part_of_corner(which),
+                    self.diag.at[which],
+                    self.corner[which],
+                    self.wires.peer(bits),
+                )
+            )
+
+    def add_cores(self):
+        for chip in (1, 2, 0):
+            self.add_core(chip)
+
+    def send_sides(self):
+        for which, (bits, chip) in enumerate(((XBIT, 2), (YBIT, 1))):
+            place = self.diag.at[which]
+            self.wires.copy(place, place, self.corner[which], self.wires.peer(bits)).wait_recv()
+            add_rows(self.held.at[chip, pl.ds(which * self.half, self.half)], [place], 64)
+            self.start(
+                self.wires.copy(
+                    self.held.at[chip],
+                    self.side.at[1 - which],
+                    self.edge[1 - which],
+                    self.wires.peer((XBIT | YBIT) ^ bits),
+                )
+            )
+
+    def end(self):
+        for which, bits in enumerate((XBIT, YBIT)):
+            place = self.side.at[which]
+            self.wires.copy(place, place, self.edge[which], self.wires.peer(bits)).wait_recv()
+        add_rows(self.held.at[0], [self.side.at[0], self.side.at[1]], 64)
+
+    def drain(self):
+        for copy in self.sent:
+            copy.wait_send()
+
+
+class LineSum:
+    def __init__(self, wires, shards, source, landing):
+        self.wires, self.shards, self.source, self.landing = wires, shards, source, landing
+        self.slots = [wires.slot() for _ in range(shards - 1)]
+        self.sent = []
+
+    def begin(self):
+        wires = self.wires
+        for step in range(1, self.shards):
+            peer = wires.peer(step=step, shards=self.shards)
+            copy = wires.copy(
+                self.source(peer[1]), self.landing(wires.shard), self.slots[step - 1], peer
+            )
+            copy.start()
+            self.sent.append(copy)
+
+    def arrive(self):
+        wires = self.wires
+        for step in range(1, self.shards):
+            peer = wires.peer(step=self.shards - step, shards=self.shards)
+            place = self.landing(peer[1])
+            wires.copy(place, place, self.slots[step - 1], peer).wait_recv()
+
+    def drain(self):
+        for copy in self.sent:
+            copy.wait_send()
+
+
+def line_total(landing, shards):
+    total = landing[0].astype(jnp.float32)
+    for shard in range(1, shards):
+        total = total + landing[shard].astype(jnp.float32)
+    return total
+
+
+def aligned(index, size):
+    return pl.ds(pl.multiple_of(index * size, size), size)
+
+
+def returning_kernel(
+    shards, ins, outs, wide,
+    in_total, out_total, wide_all,
+    held, came, diag, side, held2, came2, diag2, side2, landing, send, recv, local,
+):
+    wires = Wires(send, recv)
+    device, shard = wires.device, wires.shard
+    rows = in_total.shape[0]
+    greet(
+        [wires.peer(step=step, shards=shards) for step in range(1, shards)]
+        + [wires.peer(XBIT), wires.peer(YBIT), wires.peer(CORE)]
+    )
+
+    def rel(source):
+        return lambda chip, core: source.at[device ^ (2 * chip + core)]
+
+    grads = PlaneSum(wires, rel(ins), held, came, diag, side, local, 0)
+    values = PlaneSum(wires, rel(outs), held2, came2, diag2, side2, local, 4)
+    weights = LineSum(wires, shards, lambda t: wide.at[t], lambda s: wide_all.at[s])
+    line = LineSum(
+        wires, shards, lambda t: held.at[0, aligned(t, rows)], lambda s: landing.at[s]
+    )
+    grads.begin()
+    weights.begin()
+    own = pltpu.make_async_copy(wide.at[shard], wide_all.at[shard], local.at[8])
+    own.start()
+    grads.send_corner()
+    values.begin()
+    grads.add_cores()
+    grads.send_sides()
+    values.send_corner()
+    values.add_cores()
+    grads.end()
+    line.begin()
+    values.send_sides()
+    landing[shard] = held[0, aligned(shard, rows), :]
+    line.arrive()
+    in_total[...] = line_total(landing, shards)
+    values.end()
+    back = pltpu.make_async_copy(held2.at[0], out_total, local.at[9])
+    back.start()
+    weights.arrive()
+    own.wait()
+    back.wait()
+    for group in (grads, values, weights, line):
+        group.drain()
+
+
+def returning_call(ins, outs, wide, shards):
+    _, seq, width = ins.shape
+    rows = seq // shards
+    hbm = pl.BlockSpec(memory_space=pltpu.HBM)
+    vmem = pl.BlockSpec(memory_space=pltpu.VMEM)
+    low = jnp.bfloat16
+    work = [
+        pltpu.VMEM((4, seq, width), low),
+        pltpu.VMEM((4, seq, width), low),
+        pltpu.VMEM((2, seq // 2, width), low),
+        pltpu.VMEM((2, seq, width), low),
+    ]
+    return pl.pallas_call(
+        functools.partial(returning_kernel, shards),
+        in_specs=[hbm] * 3,
+        out_specs=[vmem, hbm, hbm],
+        out_shape=(
+            jax.ShapeDtypeStruct((rows, width), jnp.float32),
+            jax.ShapeDtypeStruct((seq, width), low),
+            jax.ShapeDtypeStruct(wide.shape, wide.dtype),
+        ),
+        scratch_shapes=work
+        + work
+        + [
+            pltpu.VMEM((shards, rows, width), low),
+            pltpu.SemaphoreType.DMA((32,)),
+            pltpu.SemaphoreType.DMA((32,)),
+            pltpu.SemaphoreType.DMA((10,)),
+        ],
+        compiler_params=pltpu.CompilerParams(
+            collective_id=4, has_side_effects=True, vmem_limit_bytes=58 * MIB
+        ),
+        cost_estimate=pl.CostEstimate(flops=0, bytes_accessed=300 * MIB, transcendentals=0),
+    )(ins, outs, wide)
+
+
+def turn_back_kernel(
+    shards, hidden, grad, out_grad, gain, weight,
+    hidden_grad_out, low_out, gain_grad_out, message_all, message, send, recv, local,
+):
+    wires = Wires(send, recv)
+    part = message.shape[2]
+    greet([wires.peer(step=step, shards=shards) for step in range(1, shards)])
+    factor = norm_factor(hidden[...])
+    gain_grad_out[...] = jnp.sum(grad[...] * hidden[...] * factor, axis=0, keepdims=True)
+    scaled = grad[...] * gain[...]
+    inner = jnp.mean(scaled * hidden[...], axis=-1, keepdims=True)
+    total = out_grad[...].astype(jnp.float32) + factor * scaled
+    total = total - hidden[...] * (factor * factor * factor) * inner
+    hidden_grad_out[...] = total
+    low = total.astype(jnp.bfloat16)
+    low_out[...] = low
+    for shard in range(shards):
+        message[shard] = nt_dot(low, weight[pl.ds(shard * part, part), :]).astype(jnp.bfloat16)
+    line = LineSum(wires, shards, lambda t: message.at[t], lambda s: message_all.at[s])
+    line.begin()
+    own = pltpu.make_async_copy(message.at[wires.shard], message_all.at[wires.shard], local.at[0])
+    own.start()
+    own.wait()
+    line.arrive()
+    line.drain()
+
+
+def turn_back_call(hidden, grad, out_grad, gain, weight, shards):
+    rows, width = hidden.shape
+    part = width // shards
+    vmem = pl.BlockSpec(memory_space=pltpu.VMEM)
+    return pl.pallas_call(
+        functools.partial(turn_back_kernel, shards),
+        in_specs=[vmem] * 5,
+        out_specs=[vmem] * 3 + [pl.BlockSpec(memory_space=pltpu.HBM)],
+        out_shape=(
+            jax.ShapeDtypeStruct((rows, width), jnp.float32),
+            jax.ShapeDtypeStruct((rows, width), jnp.bfloat16),
+            jax.ShapeDtypeStruct((1, width), jnp.float32),
+            jax.ShapeDtypeStruct((shards, rows, part), jnp.bfloat16),
+        ),
+        scratch_shapes=[
+            pltpu.VMEM((shards, rows, part), jnp.bfloat16),
+            pltpu.SemaphoreType.DMA((4,)),
+            pltpu.SemaphoreType.DMA((4,)),
+            pltpu.SemaphoreType.DMA((1,)),
+        ],
+        compiler_params=pltpu.CompilerParams(
+            collective_id=5, has_side_effects=True, vmem_limit_bytes=40 * MIB
+        ),
+        cost_estimate=pl.CostEstimate(
+            flops=2 * rows * width * width, bytes_accessed=40 * MIB, transcendentals=0
+        ),
+    )(hidden, grad, out_grad, gain, weight)
+
+
+def closing_kernel(
+    shards, planes, normed_grad, out_total, qkv_grad, out_grad, tokens, hidden_grad, hidden, gain, router, vectors,
+    input_grad, mixed_out, query_out, key_out, value_out, weight_out, gain_out, router_out, vectors_out,
+    held, came, diag, side, held2, came2, diag2, side2,
+    norm_land, out_land, qkv_land, weight_land, gain_mine, gain_land, gain_line, router_land, router_sum, router_line,
+    vector_land, vector_sum, vector_line, send, recv, local,
+):
+    wires = Wires(send, recv)
+    device, shard = wires.device, wires.shard
+    rows, width = tokens.shape
+    block = query_out.shape[0]
+    part = width // shards
+    lines = router_out.shape[0]
+    line_peers = [wires.peer(step=step, shards=shards) for step in range(1, shards)]
+    plane_peers = [wires.peer(bits) for bits in range(1, planes)]
+    greet(line_peers + plane_peers)
+
+    def rel(source):
+        return lambda chip, core: source.at[device ^ (2 * chip + core)]
+
+    norms = LineSum(wires, shards, lambda t: normed_grad.at[t], lambda s: norm_land.at[s])
+    values = LineSum(
+        wires, shards, lambda t: out_total.at[aligned(t, rows)], lambda s: out_land.at[s]
+    )
+    qkv = PlaneSum(wires, rel(qkv_grad), held, came, diag, side, local, 0)
+    weight = PlaneSum(wires, rel(out_grad), held2, came2, diag2, side2, local, 4)
+    qkv_line = LineSum(
+        wires, shards, lambda t: held.at[0, aligned(t, block)], lambda s: qkv_land.at[s]
+    )
+    weight_line = LineSum(
+        wires, shards, lambda t: held2.at[0, aligned(t, block)], lambda s: weight_land.at[s]
+    )
+    norms.begin()
+    own_norm = pltpu.make_async_copy(normed_grad.at[shard], norm_land.at[shard], local.at[8])
+    own_norm.start()
+    own_value = pltpu.make_async_copy(
+        out_total.at[aligned(shard, rows)], out_land.at[shard], local.at[9]
+    )
+    own_value.start()
+    sent = []
+
+    def spread(slots, source, landing):
+        for bits in range(1, planes):
+            copy = wires.copy(
+                source(device ^ bits), landing.at[device], slots[bits - 1], wires.peer(bits)
+            )
+            copy.start()
+            sent.append(copy)
+
+    def collect(slots, landing):
+        for bits in range(1, planes):
+            place = landing.at[device ^ bits]
+            wires.copy(place, place, slots[bits - 1], wires.peer(bits)).wait_recv()
+        total = landing[0]
+        for other in range(1, planes):
+            total = total + landing[other]
+        return total
+
+    router_slots = [wires.slot() for _ in range(1, planes)]
+    vector_slots = [wires.slot() for _ in range(1, planes)]
+    gain_slots = [wires.slot() for _ in range(1, planes)]
+    spread(router_slots, lambda e: router.at[aligned(e, shards * lines)], router_land)
+    spread(vector_slots, lambda e: vectors, vector_land)
+    qkv.begin()
+    weight.begin()
+    qkv.send_corner()
+    qkv.add_cores()
+    weight.send_corner()
+    router_land[device] = router[aligned(device, shards * lines), :]
+    vector_land[device] = vectors[...]
+    router_sum[...] = collect(router_slots, router_land)
+    vector_sum[...] = collect(vector_slots, vector_land)
+    router_pass = LineSum(
+        wires, shards, lambda t: router_sum.at[aligned(t, lines)], lambda s: router_line.at[s]
+    )
+    vector_pass = LineSum(wires, shards, lambda t: vector_sum, lambda s: vector_line.at[s])
+    router_pass.begin()
+    vector_pass.begin()
+    qkv.send_sides()
+    weight.add_cores()
+    own_norm.wait()
+    norms.arrive()
+    values.begin()
+    grad = line_total(norm_land, shards)
+    given = tokens[...].astype(jnp.float32)
+    factor = norm_factor(given)
+    gain_mine[...] = jnp.sum(grad * given * factor, axis=0, keepdims=True)
+    spread(gain_slots, lambda e: gain_mine, gain_land)
+    scaled = grad * gain[...]
+    inner = jnp.mean(scaled * given, axis=-1, keepdims=True)
+    total = hidden_grad[...] + factor * scaled - given * (factor * factor * factor) * inner
+    input_grad[...] = total.astype(jnp.bfloat16)
+    qkv.end()
+    qkv_line.begin()
+    weight.send_sides()
+    gain_land[device] = gain_mine[...]
+    gain_mine2 = collect(gain_slots, gain_land)
+    gain_line[shard] = gain_mine2
+    gain_pass = LineSum(wires, shards, lambda t: gain_line.at[shard], lambda s: gain_line.at[s])
+    gain_pass.begin()
+    weight.end()
+    weight_line.begin()
+    router_line[shard] = router_sum[aligned(shard, lines), :]
+    vector_line[shard] = vector_sum[...]
+    router_pass.arrive()
+    router_out[...] = line_total(router_line, shards)
+    vector_pass.arrive()
+    vectors_out[...] = line_total(vector_line, shards)
+    own_value.wait()
+    values.arrive()
+    mixed_out[...] = (hidden[...] + line_total(out_land, shards)).astype(jnp.bfloat16)
+    qkv_land[shard] = held[0, aligned(shard, block), :]
+    qkv_line.arrive()
+    for source in range(shards):
+        for which, result in enumerate((query_out, key_out, value_out)):
+            result[:, pl.ds(source * part, part)] = qkv_land[
+                source, :, pl.ds(which * part, part)
+            ].astype(jnp.float32)
+    gain_pass.arrive()
+    gain_out[...] = line_total(gain_line, shards)
+    weight_land[shard] = held2[0, aligned(shard, block), :]
+    weight_line.arrive()
+    weight_out[...] = line_total(weight_land, shards)
+    for copy in sent:
+        copy.wait_send()
+    groups = (norms, values, qkv, weight, qkv_line, weight_line, router_pass, vector_pass)
+    for group in groups + (gain_pass,):
+        group.drain()
+
+
+def closing_call(
+    normed_grad, out_total, qkv_grad, out_grad, tokens, hidden_grad, hidden, gain, router, vectors
+):
+    shards, rows, width = normed_grad.shape
+    planes, each, lanes = qkv_grad.shape
+    block = each // shards
+    lines = router.shape[0] // (planes * shards)
+    hbm = pl.BlockSpec(memory_space=pltpu.HBM)
+    vmem = pl.BlockSpec(memory_space=pltpu.VMEM)
+    low, full = jnp.bfloat16, jnp.float32
+
+    def work(wide):
+        return [
+            pltpu.VMEM((4, each, wide), low),
+            pltpu.VMEM((4, each, wide), low),
+            pltpu.VMEM((2, each // 2, wide), low),
+            pltpu.VMEM((2, each, wide), low),
+        ]
+
+    weight_shape = jax.ShapeDtypeStruct((block, width), full)
+    return pl.pallas_call(
+        functools.partial(closing_kernel, shards, planes),
+        in_specs=[hbm] * 4 + [vmem] * 6,
+        out_specs=[vmem] * 9,
+        out_shape=(
+            jax.ShapeDtypeStruct((rows, width), low),
+            jax.ShapeDtypeStruct((rows, width), low),
+            weight_shape,
+            weight_shape,
+            weight_shape,
+            weight_shape,
+            jax.ShapeDtypeStruct((1, width), full),
+            jax.ShapeDtypeStruct((lines, 128), full),
+            jax.ShapeDtypeStruct(vectors.shape, full),
+        ),
+        scratch_shapes=work(lanes)
+        + work(width)
+        + [
+            pltpu.VMEM((shards, rows, width), low),
+            pltpu.VMEM((shards, rows, width), low),
+            pltpu.VMEM((shards, block, lanes), low),
+            pltpu.VMEM((shards, block, width), low),
+            pltpu.VMEM((1, width), full),
+            pltpu.VMEM((planes, 1, width), full),
+            pltpu.VMEM((shards, 1, width), full),
+            pltpu.VMEM((planes, shards * lines, 128), full),
+            pltpu.VMEM((shards * lines, 128), full),
+            pltpu.VMEM((shards, lines, 128), full),
+            pltpu.VMEM((planes,) + vectors.shape, full),
+            pltpu.VMEM(vectors.shape, full),
+            pltpu.VMEM((shards,) + vectors.shape, full),
+            pltpu.SemaphoreType.DMA((72,)),
+            pltpu.SemaphoreType.DMA((72,)),
+            pltpu.SemaphoreType.DMA((10,)),
+        ],
+        compiler_params=pltpu.CompilerParams(
+            collective_id=6, has_side_effects=True, vmem_limit_bytes=58 * MIB
+        ),
+        cost_estimate=pl.CostEstimate(flops=0, bytes_accessed=300 * MIB, transcendentals=0),
+    )(normed_grad, out_total, qkv_grad, out_grad, tokens, hidden_grad, hidden, gain, router, vectors)
+
+
 LOW = jnp.bfloat16
 WIDE = jnp.float32
 
@@ -1293,39 +1729,6 @@
         got = lax.ppermute(sent, SHARD, [(i, (i + step) % size) for i in range(size)])
         result = lax.dynamic_update_slice_in_dim(result, got, (shard - step) % size, 0)
     return result
-
-
-def plane_scatter(parts, device):
-    shape = parts.shape[1:]
-    core, xbit, ybit = device & 1, (device >> 1) & 1, (device >> 2) & 1
-    cube = parts.reshape((2, 2, 2) + shape)
-    keep = lax.dynamic_index_in_dim(cube, core, 2, keepdims=False)
-    give = lax.dynamic_index_in_dim(cube, 1 - core, 2, keepdims=False)
-    cube = keep.astype(WIDE) + swap(give.astype(LOW), CORE).astype(WIDE)
-    half = shape[0] // 2
-
-    def halves(value, first, second, first_bit, second_bit, axis):
-        keep = lax.dynamic_index_in_dim(value, first, axis, keepdims=False)
-        give = lax.dynamic_index_in_dim(value, 1 - first, axis, keepdims=False)
-        value = keep + swap(give.astype(LOW), first_bit).astype(WIDE)
-        keep = lax.dynamic_index_in_dim(value, second, 0, keepdims=False)
-        give = lax.dynamic_index_in_dim(value, 1 - second, 0, keepdims=False)
-        return keep + swap(give.astype(LOW), second_bit).astype(WIDE)
-
-    low_half = halves(cube[:, :, :half], xbit, ybit, XBIT, YBIT, 1)
-    high_half = halves(cube[:, :, half:], ybit, xbit, YBIT, XBIT, 0)
-    return jnp.concatenate([low_half, high_half], axis=0)
-
-
-def tiny_scatter(table, device, shard):
-    planes, shards = lax.axis_size(EXPERT), lax.axis_size(SHARD)
-    cube = table.reshape(2, 2, 2, shards, -1)
-    for axis, bits in ((2, CORE), (1, XBIT), (0, YBIT)):
-        mine = (device // bits) & 1
-        keep = lax.dynamic_index_in_dim(cube, mine, axis, keepdims=True)
-        give = lax.dynamic_index_in_dim(cube, 1 - mine, axis, keepdims=True)
-        cube = keep + swap(give, bits)
-    return jnp.sum(shard_exchange(cube.reshape(shards, -1), shard), axis=0)
 
 
 def fast_local(
@@ -1358,46 +1761,40 @@
     device = lax.axis_index(EXPERT)
     shard = lax.axis_index(SHARD)
     part = width // shards
-    both = BOTH
-
-    order = pair_order.reshape(rows, top_count)
-    expert_ids = jnp.arange(experts, dtype=jnp.int32)
-    chosen = routes[:, :, None] == expert_ids[None, None, :]
-    dense_order = jnp.sum(jnp.where(chosen, order[:, :, None] + 1, 0), axis=1)
-    small = jnp.concatenate(
-        [
-            (dense_order // 256).astype(LOW).reshape(-1),
-            (dense_order % 256).astype(LOW).reshape(-1),
-            w_router.reshape(-1),
-            attn_gain,
-            ffn_gain,
-            query_gain,
-            key_gain,
-        ]
-    )
-    used = small.shape[0]
-    lines = -(-used // (128 * 16)) * 16
-    small = jnp.pad(small, (0, lines * 128 - used)).reshape(lines, 128)
-    small, qkv_w, tokens_seq, out_block, grad_seq = opening_call(
-        small, w_query, w_key, w_value, tokens, w_out, out_grad, planes, shards
-    )
-    small = small.reshape(planes, shards, -1)[:, :, :used]
-    cuts = [rows * experts, rows * experts, w_router.size, attn_gain.size, ffn_gain.size]
-    cuts += [query_gain.size, key_gain.size]
+
+    gains = jnp.concatenate([attn_gain, ffn_gain, query_gain, key_gain])
+    gains = jnp.pad(gains, (0, -gains.size % (16 * 128))).reshape(-1, 128)
+    router_pad = jnp.pad(w_router, ((0, 0), (0, 128 - experts)))
+    small, router_w, qkv_w, tokens_seq, out_block, grad_seq = opening_call(
+        routes,
+        pair_order.reshape(rows, top_count),
+        gains,
+        router_pad,
+        w_query,
+        w_key,
+        w_value,
+        tokens,
+        w_out,
+        out_grad,
+        experts,
+        planes,
+        shards,
+    )
+    router_w = router_w.reshape(width, 128)
+    gains = small[:, 2 * experts :].reshape(planes * shards, -1).astype(WIDE)
     fields, at = [], 0
-    for size in cuts:
-        fields.append(small[:, :, at : at + size])
+    for size in (attn_gain.size, ffn_gain.size, query_gain.size, key_gain.size):
+        fields.append(gains[:, at : at + size].reshape(1, -1))
         at += size
-    all_order = fields[0].astype(jnp.int32) * 256 + fields[1].astype(jnp.int32)
-    all_order = all_order.reshape(planes, shards, rows, experts)
-    router_w = fields[2].reshape(width, experts)
-    attn_scale = fields[3].reshape(width).astype(WIDE)
-    ffn_scale = fields[4].reshape(width).astype(WIDE)
-    query_scale = fields[5].reshape(HD).astype(WIDE)
-    key_scale = fields[6].reshape(HD).astype(WIDE)
-
-    attn_row, ffn_row = attn_scale.reshape(1, width), ffn_scale.reshape(1, width)
-    query_row, key_row = query_scale.reshape(1, HD), key_scale.reshape(1, HD)
+    attn_row, ffn_row, query_row, key_row = fields
+    digits = [
+        lax.dynamic_slice_in_dim(small, start + device * own_experts, own_experts, 1)
+        for start in (0, experts)
+    ]
+    high, low_digit = [value.transpose(1, 0, 2) for value in digits]
+    most = planes * shards * rows * top_count
+    kept = keep_call(high, low_digit, capacity, most, planes, shards)
+
     tables = turn_tables(seq)
     seg_row, seg_col = segment_ids.reshape(1, seq), segment_ids.reshape(seq, 1)
     normed_low, raw, low, mixed_own, total = attend_call(
@@ -1410,94 +1807,69 @@
         normed_seq, grad_seq, w_gate, w_up, w_down, planes, shards
     )
     wide_w = wide_w.reshape(width, -1)
-    extra = 128
-    router_pad = jnp.pad(router_w, ((0, 0), (0, extra - experts)))
     own_ids = device * own_experts + jnp.arange(own_experts, dtype=jnp.int32)
-    own_hot = (own_ids[:, None] == jnp.arange(extra, dtype=jnp.int32)[None, :]).astype(WIDE)
-    mine = jnp.stack(
-        [lax.dynamic_index_in_dim(all_order, own_ids[i], 3, keepdims=False) for i in range(own_experts)]
-    )
-    mine = mine.transpose(0, 2, 1, 3).reshape(own_experts, shards, planes * rows)
-    smaller = (mine[:, :, None, :] < mine[:, :, :, None]) & (mine[:, :, None, :] > 0)
-    rank = jnp.sum(smaller.astype(jnp.int32), axis=-1)
-    kept = ((mine > 0) & (rank < capacity)).astype(WIDE)
-    kept = kept.reshape(own_experts, shards, planes, rows).transpose(2, 1, 3, 0)
-    kept = kept.reshape(planes, seq, own_experts)
-
-    sums = None
-    out_parts, in_parts = [None] * 4, [None] * 4
-    for chip in (3, 1, 2, 0):
-        blocks = jnp.stack([device ^ (2 * chip), device ^ (2 * chip + 1)])
-        out_parts[chip], in_parts[chip], sums = expert_call(
-            blocks, token_all, grad_all, kept, wide_w, router_pad, down_w, own_hot, experts, sums
-        )
-    wide_grad, router_grad, down_grad = sums
-
-    def combine(parts):
-        total = None
-        for chip, bits in enumerate((0, XBIT, YBIT, XBIT | YBIT)):
-            value = parts[chip]
-            value = value[0].astype(WIDE) + swap(value[1], CORE).astype(WIDE)
-            if bits:
-                value = swap(value.astype(LOW), bits).astype(WIDE)
-            total = value if total is None else total + value
-        pieces = shard_exchange(total.astype(LOW).reshape(shards, rows, width), shard)
-        return jnp.sum(pieces.astype(WIDE), axis=0)
-
-    normed_two_grad = combine(in_parts)
-    out_parts, _ = lax.optimization_barrier((out_parts, normed_two_grad))
-    expert_sum = combine(out_parts)
+    own_hot = (own_ids[:, None] == jnp.arange(128, dtype=jnp.int32)[None, :]).astype(WIDE)
+    out_parts, in_parts, wide_message, router_grad, down_message = expert_call(
+        token_all, grad_all, kept, wide_w, router_w, down_w, own_hot, experts
+    )
+    normed_two_grad, out_total, wide_pieces = returning_call(
+        in_parts, out_parts, wide_message.reshape(shards, part, -1), shards
+    )
     hidden = lax.dynamic_slice_in_dim(hidden_seq, shard * rows, rows)
-    mixed_out = (hidden + expert_sum).astype(LOW)
-
-    hidden_grad, attn_low, message, ffn_scale_grad = turn_back_call(
+
+    hidden_grad, attn_low, ffn_scale_grad, mixed_grad = turn_back_call(
         hidden, normed_two_grad, out_grad, ffn_row, out_w, shards
     )
-    mixed_grad = shard_exchange(message, shard).reshape(seq, part)
+    mixed_grad = mixed_grad.reshape(seq, part)
+    down_message, _ = lax.optimization_barrier((down_message, mixed_grad))
+    down_pieces = shard_exchange(down_message, shard)
     qkv_grad, normed_grad, query_scale_grad, key_scale_grad = attend_back_call(
         mixed_grad, raw, low, total, qkv_w, query_row, key_row, tables, seg_row, seg_col
     )
-    pieces = shard_exchange(normed_grad.reshape(shards, rows, width), shard)
-    input_grad, attn_scale_grad = finish_call(pieces, tokens, hidden_grad, attn_row)
-
-    qkv_w_grad = matmul_tn(normed_low, qkv_grad).reshape(planes, -1, 3 * part)
-    qkv_w_grad = plane_scatter(qkv_w_grad, device).astype(LOW)
-    qkv_w_grad = shard_exchange(qkv_w_grad.reshape(shards, -1, 3 * part), shard).astype(WIDE)
-    qkv_w_grad = qkv_w_grad.reshape(shards, -1, 3, part).transpose(2, 1, 0, 3)
-    qkv_w_grad = qkv_w_grad.reshape(3, -1, width)
-
+    normed_grad = normed_grad.reshape(shards, rows, width)
+
+    qkv_w_grad = matmul_tn(normed_low, qkv_grad).astype(LOW).reshape(planes, -1, 3 * part)
     own_mixed = lax.dynamic_slice_in_dim(mixed, shard * rows, rows, 1)
     own_mixed = own_mixed.transpose(1, 0, 2).reshape(rows, width)
-    out_w_grad = matmul_tn(own_mixed, attn_low).reshape(planes, -1, width)
-    out_w_grad = plane_scatter(out_w_grad, device).astype(LOW)
-    out_w_grad = shard_exchange(out_w_grad.reshape(shards, -1, width), shard)
-    out_w_grad = jnp.sum(out_w_grad.astype(WIDE), axis=0)
-
-    wide_pieces = shard_exchange(wide_grad.astype(LOW).reshape(shards, part, -1), shard)
-    down_pieces = shard_exchange(down_grad.astype(LOW), shard)
+    out_w_grad = matmul_tn(own_mixed, attn_low).astype(LOW).reshape(planes, -1, width)
+    router_table = router_grad[:, :experts].reshape(-1, 128)
+    vectors = jnp.concatenate(
+        [ffn_scale_grad.reshape(-1, 128), query_scale_grad, key_scale_grad], axis=0
+    )
+    vectors = jnp.pad(vectors, ((0, -vectors.shape[0] % 8), (0, 0)))
+    closed = closing_call(
+        normed_grad,
+        out_total,
+        qkv_w_grad,
+        out_w_grad,
+        tokens,
+        hidden_grad,
+        hidden,
+        attn_row,
+        router_table,
+        vectors,
+    )
+    input_grad, mixed_out, query_w_grad, key_w_grad, value_w_grad, out_w_grad = closed[:6]
+    attn_scale_grad, router_out, vectors = closed[6:]
     gate_grad, up_grad, down_grad = unpack_units(wide_pieces, down_pieces, own_experts)
-
-    devices = planes * shards
-    tiny = [router_grad[:, :experts], ffn_scale_grad, attn_scale_grad, query_scale_grad, key_scale_grad]
-    tiny = [value.reshape(devices, -1) for value in tiny]
-    sizes = [value.shape[1] for value in tiny]
-    summed = tiny_scatter(jnp.concatenate(tiny, axis=1), device, shard)
-    fields, at = [], 0
-    for size in sizes:
-        fields.append(summed[at : at + size])
-        at += size
+    index = device * shards + shard
+    flat = vectors.reshape(-1)
+
+    def own_piece(values, start, size):
+        return lax.dynamic_slice_in_dim(values, start + index * size, size)
+
     return (
         mixed_out,
         input_grad,
-        fields[2],
-        qkv_w_grad[0],
-        qkv_w_grad[1],
-        qkv_w_grad[2],
-        fields[3],
-        fields[4],
+        own_piece(attn_scale_grad.reshape(-1), 0, attn_gain.size),
+        query_w_grad,
+        key_w_grad,
+        value_w_grad,
+        own_piece(flat, width, query_gain.size),
+        own_piece(flat, width + HD, key_gain.size),
         out_w_grad,
-        fields[1],
-        fields[0].reshape(-1, experts),
+        own_piece(flat, 0, ffn_gain.size),
+        router_out.reshape(-1, experts),
         gate_grad,
         up_grad,
         down_grad,

time: 1230 us -> 901 us (0.73)
  waiting for transfers between devices: 391 us -> 0.01 us
  Pallas kernels: 503 us -> 799 us
  starting transfers between devices: 105 us -> 3.94 us
  local copies, waits for them, and re-layouts: 140 us -> 71.2 us
  other arithmetic: 56.6 us -> 2.05 us
    pallas_call x7 -> x6, Pallas kernels: 261 us -> 559 us  [the longest x1 157 us: closing_call(): pl.pallas_call(functools.partial(closing_kernel, shards, planes), in_spec...]
    ppermute x27 -> x0, waiting for transfers between devices: 208 us -> none  [swap(): return lax.ppermute(value, EXPERT, [(i, i ^ bits) for i in range(count)])]
    ppermute x27 -> x3, waiting for transfers between devices: 183 us -> 0.01 us  [shard_exchange(): lax.ppermute(sent, SHARD, [(i, (i + step) % size) for i in range(size)])]
    ppermute x27 -> x3, starting transfers between devices: 85.2 us -> 3.94 us  [shard_exchange(): lax.ppermute(sent, SHARD, [(i, (i + step) % size) for i in range(size)])]
    convert_element_type x15 -> x2, other arithmetic: 27.4 us -> 0.65 us  [the longest x1 0.63 us: fast_local(): (own_ids[:, None] == jnp.arange(128, dtype=jnp.int32)[None, :]).astype(WIDE)]
    ppermute x27 -> x0, starting transfers between devices: 19.7 us -> none  [swap(): return lax.ppermute(value, EXPERT, [(i, i ^ bits) for i in range(count)])]
    dynamic_slice x17 -> x2, local copies, waits for them, and re-layouts: 18.3 us -> 3.07 us  [shard_exchange(): sent = lax.dynamic_index_in_dim(pieces, target, 0, keepdims=True)]
    convert_element_type x14 -> x0, local copies, waits for them, and re-layouts: 13.8 us -> none  [the longest x2 9.25 us: plane_scatter(): cube = keep.astype(WIDE) + swap(give.astype(LOW), CORE).astype(WIDE)]
  transfers between devices with their start and end apart: 54 -> 3, of which waited for: 21 -> 0; matrix products, arithmetic and copies ran while one was open for 10% -> 3% of each run, Pallas kernels for 12% -> 20%
where the time goes in v2:
time: 901 us; the launch traced here: 890 us
  Pallas kernels  799 us (89%)
  local copies, waits for them, and re-layouts  71.2 us (8%)
  matrix products  12.6 us (1%)
    pallas_call x1, Pallas kernels, closing_call(): pl.pallas_call(functools.partial(closing_kernel, shards, planes), in_spec...  157 us
    pallas_call x1, Pallas kernels, meeting_call(): pl.pallas_call(functools.partial(meeting_kernel, shards), in_specs=[hbm]...  152 us
    pallas_call x1, Pallas kernels, returning_call(): pl.pallas_call(functools.partial(returning_kernel, shards), in_specs=[hbm...  152 us
    pallas_call x1, Pallas kernels, opening_call(): pl.pallas_call(functools.partial(opening_kernel, shards, experts), in_spe...  122 us
    pallas_call x1, Pallas kernels, expert_call(): pl.pallas_call(functools.partial(expert_kernel, experts), grid=(planes *...  108 us
    unnamed x104, local copies, waits for them, and re-layouts  53.3 us
    pallas_call x1, Pallas kernels, middle_call(): pl.pallas_call(functools.partial(middle_kernel, shards), in_specs=[hbm] *...  43.7 us
  transfers between devices with their start and end apart: 3, of which 0 were waited for; matrix products, arithmetic and copies ran while one was open for 3% of the time, Pallas kernels for 20%

profile of v2, /device:TPU:0, one launch (start us, length us, event | category | flops | bytes accessed | tf_op | source)
XLA Modules:
  0.0 890.4 jit_solution(15318032431570384149)
XLA Ops:
  0.7 0.8 copy.38
  1.5 0.8 copy.39.routes
  2.3 0.8 reshape.97.order
  3.1 0.8 fusion.7.gains
  3.8 1.0 copy-done.8
  4.9 1.0 copy-done.10
  5.9 0.9 copy-done.16
  6.9 0.9 copy-done.17
  7.8 0.9 copy-done.18
  8.8 0.9 copy-done.19
  9.7 122.1 %shard_map.290 = (bf16[32,48,128]{2,1,0:T(8,128)(2,1)S(1)}, bf16[32,64,128]{2,1,0:T(8,128)(2,1)S(1)}, bf16[2048,1536]{1,0:T(8,128)(2,1)S(1)}, bf16[512,2048]{1,0...) custom-call(s32[128,8]{1,0:T(8,128)S(1)} %copy.39.routes, s32[128,8]{1,0:T(8,128)S(1)} %reshape.97.order, ...), custom_call_target="tpu_custom_call" | custom-call | bytes 209715200 | tf_op jit(solution)/shard_map/pallas_call | solution.py:1060
  131.9 2.8 copy-done.26
  134.6 1.3 copy-done.28
  136.0 0.9 copy.41
  138.3 0.8 dynamic-slice_bitcast_fusion.1
  139.1 4.4 shard_map.295.keep
  143.5 1.3 copy-done.11
  144.9 10.4 %shard_map.291 = (bf16[512,2048]{1,0:T(8,128)(2,1)}, f32[512,1024]{1,0:T(8,128)}, bf16[512,1536]{1,0:T(8,128)(2,1)}, bf16[512,512]{1,0:T(8,128)(2,1)S(1)}, f32[512,128]{1,0:T(8,128)S(1)}) custom-call(bf16[512,2048]{1,0:T(8,128)(2,1)} %copy-done.28, f32[1,2048]{1,0:T(1,128)S(1)} %reshape.99.gain, bf16[2048,1536]{1,0:T(8,128)(2,1)} %copy-done.26, ...), custom_call_target="tpu_custom_call" | custom-call | flops 3221225472 | bytes 16777216 | tf_op jit(solution)/shard_map/pallas_call | solution.py:462
  156.0 43.7 %shard_map.292 = (bf16[4,512,512]{2,1,0:T(8,128)(2,1)S(1)}, bf16[2048,2048]{1,0:T(8,128)(2,1)S(1)}) custom-call(bf16[512,512]{1,0:T(8,128)(2,1)S(1)} %get-tuple-element.64.mixed, bf16[256,2048]{1,0:T(8,128)(2,1)S(1)} %get-tuple-element.65.out_block), custom_call_target="tpu_custom_call" | custom-call | bytes 157286400 | tf_op jit(solution)/shard_map/pallas_call | solution.py:1127
  199.7 3.3 copy-done.2
  203.0 1.4 copy-done.20
  204.4 1.6 copy-done.21
  206.0 1.6 copy-done.29
  207.6 8.9 %shard_map.293 = (f32[512,2048]{1,0:T(8,128)S(1)}, bf16[512,2048]{1,0:T(8,128)(2,1)S(1)}) custom-call(bf16[4,512,512]{2,1,0:T(8,128)(2,1)S(1)} %copy-done.21, bf16[2048,2048]{1,0:T(8,128)(2,1)} %copy-done.2, bf16[512,2048]{1,0:T(8,128)(2,1)S(1)} %copy-done.29, f32[1,2048]{1,0:T(1,128)S(1)} %reshape.104.gain), custom_call_target="tpu_custom_call" | custom-call | flops 4294967296 | bytes 18874368 | tf_op jit(solution)/shard_map/pallas_call | solution.py:494
  216.6 1.8 copy-done.5
  218.5 152.1 %shard_map.294 = (bf16[8,512,2048]{2,1,0:T(8,128)(2,1)S(1)}, bf16[8,512,2048]{2,1,0:T(8,128)(2,1)S(1)}, bf16[4,512,1024]{2,1,0:T(8,128)(2,1)S(1)}, bf16[4,512,512]{2,1,0:T(8,128)(2,1)S(1)}) custom-call(bf16[512,2048]{1,0:T(8,128)(2,1)S(1)} %get-tuple-element.69.normed, bf16[512,2048]{1,0:T(8,128)(2,1)S(1)} %get-tuple-element.70.grad_seq, ...), custom_call_target="tpu_custom_call" | custom-call | bytes 314572800 | tf_op jit(solution)/shard_map/pallas_call | solution.py:1229
  370.6 5.8 copy-done.24
  376.4 5.7 copy-done.25
  382.1 2.0 copy-done.27
  384.1 1.4 copy-done.30
  385.5 107.9 %shard_map.296 = (bf16[8,512,2048]{2,1,0:T(8,128)(2,1)}, bf16[8,512,2048]{2,1,0:T(8,128)(2,1)}, bf16[2048,1024]{1,0:T(8,128)(2,1)}, f32[2048,128]{1,0:T(8,128)}, bf16[4,512,512]{2,1,0:T(8,128)(2,1)}) custom-call(bf16[8,512,2048]{2,1,0:T(8,128)(2,1)} %copy-done.24, bf16[8,512,2048]{2,1,0:T(8,128)(2,1)} %copy-done.25, f32[8,512,2]{2,1,0:T(8,128)} %copy-done.11, ...), custom_call_target="tpu_custom_call" | custom-call | flops 77309411328 | bytes 104857600 | tf_op jit(solution)/shard_map/pallas_call | solution.py:603
  493.4 151.9 %shard_map.297 = (f32[128,2048]{1,0:T(8,128)}, bf16[512,2048]{1,0:T(8,128)(2,1)}, bf16[4,512,1024]{2,1,0:T(8,128)(2,1)}) custom-call(bf16[8,512,2048]{2,1,0:T(8,128)(2,1)} %get-tuple-element.76.ins, bf16[8,512,2048]{2,1,0:T(8,128)(2,1)} %get-tuple-element.77.outs, bf16[4,512,1024]{2,1,0:T(8,128)(2,1)} %bitcast.40), custom_call_target="tpu_custom_call" | custom-call | bytes 314572800 | tf_op jit(solution)/shard_map/pallas_call | solution.py:1442
  645.4 3.4 copy-done.3
  648.8 1.2 copy-done.13
  650.0 15.4 %shard_map.298 = (f32[128,2048]{1,0:T(8,128)S(1)}, bf16[128,2048]{1,0:T(8,128)(2,1)S(1)}, f32[1,2048]{1,0:T(1,128)S(1)}, bf16[4,128,512]{2,1,0:T(8,128)(2,1)S(1)}) custom-call(f32[128,2048]{1,0:T(8,128)S(1)} %constant_dynamic-slice_fusion.4.hidden, f32[128,2048]{1,0:T(8,128)S(1)} %copy-done.13, bf16[128,2048]{1,0:T(8,128)(2,1)S(1)} %copy-done.9, ...), custom_call_target="tpu_custom_call" | custom-call | flops 1073741824 | bytes 41943040 | tf_op jit(solution)/shard_map/pallas_call | solution.py:1497
  665.4 1.0 copy-done.12
  666.4 0.8 copy-done.14
  667.2 0.8 constant_dynamic-slice_fusion.2
  668.0 2.3 collective-permute-start
  670.3 1.9 dynamic-slice_bitcast_fusion
  672.2 2.0 copy.44
  674.3 0.9 copy-done.37
  675.2 16.7 %shard_map.299 = (bf16[512,1536]{1,0:T(8,128)(2,1)}, bf16[512,2048]{1,0:T(8,128)(2,1)}, f32[1,128]{1,0:T(1,128)S(1)}, f32[1,128]{1,0:T(1,128)S(1)}) custom-call(bf16[512,512]{1,0:T(8,128)(2,1)S(1)} %bitcast.36, f32[512,1024]{1,0:T(8,128)} %get-tuple-element.81.raw, bf16[512,1536]{1,0:T(8,128)(2,1)} %get-tuple-element.82.low, f32[512,128]{1,0:T(8,128)S(1)} %copy-done.37, ...), custom_call_target="tpu_custom_call" | custom-call | flops 3221225472 | bytes 16777216 | tf_op jit(solution)/shard_map/pallas_call | solution.py:684
  691.9 7.0 convolution_convert_fusion
  698.9 2.2 constant_dynamic-slice_fusion
  701.2 1.5 collective-permute-start.2
  702.8 5.6 convolution_convert_fusion.1
  708.4 1.0 reshape.113.router
  710.0 157.3 %shard_map.300 = (bf16[128,2048]{1,0:T(8,128)(2,1)}, bf16[128,2048]{1,0:T(8,128)(2,1)}, f32[64,2048]{1,0:T(8,128)}, f32[64,2048]{1,0:T(8,128)}, f32[64,2048]{1,0...) custom-call(bf16[4,128,2048]{2,1,0:T(8,128)(2,1)} %bitcast.42, ...), custom_call_target="tpu_custom_call" | custom-call | bytes 314572800 | tf_op jit(solution)/shard_map/pallas_call | solution.py:1672
  867.3 0.8 reshape.116
  868.7 2.2 copy-done
  870.9 4.7 shard_map.301
  875.6 1.3 dynamic_slice.44
  876.9 1.2 fusion.8
  878.1 1.3 fusion.11
  879.5 1.1 constant_dynamic-update-slice_fusion.1
  880.5 1.1 constant_dynamic-update-slice_fusion.refs_0_
  881.7 3.5 shard_map.302
  885.2 0.8 copy.58
  886.0 0.8 copy.59
  886.8 0.8 copy.60
  887.6 0.8 copy.61
  888.4 0.8 copy.62
  889.2 0.8 copy.63
  (89 shorter events, 3.8 us)
Async XLA Ops:
  2.2 135.5 %copy-start.23 = (s32[512]{0:T(512)S(1)}, s32[512]{0:T(512)}, u32[]{:S(2)}) copy-start(s32[512]{0:T(512)} %param.20) | copy-start | bytes 6148
  3.8 1.0 copy-start.8
  4.9 1.0 copy-start.10
  5.9 0.9 copy-start.16
  6.9 0.9 copy-start.17
  7.8 0.9 copy-start.18
  8.8 0.9 copy-start.19
  131.9 2.8 copy-start.26
  134.6 1.3 copy-start.28
  135.9 0.9 copy-start.31
  138.3 17.0 %copy-start.22 = (f32[1,2048]{1,0:T(1,128)}, f32[1,2048]{1,0:T(1,128)S(1)}, u32[]{:S(2)}) copy-start(f32[1,2048]{1,0:T(1,128)S(1)} %reshape.99.gain) | copy-start | bytes 24580
  138.3 6.6 copy-start.32
  138.3 6.6 copy-start.34
  143.5 1.3 copy-start.11
  155.3 0.7 copy-start.36
  199.7 3.3 copy-start.2
  203.0 1.4 copy-start.20
  204.4 1.6 copy-start.21
  206.0 1.6 copy-start.29
  207.6 9.1 %copy-start.6 = (bf16[2,512,1024]{2,1,0:T(8,128)(2,1)S(1)}, bf16[2,512,1024]{2,1,0:T(8,128)(2,1)}, u32[]{:S(2)}) copy-start(bf16[2,512,1024]{2,1,0:T(8,128)(2,1)} %up.1) | copy-start | bytes 6291460
  207.6 9.1 %copy-start.7 = (bf16[2,1024,512]{2,1,0:T(8,128)(2,1)S(1)}, bf16[2,1024,512]{2,1,0:T(8,128)(2,1)}, u32[]{:S(2)}) copy-start(bf16[2,1024,512]{2,1,0:T(8,128)(2,1)} %down.1) | copy-start | bytes 6291460
  216.5 2.0 copy-start.5
  216.6 428.8 %copy-start.1 = (f32[128,2048]{1,0:T(8,128)}, f32[128,2048]{1,0:T(8,128)S(1)}, u32[]{:S(2)}) copy-start(f32[128,2048]{1,0:T(8,128)S(1)} %constant_dynamic-slice_fusion.4.hidden) | copy-start | bytes 3145732
  370.6 5.8 copy-start.24
  376.4 5.7 copy-start.25
  382.1 2.0 copy-start.27
  384.1 1.4 copy-start.30
  493.4 152.0 %copy-start.9 = (bf16[128,2048]{1,0:T(8,128)(2,1)S(1)}, bf16[128,2048]{1,0:T(8,128)(2,1)}, u32[]{:S(2)}) copy-start(bf16[128,2048]{1,0:T(8,128)(2,1)} %out_grad.3) | copy-start | bytes 1572868
  645.4 3.4 copy-start.3
  648.8 1.2 copy-start.13
  650.0 17.2 %copy-start.4 = (bf16[4,512,512]{2,1,0:T(8,128)(2,1)S(1)}, bf16[4,512,512]{2,1,0:T(8,128)(2,1)}, u32[]{:S(2)}) copy-start(bf16[4,512,512]{2,1,0:T(8,128)(2,1)} %get-tuple-element.107) | copy-start | bytes 6291460
  665.4 1.0 copy-start.12
  666.4 0.8 copy-start.14
  667.2 7.1 copy-start.33
  667.2 7.1 copy-start.35
  668.0 30.9 %collective-permute-start = (bf16[1,512,512]{2,1,0:T(8,128)(2,1)}, bf16[1,512,512]{2,1,0:T(8,128)(2,1)}, u32[]{:S(2)}, u32[]{:S(2)}) collective-permute-start(bf16[1,512,512]{2,1,0:T(8,128)(2,1)} %constant_dynamic-slice_fusion.2), channel_id=1, source_target_pairs={{0,1},{1,2},{2,3},{3,0},{4,5},{5,6},{6,7},{7,4},{8,9},{9,10},{10,1... | collective-permute-start | bytes 1572872 | tf_op jit(solution)/shard_map/ppermute | solution.py:1729
  674.2 1.0 copy-start.37
  675.2 16.7 %copy-start.46 = (bf16[512,2048]{1,0:T(8,128)(2,1)S(1)}, bf16[512,2048]{1,0:T(8,128)(2,1)}, u32[]{:S(2)}) copy-start(bf16[512,2048]{1,0:T(8,128)(2,1)} %get-tuple-element.86) | copy-start | bytes 6291460
  698.9 3.9 copy-start.15
  698.9 3.9 copy-start.38
  701.2 179.4 %collective-permute-start.2 = (bf16[1,512,512]{2,1,0:T(8,128)(2,1)}, bf16[1,512,512]{2,1,0:T(8,128)(2,1)}, u32[]{:S(2)}, u32[]{:S(2)}) collective-permute-start(bf16[1,512,512]{2,1,0:T(8,128)(2,1)} %get-tuple-element.136), channel_id=1, source_target_pairs={{0,3},{1,0},{2,1},{3,2},{4,7},{5,4},{6,5},{7,6},{8,11},{9,8},{10,9... | collective-permute-start | bytes 1572872 | tf_op jit(solution)/shard_map/ppermute | solution.py:1729
  702.7 176.8 %collective-permute-start.1 = (bf16[1,512,512]{2,1,0:T(8,128)(2,1)}, bf16[1,512,512]{2,1,0:T(8,128)(2,1)}, u32[]{:S(2)}, u32[]{:S(2)}) collective-permute-start(bf16[1,512,512]{2,1,0:T(8,128)(2,1)} %get-tuple-element.137), channel_id=1, source_target_pairs={{0,2},{1,3},{2,0},{3,1},{4,6},{5,7},{6,4},{7,5},{8,10},{9,11},{10,... | collective-permute-start | bytes 1572872 | tf_op jit(solution)/shard_map/ppermute | solution.py:1729
  702.8 5.6 copy-start.39
  868.7 2.2 copy-start
  881.6 3.5 copy-start.45
  881.6 4.3 copy-start.44
  885.2 1.6 copy-start.43
  885.2 2.4 copy-start.42
  885.2 3.2 copy-start.41
  886.0 3.2 copy-start.40

commit v3 on v2

--- a/solution.py
+++ b/solution.py
@@ -469,7 +469,7 @@
             jax.ShapeDtypeStruct((seq, 128), jnp.float32),
         ),
         scratch_shapes=[pltpu.VMEM((seq, 3 * part), jnp.float32)],
-        compiler_params=vmem_params(52),
+        compiler_params=vmem_params(28),
         cost_estimate=pl.CostEstimate(
             flops=2 * seq * width * 3 * part, bytes_accessed=16 * MIB, transcendentals=seq * seq * 4
         ),
@@ -508,224 +508,46 @@
             jax.ShapeDtypeStruct((seq, width), jnp.float32),
             jax.ShapeDtypeStruct((seq, width), jnp.bfloat16),
         ),
-        compiler_params=vmem_params(40),
+        compiler_params=vmem_params(26),
         cost_estimate=pl.CostEstimate(
             flops=2 * seq * width * width, bytes_accessed=18 * MIB, transcendentals=0
         ),
     )(mixed, weight, tokens, gain)
 
 
-def expert_kernel(
-    experts, x, g, keep, wide_w, router_w, down_w, hot,
-    out, grad, wide_sum, router_sum, down_sum, acc, racc, dacc, wide_out, down_out, sems,
-):
-    step, steps = pl.program_id(0), pl.num_programs(0)
-
-    @pl.when(step == 0)
-    def _():
-        acc[...] = jnp.zeros_like(acc)
-        racc[...] = jnp.zeros_like(racc)
-        dacc[...] = jnp.zeros_like(dacc)
-
-    shards, units, part = down_w.shape
-    own = keep.shape[1]
-    each = units // own
-    wide = jnp.dot(x[...], wide_w[...], preferred_element_type=jnp.float32)
-    logits = jnp.dot(x[...], router_w[...], preferred_element_type=jnp.float32)
-    back = nt_dot(g[:, :part], down_w[0])
-    for shard in range(1, shards):
-        back = back + nt_dot(g[:, shard * part : (shard + 1) * part], down_w[shard])
-    lane = lax.broadcasted_iota(jnp.int32, logits.shape, 1)
-    logits = jnp.where(lane < experts, logits, -1e30)
-    shifted = jnp.exp(logits - jnp.max(logits, axis=-1, keepdims=True))
-    probs = shifted / jnp.sum(shifted, axis=-1, keepdims=True)
-    dense = jnp.zeros_like(probs)
-    acts, gates, ups = [], [], []
-    for index in range(own):
-        mark = hot[index : index + 1, :]
-        kept = keep[:, index : index + 1]
-        route = jnp.sum(probs * mark, axis=-1, keepdims=True) * kept
-        gate = wide[:, index * each : (index + 1) * each]
-        up = wide[:, units + index * each : units + (index + 1) * each]
-        behind = back[:, index * each : (index + 1) * each]
-        sigma = 1.0 / (1.0 + jnp.exp(-gate))
-        silu = gate * sigma
-        act = silu * up
-        dense = dense + jnp.sum(act * behind, axis=-1, keepdims=True) * kept * mark
-        acts.append((act * route).astype(jnp.bfloat16))
-        act_grad = behind * route
-        gates.append((act_grad * up * sigma * (1.0 + gate * (1.0 - sigma))).astype(jnp.bfloat16))
-        ups.append((act_grad * silu).astype(jnp.bfloat16))
-    logit_grad = probs * (dense - jnp.sum(probs * dense, axis=-1, keepdims=True))
-    logit_low = logit_grad.astype(jnp.bfloat16)
-    act_low = jnp.concatenate(acts, axis=1)
-    wide_low = jnp.concatenate(gates + ups, axis=1)
-    for shard in range(shards):
-        out[:, shard * part : (shard + 1) * part] = jnp.dot(
-            act_low, down_w[shard], preferred_element_type=jnp.float32
-        ).astype(jnp.bfloat16)
-    grad[...] = (nt_dot(wide_low, wide_w[...]) + nt_dot(logit_low, router_w[...])).astype(
-        jnp.bfloat16
-    )
-    acc[...] += tn_dot(x[...], wide_low)
-    racc[...] += tn_dot(x[...], logit_low)
-    for shard in range(shards):
-        dacc[shard] += tn_dot(act_low, g[:, shard * part : (shard + 1) * part])
-
-    @pl.when(step == steps - 1)
-    def _():
-        router_copy = pltpu.make_async_copy(racc, router_sum, sems.at[1])
-        router_copy.start()
-        wide_out[...] = acc[...].astype(jnp.bfloat16)
-        wide_copy = pltpu.make_async_copy(wide_out, wide_sum, sems.at[0])
-        wide_copy.start()
-        down_out[...] = dacc[...].astype(jnp.bfloat16)
-        down_copy = pltpu.make_async_copy(down_out, down_sum, sems.at[2])
-        down_copy.start()
-        router_copy.wait()
-        wide_copy.wait()
-        down_copy.wait()
-
-
-def expert_call(x_all, g_all, keep, wide_w, router_w, down_w, hot, experts):
-    planes, rows, width = x_all.shape
-    tile = 256
-    per = rows // tile
-    hbm = pl.BlockSpec(memory_space=pltpu.HBM)
-
-    def whole(value):
-        zeros = (0,) * value.ndim
-        return pl.BlockSpec(value.shape, lambda i: zeros, pipeline_mode=pl.Buffered(1))
-
-    def rowwise(lanes):
-        return pl.BlockSpec((None, tile, lanes), lambda i: (i // per, i % per, 0))
-
+def unpack_kernel(gate0, gate1, up0, up1, down0, down1, gate_out, up_out, down_out):
+    for index, group in enumerate(((gate0, up0, down0), (gate1, up1, down1))):
+
+        @pl.when(pl.program_id(0) == index)
+        def _(group=group):
+            for source, result in zip(group, (gate_out, up_out, down_out), strict=True):
+                result[...] = source[...].astype(result.dtype)
+
+
+def unpack_units(wides, downs):
+    shards, part, lanes = wides[0].shape
+    each = lanes // 2
+
+    def held(index, e, s):
+        return jnp.where(e == index, s, (shards - 1) * (1 - index))
+
+    def wide_spec(index, which):
+        return pl.BlockSpec((1, part, each), lambda e, s: (held(index, e, s), 0, which))
+
+    def down_spec(index):
+        return pl.BlockSpec((1, each, part), lambda e, s: (held(index, e, s), 0, 0))
+
+    wide_out = pl.BlockSpec((1, part, each), lambda e, s: (e, 0, s))
+    shape = jax.ShapeDtypeStruct((2, part, shards * each), jnp.float32)
     return pl.pallas_call(
-        functools.partial(expert_kernel, experts),
-        grid=(planes * per,),
-        in_specs=[
-            rowwise(width),
-            rowwise(width),
-            rowwise(keep.shape[2]),
-            whole(wide_w),
-            whole(router_w),
-            whole(down_w),
-            whole(hot),
-        ],
-        out_specs=[rowwise(width), rowwise(width), hbm, hbm, hbm],
-        scratch_shapes=[
-            pltpu.VMEM(wide_w.shape, jnp.float32),
-            pltpu.VMEM(router_w.shape, jnp.float32),
-            pltpu.VMEM(down_w.shape, jnp.float32),
-            pltpu.VMEM(wide_w.shape, jnp.bfloat16),
-            pltpu.VMEM(down_w.shape, jnp.bfloat16),
-            pltpu.SemaphoreType.DMA((3,)),
-        ],
-        out_shape=(
-            jax.ShapeDtypeStruct((planes, rows, width), jnp.bfloat16),
-            jax.ShapeDtypeStruct((planes, rows, width), jnp.bfloat16),
-            jax.ShapeDtypeStruct(wide_w.shape, jnp.bfloat16),
-            jax.ShapeDtypeStruct(router_w.shape, jnp.float32),
-            jax.ShapeDtypeStruct(down_w.shape, jnp.bfloat16),
-        ),
-        compiler_params=vmem_params(56),
-        cost_estimate=pl.CostEstimate(
-            flops=2 * planes * rows * width * (3 * wide_w.shape[1] + 3 * down_w.shape[1]),
-            bytes_accessed=100 * MIB,
-            transcendentals=planes * rows * down_w.shape[1],
-        ),
-    )(x_all, g_all, keep, wide_w, router_w, down_w, hot)
-
-
-def attend_back_kernel(
-    mixed_grad, raw, low, total, weight, query_gain, key_gain, cosine, sine, seg_row, seg_col,
-    qkv_grad_out, normed_grad_out, query_gain_out, key_gain_out,
-):
-    part = mixed_grad.shape[1]
-    allowed = seg_col[...] == seg_row[...]
-    gain_sums = [None, None]
-    for head in range(part // HD):
-        span = pl.ds(head * HD, HD)
-        query, key = low[:, span], low[:, pl.ds(part + head * HD, HD)]
-        value = low[:, pl.ds(2 * part + head * HD, HD)]
-        out_grad = mixed_grad[:, span]
-        scores = jnp.where(allowed, nt_dot(query, key), -1e30)
-        probs = jnp.exp(scores - total[:, head : head + 1])
-        prob_grad = nt_dot(out_grad, value)
-        value_grad = tn_dot(probs.astype(jnp.bfloat16), out_grad)
-        qkv_grad_out[:, pl.ds(2 * part + head * HD, HD)] = value_grad.astype(jnp.bfloat16)
-        inner = jnp.sum(probs * prob_grad, axis=-1, keepdims=True)
-        score_grad = (probs * (prob_grad - inner)).astype(jnp.bfloat16)
-        rotated = (
-            jnp.dot(score_grad, key, preferred_element_type=jnp.float32) * HD ** (-0.5),
-            tn_dot(score_grad, query),
-        )
-        for which, (offset, scale_gain) in enumerate(((0, query_gain), (part, key_gain))):
-            grad = rotated[which]
-            grad = grad * cosine[...] - pltpu.roll(grad, HD // 2, 1) * sine[...]
-            source = raw[:, pl.ds(offset + head * HD, HD)]
-            factor = norm_factor(source)
-            gain_sum = jnp.sum(grad * source * factor, axis=0, keepdims=True)
-            gain_sums[which] = gain_sum if head == 0 else gain_sums[which] + gain_sum
-            scaled = grad * scale_gain[...]
-            inner = jnp.mean(scaled * source, axis=-1, keepdims=True)
-            result = factor * scaled - source * (factor * factor * factor) * inner
-            qkv_grad_out[:, pl.ds(offset + head * HD, HD)] = result.astype(jnp.bfloat16)
-    query_gain_out[...] = gain_sums[0]
-    key_gain_out[...] = gain_sums[1]
-    normed_grad_out[...] = nt_dot(qkv_grad_out[...], weight[...]).astype(jnp.bfloat16)
-
-
-def attend_back_call(
-    mixed_grad, raw, low, total, weight, query_gain, key_gain, tables, seg_row, seg_col
-):
-    seq = mixed_grad.shape[0]
-    width = weight.shape[0]
-    return pl.pallas_call(
-        attend_back_kernel,
-        out_shape=(
-            jax.ShapeDtypeStruct(low.shape, jnp.bfloat16),
-            jax.ShapeDtypeStruct((seq, width), jnp.bfloat16),
-            jax.ShapeDtypeStruct((1, HD), jnp.float32),
-            jax.ShapeDtypeStruct((1, HD), jnp.float32),
-        ),
-        compiler_params=vmem_params(52),
-        cost_estimate=pl.CostEstimate(
-            flops=2 * seq * width * low.shape[1], bytes_accessed=16 * MIB, transcendentals=seq * seq * 4
-        ),
-    )(mixed_grad, raw, low, total, weight, query_gain, key_gain, *tables, seg_row, seg_col)
-
-
-def copy_kernel(*refs):
-    half = len(refs) // 2
-    for source, result in zip(refs[:half], refs[half:], strict=True):
-        result[...] = source[...].reshape(result.shape).astype(result.dtype)
-
-
-def unpack_units(wide, narrow, own):
-    shards, part, count = wide.shape
-    each = count // (2 * own)
-    gate = pl.BlockSpec((1, part, each), lambda e, s: (s, 0, e))
-    up = pl.BlockSpec((1, part, each), lambda e, s: (s, 0, own + e))
-    result = pl.BlockSpec((1, part, each), lambda e, s: (e, 0, s))
-    shape = jax.ShapeDtypeStruct((own, part, shards * each), jnp.float32)
-    gate_grad, up_grad = pl.pallas_call(
-        copy_kernel,
-        grid=(own, shards),
-        in_specs=[gate, up],
-        out_specs=[result, result],
-        out_shape=[shape, shape],
-        compiler_params=vmem_params(16),
-    )(wide, wide)
-    down_grad = pl.pallas_call(
-        copy_kernel,
-        grid=(own, shards),
-        in_specs=[pl.BlockSpec((1, each, part), lambda e, s: (s, e, 0))],
-        out_specs=[pl.BlockSpec((1, each, part), lambda e, s: (e, s, 0))],
-        out_shape=[jax.ShapeDtypeStruct((own, shards * each, part), jnp.float32)],
-        compiler_params=vmem_params(16),
-    )(narrow)[0]
-    return gate_grad, up_grad, down_grad
+        unpack_kernel,
+        grid=(2, shards),
+        in_specs=[wide_spec(index, which) for which in range(2) for index in range(2)]
+        + [down_spec(index) for index in range(2)],
+        out_specs=[wide_out, wide_out, pl.BlockSpec((1, each, part), lambda e, s: (e, s, 0))],
+        out_shape=[shape, shape, jax.ShapeDtypeStruct((2, shards * each, part), jnp.float32)],
+        compiler_params=vmem_params(24),
+    )(wides[0], wides[1], wides[0], wides[1], *downs)
 
 
 def keep_kernel(capacity, bits, shards, high, low, keep_out):
@@ -754,7 +576,7 @@
     return pl.pallas_call(
         functools.partial(keep_kernel, capacity, most.bit_length(), shards),
         out_shape=jax.ShapeDtypeStruct((planes, shards * rows, own), jnp.float32),
-        compiler_params=vmem_params(24),
+        compiler_params=vmem_params(8),
     )(high, low)
 
 
@@ -762,6 +584,10 @@
 
 
 MESH = pl.DeviceIdType.MESH
+
+
+def held_in_hbm(*values):
+    return [pltpu.with_memory_space_constraint(value, pltpu.HBM) for value in values]
 
 
 class Wires:
@@ -821,32 +647,25 @@
         return self.wires.shard + (-step if way == 0 else step)
 
     def run(self, step, first=None):
-        for way in range(2):
-            if step > 0:
-
-                @pl.when(self.has(way, step))
-                def _(way=way):
-                    for copy in self.copies(way, step - 1, self.block(way, step)):
-                        copy.wait_recv()
-
-            if step < self.shards - 1:
-
-                @pl.when(self.sends(way, step))
-                def _(way=way):
-                    if first is None:
-                        copies = self.copies(way, step, self.block(way, step))
-                    else:
-                        wires = self.wires
-                        peer = (wires.device, wires.shard + (1 if way == 0 else -1))
-                        block = self.block(way, step)
-                        copies = [
-                            wires.copy(source, view(block), slot, peer)
-                            for source, view, slot in zip(
-                                first, self.views, self.slots[way][step], strict=True
-                            )
-                        ]
-                    for copy in copies:
-                        copy.start()
+        wires = self.wires
+        for index, view in enumerate(self.views):
+            for way in range(2):
+                block = self.block(way, step)
+                peer = (wires.device, wires.shard + (1 if way == 0 else -1))
+                if step > 0:
+
+                    @pl.when(self.has(way, step))
+                    def _(way=way, block=block, index=index, view=view, peer=peer):
+                        slot = self.slots[way][step - 1][index]
+                        wires.copy(view(block), view(block), slot, peer).wait_recv()
+
+                if step < self.shards - 1:
+
+                    @pl.when(self.sends(way, step))
+                    def _(way=way, block=block, index=index, view=view, peer=peer):
+                        source = view(block) if first is None else first[index]
+                        slot = self.slots[way][step][index]
+                        wires.copy(source, view(block), slot, peer).start()
 
     def drain(self):
         for way in range(2):
@@ -925,7 +744,7 @@
 
 def opening_kernel(
     shards, experts, routes, order, gains, router, w_query, w_key, w_value, tokens, w_out, out_grad,
-    small_all, router_all, qkv_w, tokens_all, out_block, grad_seq, small, send, recv, local,
+    small_all, router_all, qkv_w, tokens_all, out_block, grad_all, small, send, recv, local,
 ):
     wires = Wires(send, recv)
     device, shard = wires.device, wires.shard
@@ -946,46 +765,58 @@
         return weights[which].at[:, pl.ds(pl.multiple_of(target * part, part), part)]
 
     mine = device * shards + shard
-    exchange = [[wires.slot() for _ in range(5)] for _ in range(1, shards)]
-    sent = []
-    for step in range(1, shards):
-        peer = wires.peer(step=step, shards=shards)
-        slots = exchange[step - 1]
-        copies = [wires.copy(router, router_all.at[mine], slots[4], peer)] + [
-            wires.copy(cut(which, peer[1]), place(shard, which), slots[which], peer)
-            for which in range(3)
-        ]
-        for copy in copies:
-            copy.start()
-        sent += copies
+
+    def token_rows(ref):
+        return lambda b: ref.at[pl.ds(pl.multiple_of(b * rows, rows), rows)]
+
+    def grad_block(owner, source):
+        return (owner * shards + source) * rows
+
+    def grad_rows(owner, source):
+        return grad_all.at[pl.ds(pl.multiple_of(grad_block(owner, source), rows), rows)]
+
+    def grad_half(source):
+        def view(owner, half):
+            start = grad_block(owner, source) + half * (rows // 2)
+            return grad_all.at[pl.ds(pl.multiple_of(start, rows // 2), rows // 2)]
+
+        return view
+
+    grad_line = Relay(wires, shards, [lambda b: grad_rows(device, b)])
+    line = Relay(
+        wires,
+        shards,
+        [
+            token_rows(tokens_all),
+            lambda b: out_block.at[pl.ds(pl.multiple_of(b * block, block), block)],
+        ],
+    )
+    grad_line.run(0, (out_grad,))
     own = [
         pltpu.make_async_copy(cut(which, shard), place(shard, which), local.at[which])
         for which in range(3)
     ]
     own += [
         pltpu.make_async_copy(router, router_all.at[mine], local.at[3]),
-        pltpu.make_async_copy(
-            tokens, tokens_all.at[pl.ds(pl.multiple_of(shard * rows, rows), rows)], local.at[4]
-        ),
+        pltpu.make_async_copy(tokens, token_rows(tokens_all)(shard), local.at[4]),
         pltpu.make_async_copy(
             w_out, out_block.at[pl.ds(pl.multiple_of(shard * block, block), block)], local.at[5]
         ),
-        pltpu.make_async_copy(
-            out_grad, grad_seq.at[pl.ds(pl.multiple_of(shard * rows, rows), rows)], local.at[6]
-        ),
+        pltpu.make_async_copy(out_grad, grad_rows(device, shard), local.at[6]),
     ]
     for copy in own:
         copy.start()
-    line = Relay(
-        wires,
-        shards,
-        [
-            lambda b: tokens_all.at[pl.ds(pl.multiple_of(b * rows, rows), rows)],
-            lambda b: out_block.at[pl.ds(pl.multiple_of(b * block, block), block)],
-            lambda b: grad_seq.at[pl.ds(pl.multiple_of(b * rows, rows), rows)],
-        ],
-    )
-    line.run(0, (tokens, w_out, out_grad))
+    turns = [shard] + [
+        sum(jnp.where(shard == index, source, 0) for index, source in enumerate(row))
+        for row in ((1, 0, 1, 2), (2, 2, 3, 1), (3, 3, 0, 0))
+    ]
+    stages = [
+        Plane(wires, [grad_half(source)], [lambda owner, source=source: grad_rows(owner, source)])
+        for source in turns
+    ]
+    own[6].wait()
+    stages[0].step_one()
+    stages[0].start(stages[0].cores(0))
     column = lax.broadcasted_iota(jnp.int32, (rows, 128), 1)
     dense = jnp.zeros((rows, 128), jnp.int32)
     for choice in range(routes.shape[1]):
@@ -996,15 +827,38 @@
         turned = digits.astype(jnp.float32).T
         small[pl.ds(start, experts), :] = turned[:experts, :].astype(small.dtype)
     small[pl.ds(2 * experts, gains.shape[0]), :] = gains[...]
+    own.append(pltpu.make_async_copy(small, small_all.at[mine], local.at[7]))
+    own[-1].start()
+    stages[0].step_two()
+    grad_line.run(1)
+    stages[1].step_one()
+    stages[1].start(stages[1].cores(0))
+    exchange = [[wires.slot() for _ in range(5)] for _ in range(1, shards)]
+    sent = []
     for step in range(1, shards):
         peer = wires.peer(step=step, shards=shards)
-        copy = wires.copy(small, small_all.at[mine], exchange[step - 1][3], peer)
-        copy.start()
-        sent.append(copy)
-    own.append(pltpu.make_async_copy(small, small_all.at[mine], local.at[7]))
-    own[-1].start()
-    for copy in own:
-        copy.wait()
+        slots = exchange[step - 1]
+        copies = [
+            wires.copy(router, router_all.at[mine], slots[4], peer),
+            wires.copy(small, small_all.at[mine], slots[3], peer),
+        ]
+        copies += [
+            wires.copy(cut(which, peer[1]), place(shard, which), slots[which], peer)
+            for which in range(3)
+        ]
+        for copy in copies:
+            copy.start()
+        sent += copies
+    stages[0].step_three()
+    stages[1].step_two()
+    grad_line.run(2)
+    line.run(0, (tokens, w_out))
+    stages[2].step_one()
+    stages[2].start(stages[2].cores(0))
+    stages[1].step_three()
+    for index, copy in enumerate(own):
+        if index != 6:
+            copy.wait()
     for step in range(1, shards):
         peer = wires.peer(step=shards - step, shards=shards)
         source = peer[1]
@@ -1036,16 +890,24 @@
     )
     plane.step_one()
     plane.start(plane.cores(0))
+    stages[2].step_two()
+    grad_line.run(3)
+    stages[3].step_one()
+    stages[3].start(stages[3].cores(0))
     plane.step_two()
+    stages[2].step_three()
     line.run(1)
+    stages[3].step_two()
+    plane.step_three()
     line.run(2)
-    plane.step_three()
-    for step in range(3, shards):
-        line.run(step)
-    plane.finish()
+    stages[3].step_three()
+    line.run(3)
+    for group in (*stages, plane):
+        group.finish()
     for copy in sent:
         copy.wait_send()
     line.drain()
+    grad_line.drain()
 
 
 def opening_call(
@@ -1055,7 +917,7 @@
     rows = tokens.shape[0]
     hbm = pl.BlockSpec(memory_space=pltpu.HBM)
     vmem = pl.BlockSpec(memory_space=pltpu.VMEM)
-    slots = 72
+    slots = 112
     small = (2 * experts + gains.shape[0], 128)
     return pl.pallas_call(
         functools.partial(opening_kernel, shards, experts),
@@ -1067,7 +929,7 @@
             jax.ShapeDtypeStruct((planes * shards * block, 3 * width // shards), w_query.dtype),
             jax.ShapeDtypeStruct((shards * rows, width), tokens.dtype),
             jax.ShapeDtypeStruct((shards * block, width), w_out.dtype),
-            jax.ShapeDtypeStruct((shards * rows, width), out_grad.dtype),
+            jax.ShapeDtypeStruct((planes * shards * rows, width), out_grad.dtype),
         ),
         scratch_shapes=[
             pltpu.VMEM(small, gains.dtype),
@@ -1144,108 +1006,112 @@
     )(mixed, out_block)
 
 
+class Units:
+    def __init__(self, wires, shards, index, gate, up, down, wide_w, down_w, local, base):
+        self.wires, self.shards, self.index = wires, shards, index
+        self.gate, self.up, self.down, self.wide_w, self.down_w = gate, up, down, wide_w, down_w
+        self.local, self.base = local, base
+        self.slots = [[wires.slot() for _ in range(3)] for _ in range(1, shards)]
+
+    def pairs(self, source, target):
+        each = self.down_w.shape[1]
+        span = pl.ds(pl.multiple_of(target * each, each), each)
+        return [
+            (self.gate.at[self.index, :, span], self.wide_w.at[source, :, pl.ds(0, each)]),
+            (self.up.at[self.index, :, span], self.wide_w.at[source, :, pl.ds(each, each)]),
+            (self.down.at[self.index, span, :], self.down_w.at[source]),
+        ]
+
+    def own(self):
+        shard = self.wires.shard
+        return [
+            pltpu.make_async_copy(source, place, self.local.at[self.base + slot])
+            for slot, (source, place) in enumerate(self.pairs(shard, shard))
+        ]
+
+    def sends(self):
+        wires = self.wires
+        for step in range(1, self.shards):
+            peer = wires.peer(step=step, shards=self.shards)
+            pairs = self.pairs(wires.shard, peer[1])
+            for slot, (source, place) in zip(self.slots[step - 1], pairs, strict=True):
+                yield wires.copy(source, place, slot, peer)
+
+    def begin(self):
+        for copy in self.own():
+            copy.start()
+        for copy in self.sends():
+            copy.start()
+
+    def end(self):
+        wires = self.wires
+        for copy in self.own():
+            copy.wait()
+        for step in range(1, self.shards):
+            back = wires.peer(step=self.shards - step, shards=self.shards)
+            pairs = self.pairs(back[1], wires.shard)
+            for slot, (_, place) in zip(self.slots[step - 1], pairs, strict=True):
+                wires.copy(place, place, slot, back).wait_recv()
+        for copy in self.sends():
+            copy.wait_send()
+
+
 def meeting_kernel(
-    shards, normed, grad_seq, gate, up, down,
-    normed_all, grad_all, wide_w, down_w, send, recv, local,
+    shards, normed, gate, up, down, normed_all, wide_w, down_w, send, recv, local
 ):
     wires = Wires(send, recv)
-    device, shard = wires.device, wires.shard
-    own, part, hidden_units = gate.shape
-    each = hidden_units // shards
+    device = wires.device
     half = normed.shape[0] // 2
     greet(
         [wires.peer(step=step, shards=shards) for step in range(1, shards)]
         + [wires.peer(XBIT), wires.peer(YBIT), wires.peer(CORE)]
     )
-
-    def wide_pair(source, target):
-        lanes = pl.ds(pl.multiple_of(target * each, each), each)
-        pairs = []
-        for which, weight in enumerate((gate, up)):
-            for index in range(own):
-                place = wide_w.at[source, :, pl.ds((which * own + index) * each, each)]
-                pairs.append((weight.at[index, :, lanes], place))
-        return pairs
-
-    def down_pair(source, target):
-        lines = pl.ds(pl.multiple_of(target * each, each), each)
-        return [
-            (down.at[index, lines, :], down_w.at[source, pl.ds(index * each, each), :])
-            for index in range(own)
-        ]
-
-    sent, pending = [], []
-    token_plane = Plane(
-        wires, [lambda owner, part_of: normed_all.at[owner, pl.ds(part_of * half, half)]],
+    plane = Plane(
+        wires,
+        [lambda owner, part_of: normed_all.at[owner, pl.ds(part_of * half, half)]],
         [lambda owner: normed_all.at[owner]],
     )
-    grad_plane = Plane(
-        wires, [lambda owner, part_of: grad_all.at[owner, pl.ds(part_of * half, half)]],
-        [lambda owner: grad_all.at[owner]],
-    )
-    own_copies = [
-        pltpu.make_async_copy(normed, normed_all.at[device], local.at[0]),
-        pltpu.make_async_copy(grad_seq, grad_all.at[device], local.at[1]),
-    ]
-    for index, (source, place) in enumerate(wide_pair(shard, shard) + down_pair(shard, shard)):
-        own_copies.append(pltpu.make_async_copy(source, place, local.at[2 + index]))
-    for copy in own_copies:
-        copy.start()
-    for pair in (wide_pair, down_pair):
-        for step in range(1, shards):
-            peer = wires.peer(step=step, shards=shards)
-            back = wires.peer(step=shards - step, shards=shards)
-            for (source, place), (_, mine) in zip(
-                pair(shard, peer[1]), pair(back[1], shard), strict=True
-            ):
-                slot = wires.slot()
-                copy = wires.copy(source, place, slot, peer)
-                copy.start()
-                sent.append(copy)
-                pending.append((mine, slot, back))
-    for copy in own_copies:
-        copy.wait()
-    token_plane.step_one()
-    token_plane.start(token_plane.cores(0))
-    grad_plane.start(grad_plane.cores(0))
-    token_plane.step_two()
-    grad_plane.step_one()
-    token_plane.step_three()
-    grad_plane.step_two()
-    grad_plane.step_three()
-    token_plane.finish()
-    grad_plane.finish()
-    for mine, slot, back in pending:
-        wires.copy(mine, mine, slot, back).wait_recv()
-    for copy in sent:
-        copy.wait_send()
-
-
-def meeting_call(normed, grad_seq, gate, up, down, planes, shards):
+    units = Units(wires, shards, 0, gate, up, down, wide_w, down_w, local, 1)
+    own = pltpu.make_async_copy(normed, normed_all.at[device], local.at[0])
+    own.start()
+    own.wait()
+    plane.step_one()
+    units.begin()
+    plane.start(plane.cores(0))
+    plane.step_two()
+    plane.step_three()
+    plane.finish()
+    units.end()
+
+
+def unit_shapes(gate, shards):
+    _, part, hidden_units = gate.shape
+    each = hidden_units // shards
+    return (
+        jax.ShapeDtypeStruct((shards, part, 2 * each), gate.dtype),
+        jax.ShapeDtypeStruct((shards, each, part), gate.dtype),
+    )
+
+
+def meeting_call(normed, gate, up, down, planes, shards):
     hbm = pl.BlockSpec(memory_space=pltpu.HBM)
-    own, part, hidden_units = gate.shape
-    count = own * hidden_units // shards
-    slots = 48
+    slots = 24
     return pl.pallas_call(
         functools.partial(meeting_kernel, shards),
-        in_specs=[hbm] * 5,
-        out_specs=[hbm] * 4,
-        out_shape=(
-            jax.ShapeDtypeStruct((planes,) + normed.shape, normed.dtype),
-            jax.ShapeDtypeStruct((planes,) + grad_seq.shape, grad_seq.dtype),
-            jax.ShapeDtypeStruct((shards, part, 2 * count), gate.dtype),
-            jax.ShapeDtypeStruct((shards, count, part), down.dtype),
-        ),
+        in_specs=[hbm] * 4,
+        out_specs=[hbm] * 3,
+        out_shape=(jax.ShapeDtypeStruct((planes,) + normed.shape, normed.dtype),)
+        + unit_shapes(gate, shards),
         scratch_shapes=[
             pltpu.SemaphoreType.DMA((slots,)),
             pltpu.SemaphoreType.DMA((slots,)),
-            pltpu.SemaphoreType.DMA((2 + 3 * own,)),
+            pltpu.SemaphoreType.DMA((4,)),
         ],
         compiler_params=pltpu.CompilerParams(
             collective_id=3, has_side_effects=True, vmem_limit_bytes=4 * MIB
         ),
         cost_estimate=pl.CostEstimate(flops=0, bytes_accessed=300 * MIB, transcendentals=0),
-    )(normed, grad_seq, gate, up, down)
+    )(normed, gate, up, down)
 
 
 def add_rows(target, sources, lines):
@@ -1281,6 +1147,13 @@
             self.part(chip, 0), self.held.at[chip], self.local.at[self.base + chip]
         )
 
+    def give(self, chip):
+        self.start(
+            self.wires.copy(
+                self.held.at[chip], self.came.at[chip], self.core[chip], self.wires.peer(CORE)
+            )
+        )
+
     def begin(self):
         for chip in (3, 1, 2, 0):
             self.load(chip).start()
@@ -1291,7 +1164,8 @@
             )
 
     def add_core(self, chip):
-        self.load(chip).wait()
+        if self.part is not None:
+            self.load(chip).wait()
         place = self.came.at[chip]
         self.wires.copy(place, place, self.core[chip], self.wires.peer(CORE)).wait_recv()
         add_rows(self.held.at[chip], [place], 64)
@@ -1344,17 +1218,18 @@
     def __init__(self, wires, shards, source, landing):
         self.wires, self.shards, self.source, self.landing = wires, shards, source, landing
         self.slots = [wires.slot() for _ in range(shards - 1)]
-        self.sent = []
-
-    def begin(self):
+
+    def sends(self):
         wires = self.wires
         for step in range(1, self.shards):
             peer = wires.peer(step=step, shards=self.shards)
-            copy = wires.copy(
+            yield wires.copy(
                 self.source(peer[1]), self.landing(wires.shard), self.slots[step - 1], peer
             )
+
+    def begin(self):
+        for copy in self.sends():
             copy.start()
-            self.sent.append(copy)
 
     def arrive(self):
         wires = self.wires
@@ -1364,7 +1239,7 @@
             wires.copy(place, place, self.slots[step - 1], peer).wait_recv()
 
     def drain(self):
-        for copy in self.sent:
+        for copy in self.sends():
             copy.wait_send()
 
 
@@ -1379,9 +1254,184 @@
     return pl.ds(pl.multiple_of(index * size, size), size)
 
 
+def expert_kernel(
+    index, experts, shards, x, g, keep, wide_w, router_w, down_w, hot, *refs
+):
+    if index == 0:
+        gate, up, down, out, grad, pull, wide_sum, down_sum, next_wide, next_down = refs[:10]
+        acc, dacc, wide_out, down_out, send, recv, local, sems = refs[10:]
+    else:
+        old_out, old_grad, old_pull, wide_sent, down_sent = refs[:5]
+        out, grad, wide_sum, down_sum, router_sum, wide_came, down_came = refs[5:12]
+        acc, racc, dacc, wide_out, down_out, send, recv, local, sems = refs[12:]
+    step, steps = pl.program_id(0), pl.num_programs(0)
+    wires = Wires(send, recv)
+    if index == 0:
+        travel = [Units(wires, shards, 1, gate, up, down, next_wide, next_down, local, 0)]
+    else:
+        travel = [
+            LineSum(wires, shards, lambda t: wide_sent.at[t], lambda s: wide_came.at[s]),
+            LineSum(wires, shards, lambda t: down_sent.at[t], lambda s: down_came.at[s]),
+        ]
+        stay = [
+            pltpu.make_async_copy(
+                sent.at[wires.shard], came.at[wires.shard], local.at[place]
+            )
+            for place, (sent, came) in enumerate(((wide_sent, wide_came), (down_sent, down_came)))
+        ]
+
+    @pl.when(step == 0)
+    def _():
+        greet([wires.peer(step=hop, shards=shards) for hop in range(1, shards)])
+        for group in travel:
+            group.begin()
+        acc[...] = jnp.zeros_like(acc)
+        dacc[...] = jnp.zeros_like(dacc)
+        if index == 1:
+            for copy in stay:
+                copy.start()
+            racc[...] = jnp.zeros_like(racc)
+
+    _, each, part = down_w.shape
+    wide = jnp.dot(x[...], wide_w[...], preferred_element_type=jnp.float32)
+    logits = jnp.dot(x[...], router_w[...], preferred_element_type=jnp.float32)
+    back = nt_dot(g[:, :part], down_w[0])
+    for shard in range(1, shards):
+        back = back + nt_dot(g[:, shard * part : (shard + 1) * part], down_w[shard])
+    lane = lax.broadcasted_iota(jnp.int32, logits.shape, 1)
+    logits = jnp.where(lane < experts, logits, -1e30)
+    shifted = jnp.exp(logits - jnp.max(logits, axis=-1, keepdims=True))
+    probs = shifted / jnp.sum(shifted, axis=-1, keepdims=True)
+    mark = hot[index : index + 1, :]
+    kept = keep[:, index : index + 1]
+    route = jnp.sum(probs * mark, axis=-1, keepdims=True) * kept
+    gated, lifted = wide[:, :each], wide[:, each:]
+    sigma = 1.0 / (1.0 + jnp.exp(-gated))
+    silu = gated * sigma
+    act = silu * lifted
+    pulled = jnp.sum(act * back, axis=-1, keepdims=True) * kept
+    act_low = (act * route).astype(jnp.bfloat16)
+    act_grad = back * route
+    wide_low = jnp.concatenate(
+        [
+            (act_grad * lifted * sigma * (1.0 + gated * (1.0 - sigma))).astype(jnp.bfloat16),
+            (act_grad * silu).astype(jnp.bfloat16),
+        ],
+        axis=1,
+    )
+    result = nt_dot(wide_low, wide_w[...])
+    if index == 0:
+        pull[...] = pulled
+    else:
+        dense = pulled * mark + old_pull[...] * hot[0:1, :]
+        logit_grad = probs * (dense - jnp.sum(probs * dense, axis=-1, keepdims=True))
+        logit_low = logit_grad.astype(jnp.bfloat16)
+        result = result + nt_dot(logit_low, router_w[...]) + old_grad[...].astype(jnp.float32)
+        racc[...] += tn_dot(x[...], logit_low)
+    grad[...] = result.astype(jnp.bfloat16)
+    for shard in range(shards):
+        span = slice(shard * part, (shard + 1) * part)
+        value = jnp.dot(act_low, down_w[shard], preferred_element_type=jnp.float32)
+        if index == 1:
+            value = value + old_out[:, span].astype(jnp.float32)
+        out[:, span] = value.astype(jnp.bfloat16)
+        dacc[shard] += tn_dot(act_low, g[:, span])
+    acc[...] += tn_dot(x[...], wide_low)
+
+    @pl.when(step == steps - 1)
+    def _():
+        wide_out[...] = acc[...].astype(jnp.bfloat16)
+        wide_copy = pltpu.make_async_copy(wide_out, wide_sum, sems.at[0])
+        wide_copy.start()
+        down_out[...] = dacc[...].astype(jnp.bfloat16)
+        down_copy = pltpu.make_async_copy(down_out, down_sum, sems.at[1])
+        down_copy.start()
+        if index == 1:
+            router_copy = pltpu.make_async_copy(racc, router_sum, sems.at[2])
+            router_copy.start()
+            router_copy.wait()
+        wide_copy.wait()
+        down_copy.wait()
+        if index == 0:
+            travel[0].end()
+        else:
+            for copy in stay:
+                copy.wait()
+            for group in travel:
+                group.arrive()
+                group.drain()
+
+
+def expert_call(index, x_all, g_all, keep, wide_w, router_w, down_w, hot, experts, weights, before):
+    planes, rows, width = x_all.shape
+    shards = down_w.shape[0]
+    tile = 512
+    per = rows // tile
+    hbm = pl.BlockSpec(memory_space=pltpu.HBM)
+
+    def whole(value):
+        zeros = (0,) * value.ndim
+        return pl.BlockSpec(value.shape, lambda i: zeros, pipeline_mode=pl.Buffered(1))
+
+    def rowwise(lanes):
+        return pl.BlockSpec((None, tile, lanes), lambda i: (i // per, i % per, 0))
+
+    low = jnp.bfloat16
+    tall = pltpu.HBM((planes, rows, width), low)
+    narrow = pltpu.HBM((planes, rows, 1), jnp.float32)
+    wide_shape = pltpu.HBM(wide_w.shape, low)
+    down_shape = pltpu.HBM(down_w.shape, low)
+    came = pltpu.HBM((shards, width // shards, wide_w.shape[1]), low)
+    if index == 0:
+        extra = [hbm] * 3
+        out_specs = [rowwise(width)] * 2 + [rowwise(1)] + [hbm] * 4
+        shapes = (tall, tall, narrow, wide_shape, down_shape, came, down_shape)
+        operands = held_in_hbm(*weights)
+    else:
+        extra = [rowwise(width)] * 2 + [rowwise(1)] + [hbm] * 2
+        out_specs = [rowwise(width)] * 2 + [hbm] * 5
+        router_shape = pltpu.HBM(router_w.shape, jnp.float32)
+        shapes = (tall, tall, wide_shape, down_shape, router_shape, came, down_shape)
+        operands = held_in_hbm(*before)
+    return pl.pallas_call(
+        functools.partial(expert_kernel, index, experts, shards),
+        grid=(planes * per,),
+        in_specs=[
+            rowwise(width),
+            rowwise(width),
+            rowwise(keep.shape[2]),
+            whole(wide_w),
+            whole(router_w),
+            whole(down_w),
+            whole(hot),
+        ]
+        + extra,
+        out_specs=out_specs,
+        scratch_shapes=[pltpu.VMEM(wide_w.shape, jnp.float32)]
+        + ([] if index == 0 else [pltpu.VMEM(router_w.shape, jnp.float32)])
+        + [
+            pltpu.VMEM(down_w.shape, jnp.float32),
+            pltpu.VMEM(wide_w.shape, low),
+            pltpu.VMEM(down_w.shape, low),
+            pltpu.SemaphoreType.DMA((12,)),
+            pltpu.SemaphoreType.DMA((12,)),
+            pltpu.SemaphoreType.DMA((3,)),
+            pltpu.SemaphoreType.DMA((3,)),
+        ],
+        out_shape=shapes,
+        compiler_params=pltpu.CompilerParams(
+            collective_id=7 + index, has_side_effects=True, vmem_limit_bytes=52 * MIB
+        ),
+        cost_estimate=pl.CostEstimate(
+            flops=planes * rows * width * 12 * down_w.shape[1],
+            bytes_accessed=100 * MIB,
+            transcendentals=planes * rows * down_w.shape[1],
+        ),
+    )(*held_in_hbm(x_all, g_all), keep, wide_w, router_w, down_w, hot, *operands)
+
+
 def returning_kernel(
-    shards, ins, outs, wide,
-    in_total, out_total, wide_all,
+    shards, ins, outs, wide, down, in_total, out_total, wide_all, down_all,
     held, came, diag, side, held2, came2, diag2, side2, landing, send, recv, local,
 ):
     wires = Wires(send, recv)
@@ -1396,15 +1446,23 @@
         return lambda chip, core: source.at[device ^ (2 * chip + core)]
 
     grads = PlaneSum(wires, rel(ins), held, came, diag, side, local, 0)
-    values = PlaneSum(wires, rel(outs), held2, came2, diag2, side2, local, 4)
-    weights = LineSum(wires, shards, lambda t: wide.at[t], lambda s: wide_all.at[s])
+    values = PlaneSum(wires, rel(outs), held2, came2, diag2, side2, local, 6)
+    weights = [
+        LineSum(wires, shards, lambda t: wide.at[t], lambda s: wide_all.at[s]),
+        LineSum(wires, shards, lambda t: down.at[t], lambda s: down_all.at[s]),
+    ]
     line = LineSum(
         wires, shards, lambda t: held.at[0, aligned(t, rows)], lambda s: landing.at[s]
     )
     grads.begin()
-    weights.begin()
-    own = pltpu.make_async_copy(wide.at[shard], wide_all.at[shard], local.at[8])
-    own.start()
+    for group in weights:
+        group.begin()
+    own = [
+        pltpu.make_async_copy(wide.at[shard], wide_all.at[shard], local.at[4]),
+        pltpu.make_async_copy(down.at[shard], down_all.at[shard], local.at[5]),
+    ]
+    for copy in own:
+        copy.start()
     grads.send_corner()
     values.begin()
     grads.add_cores()
@@ -1418,111 +1476,100 @@
     line.arrive()
     in_total[...] = line_total(landing, shards)
     values.end()
-    back = pltpu.make_async_copy(held2.at[0], out_total, local.at[9])
+    back = pltpu.make_async_copy(held2.at[0], out_total, local.at[10])
     back.start()
-    weights.arrive()
-    own.wait()
+    for copy in own:
+        copy.wait()
     back.wait()
-    for group in (grads, values, weights, line):
+    for group in weights:
+        group.arrive()
+    for group in (grads, values, line, *weights):
         group.drain()
 
 
-def returning_call(ins, outs, wide, shards):
+def sum_work(rows, lanes):
+    low = jnp.bfloat16
+    return [
+        pltpu.VMEM((4, rows, lanes), low),
+        pltpu.VMEM((4, rows, lanes), low),
+        pltpu.VMEM((2, rows // 2, lanes), low),
+        pltpu.VMEM((2, rows, lanes), low),
+    ]
+
+
+def returning_call(ins, outs, wide, down):
     _, seq, width = ins.shape
+    shards = wide.shape[0]
     rows = seq // shards
     hbm = pl.BlockSpec(memory_space=pltpu.HBM)
     vmem = pl.BlockSpec(memory_space=pltpu.VMEM)
-    low = jnp.bfloat16
-    work = [
-        pltpu.VMEM((4, seq, width), low),
-        pltpu.VMEM((4, seq, width), low),
-        pltpu.VMEM((2, seq // 2, width), low),
-        pltpu.VMEM((2, seq, width), low),
-    ]
     return pl.pallas_call(
         functools.partial(returning_kernel, shards),
-        in_specs=[hbm] * 3,
-        out_specs=[vmem, hbm, hbm],
+        in_specs=[hbm] * 4,
+        out_specs=[vmem, hbm, hbm, hbm],
         out_shape=(
             jax.ShapeDtypeStruct((rows, width), jnp.float32),
-            jax.ShapeDtypeStruct((seq, width), low),
-            jax.ShapeDtypeStruct(wide.shape, wide.dtype),
+            jax.ShapeDtypeStruct((seq, width), jnp.bfloat16),
+            pltpu.HBM(wide.shape, wide.dtype),
+            pltpu.HBM(down.shape, down.dtype),
         ),
-        scratch_shapes=work
-        + work
+        scratch_shapes=sum_work(seq, width)
+        + sum_work(seq, width)
         + [
-            pltpu.VMEM((shards, rows, width), low),
-            pltpu.SemaphoreType.DMA((32,)),
-            pltpu.SemaphoreType.DMA((32,)),
-            pltpu.SemaphoreType.DMA((10,)),
+            pltpu.VMEM((shards, rows, width), jnp.bfloat16),
+            pltpu.SemaphoreType.DMA((36,)),
+            pltpu.SemaphoreType.DMA((36,)),
+            pltpu.SemaphoreType.DMA((11,)),
         ],
         compiler_params=pltpu.CompilerParams(
-            collective_id=4, has_side_effects=True, vmem_limit_bytes=58 * MIB
+            collective_id=4, has_side_effects=True, vmem_limit_bytes=56 * MIB
         ),
         cost_estimate=pl.CostEstimate(flops=0, bytes_accessed=300 * MIB, transcendentals=0),
-    )(ins, outs, wide)
-
-
-def turn_back_kernel(
-    shards, hidden, grad, out_grad, gain, weight,
-    hidden_grad_out, low_out, gain_grad_out, message_all, message, send, recv, local,
+    )(*held_in_hbm(ins, outs, wide, down))
+
+
+def back_through_heads(
+    mixed_grad, raw, low, total, query_gain, key_gain, cosine, sine, allowed, qkv_grad
 ):
-    wires = Wires(send, recv)
-    part = message.shape[2]
-    greet([wires.peer(step=step, shards=shards) for step in range(1, shards)])
-    factor = norm_factor(hidden[...])
-    gain_grad_out[...] = jnp.sum(grad[...] * hidden[...] * factor, axis=0, keepdims=True)
-    scaled = grad[...] * gain[...]
-    inner = jnp.mean(scaled * hidden[...], axis=-1, keepdims=True)
-    total = out_grad[...].astype(jnp.float32) + factor * scaled
-    total = total - hidden[...] * (factor * factor * factor) * inner
-    hidden_grad_out[...] = total
-    low = total.astype(jnp.bfloat16)
-    low_out[...] = low
-    for shard in range(shards):
-        message[shard] = nt_dot(low, weight[pl.ds(shard * part, part), :]).astype(jnp.bfloat16)
-    line = LineSum(wires, shards, lambda t: message.at[t], lambda s: message_all.at[s])
-    line.begin()
-    own = pltpu.make_async_copy(message.at[wires.shard], message_all.at[wires.shard], local.at[0])
-    own.start()
-    own.wait()
-    line.arrive()
-    line.drain()
-
-
-def turn_back_call(hidden, grad, out_grad, gain, weight, shards):
-    rows, width = hidden.shape
-    part = width // shards
-    vmem = pl.BlockSpec(memory_space=pltpu.VMEM)
-    return pl.pallas_call(
-        functools.partial(turn_back_kernel, shards),
-        in_specs=[vmem] * 5,
-        out_specs=[vmem] * 3 + [pl.BlockSpec(memory_space=pltpu.HBM)],
-        out_shape=(
-            jax.ShapeDtypeStruct((rows, width), jnp.float32),
-            jax.ShapeDtypeStruct((rows, width), jnp.bfloat16),
-            jax.ShapeDtypeStruct((1, width), jnp.float32),
-            jax.ShapeDtypeStruct((shards, rows, part), jnp.bfloat16),
-        ),
-        scratch_shapes=[
-            pltpu.VMEM((shards, rows, part), jnp.bfloat16),
-            pltpu.SemaphoreType.DMA((4,)),
-            pltpu.SemaphoreType.DMA((4,)),
-            pltpu.SemaphoreType.DMA((1,)),
-        ],
-        compiler_params=pltpu.CompilerParams(
-            collective_id=5, has_side_effects=True, vmem_limit_bytes=40 * MIB
-        ),
-        cost_estimate=pl.CostEstimate(
-            flops=2 * rows * width * width, bytes_accessed=40 * MIB, transcendentals=0
-        ),
-    )(hidden, grad, out_grad, gain, weight)
+    part = raw.shape[1] // 2
+    gain_sums = [None, None]
+    for head in range(part // HD):
+        span = pl.ds(head * HD, HD)
+        query, key = low[:, span], low[:, pl.ds(part + head * HD, HD)]
+        value = low[:, pl.ds(2 * part + head * HD, HD)]
+        out_grad = mixed_grad[:, span]
+        scores = jnp.where(allowed, nt_dot(query, key), -1e30)
+        probs = jnp.exp(scores - total[:, head : head + 1])
+        prob_grad = nt_dot(out_grad, value)
+        value_grad = tn_dot(probs.astype(jnp.bfloat16), out_grad)
+        qkv_grad[:, pl.ds(2 * part + head * HD, HD)] = value_grad.astype(jnp.bfloat16)
+        inner = jnp.sum(probs * prob_grad, axis=-1, keepdims=True)
+        score_grad = (probs * (prob_grad - inner)).astype(jnp.bfloat16)
+        rotated = (
+            jnp.dot(score_grad, key, preferred_element_type=jnp.float32) * HD ** (-0.5),
+            tn_dot(score_grad, query),
+        )
+        for which, (offset, scale_gain) in enumerate(((0, query_gain), (part, key_gain))):
+            grad = rotated[which]
+            grad = grad * cosine[...] - pltpu.roll(grad, HD // 2, 1) * sine[...]
+            source = raw[:, pl.ds(offset + head * HD, HD)]
+            factor = norm_factor(source)
+            gain_sum = jnp.sum(grad * source * factor, axis=0, keepdims=True)
+            gain_sums[which] = gain_sum if head == 0 else gain_sums[which] + gain_sum
+            scaled = grad * scale_gain[...]
+            inner = jnp.mean(scaled * source, axis=-1, keepdims=True)
+            result = factor * scaled - source * (factor * factor * factor) * inner
+            qkv_grad[:, pl.ds(offset + head * HD, HD)] = result.astype(jnp.bfloat16)
+    return gain_sums
 
 
 def closing_kernel(
-    shards, planes, normed_grad, out_total, qkv_grad, out_grad, tokens, hidden_grad, hidden, gain, router, vectors,
+    shards, planes,
+    hidden, grad, out_grad, ffn_gain, raw, low, total, query_gain, key_gain, cosine, sine, seg_row, seg_col,
+    tokens, gain, own_mixed, normed, router, out_w, qkv_w, out_total,
     input_grad, mixed_out, query_out, key_out, value_out, weight_out, gain_out, router_out, vectors_out,
     held, came, diag, side, held2, came2, diag2, side2,
+    weights, hidden_grad, attn_low, message, message_land, qkv_grad, normed_grad, vectors,
     norm_land, out_land, qkv_land, weight_land, gain_mine, gain_land, gain_line, router_land, router_sum, router_line,
     vector_land, vector_sum, vector_line, send, recv, local,
 ):
@@ -1532,32 +1579,28 @@
     block = query_out.shape[0]
     part = width // shards
     lines = router_out.shape[0]
+    lanes = qkv_w.shape[1]
     line_peers = [wires.peer(step=step, shards=shards) for step in range(1, shards)]
     plane_peers = [wires.peer(bits) for bits in range(1, planes)]
+    load_out = pltpu.make_async_copy(out_w, weights, local.at[0])
+    load_out.start()
     greet(line_peers + plane_peers)
 
-    def rel(source):
-        return lambda chip, core: source.at[device ^ (2 * chip + core)]
-
-    norms = LineSum(wires, shards, lambda t: normed_grad.at[t], lambda s: norm_land.at[s])
+    back = LineSum(
+        wires, shards, lambda t: message.at[t], lambda s: message_land.at[aligned(s, rows)]
+    )
+    norms = LineSum(wires, shards, lambda t: normed_grad.at[aligned(t, rows)], lambda s: norm_land.at[s])
     values = LineSum(
         wires, shards, lambda t: out_total.at[aligned(t, rows)], lambda s: out_land.at[s]
     )
-    qkv = PlaneSum(wires, rel(qkv_grad), held, came, diag, side, local, 0)
-    weight = PlaneSum(wires, rel(out_grad), held2, came2, diag2, side2, local, 4)
+    qkv = PlaneSum(wires, None, held, came, diag, side, local, 0)
+    weight = PlaneSum(wires, None, held2, came2, diag2, side2, local, 0)
     qkv_line = LineSum(
         wires, shards, lambda t: held.at[0, aligned(t, block)], lambda s: qkv_land.at[s]
     )
     weight_line = LineSum(
         wires, shards, lambda t: held2.at[0, aligned(t, block)], lambda s: weight_land.at[s]
     )
-    norms.begin()
-    own_norm = pltpu.make_async_copy(normed_grad.at[shard], norm_land.at[shard], local.at[8])
-    own_norm.start()
-    own_value = pltpu.make_async_copy(
-        out_total.at[aligned(shard, rows)], out_land.at[shard], local.at[9]
-    )
-    own_value.start()
     sent = []
 
     def spread(slots, source, landing):
@@ -1581,154 +1624,190 @@
     vector_slots = [wires.slot() for _ in range(1, planes)]
     gain_slots = [wires.slot() for _ in range(1, planes)]
     spread(router_slots, lambda e: router.at[aligned(e, shards * lines)], router_land)
+    router_land[device] = router[aligned(device, shards * lines), :]
+
+    factor = norm_factor(hidden[...])
+    vectors[:, :width] = jnp.sum(grad[...] * hidden[...] * factor, axis=0, keepdims=True)
+    scaled = grad[...] * ffn_gain[...]
+    inner = jnp.mean(scaled * hidden[...], axis=-1, keepdims=True)
+    change = out_grad[...].astype(jnp.float32) + factor * scaled
+    change = change - hidden[...] * (factor * factor * factor) * inner
+    hidden_grad[...] = change
+    attn_low[...] = change.astype(jnp.bfloat16)
+    load_out.wait()
+    for target in range(shards):
+        message[target] = nt_dot(attn_low[...], weights[pl.ds(target * part, part), :]).astype(
+            jnp.bfloat16
+        )
+    back.begin()
+    values.begin()
+    load_qkv = pltpu.make_async_copy(qkv_w, weights.at[:, pl.ds(0, lanes)], local.at[1])
+    load_qkv.start()
+    own_value = pltpu.make_async_copy(
+        out_total.at[aligned(shard, rows)], out_land.at[shard], local.at[2]
+    )
+    own_value.start()
+    message_land[aligned(shard, rows), :] = message[shard]
+
+    def addends(group, left, right):
+        for core in (1, 0):
+            for chip in (3, 1, 2, 0):
+                owner = device ^ (2 * chip + core)
+                columns = pl.ds(pl.multiple_of(owner * shards * block, shards * block), shards * block)
+                if core == 0:
+                    group.sent[(3, 1, 2, 0).index(chip)].wait_send()
+                group.held[chip] = tn_dot(left[:, columns], right[...]).astype(jnp.bfloat16)
+                if core == 1:
+                    group.give(chip)
+        group.sent = []
+
+    addends(weight, own_mixed, attn_low)
+    weight.send_corner()
+    weight.add_cores()
+    router_sum[...] = collect(router_slots, router_land)
+    router_pass = LineSum(
+        wires, shards, lambda t: router_sum.at[aligned(t, lines)], lambda s: router_line.at[s]
+    )
+
+    back.arrive()
+    allowed = seg_col[...] == seg_row[...]
+    query_sum, key_sum = back_through_heads(
+        message_land, raw, low, total, query_gain, key_gain, cosine, sine, allowed, qkv_grad
+    )
+    vectors[:, pl.ds(width, HD)] = query_sum
+    vectors[:, pl.ds(width + HD, HD)] = key_sum
+    load_qkv.wait()
+    normed_grad[...] = nt_dot(qkv_grad[...], weights[:, pl.ds(0, lanes)]).astype(jnp.bfloat16)
+    norms.begin()
+    norm_land[shard] = normed_grad[aligned(shard, rows), :]
+    router_pass.begin()
     spread(vector_slots, lambda e: vectors, vector_land)
-    qkv.begin()
-    weight.begin()
+    vector_land[device] = vectors[...]
+    weight.send_sides()
+    addends(qkv, normed, qkv_grad)
     qkv.send_corner()
     qkv.add_cores()
-    weight.send_corner()
-    router_land[device] = router[aligned(device, shards * lines), :]
-    vector_land[device] = vectors[...]
-    router_sum[...] = collect(router_slots, router_land)
     vector_sum[...] = collect(vector_slots, vector_land)
-    router_pass = LineSum(
-        wires, shards, lambda t: router_sum.at[aligned(t, lines)], lambda s: router_line.at[s]
-    )
     vector_pass = LineSum(wires, shards, lambda t: vector_sum, lambda s: vector_line.at[s])
-    router_pass.begin()
     vector_pass.begin()
+    vector_line[shard] = vector_sum[...]
+    router_line[shard] = router_sum[aligned(shard, lines), :]
     qkv.send_sides()
-    weight.add_cores()
-    own_norm.wait()
+    weight.end()
+    weight_line.begin()
+    weight_land[shard] = held2[0, aligned(shard, block), :]
+    out_land_ready = own_value
+    out_land_ready.wait()
+    values.arrive()
+    mixed_out[...] = (hidden[...] + line_total(out_land, shards)).astype(jnp.bfloat16)
+
     norms.arrive()
-    values.begin()
-    grad = line_total(norm_land, shards)
+    change = line_total(norm_land, shards)
     given = tokens[...].astype(jnp.float32)
     factor = norm_factor(given)
-    gain_mine[...] = jnp.sum(grad * given * factor, axis=0, keepdims=True)
+    gain_mine[...] = jnp.sum(change * given * factor, axis=0, keepdims=True)
     spread(gain_slots, lambda e: gain_mine, gain_land)
-    scaled = grad * gain[...]
+    scaled = change * gain[...]
     inner = jnp.mean(scaled * given, axis=-1, keepdims=True)
-    total = hidden_grad[...] + factor * scaled - given * (factor * factor * factor) * inner
-    input_grad[...] = total.astype(jnp.bfloat16)
+    result = hidden_grad[...] + factor * scaled - given * (factor * factor * factor) * inner
+    input_grad[...] = result.astype(jnp.bfloat16)
     qkv.end()
     qkv_line.begin()
-    weight.send_sides()
+    qkv_land[shard] = held[0, aligned(shard, block), :]
     gain_land[device] = gain_mine[...]
-    gain_mine2 = collect(gain_slots, gain_land)
-    gain_line[shard] = gain_mine2
+    gain_line[shard] = collect(gain_slots, gain_land)
     gain_pass = LineSum(wires, shards, lambda t: gain_line.at[shard], lambda s: gain_line.at[s])
     gain_pass.begin()
-    weight.end()
-    weight_line.begin()
-    router_line[shard] = router_sum[aligned(shard, lines), :]
-    vector_line[shard] = vector_sum[...]
     router_pass.arrive()
     router_out[...] = line_total(router_line, shards)
     vector_pass.arrive()
     vectors_out[...] = line_total(vector_line, shards)
-    own_value.wait()
-    values.arrive()
-    mixed_out[...] = (hidden[...] + line_total(out_land, shards)).astype(jnp.bfloat16)
-    qkv_land[shard] = held[0, aligned(shard, block), :]
+    weight_line.arrive()
+    weight_out[...] = line_total(weight_land, shards)
     qkv_line.arrive()
     for source in range(shards):
-        for which, result in enumerate((query_out, key_out, value_out)):
-            result[:, pl.ds(source * part, part)] = qkv_land[
+        for which, result_out in enumerate((query_out, key_out, value_out)):
+            result_out[:, pl.ds(source * part, part)] = qkv_land[
                 source, :, pl.ds(which * part, part)
             ].astype(jnp.float32)
     gain_pass.arrive()
     gain_out[...] = line_total(gain_line, shards)
-    weight_land[shard] = held2[0, aligned(shard, block), :]
-    weight_line.arrive()
-    weight_out[...] = line_total(weight_land, shards)
     for copy in sent:
         copy.wait_send()
-    groups = (norms, values, qkv, weight, qkv_line, weight_line, router_pass, vector_pass)
-    for group in groups + (gain_pass,):
+    groups = (back, norms, values, qkv, weight, qkv_line, weight_line, router_pass, vector_pass)
+    for group in (*groups, gain_pass):
         group.drain()
 
 
 def closing_call(
-    normed_grad, out_total, qkv_grad, out_grad, tokens, hidden_grad, hidden, gain, router, vectors
+    hidden, grad, out_grad, ffn_gain, raw, low, total, query_gain, key_gain, tables, seg_row, seg_col,
+    tokens, gain, own_mixed, normed, router, out_w, qkv_w, out_total, planes, shards,
 ):
-    shards, rows, width = normed_grad.shape
-    planes, each, lanes = qkv_grad.shape
+    rows, width = tokens.shape
+    seq, lanes = low.shape
+    each = width // planes
     block = each // shards
     lines = router.shape[0] // (planes * shards)
     hbm = pl.BlockSpec(memory_space=pltpu.HBM)
     vmem = pl.BlockSpec(memory_space=pltpu.VMEM)
-    low, full = jnp.bfloat16, jnp.float32
-
-    def work(wide):
-        return [
-            pltpu.VMEM((4, each, wide), low),
-            pltpu.VMEM((4, each, wide), low),
-            pltpu.VMEM((2, each // 2, wide), low),
-            pltpu.VMEM((2, each, wide), low),
-        ]
-
+    half, full = jnp.bfloat16, jnp.float32
     weight_shape = jax.ShapeDtypeStruct((block, width), full)
+    vector = width + 2 * HD
     return pl.pallas_call(
         functools.partial(closing_kernel, shards, planes),
-        in_specs=[hbm] * 4 + [vmem] * 6,
+        in_specs=[vmem] * 18 + [hbm] * 3,
         out_specs=[vmem] * 9,
         out_shape=(
-            jax.ShapeDtypeStruct((rows, width), low),
-            jax.ShapeDtypeStruct((rows, width), low),
+            jax.ShapeDtypeStruct((rows, width), half),
+            jax.ShapeDtypeStruct((rows, width), half),
             weight_shape,
             weight_shape,
             weight_shape,
             weight_shape,
             jax.ShapeDtypeStruct((1, width), full),
             jax.ShapeDtypeStruct((lines, 128), full),
-            jax.ShapeDtypeStruct(vectors.shape, full),
+            jax.ShapeDtypeStruct((1, vector), full),
         ),
-        scratch_shapes=work(lanes)
-        + work(width)
+        scratch_shapes=sum_work(each, lanes)
+        + sum_work(each, width)
         + [
-            pltpu.VMEM((shards, rows, width), low),
-            pltpu.VMEM((shards, rows, width), low),
-            pltpu.VMEM((shards, block, lanes), low),
-            pltpu.VMEM((shards, block, width), low),
+            pltpu.VMEM((width, width), half),
+            pltpu.VMEM((rows, width), full),
+            pltpu.VMEM((rows, width), half),
+            pltpu.VMEM((shards, rows, width // shards), half),
+            pltpu.VMEM((seq, width // shards), half),
+            pltpu.VMEM((seq, lanes), half),
+            pltpu.VMEM((seq, width), half),
+            pltpu.VMEM((1, vector), full),
+            pltpu.VMEM((shards, rows, width), half),
+            pltpu.VMEM((shards, rows, width), half),
+            pltpu.VMEM((shards, block, lanes), half),
+            pltpu.VMEM((shards, block, width), half),
             pltpu.VMEM((1, width), full),
             pltpu.VMEM((planes, 1, width), full),
             pltpu.VMEM((shards, 1, width), full),
             pltpu.VMEM((planes, shards * lines, 128), full),
             pltpu.VMEM((shards * lines, 128), full),
             pltpu.VMEM((shards, lines, 128), full),
-            pltpu.VMEM((planes,) + vectors.shape, full),
-            pltpu.VMEM(vectors.shape, full),
-            pltpu.VMEM((shards,) + vectors.shape, full),
+            pltpu.VMEM((planes, 1, vector), full),
+            pltpu.VMEM((1, vector), full),
+            pltpu.VMEM((shards, 1, vector), full),
             pltpu.SemaphoreType.DMA((72,)),
             pltpu.SemaphoreType.DMA((72,)),
-            pltpu.SemaphoreType.DMA((10,)),
+            pltpu.SemaphoreType.DMA((3,)),
         ],
         compiler_params=pltpu.CompilerParams(
-            collective_id=6, has_side_effects=True, vmem_limit_bytes=58 * MIB
+            collective_id=6, has_side_effects=True, vmem_limit_bytes=60 * MIB
         ),
         cost_estimate=pl.CostEstimate(flops=0, bytes_accessed=300 * MIB, transcendentals=0),
-    )(normed_grad, out_total, qkv_grad, out_grad, tokens, hidden_grad, hidden, gain, router, vectors)
+    )(
+        hidden, grad, out_grad, ffn_gain, raw, low, total, query_gain, key_gain, *tables, seg_row, seg_col,
+        tokens, gain, own_mixed, normed, router, *held_in_hbm(out_w, qkv_w, out_total),
+    )
 
 
 LOW = jnp.bfloat16
 WIDE = jnp.float32
-
-
-def swap(value, bits):
-    count = lax.axis_size(EXPERT)
-    return lax.ppermute(value, EXPERT, [(i, i ^ bits) for i in range(count)])
-
-
-def shard_exchange(pieces, shard):
-    size = lax.axis_size(SHARD)
-    result = pieces
-    for step in range(1, size):
-        target = (shard + step) % size
-        sent = lax.dynamic_index_in_dim(pieces, target, 0, keepdims=True)
-        got = lax.ppermute(sent, SHARD, [(i, (i + step) % size) for i in range(size)])
-        result = lax.dynamic_update_slice_in_dim(result, got, (shard - step) % size, 0)
-    return result
 
 
 def fast_local(
@@ -1765,7 +1844,7 @@
     gains = jnp.concatenate([attn_gain, ffn_gain, query_gain, key_gain])
     gains = jnp.pad(gains, (0, -gains.size % (16 * 128))).reshape(-1, 128)
     router_pad = jnp.pad(w_router, ((0, 0), (0, 128 - experts)))
-    small, router_w, qkv_w, tokens_seq, out_block, grad_seq = opening_call(
+    small, router_w, qkv_w, tokens_seq, out_block, grad_all = opening_call(
         routes,
         pair_order.reshape(rows, top_count),
         gains,
@@ -1803,55 +1882,70 @@
     mixed, out_w = middle_call(mixed_own, out_block, planes, shards)
     hidden_seq, normed_seq = join_call(mixed, out_w, tokens_seq, ffn_row)
 
-    token_all, grad_all, wide_w, down_w = meeting_call(
-        normed_seq, grad_seq, w_gate, w_up, w_down, planes, shards
-    )
-    wide_w = wide_w.reshape(width, -1)
+    token_all, wide_w, down_w = meeting_call(normed_seq, w_gate, w_up, w_down, planes, shards)
+    grad_all = grad_all.reshape(planes, seq, width)
     own_ids = device * own_experts + jnp.arange(own_experts, dtype=jnp.int32)
     own_hot = (own_ids[:, None] == jnp.arange(128, dtype=jnp.int32)[None, :]).astype(WIDE)
-    out_parts, in_parts, wide_message, router_grad, down_message = expert_call(
-        token_all, grad_all, kept, wide_w, router_w, down_w, own_hot, experts
-    )
-    normed_two_grad, out_total, wide_pieces = returning_call(
-        in_parts, out_parts, wide_message.reshape(shards, part, -1), shards
+    out_first, in_first, pull, wide_sum, down_sum, wide_next, down_next = expert_call(
+        0,
+        token_all,
+        grad_all,
+        kept,
+        wide_w.reshape(width, -1),
+        router_w,
+        down_w,
+        own_hot,
+        experts,
+        (w_gate, w_up, w_down),
+        None,
+    )
+    before = (out_first, in_first, pull, wide_sum.reshape(shards, part, -1), down_sum)
+    out_parts, in_parts, wide_sum, down_sum, router_grad, wide0, down0 = expert_call(
+        1,
+        token_all,
+        grad_all,
+        kept,
+        wide_next.reshape(width, -1),
+        router_w,
+        down_next,
+        own_hot,
+        experts,
+        None,
+        before,
+    )
+    normed_two_grad, out_total, wide1, down1 = returning_call(
+        in_parts, out_parts, wide_sum.reshape(shards, part, -1), down_sum
     )
     hidden = lax.dynamic_slice_in_dim(hidden_seq, shard * rows, rows)
-
-    hidden_grad, attn_low, ffn_scale_grad, mixed_grad = turn_back_call(
-        hidden, normed_two_grad, out_grad, ffn_row, out_w, shards
-    )
-    mixed_grad = mixed_grad.reshape(seq, part)
-    down_message, _ = lax.optimization_barrier((down_message, mixed_grad))
-    down_pieces = shard_exchange(down_message, shard)
-    qkv_grad, normed_grad, query_scale_grad, key_scale_grad = attend_back_call(
-        mixed_grad, raw, low, total, qkv_w, query_row, key_row, tables, seg_row, seg_col
-    )
-    normed_grad = normed_grad.reshape(shards, rows, width)
-
-    qkv_w_grad = matmul_tn(normed_low, qkv_grad).astype(LOW).reshape(planes, -1, 3 * part)
     own_mixed = lax.dynamic_slice_in_dim(mixed, shard * rows, rows, 1)
     own_mixed = own_mixed.transpose(1, 0, 2).reshape(rows, width)
-    out_w_grad = matmul_tn(own_mixed, attn_low).astype(LOW).reshape(planes, -1, width)
-    router_table = router_grad[:, :experts].reshape(-1, 128)
-    vectors = jnp.concatenate(
-        [ffn_scale_grad.reshape(-1, 128), query_scale_grad, key_scale_grad], axis=0
-    )
-    vectors = jnp.pad(vectors, ((0, -vectors.shape[0] % 8), (0, 0)))
     closed = closing_call(
-        normed_grad,
+        hidden,
+        normed_two_grad,
+        out_grad,
+        ffn_row,
+        raw,
+        low,
+        total,
+        query_row,
+        key_row,
+        tables,
+        seg_row,
+        seg_col,
+        tokens,
+        attn_row,
+        own_mixed,
+        normed_low,
+        router_grad[:, :experts].reshape(-1, 128),
+        out_w,
+        qkv_w,
         out_total,
-        qkv_w_grad,
-        out_w_grad,
-        tokens,
-        hidden_grad,
-        hidden,
-        attn_row,
-        router_table,
-        vectors,
+        planes,
+        shards,
     )
     input_grad, mixed_out, query_w_grad, key_w_grad, value_w_grad, out_w_grad = closed[:6]
     attn_scale_grad, router_out, vectors = closed[6:]
-    gate_grad, up_grad, down_grad = unpack_units(wide_pieces, down_pieces, own_experts)
+    gate_grad, up_grad, down_grad = unpack_units((wide0, wide1), (down0, down1))
     index = device * shards + shard
     flat = vectors.reshape(-1)
 

time: 901 us -> 793 us (0.88)
  Pallas kernels: 799 us -> 731 us
  local copies, waits for them, and re-layouts: 71.2 us -> 50.8 us
  matrix products: 12.6 us -> 0 us
    pallas_call x1, Pallas kernels: 152 us -> 83.6 us  [meeting_call(): pl.pallas_call(functools.partial(meeting_kernel, shards), in_specs=[hbm]...]
    pallas_call x5 -> x3, Pallas kernels: 148 us -> 162 us  [the longest x2 156 us: expert_call(): pl.pallas_call(functools.partial(expert_kernel, index, experts, shards),...]
    dot_general x2 -> x0, matrix products: 12.6 us -> none  [matmul_tn(): lax.dot_general(left, right, (((0,), (0,)), ((), ())), preferred_element_...]
    unnamed x104 -> x95, local copies, waits for them, and re-layouts: 53.3 us -> 42.3 us
  transfers between devices with their start and end apart: 3 -> 0, of which waited for: 0 -> 0; matrix products, arithmetic and copies ran while one was open for 3% -> 0% of each run, Pallas kernels for 20% -> 0%
where the time goes in v3:
time: 793 us; the launch traced here: 784 us
  Pallas kernels  731 us (92%)
  local copies, waits for them, and re-layouts  50.8 us (6%)
    pallas_call x1, Pallas kernels, closing_call(): pl.pallas_call(functools.partial(closing_kernel, shards, planes), in_spec...  157 us
    pallas_call x2, Pallas kernels, expert_call(): pl.pallas_call(functools.partial(expert_kernel, index, experts, shards),...  156 us
    pallas_call x1, Pallas kernels, returning_call(): pl.pallas_call(functools.partial(returning_kernel, shards), in_specs=[hbm...  152 us
    pallas_call x1, Pallas kernels, opening_call(): pl.pallas_call(functools.partial(opening_kernel, shards, experts), in_spe...  117 us
    pallas_call x1, Pallas kernels, meeting_call(): pl.pallas_call(functools.partial(meeting_kernel, shards), in_specs=[hbm]...  83.6 us
    pallas_call x1, Pallas kernels, middle_call(): pl.pallas_call(functools.partial(middle_kernel, shards), in_specs=[hbm] *...  42.5 us
    unnamed x95, local copies, waits for them, and re-layouts  42.3 us

profile of v3, /device:TPU:0, one launch (start us, length us, event | category | flops | bytes accessed | tf_op | source)
XLA Modules:
  0.0 783.9 jit_solution(7481371582438013455)
XLA Ops:
  0.7 0.1 compare_convert_fusion.hot
  0.7 0.8 fusion.7.gains
  1.5 0.8 copy.39
  2.3 0.8 copy.40.routes
  3.1 0.8 reshape.92.order
  3.9 0.8 copy.41.seg_col
  4.7 0.0 copy-start.7
  4.7 1.0 copy-done.7
  5.8 1.0 copy-done.8
  6.8 0.9 copy-done.20
  7.7 0.9 copy-done.21
  8.7 0.9 copy-done.22
  9.6 0.9 copy-done.23
  10.6 117.3 %shard_map.290 = (bf16[32,48,128]{2,1,0:T(8,128)(2,1)S(1)}, bf16[32,64,128]{2,1,0:T(8,128)(2,1)S(1)}, bf16[2048,1536]{1,0:T(8,128)(2,1)S(1)}, bf16[512,2048]{1,0...) custom-call(s32[128,8]{1,0:T(8,128)S(1)} %copy.40.routes, s32[128,8]{1,0:T(8,128)S(1)} %reshape.92.order, ...), custom_call_target="tpu_custom_call" | custom-call | bytes 209715200 | tf_op jit(solution)/shard_map/pallas_call | solution.py:922
  127.9 2.7 copy-done.3
  130.6 5.8 copy-done.29
  136.4 1.3 copy-done.31
  137.7 0.1 copy.42
  137.8 0.1 copy.50
  137.9 0.1 fusion.12
  138.0 0.1 fusion.13
  138.1 0.1 reshape.96.key_gain
  138.2 0.0 copy-start.27
  138.2 0.1 reshape.99.gain.ffn_gain
  138.3 0.1 reshape.95.query_gain
  138.4 0.0 copy-start.28
  138.4 0.1 reshape.94.gain
  138.5 0.0 copy-start.32
  138.5 4.4 shard_map.295.keep
  142.9 0.0 copy-start.9
  142.9 1.3 copy-done.9
  144.3 2.8 copy-done.4
  147.1 6.8 shard_map.291
  153.9 1.3 copy-done.5
  155.2 1.3 copy-done.6
  156.5 0.7 copy-done.19
  157.2 42.5 %shard_map.292 = (bf16[4,512,512]{2,1,0:T(8,128)(2,1)S(1)}, bf16[2048,2048]{1,0:T(8,128)(2,1)S(1)}) custom-call(bf16[512,512]{1,0:T(8,128)(2,1)S(1)} %get-tuple-element.65.mixed, bf16[256,2048]{1,0:T(8,128)(2,1)S(1)} %get-tuple-element.66.out_block), custom_call_target="tpu_custom_call" | custom-call | bytes 157286400 | tf_op jit(solution)/shard_map/pallas_call | solution.py:989
  199.8 1.0 copy.47
  200.8 5.5 shard_map.293
  206.3 0.0 copy-start.10
  206.4 1.1 constant_dynamic-slice_fusion.4.hidden
  207.4 0.9 copy-done.10
  208.3 83.6 %shard_map.294 = (bf16[8,512,2048]{2,1,0:T(8,128)(2,1)S(1)}, bf16[4,512,512]{2,1,0:T(8,128)(2,1)S(1)}, bf16[4,256,512]{2,1,0:T(8,128)(2,1)S(1)}) custom-call(bf16[512,2048]{1,0:T(8,128)(2,1)S(1)} %get-tuple-element.70.normed, bf16[2,512,1024]{2,1,0:T(8,128)(2,1)S(1)} %copy-done.10, bf16[2,512,1024]{2,1,0:T(8,128)(2,1)S(1)} %copy-done.11, ...), custom_call_target="tpu_custom_call" | custom-call | bytes 314572800 | tf_op jit(solution)/shard_map/pallas_call | solution.py:1099
  291.9 5.7 copy-done.30
  297.6 1.3 copy-done.33
  298.9 62.4 %shard_map.296 = (bf16[8,512,2048]{2,1,0:T(8,128)(2,1)}, bf16[8,512,2048]{2,1,0:T(8,128)(2,1)}, f32[8,512,1]{2,1,0:T(8,128)}, bf16[2048,512]{1,0:T(8,128)(2,1)},...) custom-call(bf16[8,512,2048]{2,1,0:T(8,128)(2,1)} %copy-done.30, ...), custom_call_target="tpu_custom_call" | custom-call | flops 25769803776 | bytes 104857600 | tf_op jit(solution)/shard_map/pallas_call | solution.py:1396
  361.4 1.2 copy-done.34
  362.6 93.6 %shard_map.297 = (bf16[8,512,2048]{2,1,0:T(8,128)(2,1)}, bf16[8,512,2048]{2,1,0:T(8,128)(2,1)}, bf16[2048,512]{1,0:T(8,128)(2,1)}, bf16[4,256,512]{2,1,0:T(8,128...) custom-call(bf16[8,512,2048]{2,1,0:T(8,128)(2,1)} %copy-done.30, ...), custom_call_target="tpu_custom_call" | custom-call | flops 25769803776 | bytes 104857600 | tf_op jit(solution)/shard_map/pallas_call | solution.py:1396
  456.2 151.7 %shard_map.298 = (f32[128,2048]{1,0:T(8,128)}, bf16[512,2048]{1,0:T(8,128)(2,1)}, bf16[4,512,512]{2,1,0:T(8,128)(2,1)}, bf16[4,256,512]{2,1,0:T(8,128)(2,1)}) custom-call(bf16[8,512,2048]{2,1,0:T(8,128)(2,1)} %get-tuple-element.83.ins, bf16[8,512,2048]{2,1,0:T(8,128)(2,1)} %get-tuple-element.84.outs, bf16[4,512,512]{2,1,0:T(8,128)(2,1)} %bitcast.39, ...), custom_call_target="tpu_custom_call" | custom-call | bytes 314572800 | tf_op jit(solution)/shard_map/pallas_call | solution.py:1506
  607.9 1.0 reshape.107.router
  608.9 157.4 %shard_map.299 = (bf16[128,2048]{1,0:T(8,128)(2,1)}, bf16[128,2048]{1,0:T(8,128)(2,1)}, f32[64,2048]{1,0:T(8,128)}, f32[64,2048]{1,0:T(8,128)}, f32[64,2048]{1,0...) custom-call(f32[128,2048]{1,0:T(8,128)} %constant_dynamic-slice_fusion.4.hidden, ...), custom_call_target="tpu_custom_call" | custom-call | bytes 314572800 | tf_op jit(solution)/shard_map/pallas_call | solution.py:1756
  766.3 1.3 fusion.8
  767.6 1.3 fusion.10
  768.8 0.7 reshape.108
  769.6 0.7 copy.46
  770.3 1.6 copy-done.1
  771.9 1.2 copy-done.16
  773.1 5.8 shard_map.300
  778.9 0.8 copy.57
  779.7 0.8 copy.58
  780.5 0.8 copy.59
  781.3 0.8 copy.60
  782.1 0.8 copy.61
  782.9 0.8 copy.62
  (63 shorter events, 0.2 us)
Async XLA Ops:
  4.7 1.0 copy-start.7
  5.8 1.0 copy-start.8
  6.8 0.9 copy-start.20
  7.7 0.9 copy-start.21
  8.7 0.9 copy-start.22
  9.6 0.9 copy-start.23
  10.6 132.3 %copy-start.14 = (s32[512,1]{1,0:T(8,128)}, s32[512,1]{1,0:T(8,128)S(1)}, u32[]{:S(2)}) copy-start(s32[512,1]{1,0:T(8,128)S(1)} %copy.41.seg_col) | copy-start | bytes 6148
  127.9 2.7 copy-start.3
  130.6 5.8 copy-start.29
  136.4 1.3 copy-start.31
  137.7 6.6 copy-start.17
  137.7 6.6 copy-start.18
  137.7 6.6 copy-start.26
  138.2 15.7 %copy-start.27 = (f32[1,128]{1,0:T(1,128)}, f32[1,128]{1,0:T(1,128)S(1)}, u32[]{:S(2)}) copy-start(f32[1,128]{1,0:T(1,128)S(1)} %reshape.96.key_gain) | copy-start | bytes 1540
  138.3 62.5 %copy-start.24 = (f32[1,2048]{1,0:T(1,128)}, f32[1,2048]{1,0:T(1,128)S(1)}, u32[]{:S(2)}) copy-start(f32[1,2048]{1,0:T(1,128)S(1)} %reshape.99.gain.ffn_gain) | copy-start | bytes 24580
  138.4 15.5 %copy-start.28 = (f32[1,128]{1,0:T(1,128)}, f32[1,128]{1,0:T(1,128)S(1)}, u32[]{:S(2)}) copy-start(f32[1,128]{1,0:T(1,128)S(1)} %reshape.95.query_gain) | copy-start | bytes 1540
  138.5 15.4 %copy-start.25 = (f32[1,2048]{1,0:T(1,128)}, f32[1,2048]{1,0:T(1,128)S(1)}, u32[]{:S(2)}) copy-start(f32[1,2048]{1,0:T(1,128)S(1)} %reshape.94.gain) | copy-start | bytes 24580
  138.5 5.8 copy-start.32
  142.9 1.3 copy-start.9
  144.3 2.8 copy-start.4
  153.9 1.3 copy-start.5
  155.2 1.3 copy-start.6
  156.5 0.7 copy-start.19
  157.2 43.6 %copy-start.13 = (bf16[512,1536]{1,0:T(8,128)(2,1)}, bf16[512,1536]{1,0:T(8,128)(2,1)S(1)}, u32[]{:S(2)}) copy-start(bf16[512,1536]{1,0:T(8,128)(2,1)S(1)} %get-tuple-element.89.low) | copy-start | bytes 4718596
  199.8 6.6 copy-start.2
  200.8 6.6 copy-start.11
  200.8 6.6 copy-start.12
  206.3 2.0 copy-start.10
  291.9 5.7 copy-start.30
  297.6 1.3 copy-start.33
  361.4 1.2 copy-start.34
  456.2 151.7 %copy-start.35 = (f32[2048,128]{1,0:T(8,128)S(1)}, f32[2048,128]{1,0:T(8,128)}, u32[]{:S(2)}) copy-start(f32[2048,128]{1,0:T(8,128)} %get-tuple-element.92) | copy-start | bytes 3145732
  608.9 161.4 %copy-start = (bf16[4,512,512]{2,1,0:T(8,128)(2,1)S(1)}, bf16[4,512,512]{2,1,0:T(8,128)(2,1)}, u32[]{:S(2)}) copy-start(bf16[4,512,512]{2,1,0:T(8,128)(2,1)} %get-tuple-element.103.gate0.up0) | copy-start | bytes 6291460
  608.9 161.4 %copy-start.15 = (bf16[4,256,512]{2,1,0:T(8,128)(2,1)S(1)}, bf16[4,256,512]{2,1,0:T(8,128)(2,1)}, u32[]{:S(2)}) copy-start(bf16[4,256,512]{2,1,0:T(8,128)(2,1)} %get-tuple-element.105.down0) | copy-start | bytes 3145732
  770.3 1.6 copy-start.1
  771.9 1.2 copy-start.16
  773.1 5.8 copy-start.41
  773.1 6.6 copy-start.40
  778.9 1.6 copy-start.39
  778.9 2.4 copy-start.38
  778.9 3.2 copy-start.37
  779.7 3.2 copy-start.36

commit v4 on v3

--- a/solution.py
+++ b/solution.py
@@ -424,7 +424,7 @@
     return lax.rsqrt(jnp.mean(values * values, axis=-1, keepdims=True) + EPSILON)
 
 
-def attend_kernel(
+def attend(
     tokens, gain, weight, query_gain, key_gain, cosine, sine, seg_row, seg_col,
     normed_out, raw_out, low_out, mixed_out, total_out, qkv,
 ):
@@ -456,65 +456,6 @@
         total_out[:, head : head + 1] = top + jnp.log(total)
 
 
-def attend_call(tokens, gain, weight, query_gain, key_gain, tables, seg_row, seg_col):
-    seq, width = tokens.shape
-    part = weight.shape[1] // 3
-    return pl.pallas_call(
-        attend_kernel,
-        out_shape=(
-            jax.ShapeDtypeStruct((seq, width), jnp.bfloat16),
-            jax.ShapeDtypeStruct((seq, 2 * part), jnp.float32),
-            jax.ShapeDtypeStruct((seq, 3 * part), jnp.bfloat16),
-            jax.ShapeDtypeStruct((seq, part), jnp.bfloat16),
-            jax.ShapeDtypeStruct((seq, 128), jnp.float32),
-        ),
-        scratch_shapes=[pltpu.VMEM((seq, 3 * part), jnp.float32)],
-        compiler_params=vmem_params(28),
-        cost_estimate=pl.CostEstimate(
-            flops=2 * seq * width * 3 * part, bytes_accessed=16 * MIB, transcendentals=seq * seq * 4
-        ),
-    )(tokens, gain, weight, query_gain, key_gain, *tables, seg_row, seg_col)
-
-
-def join_kernel(mixed, weight, tokens, gain, hidden_out, normed_out):
-    shards, _, part = mixed.shape
-    total = tokens[...].astype(jnp.float32)
-    for shard in range(shards):
-        total = total + jnp.dot(
-            mixed[shard], weight[pl.ds(shard * part, part), :], preferred_element_type=jnp.float32
-        )
-    hidden_out[...] = total
-    normed_out[...] = (total * norm_factor(total) * gain[...]).astype(jnp.bfloat16)
-
-
-def join_call(mixed, weight, tokens, gain):
-    shards, seq, part = mixed.shape
-    width = weight.shape[1]
-    tile = seq // 2
-    return pl.pallas_call(
-        join_kernel,
-        grid=(2,),
-        in_specs=[
-            pl.BlockSpec((shards, tile, part), lambda i: (0, i, 0)),
-            pl.BlockSpec(weight.shape, lambda i: (0, 0), pipeline_mode=pl.Buffered(1)),
-            pl.BlockSpec((tile, width), lambda i: (i, 0)),
-            pl.BlockSpec((1, width), lambda i: (0, 0)),
-        ],
-        out_specs=[
-            pl.BlockSpec((tile, width), lambda i: (i, 0)),
-            pl.BlockSpec((tile, width), lambda i: (i, 0)),
-        ],
-        out_shape=(
-            jax.ShapeDtypeStruct((seq, width), jnp.float32),
-            jax.ShapeDtypeStruct((seq, width), jnp.bfloat16),
-        ),
-        compiler_params=vmem_params(26),
-        cost_estimate=pl.CostEstimate(
-            flops=2 * seq * width * width, bytes_accessed=18 * MIB, transcendentals=0
-        ),
-    )(mixed, weight, tokens, gain)
-
-
 def unpack_kernel(gate0, gate1, up0, up1, down0, down1, gate_out, up_out, down_out):
     for index, group in enumerate(((gate0, up0, down0), (gate1, up1, down1))):
 
@@ -550,13 +491,17 @@
     )(wides[0], wides[1], wides[0], wides[1], *downs)
 
 
-def keep_kernel(capacity, bits, shards, high, low, keep_out):
-    own, _, rows = high.shape
+def mark_kept(small_all, first, experts, own, capacity, bits, shards, keep_out):
+    devices, _, rows = small_all.shape
+    row = lax.broadcasted_iota(jnp.int32, (devices, rows), 0)
+    group = lax.rem(row, shards)
     for index in range(own):
-        order = high[index].astype(jnp.float32) * 256.0 + low[index].astype(jnp.float32)
+        order = jnp.zeros((devices, rows), jnp.float32)
+        for expert in range(experts):
+            high = small_all[:, expert, :].astype(jnp.float32)
+            low = small_all[:, experts + expert, :].astype(jnp.float32)
+            order = order + jnp.where(first + index == expert, high * 256.0 + low, 0.0)
         there = order > 0.0
-        row = lax.broadcasted_iota(jnp.int32, order.shape, 0)
-        group = lax.rem(row, shards)
         bound = jnp.zeros_like(order)
         for bit in reversed(range(bits)):
             trial = bound + float(1 << bit)
@@ -566,18 +511,9 @@
                 count = jnp.sum(jnp.where(here, within, 0.0), keepdims=True)
                 bound = jnp.where(here & (count <= float(capacity)), trial, bound)
         kept = jnp.where(there & (order <= bound), 1.0, 0.0).T
-        for block in range(order.shape[0]):
+        for block in range(devices):
             place = keep_out.at[block // shards, pl.ds(block % shards * rows, rows)]
             place[:, index : index + 1] = kept[:, block : block + 1]
-
-
-def keep_call(high, low, capacity, most, planes, shards):
-    own, _, rows = high.shape
-    return pl.pallas_call(
-        functools.partial(keep_kernel, capacity, most.bit_length(), shards),
-        out_shape=jax.ShapeDtypeStruct((planes, shards * rows, own), jnp.float32),
-        compiler_params=vmem_params(8),
-    )(high, low)
 
 
 CORE, XBIT, YBIT = 1, 2, 4
@@ -743,8 +679,12 @@
 
 
 def opening_kernel(
-    shards, experts, routes, order, gains, router, w_query, w_key, w_value, tokens, w_out, out_grad,
-    small_all, router_all, qkv_w, tokens_all, out_block, grad_all, small, send, recv, local,
+    shards, planes, experts, own_experts, capacity, bits,
+    routes, order, gains, seg_row, seg_col, cosine, sine,
+    router, w_query, w_key, w_value, tokens, w_out, out_grad,
+    kept_out, attn_row, ffn_row, query_row, key_row, normed_out, raw_out, low_out, total_out, mixed_all,
+    router_all, qkv_w_out, tokens_all, out_w_out, grad_out,
+    small, small_all, grad_all, qkv_w, out_w, mixed, qkv, send, recv, local, store,
 ):
     wires = Wires(send, recv)
     device, shard = wires.device, wires.shard
@@ -752,6 +692,7 @@
     block, width = w_query.shape
     rows = tokens.shape[0]
     part = width // shards
+    mine = device * shards + shard
     greet(
         [wires.peer(step=step, shards=shards) for step in range(1, shards)]
         + [wires.peer(XBIT), wires.peer(YBIT), wires.peer(CORE)]
@@ -764,10 +705,11 @@
     def cut(which, target):
         return weights[which].at[:, pl.ds(pl.multiple_of(target * part, part), part)]
 
-    mine = device * shards + shard
-
-    def token_rows(ref):
-        return lambda b: ref.at[pl.ds(pl.multiple_of(b * rows, rows), rows)]
+    def token_rows(b):
+        return tokens_all.at[pl.ds(pl.multiple_of(b * rows, rows), rows)]
+
+    def out_rows(owner, source):
+        return out_w.at[pl.ds(pl.multiple_of((owner * shards + source) * block, block), block)]
 
     def grad_block(owner, source):
         return (owner * shards + source) * rows
@@ -782,27 +724,32 @@
 
         return view
 
+    exchange = [[wires.slot() for _ in range(5)] for _ in range(1, shards)]
+    sent = []
+    for step in range(1, shards):
+        peer = wires.peer(step=step, shards=shards)
+        slots = exchange[step - 1]
+        copies = [
+            wires.copy(cut(which, peer[1]), place(shard, which), slots[which], peer)
+            for which in range(3)
+        ]
+        copies.append(wires.copy(router, router_all.at[mine], slots[4], peer))
+        for copy in copies:
+            copy.start()
+        sent += copies
     grad_line = Relay(wires, shards, [lambda b: grad_rows(device, b)])
-    line = Relay(
-        wires,
-        shards,
-        [
-            token_rows(tokens_all),
-            lambda b: out_block.at[pl.ds(pl.multiple_of(b * block, block), block)],
-        ],
-    )
-    grad_line.run(0, (out_grad,))
+    token_line = Relay(wires, shards, [token_rows])
+    out_line = Relay(wires, shards, [lambda b: out_rows(device, b)])
+    mixed_line = Relay(wires, shards, [lambda b: mixed_all.at[b]])
     own = [
-        pltpu.make_async_copy(cut(which, shard), place(shard, which), local.at[which])
-        for which in range(3)
+        pltpu.make_async_copy(out_grad, grad_rows(device, shard), local.at[0]),
+        pltpu.make_async_copy(router, router_all.at[mine], local.at[1]),
+        pltpu.make_async_copy(tokens, token_rows(shard), local.at[2]),
+        pltpu.make_async_copy(w_out, out_rows(device, shard), local.at[3]),
     ]
     own += [
-        pltpu.make_async_copy(router, router_all.at[mine], local.at[3]),
-        pltpu.make_async_copy(tokens, token_rows(tokens_all)(shard), local.at[4]),
-        pltpu.make_async_copy(
-            w_out, out_block.at[pl.ds(pl.multiple_of(shard * block, block), block)], local.at[5]
-        ),
-        pltpu.make_async_copy(out_grad, grad_rows(device, shard), local.at[6]),
+        pltpu.make_async_copy(cut(which, shard), place(shard, which), local.at[4 + which])
+        for which in range(3)
     ]
     for copy in own:
         copy.start()
@@ -814,9 +761,26 @@
         Plane(wires, [grad_half(source)], [lambda owner, source=source: grad_rows(owner, source)])
         for source in turns
     ]
-    own[6].wait()
-    stages[0].step_one()
-    stages[0].start(stages[0].cores(0))
+    stored = []
+
+    def begin(stage):
+        stage.step_one()
+        stage.start(stage.cores(0))
+
+    def keep(turn):
+        stages[turn].finish()
+        for owner in range(planes):
+            start = pl.multiple_of(grad_block(owner, turns[turn]), rows)
+            copy = pltpu.make_async_copy(
+                grad_rows(owner, turns[turn]),
+                grad_out.at[pl.ds(start, rows)],
+                store.at[turn * planes + owner],
+            )
+            copy.start()
+            stored.append(copy)
+
+    own[0].wait()
+    begin(stages[0])
     column = lax.broadcasted_iota(jnp.int32, (rows, 128), 1)
     dense = jnp.zeros((rows, 128), jnp.int32)
     for choice in range(routes.shape[1]):
@@ -827,46 +791,25 @@
         turned = digits.astype(jnp.float32).T
         small[pl.ds(start, experts), :] = turned[:experts, :].astype(small.dtype)
     small[pl.ds(2 * experts, gains.shape[0]), :] = gains[...]
-    own.append(pltpu.make_async_copy(small, small_all.at[mine], local.at[7]))
-    own[-1].start()
-    stages[0].step_two()
-    grad_line.run(1)
-    stages[1].step_one()
-    stages[1].start(stages[1].cores(0))
-    exchange = [[wires.slot() for _ in range(5)] for _ in range(1, shards)]
-    sent = []
+    small_all[mine] = small[...]
     for step in range(1, shards):
         peer = wires.peer(step=step, shards=shards)
-        slots = exchange[step - 1]
-        copies = [
-            wires.copy(router, router_all.at[mine], slots[4], peer),
-            wires.copy(small, small_all.at[mine], slots[3], peer),
-        ]
-        copies += [
-            wires.copy(cut(which, peer[1]), place(shard, which), slots[which], peer)
-            for which in range(3)
-        ]
-        for copy in copies:
-            copy.start()
-        sent += copies
-    stages[0].step_three()
-    stages[1].step_two()
-    grad_line.run(2)
-    line.run(0, (tokens, w_out))
-    stages[2].step_one()
-    stages[2].start(stages[2].cores(0))
-    stages[1].step_three()
-    for index, copy in enumerate(own):
-        if index != 6:
-            copy.wait()
+        copy = wires.copy(small, small_all.at[mine], exchange[step - 1][3], peer)
+        copy.start()
+        sent.append(copy)
+    out_line.run(0, (w_out,))
+    token_line.run(0, (tokens,))
+    stages[0].step_two()
+    for copy in own[1:]:
+        copy.wait()
     for step in range(1, shards):
         peer = wires.peer(step=shards - step, shards=shards)
         source = peer[1]
         slots = exchange[step - 1]
-        wires.copy(small, small_all.at[device * shards + source], slots[3], peer).wait_recv()
-        wires.copy(router, router_all.at[device * shards + source], slots[4], peer).wait_recv()
         for which in range(3):
             wires.copy(place(source, which), place(source, which), slots[which], peer).wait_recv()
+        wires.copy(router, router_all.at[device * shards + source], slots[4], peer).wait_recv()
+        wires.copy(small, small_all.at[device * shards + source], slots[3], peer).wait_recv()
 
     each = shards * block // 2
 
@@ -888,122 +831,154 @@
             lambda owner: router_all.at[pl.ds(owner * shards, shards)],
         ],
     )
-    plane.step_one()
-    plane.start(plane.cores(0))
+    outs = [
+        Plane(
+            wires,
+            [
+                lambda owner, side, index=index: out_w.at[
+                    pl.ds(
+                        pl.multiple_of(owner * 2 * each + index * each + side * (each // 2), each // 2),
+                        each // 2,
+                    )
+                ]
+            ],
+            [
+                lambda owner, index=index: out_w.at[
+                    pl.ds(pl.multiple_of((owner * 2 + index) * each, each), each)
+                ]
+            ],
+        )
+        for index in range(2)
+    ]
+    begin(plane)
+    stages[0].step_three()
+    out_line.run(1)
+    token_line.run(1)
+    plane.step_two()
+    out_line.run(2)
+    token_line.run(2)
+    grad_line.run(0, (out_grad,))
+    plane.step_three()
+    keep(0)
+    out_line.run(3)
+    for stage in outs:
+        begin(stage)
+    plane.finish()
+
+    count = width // 128
+    start = 2 * experts
+    summed = small_all[0, pl.ds(start, gains.shape[0]), :].astype(jnp.float32)
+    for other in range(1, planes * shards):
+        summed = summed + small_all[other, pl.ds(start, gains.shape[0]), :].astype(jnp.float32)
+    attn_row[...] = jnp.concatenate([summed[i : i + 1] for i in range(count)], axis=1)
+    ffn_row[...] = jnp.concatenate([summed[count + i : count + i + 1] for i in range(count)], axis=1)
+    query_row[...] = summed[2 * count : 2 * count + 1]
+    key_row[...] = summed[2 * count + 1 : 2 * count + 2]
+    for stage in outs:
+        stage.step_two()
+    token_line.run(3)
+    attend(
+        tokens_all, attn_row, qkv_w, query_row, key_row, cosine, sine, seg_row, seg_col,
+        normed_out, raw_out, low_out, mixed, total_out, qkv,
+    )
+    mixed_line.run(0, (mixed,))
+    mixed_all[shard] = mixed[...]
+    save_qkv = pltpu.make_async_copy(qkv_w, qkv_w_out, local.at[7])
+    save_qkv.start()
+    grad_line.run(1)
+    begin(stages[1])
+    for stage in outs:
+        stage.step_three()
+    mixed_line.run(1)
+    stages[1].step_two()
+    grad_line.run(2)
+    begin(stages[2])
+    for stage in outs:
+        stage.finish()
+    save_out = pltpu.make_async_copy(out_w, out_w_out, local.at[8])
+    save_out.start()
+    mixed_line.run(2)
+    stages[1].step_three()
     stages[2].step_two()
+    mark_kept(
+        small_all, device * own_experts, experts, own_experts, capacity, bits, shards, kept_out
+    )
     grad_line.run(3)
-    stages[3].step_one()
-    stages[3].start(stages[3].cores(0))
-    plane.step_two()
+    begin(stages[3])
     stages[2].step_three()
-    line.run(1)
+    keep(1)
+    mixed_line.run(3)
     stages[3].step_two()
-    plane.step_three()
-    line.run(2)
+    keep(2)
     stages[3].step_three()
-    line.run(3)
-    for group in (*stages, plane):
-        group.finish()
+    keep(3)
     for copy in sent:
         copy.wait_send()
-    line.drain()
-    grad_line.drain()
+    for group in (token_line, grad_line, out_line, mixed_line):
+        group.drain()
+    for copy in stored:
+        copy.wait()
+    save_qkv.wait()
+    save_out.wait()
 
 
 def opening_call(
-    routes, order, gains, router, w_query, w_key, w_value, tokens, w_out, out_grad, experts, planes, shards
+    routes, order, gains, seg_row, seg_col, tables, router, w_query, w_key, w_value, tokens, w_out, out_grad,
+    experts, own_experts, capacity, planes, shards,
 ):
     block, width = w_query.shape
-    rows = tokens.shape[0]
+    rows, top_count = routes.shape
+    seq, part = shards * rows, width // shards
     hbm = pl.BlockSpec(memory_space=pltpu.HBM)
     vmem = pl.BlockSpec(memory_space=pltpu.VMEM)
-    slots = 112
+    place = pl.BlockSpec(memory_space=pl.ANY)
+    slots = 144
+    low, full = tokens.dtype, jnp.float32
     small = (2 * experts + gains.shape[0], 128)
+    most = planes * shards * rows * top_count
     return pl.pallas_call(
-        functools.partial(opening_kernel, shards, experts),
-        in_specs=[vmem] * 3 + [hbm] * 7,
-        out_specs=[hbm] * 6,
+        functools.partial(
+            opening_kernel, shards, planes, experts, own_experts, capacity, most.bit_length()
+        ),
+        in_specs=[vmem] * 7 + [place] * 7,
+        out_specs=[vmem] * 10 + [place, hbm, vmem, hbm, hbm],
         out_shape=(
-            jax.ShapeDtypeStruct((planes * shards,) + small, gains.dtype),
+            jax.ShapeDtypeStruct((planes, seq, own_experts), full),
+            jax.ShapeDtypeStruct((1, width), full),
+            jax.ShapeDtypeStruct((1, width), full),
+            jax.ShapeDtypeStruct((1, HD), full),
+            jax.ShapeDtypeStruct((1, HD), full),
+            jax.ShapeDtypeStruct((seq, width), low),
+            jax.ShapeDtypeStruct((seq, 2 * part), full),
+            jax.ShapeDtypeStruct((seq, 3 * part), low),
+            jax.ShapeDtypeStruct((seq, 128), full),
+            jax.ShapeDtypeStruct((shards, seq, part), low),
             jax.ShapeDtypeStruct((planes * shards,) + router.shape, router.dtype),
-            jax.ShapeDtypeStruct((planes * shards * block, 3 * width // shards), w_query.dtype),
-            jax.ShapeDtypeStruct((shards * rows, width), tokens.dtype),
-            jax.ShapeDtypeStruct((shards * block, width), w_out.dtype),
-            jax.ShapeDtypeStruct((planes * shards * rows, width), out_grad.dtype),
+            pltpu.HBM((width, 3 * part), low),
+            jax.ShapeDtypeStruct((seq, width), low),
+            pltpu.HBM((width, width), low),
+            pltpu.HBM((planes * seq, width), low),
         ),
         scratch_shapes=[
             pltpu.VMEM(small, gains.dtype),
+            pltpu.VMEM((planes * shards,) + small, gains.dtype),
+            pltpu.VMEM((planes * seq, width), low),
+            pltpu.VMEM((width, 3 * part), low),
+            pltpu.VMEM((width, width), low),
+            pltpu.VMEM((seq, part), low),
+            pltpu.VMEM((seq, 3 * part), full),
             pltpu.SemaphoreType.DMA((slots,)),
             pltpu.SemaphoreType.DMA((slots,)),
-            pltpu.SemaphoreType.DMA((8,)),
+            pltpu.SemaphoreType.DMA((9,)),
+            pltpu.SemaphoreType.DMA((planes * shards,)),
         ],
         compiler_params=pltpu.CompilerParams(
-            collective_id=1, has_side_effects=True, vmem_limit_bytes=4 * MIB
+            collective_id=1, has_side_effects=True, vmem_limit_bytes=60 * MIB
         ),
         cost_estimate=pl.CostEstimate(flops=0, bytes_accessed=200 * MIB, transcendentals=0),
-    )(routes, order, gains, router, w_query, w_key, w_value, tokens, w_out, out_grad)
-
-
-def middle_kernel(shards, mixed, out_block, mixed_all, out_w, send, recv, local):
-    wires = Wires(send, recv)
-    device, shard = wires.device, wires.shard
-    greet(
-        [wires.peer(step=step, shards=shards) for step in range(1, shards)]
-        + [wires.peer(XBIT), wires.peer(YBIT), wires.peer(CORE)]
-    )
-    each = out_block.shape[0] // 2
-    line = Relay(wires, shards, [lambda b: mixed_all.at[b]])
-    line.run(0, (mixed,))
-    own = [
-        pltpu.make_async_copy(
-            out_block,
-            out_w.at[pl.ds(pl.multiple_of(device * 2 * each, 2 * each), 2 * each)],
-            local.at[0],
-        ),
-        pltpu.make_async_copy(mixed, mixed_all.at[shard], local.at[1]),
-    ]
-    for copy in own:
-        copy.start()
-    for copy in own:
-        copy.wait()
-    plane = Plane(
-        wires,
-        [lambda owner, half: out_w.at[pl.ds(pl.multiple_of((owner * 2 + half) * each, each), each)]],
-        [lambda owner: out_w.at[pl.ds(pl.multiple_of(owner * 2 * each, 2 * each), 2 * each)]],
-    )
-    plane.step_one()
-    plane.start(plane.cores(0))
-    line.run(1)
-    plane.step_two()
-    line.run(2)
-    for step in range(3, shards):
-        line.run(step)
-    plane.step_three()
-    plane.finish()
-    line.drain()
-
-
-def middle_call(mixed, out_block, planes, shards):
-    hbm = pl.BlockSpec(memory_space=pltpu.HBM)
-    slots = 32
-    return pl.pallas_call(
-        functools.partial(middle_kernel, shards),
-        in_specs=[hbm] * 2,
-        out_specs=[hbm] * 2,
-        out_shape=(
-            jax.ShapeDtypeStruct((shards,) + mixed.shape, mixed.dtype),
-            jax.ShapeDtypeStruct((planes * out_block.shape[0], out_block.shape[1]), mixed.dtype),
-        ),
-        scratch_shapes=[
-            pltpu.SemaphoreType.DMA((slots,)),
-            pltpu.SemaphoreType.DMA((slots,)),
-            pltpu.SemaphoreType.DMA((2,)),
-        ],
-        compiler_params=pltpu.CompilerParams(
-            collective_id=2, has_side_effects=True, vmem_limit_bytes=4 * MIB
-        ),
-        cost_estimate=pl.CostEstimate(flops=0, bytes_accessed=150 * MIB, transcendentals=0),
-    )(mixed, out_block)
+    )(
+        routes, order, gains, seg_row, seg_col, *tables, router, w_query, w_key, w_value, tokens, w_out, out_grad
+    )
 
 
 class Units:
@@ -1057,31 +1032,79 @@
 
 
 def meeting_kernel(
-    shards, normed, gate, up, down, normed_all, wide_w, down_w, send, recv, local
+    shards, planes, tokens, gain, mixed_all, out_w, gate, up, down,
+    hidden_out, mixed_own, normed_out, wide_w, down_w, normed_all, send, recv, local, store,
 ):
     wires = Wires(send, recv)
-    device = wires.device
-    half = normed.shape[0] // 2
+    device, shard = wires.device, wires.shard
+    seq, _ = tokens.shape
+    rows, part = hidden_out.shape[0], mixed_all.shape[2]
+    half = seq // 2
     greet(
         [wires.peer(step=step, shards=shards) for step in range(1, shards)]
         + [wires.peer(XBIT), wires.peer(YBIT), wires.peer(CORE)]
     )
-    plane = Plane(
-        wires,
-        [lambda owner, part_of: normed_all.at[owner, pl.ds(part_of * half, half)]],
-        [lambda owner: normed_all.at[owner]],
-    )
-    units = Units(wires, shards, 0, gate, up, down, wide_w, down_w, local, 1)
-    own = pltpu.make_async_copy(normed, normed_all.at[device], local.at[0])
-    own.start()
-    own.wait()
-    plane.step_one()
+    units = Units(wires, shards, 0, gate, up, down, wide_w, down_w, local, 0)
     units.begin()
-    plane.start(plane.cores(0))
-    plane.step_two()
-    plane.step_three()
-    plane.finish()
+
+    def stage(index):
+        def view(owner, start, size):
+            return normed_all.at[owner, pl.ds(start, size)]
+
+        return Plane(
+            wires,
+            [lambda owner, side: view(owner, index * half + side * (half // 2), half // 2)],
+            [lambda owner: view(owner, index * half, half)],
+        )
+
+    stages = [stage(index) for index in range(2)]
+    for side in range(2):
+        span = pl.ds(side * half, half)
+        total = tokens[span, :].astype(jnp.float32)
+        for source in range(shards):
+            total = total + jnp.dot(
+                mixed_all[source, span, :],
+                out_w[pl.ds(source * part, part), :],
+                preferred_element_type=jnp.float32,
+            )
+        normed_all[device, span, :] = (total * norm_factor(total) * gain[...]).astype(
+            normed_all.dtype
+        )
+        stages[side].step_one()
+        stages[side].start(stages[side].cores(0))
+        for inner in range(half // rows):
+
+            @pl.when(shard == side * (half // rows) + inner)
+            def _(total=total, inner=inner):
+                hidden_out[...] = total[inner * rows : (inner + 1) * rows, :]
+
+    stored = []
+
+    def keep(owner, side):
+        span = pl.ds(side * half, half)
+        copy = pltpu.make_async_copy(
+            normed_all.at[owner, span], normed_out.at[owner, span], store.at[len(stored)]
+        )
+        copy.start()
+        stored.append(copy)
+
+    for source in range(shards):
+        mixed_own[:, pl.ds(source * part, part)] = mixed_all[
+            source, pl.ds(pl.multiple_of(shard * rows, rows), rows), :
+        ]
+    for plane in stages:
+        plane.step_two()
+    for side, plane in enumerate(stages):
+        plane.step_three()
+        for chip in range(4):
+            keep(device ^ (2 * chip), side)
+    for side, plane in enumerate(stages):
+        plane.finish()
+        for chip in range(4):
+            keep(device ^ (2 * chip + 1), side)
     units.end()
+    for copy in stored:
+        copy.wait()
 
 
 def unit_shapes(gate, shards):
@@ -1093,25 +1116,37 @@
     )
 
 
-def meeting_call(normed, gate, up, down, planes, shards):
+def meeting_call(tokens, gain, mixed_all, out_w, gate, up, down, planes, shards):
     hbm = pl.BlockSpec(memory_space=pltpu.HBM)
-    slots = 24
+    vmem = pl.BlockSpec(memory_space=pltpu.VMEM)
+    seq, width = tokens.shape
+    rows = seq // shards
+    slots = 32
+    low = tokens.dtype
     return pl.pallas_call(
-        functools.partial(meeting_kernel, shards),
-        in_specs=[hbm] * 4,
-        out_specs=[hbm] * 3,
-        out_shape=(jax.ShapeDtypeStruct((planes,) + normed.shape, normed.dtype),)
+        functools.partial(meeting_kernel, shards, planes),
+        in_specs=[vmem] * 4 + [hbm] * 3,
+        out_specs=[vmem] * 2 + [hbm] * 3,
+        out_shape=(
+            jax.ShapeDtypeStruct((rows, width), jnp.float32),
+            jax.ShapeDtypeStruct((rows, width), low),
+            pltpu.HBM((planes, seq, width), low),
+        )
         + unit_shapes(gate, shards),
         scratch_shapes=[
+            pltpu.VMEM((planes, seq, width), low),
             pltpu.SemaphoreType.DMA((slots,)),
             pltpu.SemaphoreType.DMA((slots,)),
-            pltpu.SemaphoreType.DMA((4,)),
+            pltpu.SemaphoreType.DMA((3,)),
+            pltpu.SemaphoreType.DMA((2 * planes,)),
         ],
         compiler_params=pltpu.CompilerParams(
-            collective_id=3, has_side_effects=True, vmem_limit_bytes=4 * MIB
+            collective_id=3, has_side_effects=True, vmem_limit_bytes=40 * MIB
         ),
-        cost_estimate=pl.CostEstimate(flops=0, bytes_accessed=300 * MIB, transcendentals=0),
-    )(normed, gate, up, down)
+        cost_estimate=pl.CostEstimate(
+            flops=2 * seq * width * width, bytes_accessed=300 * MIB, transcendentals=0
+        ),
+    )(tokens, gain, mixed_all, out_w, gate, up, down)
 
 
 def add_rows(target, sources, lines):
@@ -1294,14 +1329,18 @@
 
     _, each, part = down_w.shape
     wide = jnp.dot(x[...], wide_w[...], preferred_element_type=jnp.float32)
-    logits = jnp.dot(x[...], router_w[...], preferred_element_type=jnp.float32)
     back = nt_dot(g[:, :part], down_w[0])
     for shard in range(1, shards):
         back = back + nt_dot(g[:, shard * part : (shard + 1) * part], down_w[shard])
-    lane = lax.broadcasted_iota(jnp.int32, logits.shape, 1)
-    logits = jnp.where(lane < experts, logits, -1e30)
-    shifted = jnp.exp(logits - jnp.max(logits, axis=-1, keepdims=True))
-    probs = shifted / jnp.sum(shifted, axis=-1, keepdims=True)
+    if index == 0:
+        logits = jnp.dot(x[...], router_w[...], preferred_element_type=jnp.float32)
+        lane = lax.broadcasted_iota(jnp.int32, logits.shape, 1)
+        logits = jnp.where(lane < experts, logits, -1e30)
+        shifted = jnp.exp(logits - jnp.max(logits, axis=-1, keepdims=True))
+        probs = shifted / jnp.sum(shifted, axis=-1, keepdims=True)
+    else:
+        lane = lax.broadcasted_iota(jnp.int32, old_pull.shape, 1)
+        probs = jnp.where(lane < experts, old_pull[...], 0.0)
     mark = hot[index : index + 1, :]
     kept = keep[:, index : index + 1]
     route = jnp.sum(probs * mark, axis=-1, keepdims=True) * kept
@@ -1321,9 +1360,9 @@
     )
     result = nt_dot(wide_low, wide_w[...])
     if index == 0:
-        pull[...] = pulled
+        pull[...] = jnp.where(lane < experts, probs, jnp.where(lane == 127, pulled, 0.0))
     else:
-        dense = pulled * mark + old_pull[...] * hot[0:1, :]
+        dense = pulled * mark + old_pull[:, 127:] * hot[0:1, :]
         logit_grad = probs * (dense - jnp.sum(probs * dense, axis=-1, keepdims=True))
         logit_low = logit_grad.astype(jnp.bfloat16)
         result = result + nt_dot(logit_low, router_w[...]) + old_grad[...].astype(jnp.float32)
@@ -1378,17 +1417,17 @@
 
     low = jnp.bfloat16
     tall = pltpu.HBM((planes, rows, width), low)
-    narrow = pltpu.HBM((planes, rows, 1), jnp.float32)
+    narrow = pltpu.HBM((planes, rows, 128), jnp.float32)
     wide_shape = pltpu.HBM(wide_w.shape, low)
     down_shape = pltpu.HBM(down_w.shape, low)
     came = pltpu.HBM((shards, width // shards, wide_w.shape[1]), low)
     if index == 0:
         extra = [hbm] * 3
-        out_specs = [rowwise(width)] * 2 + [rowwise(1)] + [hbm] * 4
+        out_specs = [rowwise(width)] * 2 + [rowwise(128)] + [hbm] * 4
         shapes = (tall, tall, narrow, wide_shape, down_shape, came, down_shape)
         operands = held_in_hbm(*weights)
     else:
-        extra = [rowwise(width)] * 2 + [rowwise(1)] + [hbm] * 2
+        extra = [rowwise(width)] * 2 + [rowwise(128)] + [hbm] * 2
         out_specs = [rowwise(width)] * 2 + [hbm] * 5
         router_shape = pltpu.HBM(router_w.shape, jnp.float32)
         shapes = (tall, tall, wide_shape, down_shape, router_shape, came, down_shape)
@@ -1841,13 +1880,26 @@
     shard = lax.axis_index(SHARD)
     part = width // shards
 
-    gains = jnp.concatenate([attn_gain, ffn_gain, query_gain, key_gain])
+    index = device * shards + shard
+
+    def placed(values, size):
+        zeros = jnp.zeros((size,), values.dtype)
+        return lax.dynamic_update_slice_in_dim(zeros, values, index * values.size, 0)
+
+    gains = [placed(attn_gain, width), placed(ffn_gain, width)]
+    gains += [placed(query_gain, HD), placed(key_gain, HD)]
+    gains = jnp.concatenate(gains)
     gains = jnp.pad(gains, (0, -gains.size % (16 * 128))).reshape(-1, 128)
     router_pad = jnp.pad(w_router, ((0, 0), (0, 128 - experts)))
-    small, router_w, qkv_w, tokens_seq, out_block, grad_all = opening_call(
+    tables = turn_tables(seq)
+    seg_row, seg_col = segment_ids.reshape(1, seq), segment_ids.reshape(seq, 1)
+    opened = opening_call(
         routes,
         pair_order.reshape(rows, top_count),
         gains,
+        seg_row,
+        seg_col,
+        tables,
         router_pad,
         w_query,
         w_key,
@@ -1856,33 +1908,17 @@
         w_out,
         out_grad,
         experts,
+        own_experts,
+        capacity,
         planes,
         shards,
     )
+    kept, attn_row, ffn_row, query_row, key_row, normed_low, raw, low, total, mixed_all = opened[:10]
+    router_w, qkv_w, tokens_seq, out_w, grad_all = opened[10:]
     router_w = router_w.reshape(width, 128)
-    gains = small[:, 2 * experts :].reshape(planes * shards, -1).astype(WIDE)
-    fields, at = [], 0
-    for size in (attn_gain.size, ffn_gain.size, query_gain.size, key_gain.size):
-        fields.append(gains[:, at : at + size].reshape(1, -1))
-        at += size
-    attn_row, ffn_row, query_row, key_row = fields
-    digits = [
-        lax.dynamic_slice_in_dim(small, start + device * own_experts, own_experts, 1)
-        for start in (0, experts)
-    ]
-    high, low_digit = [value.transpose(1, 0, 2) for value in digits]
-    most = planes * shards * rows * top_count
-    kept = keep_call(high, low_digit, capacity, most, planes, shards)
-
-    tables = turn_tables(seq)
-    seg_row, seg_col = segment_ids.reshape(1, seq), segment_ids.reshape(seq, 1)
-    normed_low, raw, low, mixed_own, total = attend_call(
-        tokens_seq, attn_row, qkv_w, query_row, key_row, tables, seg_row, seg_col
-    )
-    mixed, out_w = middle_call(mixed_own, out_block, planes, shards)
-    hidden_seq, normed_seq = join_call(mixed, out_w, tokens_seq, ffn_row)
-
-    token_all, wide_w, down_w = meeting_call(normed_seq, w_gate, w_up, w_down, planes, shards)
+    hidden, own_mixed, token_all, wide_w, down_w = meeting_call(
+        tokens_seq, ffn_row, mixed_all, out_w, w_gate, w_up, w_down, planes, shards
+    )
     grad_all = grad_all.reshape(planes, seq, width)
     own_ids = device * own_experts + jnp.arange(own_experts, dtype=jnp.int32)
     own_hot = (own_ids[:, None] == jnp.arange(128, dtype=jnp.int32)[None, :]).astype(WIDE)
@@ -1916,9 +1952,6 @@
     normed_two_grad, out_total, wide1, down1 = returning_call(
         in_parts, out_parts, wide_sum.reshape(shards, part, -1), down_sum
     )
-    hidden = lax.dynamic_slice_in_dim(hidden_seq, shard * rows, rows)
-    own_mixed = lax.dynamic_slice_in_dim(mixed, shard * rows, rows, 1)
-    own_mixed = own_mixed.transpose(1, 0, 2).reshape(rows, width)
     closed = closing_call(
         hidden,
         normed_two_grad,
@@ -1946,7 +1979,6 @@
     input_grad, mixed_out, query_w_grad, key_w_grad, value_w_grad, out_w_grad = closed[:6]
     attn_scale_grad, router_out, vectors = closed[6:]
     gate_grad, up_grad, down_grad = unpack_units((wide0, wide1), (down0, down1))
-    index = device * shards + shard
     flat = vectors.reshape(-1)
 
     def own_piece(values, start, size):

time: 793 us -> 774 us (0.976)
  local copies, waits for them, and re-layouts: 50.8 us -> 31.5 us
    unnamed x95 -> x51, local copies, waits for them, and re-layouts: 42.3 us -> 20.2 us
    pallas_call x2, Pallas kernels: 156 us -> 167 us  [expert_call(): pl.pallas_call(functools.partial(expert_kernel, index, experts, shards),...]
    pallas_call x6 -> x2, Pallas kernels: 260 us -> 250 us  [the longest x1 164 us: opening_call(): pl.pallas_call(functools.partial(opening_kernel, shards, planes, experts,...]
where the time goes in v4:
time: 774 us; the launch traced here: 765 us
  Pallas kernels  731 us (94%)
  local copies, waits for them, and re-layouts  31.5 us (4%)
    pallas_call x2, Pallas kernels, expert_call(): pl.pallas_call(functools.partial(expert_kernel, index, experts, shards),...  167 us
    pallas_call x1, Pallas kernels, opening_call(): pl.pallas_call(functools.partial(opening_kernel, shards, planes, experts,...  164 us
    pallas_call x1, Pallas kernels, closing_call(): pl.pallas_call(functools.partial(closing_kernel, shards, planes), in_spec...  159 us
    pallas_call x1, Pallas kernels, returning_call(): pl.pallas_call(functools.partial(returning_kernel, shards), in_specs=[hbm...  149 us
    pallas_call x1, Pallas kernels, meeting_call(): pl.pallas_call(functools.partial(meeting_kernel, shards, planes), in_spec...  86.5 us
    unnamed x51, local copies, waits for them, and re-layouts  20.2 us

profile of v4, /device:TPU:0, one launch (start us, length us, event | category | flops | bytes accessed | tf_op | source)
XLA Modules:
  0.0 764.5 jit_solution(7594939939807912768)
XLA Ops:
  0.6 0.0 copy-start.2
  0.7 0.1 compare_convert_fusion.hot
  0.8 1.0 dynamic_update_slice.15
  1.7 0.8 dynamic_update_slice.14
  2.6 0.8 dynamic_update_slice.13
  3.4 0.8 dynamic_update_slice.12
  4.3 0.6 fusion.7.gains
  4.9 0.8 copy.36
  5.7 0.6 pad.9.router
  6.3 1.4 copy.37.routes
  7.7 1.4 reshape.74.order
  9.1 1.5 copy.38.seg_col
  10.6 163.6 %shard_map.290 = (f32[8,512,2]{2,1,0:T(8,128)}, f32[1,2048]{1,0:T(1,128)}, f32[1,2048]{1,0:T(1,128)}, f32[1,128]{1,0:T(1,128)}, f32[1,128]{1,0:T(1,128)}, /*inde...) custom-call(s32[128,8]{1,0:T(8,128)} %copy.37.routes, ...), custom_call_target="tpu_custom_call" | custom-call | bytes 209715200 | tf_op jit(solution)/shard_map/pallas_call | solution.py:939
  174.2 0.0 copy-done.2
  174.2 0.0 copy-start.3
  174.2 1.6 copy-done.3
  175.8 0.0 copy-start.4
  175.8 1.6 copy-done.4
  177.4 0.0 copy-start.5
  177.4 1.6 copy-done.5
  179.0 0.0 copy-start.10
  179.0 0.7 copy-done.10
  179.7 0.0 copy-start.12
  179.7 86.5 %shard_map.291 = (f32[128,2048]{1,0:T(8,128)S(1)}, bf16[128,2048]{1,0:T(8,128)(2,1)S(1)}, bf16[8,512,2048]{2,1,0:T(8,128)(2,1)}, bf16[4,512,512]{2,1,0:T(8,128)(2,1)S(1)}, bf16[4,256,512]{2,1,0:T(8,128)(2,1)S(1)}) custom-call(bf16[512,2048]{1,0:T(8,128)(2,1)S(1)} %copy-done.5, f32[1,2048]{1,0:T(1,128)S(1)} %copy-done.10, bf16[4,512,512]{2,1,0:T(8,128)(2,1)S(1)} %copy-done.4, ...), custom_call_target="tpu_custom_call" | custom-call | flops 4294967296 | bytes 314572800 | tf_op jit(solution)/shard_map/pallas_call | solution.py:1126
  266.2 0.0 copy-start.7
  266.2 1.0 copy-done.7
  267.2 0.0 copy-start.9
  267.2 0.8 copy-done.9
  268.0 0.0 copy-start.11
  268.0 1.3 copy-done.11
  269.3 0.0 copy-done.12
  269.3 61.8 %shard_map.292 = (bf16[8,512,2048]{2,1,0:T(8,128)(2,1)}, bf16[8,512,2048]{2,1,0:T(8,128)(2,1)}, f32[8,512,128]{2,1,0:T(8,128)}, bf16[2048,512]{1,0:T(8,128)(2,1)...) custom-call(bf16[8,512,2048]{2,1,0:T(8,128)(2,1)} %get-tuple-element.69.x, ...), custom_call_target="tpu_custom_call" | custom-call | flops 25769803776 | bytes 104857600 | tf_op jit(solution)/shard_map/pallas_call | solution.py:1435
  331.1 0.0 copy-start.13
  331.2 1.2 copy-done.13
  332.4 105.0 %shard_map.293 = (bf16[8,512,2048]{2,1,0:T(8,128)(2,1)}, bf16[8,512,2048]{2,1,0:T(8,128)(2,1)}, bf16[2048,512]{1,0:T(8,128)(2,1)}, bf16[4,256,512]{2,1,0:T(8,128...) custom-call(bf16[8,512,2048]{2,1,0:T(8,128)(2,1)} %get-tuple-element.69.x, ...), custom_call_target="tpu_custom_call" | custom-call | flops 25769803776 | bytes 104857600 | tf_op jit(solution)/shard_map/pallas_call | solution.py:1435
  437.4 0.0 copy-start.14
  437.4 149.0 %shard_map.294 = (f32[128,2048]{1,0:T(8,128)}, bf16[512,2048]{1,0:T(8,128)(2,1)}, bf16[4,512,512]{2,1,0:T(8,128)(2,1)}, bf16[4,256,512]{2,1,0:T(8,128)(2,1)}) custom-call(bf16[8,512,2048]{2,1,0:T(8,128)(2,1)} %get-tuple-element.82.ins, bf16[8,512,2048]{2,1,0:T(8,128)(2,1)} %get-tuple-element.83.outs, bf16[4,512,512]{2,1,0:T(8,128)(2,1)} %bitcast.22, ...), custom_call_target="tpu_custom_call" | custom-call | bytes 314572800 | tf_op jit(solution)/shard_map/pallas_call | solution.py:1545
  586.5 0.0 copy-done.14
  586.5 1.0 reshape.84.router
  587.4 0.0 copy-start.6
  587.4 159.3 %shard_map.295 = (bf16[128,2048]{1,0:T(8,128)(2,1)}, bf16[128,2048]{1,0:T(8,128)(2,1)}, f32[64,2048]{1,0:T(8,128)}, f32[64,2048]{1,0:T(8,128)}, f32[64,2048]{1,0...) custom-call(f32[128,2048]{1,0:T(8,128)} %copy-done.7, ...), custom_call_target="tpu_custom_call" | custom-call | bytes 314572800 | tf_op jit(solution)/shard_map/pallas_call | solution.py:1795
  746.8 1.3 fusion.8
  748.0 1.2 fusion.10
  749.3 0.7 reshape.85
  750.0 0.7 copy.40
  750.7 0.0 copy-done
  750.7 0.0 copy-done.6
  750.7 0.0 copy-start.1
  750.7 1.6 copy-done.1
  752.3 1.2 copy-done.8
  753.5 5.8 shard_map.296
  759.3 0.0 copy-done.20
  759.3 0.0 copy-start.16
  759.3 0.8 copy.52
  760.1 0.0 copy-done.19
  760.1 0.8 copy.53
  760.9 0.0 copy-done.18
  760.9 0.8 copy.54
  761.7 0.0 copy-done.17
  761.7 0.8 copy.55
  762.5 0.0 copy-done.16
  762.5 0.8 copy.56
  763.3 0.0 copy-done.15
  763.3 0.8 copy.57
  (12 shorter events, 0.0 us)
Async XLA Ops:
  0.6 173.6 %copy-start.2 = (bf16[2,512,1024]{2,1,0:T(8,128)(2,1)S(1)}, bf16[2,512,1024]{2,1,0:T(8,128)(2,1)}, u32[]{:S(2)}) copy-start(bf16[2,512,1024]{2,1,0:T(8,128)(2,1)} %refs_0_.1) | copy-start | bytes 6291460
  174.2 1.6 copy-start.3
  175.8 1.6 copy-start.4
  177.4 1.6 copy-start.5
  179.0 0.7 copy-start.10
  179.7 89.6 %copy-start.12 = (bf16[32,64,128]{2,1,0:T(8,128)(2,1)S(1)}, bf16[32,64,128]{2,1,0:T(8,128)(2,1)}, u32[]{:S(2)}) copy-start(bf16[32,64,128]{2,1,0:T(8,128)(2,1)} %get-tuple-element.73) | copy-start | bytes 1572868
  266.2 1.0 copy-start.7
  267.2 0.8 copy-start.9
  268.0 1.3 copy-start.11
  331.1 1.2 copy-start.13
  437.4 149.0 %copy-start.14 = (f32[2048,128]{1,0:T(8,128)S(1)}, f32[2048,128]{1,0:T(8,128)}, u32[]{:S(2)}) copy-start(f32[2048,128]{1,0:T(8,128)} %get-tuple-element.95) | copy-start | bytes 3145732
  587.4 163.3 %copy-start = (bf16[4,512,512]{2,1,0:T(8,128)(2,1)S(1)}, bf16[4,512,512]{2,1,0:T(8,128)(2,1)}, u32[]{:S(2)}) copy-start(bf16[4,512,512]{2,1,0:T(8,128)(2,1)} %get-tuple-element.107.gate0.up0) | copy-start | bytes 6291460
  587.4 163.3 %copy-start.6 = (bf16[4,256,512]{2,1,0:T(8,128)(2,1)S(1)}, bf16[4,256,512]{2,1,0:T(8,128)(2,1)}, u32[]{:S(2)}) copy-start(bf16[4,256,512]{2,1,0:T(8,128)(2,1)} %get-tuple-element.109.down0) | copy-start | bytes 3145732
  750.7 1.6 copy-start.1
  752.3 1.2 copy-start.8
  753.5 5.8 copy-start.20
  753.5 6.6 copy-start.19
  759.3 1.6 copy-start.18
  759.3 2.4 copy-start.17
  759.3 3.2 copy-start.16
  760.1 3.2 copy-start.15

commit v5 on v4

--- a/solution.py
+++ b/solution.py
@@ -1130,7 +1130,7 @@
         out_shape=(
             jax.ShapeDtypeStruct((rows, width), jnp.float32),
             jax.ShapeDtypeStruct((rows, width), low),
-            pltpu.HBM((planes, seq, width), low),
+            pltpu.HBM((planes, seq + 16, width), low),
         )
         + unit_shapes(gate, shards),
         scratch_shapes=[
@@ -1276,6 +1276,69 @@
     def drain(self):
         for copy in self.sends():
             copy.wait_send()
+
+
+class LineFlow:
+    def __init__(self, wires, shards, own, flow):
+        self.wires, self.shards, self.own, self.flow = wires, shards, own, flow
+        self.slots = [[wires.slot() for _ in range(shards)] for _ in range(2)]
+        self.order = [
+            (way, (shards - 1 - step) if way == 0 else step)
+            for step in range(shards - 1)
+            for way in range(2)
+        ]
+
+    def copy(self, way, block, source):
+        wires = self.wires
+        peer = (wires.device, wires.shard + (1 if way == 0 else -1))
+        return wires.copy(source, self.flow.at[way, block], self.slots[way][block], peer)
+
+    def first(self, way):
+        return self.wires.shard == (0 if way == 0 else self.shards - 1)
+
+    def passes(self, way, block):
+        shard = self.wires.shard
+        inner = jnp.logical_and(shard > 0, shard < block)
+        if way == 1:
+            inner = jnp.logical_and(shard < self.shards - 1, shard > block)
+        return inner
+
+    def begin(self):
+        for way, block in self.order:
+
+            @pl.when(self.first(way))
+            def _(way=way, block=block):
+                self.copy(way, block, self.own(block)).start()
+
+    def forward(self, way, block):
+        @pl.when(self.passes(way, block))
+        def _():
+            place = self.flow.at[way, block]
+            self.copy(way, block, place).wait_recv()
+            add_rows(place, [self.own(block)], 64)
+            self.copy(way, block, place).start()
+
+    def end(self):
+        shard = self.wires.shard
+        for block in range(self.shards):
+
+            @pl.when(shard == block)
+            def _(block=block):
+                sources = []
+                for way in range(2):
+                    if block != (0 if way == 0 else self.shards - 1):
+                        place = self.flow.at[way, block]
+                        self.copy(way, block, place).wait_recv()
+                        sources.append(place)
+                add_rows(self.own(block), sources, 64)
+
+    def drain(self):
+        for way, block in self.order:
+            sends = jnp.logical_or(self.first(way), self.passes(way, block))
+
+            @pl.when(sends)
+            def _(way=way, block=block):
+                self.copy(way, block, self.own(block)).wait_send()
 
 
 def line_total(landing, shards):
@@ -1402,7 +1465,8 @@
 
 
 def expert_call(index, x_all, g_all, keep, wide_w, router_w, down_w, hot, experts, weights, before):
-    planes, rows, width = x_all.shape
+    planes, _, width = x_all.shape
+    rows = keep.shape[1]
     shards = down_w.shape[0]
     tile = 512
     per = rows // tile
@@ -1422,12 +1486,13 @@
     down_shape = pltpu.HBM(down_w.shape, low)
     came = pltpu.HBM((shards, width // shards, wide_w.shape[1]), low)
     if index == 0:
-        extra = [hbm] * 3
+        others = [hbm] * 3
         out_specs = [rowwise(width)] * 2 + [rowwise(128)] + [hbm] * 4
-        shapes = (tall, tall, narrow, wide_shape, down_shape, came, down_shape)
+        spare = [pltpu.HBM((planes, rows + extra, width), low) for extra in (32, 48)]
+        shapes = (*spare, narrow, wide_shape, down_shape, came, down_shape)
         operands = held_in_hbm(*weights)
     else:
-        extra = [rowwise(width)] * 2 + [rowwise(128)] + [hbm] * 2
+        others = [rowwise(width)] * 2 + [rowwise(128)] + [hbm] * 2
         out_specs = [rowwise(width)] * 2 + [hbm] * 5
         router_shape = pltpu.HBM(router_w.shape, jnp.float32)
         shapes = (tall, tall, wide_shape, down_shape, router_shape, came, down_shape)
@@ -1444,7 +1509,7 @@
             whole(down_w),
             whole(hot),
         ]
-        + extra,
+        + others,
         out_specs=out_specs,
         scratch_shapes=[pltpu.VMEM(wide_w.shape, jnp.float32)]
         + ([] if index == 0 else [pltpu.VMEM(router_w.shape, jnp.float32)])
@@ -1609,7 +1674,7 @@
     input_grad, mixed_out, query_out, key_out, value_out, weight_out, gain_out, router_out, vectors_out,
     held, came, diag, side, held2, came2, diag2, side2,
     weights, hidden_grad, attn_low, message, message_land, qkv_grad, normed_grad, vectors,
-    norm_land, out_land, qkv_land, weight_land, gain_mine, gain_land, gain_line, router_land, router_sum, router_line,
+    out_own, norm_land, out_land, qkv_land, weight_land, gain_mine, gain_land, gain_line, router_land, router_sum, router_line,
     vector_land, vector_sum, vector_line, send, recv, local,
 ):
     wires = Wires(send, recv)
@@ -1623,15 +1688,15 @@
     plane_peers = [wires.peer(bits) for bits in range(1, planes)]
     load_out = pltpu.make_async_copy(out_w, weights, local.at[0])
     load_out.start()
+    load_value = pltpu.make_async_copy(out_total, out_own, local.at[2])
+    load_value.start()
     greet(line_peers + plane_peers)
 
     back = LineSum(
         wires, shards, lambda t: message.at[t], lambda s: message_land.at[aligned(s, rows)]
     )
-    norms = LineSum(wires, shards, lambda t: normed_grad.at[aligned(t, rows)], lambda s: norm_land.at[s])
-    values = LineSum(
-        wires, shards, lambda t: out_total.at[aligned(t, rows)], lambda s: out_land.at[s]
-    )
+    norms = LineFlow(wires, shards, lambda b: normed_grad.at[aligned(b, rows)], norm_land)
+    values = LineFlow(wires, shards, lambda b: out_own.at[aligned(b, rows)], out_land)
     qkv = PlaneSum(wires, None, held, came, diag, side, local, 0)
     weight = PlaneSum(wires, None, held2, came2, diag2, side2, local, 0)
     qkv_line = LineSum(
@@ -1679,13 +1744,10 @@
             jnp.bfloat16
         )
     back.begin()
+    load_value.wait()
     values.begin()
     load_qkv = pltpu.make_async_copy(qkv_w, weights.at[:, pl.ds(0, lanes)], local.at[1])
     load_qkv.start()
-    own_value = pltpu.make_async_copy(
-        out_total.at[aligned(shard, rows)], out_land.at[shard], local.at[2]
-    )
-    own_value.start()
     message_land[aligned(shard, rows), :] = message[shard]
 
     def addends(group, left, right):
@@ -1703,6 +1765,9 @@
     addends(weight, own_mixed, attn_low)
     weight.send_corner()
     weight.add_cores()
+    far = shards - 1
+    values.forward(0, far)
+    values.forward(1, 0)
     router_sum[...] = collect(router_slots, router_land)
     router_pass = LineSum(
         wires, shards, lambda t: router_sum.at[aligned(t, lines)], lambda s: router_line.at[s]
@@ -1718,14 +1783,21 @@
     load_qkv.wait()
     normed_grad[...] = nt_dot(qkv_grad[...], weights[:, pl.ds(0, lanes)]).astype(jnp.bfloat16)
     norms.begin()
-    norm_land[shard] = normed_grad[aligned(shard, rows), :]
+    for step in range(1, shards - 1):
+        values.forward(0, far - step)
+        values.forward(1, step)
     router_pass.begin()
     spread(vector_slots, lambda e: vectors, vector_land)
     vector_land[device] = vectors[...]
     weight.send_sides()
     addends(qkv, normed, qkv_grad)
+    norms.forward(0, far)
+    norms.forward(1, 0)
     qkv.send_corner()
     qkv.add_cores()
+    for step in range(1, shards - 1):
+        norms.forward(0, far - step)
+        norms.forward(1, step)
     vector_sum[...] = collect(vector_slots, vector_land)
     vector_pass = LineSum(wires, shards, lambda t: vector_sum, lambda s: vector_line.at[s])
     vector_pass.begin()
@@ -1735,13 +1807,12 @@
     weight.end()
     weight_line.begin()
     weight_land[shard] = held2[0, aligned(shard, block), :]
-    out_land_ready = own_value
-    out_land_ready.wait()
-    values.arrive()
-    mixed_out[...] = (hidden[...] + line_total(out_land, shards)).astype(jnp.bfloat16)
-
-    norms.arrive()
-    change = line_total(norm_land, shards)
+    values.end()
+    mine = aligned(shard, rows)
+    mixed_out[...] = (hidden[...] + out_own[mine, :].astype(jnp.float32)).astype(jnp.bfloat16)
+
+    norms.end()
+    change = normed_grad[mine, :].astype(jnp.float32)
     given = tokens[...].astype(jnp.float32)
     factor = norm_factor(given)
     gain_mine[...] = jnp.sum(change * given * factor, axis=0, keepdims=True)
@@ -1818,8 +1889,9 @@
             pltpu.VMEM((seq, lanes), half),
             pltpu.VMEM((seq, width), half),
             pltpu.VMEM((1, vector), full),
-            pltpu.VMEM((shards, rows, width), half),
-            pltpu.VMEM((shards, rows, width), half),
+            pltpu.VMEM((seq, width), half),
+            pltpu.VMEM((2, shards, rows, width), half),
+            pltpu.VMEM((2, shards, rows, width), half),
             pltpu.VMEM((shards, block, lanes), half),
             pltpu.VMEM((shards, block, width), half),
             pltpu.VMEM((1, width), full),
@@ -1831,12 +1903,12 @@
             pltpu.VMEM((planes, 1, vector), full),
             pltpu.VMEM((1, vector), full),
             pltpu.VMEM((shards, 1, vector), full),
-            pltpu.SemaphoreType.DMA((72,)),
-            pltpu.SemaphoreType.DMA((72,)),
+            pltpu.SemaphoreType.DMA((80,)),
+            pltpu.SemaphoreType.DMA((80,)),
             pltpu.SemaphoreType.DMA((3,)),
         ],
         compiler_params=pltpu.CompilerParams(
-            collective_id=6, has_side_effects=True, vmem_limit_bytes=60 * MIB
+            collective_id=6, has_side_effects=True, vmem_limit_bytes=62 * MIB
         ),
         cost_estimate=pl.CostEstimate(flops=0, bytes_accessed=300 * MIB, transcendentals=0),
     )(

time: 774 us -> 759 us (0.981)
  Pallas kernels: 731 us -> 715 us
    pallas_call x2, Pallas kernels: 167 us -> 156 us  [expert_call(): pl.pallas_call(functools.partial(expert_kernel, index, experts, shards),...]
where the time goes in v5:
time: 759 us; the launch traced here: 750 us
  Pallas kernels  715 us (94%)
  local copies, waits for them, and re-layouts  33.1 us (4%)
    pallas_call x1, Pallas kernels, opening_call(): pl.pallas_call(functools.partial(opening_kernel, shards, planes, experts,...  164 us
    pallas_call x2, Pallas kernels, expert_call(): pl.pallas_call(functools.partial(expert_kernel, index, experts, shards),...  156 us
    pallas_call x1, Pallas kernels, closing_call(): pl.pallas_call(functools.partial(closing_kernel, shards, planes), in_spec...  153 us
    pallas_call x1, Pallas kernels, returning_call(): pl.pallas_call(functools.partial(returning_kernel, shards), in_specs=[hbm...  150 us
    pallas_call x1, Pallas kernels, meeting_call(): pl.pallas_call(functools.partial(meeting_kernel, shards, planes), in_spec...  86.8 us
    unnamed x51, local copies, waits for them, and re-layouts  21.8 us

profile of v5, /device:TPU:0, one launch (start us, length us, event | category | flops | bytes accessed | tf_op | source)
XLA Modules:
  0.0 750.3 jit_solution(11824959292072978856)
XLA Ops:
  0.6 0.0 copy-start.2
  0.7 0.1 compare_convert_fusion.hot
  0.8 1.0 dynamic_update_slice.15
  1.7 0.8 dynamic_update_slice.14
  2.6 0.8 dynamic_update_slice.13
  3.4 0.8 dynamic_update_slice.12
  4.3 0.6 fusion.7.gains
  4.9 0.8 copy.36
  5.7 0.6 pad.9.router
  6.3 1.4 copy.37.routes
  7.7 1.4 reshape.74.order
  9.1 1.5 copy.38.seg_col
  10.6 163.6 %shard_map.290 = (f32[8,512,2]{2,1,0:T(8,128)}, f32[1,2048]{1,0:T(1,128)}, f32[1,2048]{1,0:T(1,128)}, f32[1,128]{1,0:T(1,128)}, f32[1,128]{1,0:T(1,128)}, /*inde...) custom-call(s32[128,8]{1,0:T(8,128)} %copy.37.routes, ...), custom_call_target="tpu_custom_call" | custom-call | bytes 209715200 | tf_op jit(solution)/shard_map/pallas_call | solution.py:939
  174.2 0.0 copy-done.2
  174.2 0.0 copy-start.3
  174.2 1.6 copy-done.3
  175.8 0.0 copy-start.4
  175.8 1.6 copy-done.4
  177.4 0.0 copy-start.5
  177.4 1.6 copy-done.5
  179.0 0.7 copy-done.10
  179.7 0.0 copy-start.12
  179.7 86.8 %shard_map.291 = (f32[128,2048]{1,0:T(8,128)S(1)}, bf16[128,2048]{1,0:T(8,128)(2,1)S(1)}, bf16[8,528,2048]{2,1,0:T(8,128)(2,1)}, bf16[4,512,512]{2,1,0:T(8,128)(2,1)S(1)}, bf16[4,256,512]{2,1,0:T(8,128)(2,1)S(1)}) custom-call(bf16[512,2048]{1,0:T(8,128)(2,1)S(1)} %copy-done.5, f32[1,2048]{1,0:T(1,128)S(1)} %copy-done.10, bf16[4,512,512]{2,1,0:T(8,128)(2,1)S(1)} %copy-done.4, ...), custom_call_target="tpu_custom_call" | custom-call | flops 4294967296 | bytes 314572800 | tf_op jit(solution)/shard_map/pallas_call | solution.py:1126
  266.5 0.0 copy-start.7
  266.5 1.0 copy-done.7
  267.5 0.0 copy-start.9
  267.5 0.8 copy-done.9
  268.3 0.0 copy-start.11
  268.3 1.3 copy-done.11
  269.6 0.0 copy-done.12
  269.6 61.8 %shard_map.292 = (bf16[8,544,2048]{2,1,0:T(8,128)(2,1)}, bf16[8,560,2048]{2,1,0:T(8,128)(2,1)}, f32[8,512,128]{2,1,0:T(8,128)}, bf16[2048,512]{1,0:T(8,128)(2,1)...) custom-call(bf16[8,528,2048]{2,1,0:T(8,128)(2,1)} %get-tuple-element.69.x, ...), custom_call_target="tpu_custom_call" | custom-call | flops 25769803776 | bytes 104857600 | tf_op jit(solution)/shard_map/pallas_call | solution.py:1500
  331.4 0.0 copy-start.13
  331.4 1.2 copy-done.13
  332.6 94.6 %shard_map.293 = (bf16[8,512,2048]{2,1,0:T(8,128)(2,1)}, bf16[8,512,2048]{2,1,0:T(8,128)(2,1)}, bf16[2048,512]{1,0:T(8,128)(2,1)}, bf16[4,256,512]{2,1,0:T(8,128...) custom-call(bf16[8,528,2048]{2,1,0:T(8,128)(2,1)} %get-tuple-element.69.x, ...), custom_call_target="tpu_custom_call" | custom-call | flops 25769803776 | bytes 104857600 | tf_op jit(solution)/shard_map/pallas_call | solution.py:1500
  427.2 0.0 copy-start.14
  427.2 150.0 %shard_map.294 = (f32[128,2048]{1,0:T(8,128)}, bf16[512,2048]{1,0:T(8,128)(2,1)}, bf16[4,512,512]{2,1,0:T(8,128)(2,1)}, bf16[4,256,512]{2,1,0:T(8,128)(2,1)}) custom-call(bf16[8,512,2048]{2,1,0:T(8,128)(2,1)} %get-tuple-element.82.ins, bf16[8,512,2048]{2,1,0:T(8,128)(2,1)} %get-tuple-element.83.outs, bf16[4,512,512]{2,1,0:T(8,128)(2,1)} %bitcast.22, ...), custom_call_target="tpu_custom_call" | custom-call | bytes 314572800 | tf_op jit(solution)/shard_map/pallas_call | solution.py:1610
  577.2 0.0 copy-done.14
  577.2 1.0 reshape.84.router
  578.2 0.0 copy-start.6
  578.2 152.7 %shard_map.295 = (bf16[128,2048]{1,0:T(8,128)(2,1)}, bf16[128,2048]{1,0:T(8,128)(2,1)}, f32[64,2048]{1,0:T(8,128)}, f32[64,2048]{1,0:T(8,128)}, f32[64,2048]{1,0...) custom-call(f32[128,2048]{1,0:T(8,128)} %copy-done.7, ...), custom_call_target="tpu_custom_call" | custom-call | bytes 314572800 | tf_op jit(solution)/shard_map/pallas_call | solution.py:1866
  730.9 1.3 fusion.8
  732.1 1.3 fusion.10
  733.4 0.8 reshape.85
  734.2 0.7 copy.40
  734.8 0.0 copy-done.6
  734.8 0.0 copy-start
  734.8 1.6 copy-done
  736.4 0.0 copy-start.1
  736.4 1.6 copy-done.1
  738.0 1.2 copy-done.8
  739.3 5.8 shard_map.296
  745.0 0.0 copy-done.20
  745.0 0.0 copy-start.16
  745.0 0.8 copy.52
  745.8 0.0 copy-done.19
  745.8 0.8 copy.53
  746.6 0.0 copy-done.18
  746.6 0.8 copy.54
  747.4 0.0 copy-done.17
  747.4 0.8 copy.55
  748.2 0.0 copy-done.16
  748.2 0.8 copy.56
  749.0 0.0 copy-done.15
  749.0 0.8 copy.57
  (12 shorter events, 0.0 us)
Async XLA Ops:
  0.6 173.6 %copy-start.2 = (bf16[2,512,1024]{2,1,0:T(8,128)(2,1)S(1)}, bf16[2,512,1024]{2,1,0:T(8,128)(2,1)}, u32[]{:S(2)}) copy-start(bf16[2,512,1024]{2,1,0:T(8,128)(2,1)} %refs_0_.1) | copy-start | bytes 6291460
  174.2 1.6 copy-start.3
  175.8 1.6 copy-start.4
  177.4 1.6 copy-start.5
  179.0 0.7 copy-start.10
  179.7 89.9 %copy-start.12 = (bf16[32,64,128]{2,1,0:T(8,128)(2,1)S(1)}, bf16[32,64,128]{2,1,0:T(8,128)(2,1)}, u32[]{:S(2)}) copy-start(bf16[32,64,128]{2,1,0:T(8,128)(2,1)} %get-tuple-element.73) | copy-start | bytes 1572868
  266.5 1.0 copy-start.7
  267.5 0.8 copy-start.9
  268.3 1.3 copy-start.11
  331.4 1.2 copy-start.13
  427.2 150.0 %copy-start.14 = (f32[2048,128]{1,0:T(8,128)S(1)}, f32[2048,128]{1,0:T(8,128)}, u32[]{:S(2)}) copy-start(f32[2048,128]{1,0:T(8,128)} %get-tuple-element.95) | copy-start | bytes 3145732
  578.2 156.7 %copy-start.6 = (bf16[4,256,512]{2,1,0:T(8,128)(2,1)S(1)}, bf16[4,256,512]{2,1,0:T(8,128)(2,1)}, u32[]{:S(2)}) copy-start(bf16[4,256,512]{2,1,0:T(8,128)(2,1)} %get-tuple-element.109.down0) | copy-start | bytes 3145732
  734.8 1.6 copy-start
  736.4 1.6 copy-start.1
  738.0 1.2 copy-start.8
  739.2 5.8 copy-start.20
  739.3 6.6 copy-start.19
  745.0 1.6 copy-start.18
  745.0 2.4 copy-start.17
  745.0 3.2 copy-start.16
  745.8 3.2 copy-start.15

commit v6 on v5

--- a/solution.py
+++ b/solution.py
@@ -424,8 +424,14 @@
     return lax.rsqrt(jnp.mean(values * values, axis=-1, keepdims=True) + EPSILON)
 
 
+def same_document(seg_row):
+    row = seg_row[...].astype(jnp.float32)
+    column = jnp.broadcast_to(row, (128, row.shape[1])).T[:, :1]
+    return column == row
+
+
 def attend(
-    tokens, gain, weight, query_gain, key_gain, cosine, sine, seg_row, seg_col,
+    tokens, gain, weight, query_gain, key_gain, cosine, sine, allowed,
     normed_out, raw_out, low_out, mixed_out, total_out, qkv,
 ):
     part = mixed_out.shape[1]
@@ -435,7 +441,6 @@
     qkv[...] = jnp.dot(normed, weight[...], preferred_element_type=jnp.float32)
     raw_out[...] = qkv[:, : 2 * part]
     low_out[:, 2 * part :] = qkv[:, 2 * part :].astype(jnp.bfloat16)
-    allowed = seg_col[...] == seg_row[...]
     for head in range(part // HD):
         span = pl.ds(head * HD, HD)
         for offset, scale_gain, scale in ((0, query_gain, HD ** (-0.5)), (part, key_gain, 1.0)):
@@ -680,7 +685,7 @@
 
 def opening_kernel(
     shards, planes, experts, own_experts, capacity, bits,
-    routes, order, gains, seg_row, seg_col, cosine, sine,
+    routes, order, gains, seg_row, cosine, sine,
     router, w_query, w_key, w_value, tokens, w_out, out_grad,
     kept_out, attn_row, ffn_row, query_row, key_row, normed_out, raw_out, low_out, total_out, mixed_all,
     router_all, qkv_w_out, tokens_all, out_w_out, grad_out,
@@ -781,15 +786,14 @@
 
     own[0].wait()
     begin(stages[0])
-    column = lax.broadcasted_iota(jnp.int32, (rows, 128), 1)
-    dense = jnp.zeros((rows, 128), jnp.int32)
-    for choice in range(routes.shape[1]):
-        named = routes[:, choice : choice + 1] == column
-        dense = dense + jnp.where(named, order[:, choice : choice + 1] + 1, 0)
+    expert = lax.broadcasted_iota(jnp.int32, (experts, rows), 0)
+    dense = jnp.zeros((experts, rows), jnp.int32)
+    for choice in range(routes.shape[0]):
+        named = routes[choice : choice + 1, :] == expert
+        dense = dense + jnp.where(named, order[choice : choice + 1, :] + 1, 0)
     high = lax.shift_right_logical(dense, 8)
     for start, digits in ((0, high), (experts, dense - high * 256)):
-        turned = digits.astype(jnp.float32).T
-        small[pl.ds(start, experts), :] = turned[:experts, :].astype(small.dtype)
+        small[pl.ds(start, experts), :] = digits.astype(jnp.float32).astype(small.dtype)
     small[pl.ds(2 * experts, gains.shape[0]), :] = gains[...]
     small_all[mine] = small[...]
     for step in range(1, shards):
@@ -878,7 +882,7 @@
         stage.step_two()
     token_line.run(3)
     attend(
-        tokens_all, attn_row, qkv_w, query_row, key_row, cosine, sine, seg_row, seg_col,
+        tokens_all, attn_row, qkv_w, query_row, key_row, cosine, sine, same_document(seg_row),
         normed_out, raw_out, low_out, mixed, total_out, qkv,
     )
     mixed_line.run(0, (mixed,))
@@ -923,11 +927,11 @@
 
 
 def opening_call(
-    routes, order, gains, seg_row, seg_col, tables, router, w_query, w_key, w_value, tokens, w_out, out_grad,
+    routes, order, gains, seg_row, tables, router, w_query, w_key, w_value, tokens, w_out, out_grad,
     experts, own_experts, capacity, planes, shards,
 ):
     block, width = w_query.shape
-    rows, top_count = routes.shape
+    top_count, rows = routes.shape
     seq, part = shards * rows, width // shards
     hbm = pl.BlockSpec(memory_space=pltpu.HBM)
     vmem = pl.BlockSpec(memory_space=pltpu.VMEM)
@@ -940,7 +944,7 @@
         functools.partial(
             opening_kernel, shards, planes, experts, own_experts, capacity, most.bit_length()
         ),
-        in_specs=[vmem] * 7 + [place] * 7,
+        in_specs=[vmem] * 6 + [place] * 7,
         out_specs=[vmem] * 10 + [place, hbm, vmem, hbm, hbm],
         out_shape=(
             jax.ShapeDtypeStruct((planes, seq, own_experts), full),
@@ -977,25 +981,34 @@
         ),
         cost_estimate=pl.CostEstimate(flops=0, bytes_accessed=200 * MIB, transcendentals=0),
     )(
-        routes, order, gains, seg_row, seg_col, *tables, router, w_query, w_key, w_value, tokens, w_out, out_grad
+        routes, order, gains, seg_row, *tables, router, w_query, w_key, w_value, tokens, w_out, out_grad
     )
 
 
 class Units:
-    def __init__(self, wires, shards, index, gate, up, down, wide_w, down_w, local, base):
+    def __init__(self, wires, shards, index, gate, up, down, wide_w, down_w, local, base, piece=(0, 1)):
         self.wires, self.shards, self.index = wires, shards, index
         self.gate, self.up, self.down, self.wide_w, self.down_w = gate, up, down, wide_w, down_w
-        self.local, self.base = local, base
-        self.slots = [[wires.slot() for _ in range(3)] for _ in range(1, shards)]
+        self.local, self.base, self.piece = local, base, piece
+        count = (0 if wide_w is None else 2) + (0 if down_w is None else 1)
+        self.slots = [[wires.slot() for _ in range(count)] for _ in range(1, shards)]
 
     def pairs(self, source, target):
-        each = self.down_w.shape[1]
+        each = self.gate.shape[2] // self.shards
         span = pl.ds(pl.multiple_of(target * each, each), each)
-        return [
-            (self.gate.at[self.index, :, span], self.wide_w.at[source, :, pl.ds(0, each)]),
-            (self.up.at[self.index, :, span], self.wide_w.at[source, :, pl.ds(each, each)]),
-            (self.down.at[self.index, span, :], self.down_w.at[source]),
-        ]
+        result = []
+        if self.wide_w is not None:
+            result += [
+                (self.gate.at[self.index, :, span], self.wide_w.at[source, :, pl.ds(0, each)]),
+                (self.up.at[self.index, :, span], self.wide_w.at[source, :, pl.ds(each, each)]),
+            ]
+        if self.down_w is not None:
+            number, pieces = self.piece
+            size = each // pieces
+            start = pl.multiple_of(target * each + number * size, size)
+            place = self.down_w.at[source, pl.ds(number * size, size), :]
+            result.append((self.down.at[self.index, pl.ds(start, size), :], place))
+        return result
 
     def own(self):
         shard = self.wires.shard
@@ -1033,7 +1046,7 @@
 
 def meeting_kernel(
     shards, planes, tokens, gain, mixed_all, out_w, gate, up, down,
-    hidden_out, mixed_own, normed_out, wide_w, down_w, normed_all, send, recv, local, store,
+    hidden_out, mixed_own, normed_out, wide_w, down_w, down_next, normed_all, send, recv, local, store,
 ):
     wires = Wires(send, recv)
     device, shard = wires.device, wires.shard
@@ -1044,8 +1057,12 @@
         [wires.peer(step=step, shards=shards) for step in range(1, shards)]
         + [wires.peer(XBIT), wires.peer(YBIT), wires.peer(CORE)]
     )
-    units = Units(wires, shards, 0, gate, up, down, wide_w, down_w, local, 0)
-    units.begin()
+    units = [
+        Units(wires, shards, 0, gate, up, down, wide_w, down_w, local, 0),
+        Units(wires, shards, 1, gate, up, down, None, down_next, local, 3, (0, 2)),
+    ]
+    for group in units:
+        group.begin()
 
     def stage(index):
         def view(owner, start, size):
@@ -1102,7 +1119,8 @@
         plane.finish()
         for chip in range(4):
             keep(device ^ (2 * chip + 1), side)
-    units.end()
+    for group in units:
+        group.end()
     for copy in stored:
         copy.wait()
 
@@ -1126,18 +1144,19 @@
     return pl.pallas_call(
         functools.partial(meeting_kernel, shards, planes),
         in_specs=[vmem] * 4 + [hbm] * 3,
-        out_specs=[vmem] * 2 + [hbm] * 3,
+        out_specs=[vmem] * 2 + [hbm] * 4,
         out_shape=(
-            jax.ShapeDtypeStruct((rows, width), jnp.float32),
-            jax.ShapeDtypeStruct((rows, width), low),
+            pltpu.HBM((rows, width), jnp.float32),
+            pltpu.HBM((rows, width), low),
             pltpu.HBM((planes, seq + 16, width), low),
         )
-        + unit_shapes(gate, shards),
+        + unit_shapes(gate, shards)
+        + unit_shapes(gate, shards)[1:],
         scratch_shapes=[
             pltpu.VMEM((planes, seq, width), low),
             pltpu.SemaphoreType.DMA((slots,)),
             pltpu.SemaphoreType.DMA((slots,)),
-            pltpu.SemaphoreType.DMA((3,)),
+            pltpu.SemaphoreType.DMA((4,)),
             pltpu.SemaphoreType.DMA((2 * planes,)),
         ],
         compiler_params=pltpu.CompilerParams(
@@ -1146,7 +1165,7 @@
         cost_estimate=pl.CostEstimate(
             flops=2 * seq * width * width, bytes_accessed=300 * MIB, transcendentals=0
         ),
-    )(tokens, gain, mixed_all, out_w, gate, up, down)
+    )(tokens, gain, mixed_all, out_w, *held_in_hbm(gate, up, down))
 
 
 def add_rows(target, sources, lines):
@@ -1356,8 +1375,8 @@
     index, experts, shards, x, g, keep, wide_w, router_w, down_w, hot, *refs
 ):
     if index == 0:
-        gate, up, down, out, grad, pull, wide_sum, down_sum, next_wide, next_down = refs[:10]
-        acc, dacc, wide_out, down_out, send, recv, local, sems = refs[10:]
+        gate, up, down, _, out, grad, pull, wide_sum, down_sum, next_wide, next_down = refs[:11]
+        acc, dacc, wide_out, down_out, send, recv, local, sems = refs[11:]
     else:
         old_out, old_grad, old_pull, wide_sent, down_sent = refs[:5]
         out, grad, wide_sum, down_sum, router_sum, wide_came, down_came = refs[5:12]
@@ -1365,7 +1384,7 @@
     step, steps = pl.program_id(0), pl.num_programs(0)
     wires = Wires(send, recv)
     if index == 0:
-        travel = [Units(wires, shards, 1, gate, up, down, next_wide, next_down, local, 0)]
+        travel = [Units(wires, shards, 1, gate, up, down, next_wide, next_down, local, 0, (1, 2))]
     else:
         travel = [
             LineSum(wires, shards, lambda t: wide_sent.at[t], lambda s: wide_came.at[s]),
@@ -1486,7 +1505,7 @@
     down_shape = pltpu.HBM(down_w.shape, low)
     came = pltpu.HBM((shards, width // shards, wide_w.shape[1]), low)
     if index == 0:
-        others = [hbm] * 3
+        others = [hbm] * 4
         out_specs = [rowwise(width)] * 2 + [rowwise(128)] + [hbm] * 4
         spare = [pltpu.HBM((planes, rows + extra, width), low) for extra in (32, 48)]
         shapes = (*spare, narrow, wide_shape, down_shape, came, down_shape)
@@ -1523,6 +1542,7 @@
             pltpu.SemaphoreType.DMA((3,)),
         ],
         out_shape=shapes,
+        input_output_aliases={10: 6} if index == 0 else {},
         compiler_params=pltpu.CompilerParams(
             collective_id=7 + index, has_side_effects=True, vmem_limit_bytes=52 * MIB
         ),
@@ -1669,7 +1689,7 @@
 
 def closing_kernel(
     shards, planes,
-    hidden, grad, out_grad, ffn_gain, raw, low, total, query_gain, key_gain, cosine, sine, seg_row, seg_col,
+    hidden, grad, out_grad, ffn_gain, raw, low, total, query_gain, key_gain, cosine, sine, seg_row,
     tokens, gain, own_mixed, normed, router, out_w, qkv_w, out_total,
     input_grad, mixed_out, query_out, key_out, value_out, weight_out, gain_out, router_out, vectors_out,
     held, came, diag, side, held2, came2, diag2, side2,
@@ -1766,15 +1786,13 @@
     weight.send_corner()
     weight.add_cores()
     far = shards - 1
-    values.forward(0, far)
-    values.forward(1, 0)
     router_sum[...] = collect(router_slots, router_land)
     router_pass = LineSum(
         wires, shards, lambda t: router_sum.at[aligned(t, lines)], lambda s: router_line.at[s]
     )
 
     back.arrive()
-    allowed = seg_col[...] == seg_row[...]
+    allowed = same_document(seg_row)
     query_sum, key_sum = back_through_heads(
         message_land, raw, low, total, query_gain, key_gain, cosine, sine, allowed, qkv_grad
     )
@@ -1783,13 +1801,15 @@
     load_qkv.wait()
     normed_grad[...] = nt_dot(qkv_grad[...], weights[:, pl.ds(0, lanes)]).astype(jnp.bfloat16)
     norms.begin()
-    for step in range(1, shards - 1):
-        values.forward(0, far - step)
-        values.forward(1, step)
+    values.forward(0, far)
+    values.forward(1, 0)
     router_pass.begin()
     spread(vector_slots, lambda e: vectors, vector_land)
     vector_land[device] = vectors[...]
     weight.send_sides()
+    for step in range(1, shards - 1):
+        values.forward(0, far - step)
+        values.forward(1, step)
     addends(qkv, normed, qkv_grad)
     norms.forward(0, far)
     norms.forward(1, 0)
@@ -1850,7 +1870,7 @@
 
 
 def closing_call(
-    hidden, grad, out_grad, ffn_gain, raw, low, total, query_gain, key_gain, tables, seg_row, seg_col,
+    hidden, grad, out_grad, ffn_gain, raw, low, total, query_gain, key_gain, tables, seg_row,
     tokens, gain, own_mixed, normed, router, out_w, qkv_w, out_total, planes, shards,
 ):
     rows, width = tokens.shape
@@ -1865,7 +1885,7 @@
     vector = width + 2 * HD
     return pl.pallas_call(
         functools.partial(closing_kernel, shards, planes),
-        in_specs=[vmem] * 18 + [hbm] * 3,
+        in_specs=[vmem] * 17 + [hbm] * 3,
         out_specs=[vmem] * 9,
         out_shape=(
             jax.ShapeDtypeStruct((rows, width), half),
@@ -1912,7 +1932,7 @@
         ),
         cost_estimate=pl.CostEstimate(flops=0, bytes_accessed=300 * MIB, transcendentals=0),
     )(
-        hidden, grad, out_grad, ffn_gain, raw, low, total, query_gain, key_gain, *tables, seg_row, seg_col,
+        hidden, grad, out_grad, ffn_gain, raw, low, total, query_gain, key_gain, *tables, seg_row,
         tokens, gain, own_mixed, normed, router, *held_in_hbm(out_w, qkv_w, out_total),
     )
 
@@ -1955,8 +1975,8 @@
     index = device * shards + shard
 
     def placed(values, size):
-        zeros = jnp.zeros((size,), values.dtype)
-        return lax.dynamic_update_slice_in_dim(zeros, values, index * values.size, 0)
+        owner = jnp.arange(size) // values.size
+        return jnp.where(owner == index, jnp.tile(values, size // values.size), 0)
 
     gains = [placed(attn_gain, width), placed(ffn_gain, width)]
     gains += [placed(query_gain, HD), placed(key_gain, HD)]
@@ -1964,13 +1984,12 @@
     gains = jnp.pad(gains, (0, -gains.size % (16 * 128))).reshape(-1, 128)
     router_pad = jnp.pad(w_router, ((0, 0), (0, 128 - experts)))
     tables = turn_tables(seq)
-    seg_row, seg_col = segment_ids.reshape(1, seq), segment_ids.reshape(seq, 1)
+    seg_row = segment_ids.reshape(1, seq)
     opened = opening_call(
-        routes,
-        pair_order.reshape(rows, top_count),
+        routes.T,
+        pair_order.reshape(rows, top_count).T,
         gains,
         seg_row,
-        seg_col,
         tables,
         router_pad,
         w_query,
@@ -1988,7 +2007,7 @@
     kept, attn_row, ffn_row, query_row, key_row, normed_low, raw, low, total, mixed_all = opened[:10]
     router_w, qkv_w, tokens_seq, out_w, grad_all = opened[10:]
     router_w = router_w.reshape(width, 128)
-    hidden, own_mixed, token_all, wide_w, down_w = meeting_call(
+    hidden, own_mixed, token_all, wide_w, down_w, down_next = meeting_call(
         tokens_seq, ffn_row, mixed_all, out_w, w_gate, w_up, w_down, planes, shards
     )
     grad_all = grad_all.reshape(planes, seq, width)
@@ -2004,7 +2023,7 @@
         down_w,
         own_hot,
         experts,
-        (w_gate, w_up, w_down),
+        (w_gate, w_up, w_down, down_next),
         None,
     )
     before = (out_first, in_first, pull, wide_sum.reshape(shards, part, -1), down_sum)
@@ -2036,7 +2055,6 @@
         key_row,
         tables,
         seg_row,
-        seg_col,
         tokens,
         attn_row,
         own_mixed,

time: 759 us -> 741 us (0.976)
  Pallas kernels: 715 us -> 701 us
    pallas_call x2, Pallas kernels: 156 us -> 145 us  [expert_call(): pl.pallas_call(functools.partial(expert_kernel, index, experts, shards),...]
    unnamed x51 -> x40, local copies, waits for them, and re-layouts: 21.8 us -> 18.7 us
where the time goes in v6:
time: 741 us; the launch traced here: 733 us
  Pallas kernels  701 us (95%)
  local copies, waits for them, and re-layouts  29.3 us (4%)
    pallas_call x1, Pallas kernels, opening_call(): pl.pallas_call(functools.partial(opening_kernel, shards, planes, experts,...  163 us
    pallas_call x1, Pallas kernels, returning_call(): pl.pallas_call(functools.partial(returning_kernel, shards), in_specs=[hbm...  151 us
    pallas_call x1, Pallas kernels, closing_call(): pl.pallas_call(functools.partial(closing_kernel, shards, planes), in_spec...  148 us
    pallas_call x2, Pallas kernels, expert_call(): pl.pallas_call(functools.partial(expert_kernel, index, experts, shards),...  145 us
    pallas_call x1, Pallas kernels, meeting_call(): pl.pallas_call(functools.partial(meeting_kernel, shards, planes), in_spec...  87.7 us
    unnamed x40, local copies, waits for them, and re-layouts  18.7 us

profile of v6, /device:TPU:0, one launch (start us, length us, event | category | flops | bytes accessed | tf_op | source)
XLA Modules:
  0.0 732.6 jit_solution(14868300169968125490)
XLA Ops:
  0.7 0.7 tile.16
  1.3 0.1 tile.17
  1.4 0.7 tile.18
  2.1 0.1 tile.19
  2.2 0.7 tile.40
  2.8 0.1 tile.41
  2.9 0.7 tile.42
  3.6 0.1 tile.43
  3.7 0.6 fusion.7.gains
  4.3 0.8 reshape.75
  5.1 0.7 copy.36
  5.8 0.8 copy.37
  6.5 0.6 pad.9.router
  7.2 163.4 %shard_map.290 = (f32[8,512,2]{2,1,0:T(8,128)}, f32[1,2048]{1,0:T(1,128)}, f32[1,2048]{1,0:T(1,128)}, f32[1,128]{1,0:T(1,128)}, f32[1,128]{1,0:T(1,128)}, /*inde...) custom-call(s32[8,128]{1,0:T(8,128)} %bitcast.28, ...), custom_call_target="tpu_custom_call" | custom-call | bytes 209715200 | tf_op jit(solution)/shard_map/pallas_call | solution.py:943
  170.6 0.0 copy-start.2
  170.6 1.6 copy-done.2
  172.2 1.6 copy-done.3
  173.8 0.0 copy-start.6
  173.8 0.7 copy-done.6
  174.5 0.0 copy-start.10
  174.5 87.7 %shard_map.291 = (f32[128,2048]{1,0:T(8,128)}, bf16[128,2048]{1,0:T(8,128)(2,1)}, bf16[8,528,2048]{2,1,0:T(8,128)(2,1)}, bf16[4,512,512]{2,1,0:T(8,128)(2,1)S(1)...) custom-call(bf16[512,2048]{1,0:T(8,128)(2,1)S(1)} %copy-done.3, f32[1,2048]{1,0:T(1,128)S(1)} %copy-done.6, ...), custom_call_target="tpu_custom_call" | custom-call | flops 4294967296 | bytes 314572800 | tf_op jit(solution)/shard_map/pallas_call | solution.py:1144
  262.2 0.0 copy-start.7
  262.2 1.3 copy-done.7
  263.5 0.0 copy-start.8
  263.5 1.0 copy-done.8
  264.5 0.1 compare_convert_fusion.hot
  264.5 0.0 copy-done.10
  264.5 62.3 %shard_map.292 = (bf16[8,544,2048]{2,1,0:T(8,128)(2,1)}, bf16[8,560,2048]{2,1,0:T(8,128)(2,1)}, f32[8,512,128]{2,1,0:T(8,128)}, bf16[2048,512]{1,0:T(8,128)(2,1)...) custom-call(bf16[8,528,2048]{2,1,0:T(8,128)(2,1)} %get-tuple-element, ...), custom_call_target="tpu_custom_call", output_to_operand_aliasing={{6}: (10, {})} | custom-call | flops 25769803776 | bytes 104857600 | tf_op jit(solution)/shard_map/pallas_call | solution.py:1519
  326.9 0.0 copy-start.9
  326.9 1.2 copy-done.9
  328.1 83.1 %shard_map.293 = (bf16[8,512,2048]{2,1,0:T(8,128)(2,1)}, bf16[8,512,2048]{2,1,0:T(8,128)(2,1)}, bf16[2048,512]{1,0:T(8,128)(2,1)}, bf16[4,256,512]{2,1,0:T(8,128...) custom-call(bf16[8,528,2048]{2,1,0:T(8,128)(2,1)} %get-tuple-element.70.x, ...), custom_call_target="tpu_custom_call" | custom-call | flops 25769803776 | bytes 104857600 | tf_op jit(solution)/shard_map/pallas_call | solution.py:1519
  411.2 0.0 copy-start
  411.2 0.0 copy-start.4
  411.2 150.9 %shard_map.294 = (f32[128,2048]{1,0:T(8,128)}, bf16[512,2048]{1,0:T(8,128)(2,1)}, bf16[4,512,512]{2,1,0:T(8,128)(2,1)}, bf16[4,256,512]{2,1,0:T(8,128)(2,1)}) custom-call(bf16[8,512,2048]{2,1,0:T(8,128)(2,1)} %get-tuple-element.84.ins, bf16[8,512,2048]{2,1,0:T(8,128)(2,1)} %get-tuple-element.85.outs, bf16[4,512,512]{2,1,0:T(8,128)(2,1)} %bitcast.23, ...), custom_call_target="tpu_custom_call" | custom-call | bytes 314572800 | tf_op jit(solution)/shard_map/pallas_call | solution.py:1630
  562.1 0.0 copy-done
  562.2 0.0 copy-done.4
  562.2 0.0 copy-start.1
  562.2 1.6 copy-done.1
  563.8 0.0 copy-start.5
  563.8 1.2 copy-done.5
  565.0 0.0 copy-start.11
  565.0 5.9 shard_map.296
  570.9 0.0 copy-done.11
  570.9 1.0 reshape.84.router
  571.9 147.8 %shard_map.295 = (bf16[128,2048]{1,0:T(8,128)(2,1)}, bf16[128,2048]{1,0:T(8,128)(2,1)}, f32[64,2048]{1,0:T(8,128)}, f32[64,2048]{1,0:T(8,128)}, f32[64,2048]{1,0...) custom-call(f32[128,2048]{1,0:T(8,128)} %get-tuple-element.69.hidden, ...), custom_call_target="tpu_custom_call" | custom-call | bytes 314572800 | tf_op jit(solution)/shard_map/pallas_call | solution.py:1886
  719.7 0.0 copy-start.15
  719.7 0.0 copy-start.14
  719.7 0.8 reshape.85
  720.6 0.7 copy.38
  721.2 1.3 fusion.16
  722.5 1.2 fusion.14
  723.7 1.3 fusion.17
  725.0 0.0 copy-start.13
  725.0 1.9 copy.46
  726.9 0.0 copy-start.12
  726.9 1.9 copy.47
  728.9 0.0 copy-done.15
  728.9 0.8 copy.48
  729.7 0.0 copy-done.14
  729.7 0.8 copy.49
  730.5 0.0 copy-done.13
  730.5 0.8 copy.50
  731.3 0.0 copy-done.12
  731.3 0.8 copy.51
  (4 shorter events, 0.0 us)
Async XLA Ops:
  170.6 1.6 copy-start.2
  172.2 1.6 copy-start.3
  173.8 0.7 copy-start.6
  174.5 90.1 %copy-start.10 = (bf16[32,64,128]{2,1,0:T(8,128)(2,1)S(1)}, bf16[32,64,128]{2,1,0:T(8,128)(2,1)}, u32[]{:S(2)}) copy-start(bf16[32,64,128]{2,1,0:T(8,128)(2,1)} %get-tuple-element.74) | copy-start | bytes 1572868
  262.2 1.3 copy-start.7
  263.5 1.0 copy-start.8
  326.9 1.2 copy-start.9
  411.2 151.0 %copy-start = (bf16[4,512,512]{2,1,0:T(8,128)(2,1)S(1)}, bf16[4,512,512]{2,1,0:T(8,128)(2,1)}, u32[]{:S(2)}) copy-start(bf16[4,512,512]{2,1,0:T(8,128)(2,1)} %get-tuple-element.109.gate0.up0) | copy-start | bytes 6291460
  411.2 151.0 %copy-start.4 = (bf16[4,256,512]{2,1,0:T(8,128)(2,1)S(1)}, bf16[4,256,512]{2,1,0:T(8,128)(2,1)}, u32[]{:S(2)}) copy-start(bf16[4,256,512]{2,1,0:T(8,128)(2,1)} %get-tuple-element.111.down0) | copy-start | bytes 3145732
  562.2 1.6 copy-start.1
  563.8 1.2 copy-start.5
  565.0 6.0 copy-start.11
  719.7 9.2 %copy-start.15 = (f32[64,2048]{1,0:T(8,128)S(1)}, f32[64,2048]{1,0:T(8,128)}, u32[]{:S(2)}) copy-start(f32[64,2048]{1,0:T(8,128)} %get-tuple-element.167) | copy-start | bytes 1572868
  719.7 10.0 %copy-start.14 = (f32[64,2048]{1,0:T(8,128)S(1)}, f32[64,2048]{1,0:T(8,128)}, u32[]{:S(2)}) copy-start(f32[64,2048]{1,0:T(8,128)} %get-tuple-element.168) | copy-start | bytes 1572868
  725.0 5.5 copy-start.13
  726.9 4.3 copy-start.12

commit v7 on v6

--- a/solution.py
+++ b/solution.py
@@ -1487,7 +1487,7 @@
     planes, _, width = x_all.shape
     rows = keep.shape[1]
     shards = down_w.shape[0]
-    tile = 512
+    tile = 512 if index == 0 else 256
     per = rows // tile
     hbm = pl.BlockSpec(memory_space=pltpu.HBM)
 

time: 741 us -> 738 us (level)
  no operation moved by 1% of the time
where the time goes in v7:
time: 738 us; the launch traced here: 728 us
  Pallas kernels  697 us (94%)
  local copies, waits for them, and re-layouts  29.3 us (4%)
    pallas_call x1, Pallas kernels, opening_call(): pl.pallas_call(functools.partial(opening_kernel, shards, planes, experts,...  163 us
    pallas_call x1, Pallas kernels, returning_call(): pl.pallas_call(functools.partial(returning_kernel, shards), in_specs=[hbm...  151 us
    pallas_call x1, Pallas kernels, closing_call(): pl.pallas_call(functools.partial(closing_kernel, shards, planes), in_spec...  145 us
    pallas_call x2, Pallas kernels, expert_call(): pl.pallas_call(functools.partial(expert_kernel, index, experts, shards),...  143 us
    pallas_call x1, Pallas kernels, meeting_call(): pl.pallas_call(functools.partial(meeting_kernel, shards, planes), in_spec...  87.7 us
    unnamed x40, local copies, waits for them, and re-layouts  18.7 us

profile of v7, /device:TPU:0, one launch (start us, length us, event | category | flops | bytes accessed | tf_op | source)
XLA Modules:
  0.0 727.9 jit_solution(11801989469629857158)
XLA Ops:
  0.7 0.7 tile.16
  1.3 0.1 tile.17
  1.4 0.7 tile.18
  2.1 0.1 tile.19
  2.2 0.7 tile.40
  2.8 0.1 tile.41
  2.9 0.7 tile.42
  3.6 0.1 tile.43
  3.7 0.6 fusion.7.gains
  4.3 0.8 reshape.75
  5.1 0.7 copy.36
  5.8 0.8 copy.37
  6.5 0.6 pad.9.router
  7.2 163.4 %shard_map.290 = (f32[8,512,2]{2,1,0:T(8,128)}, f32[1,2048]{1,0:T(1,128)}, f32[1,2048]{1,0:T(1,128)}, f32[1,128]{1,0:T(1,128)}, f32[1,128]{1,0:T(1,128)}, /*inde...) custom-call(s32[8,128]{1,0:T(8,128)} %bitcast.28, ...), custom_call_target="tpu_custom_call" | custom-call | bytes 209715200 | tf_op jit(solution)/shard_map/pallas_call | solution.py:943
  170.6 0.0 copy-start.2
  170.6 1.6 copy-done.2
  172.2 0.0 copy-start.3
  172.2 1.6 copy-done.3
  173.8 0.0 copy-start.6
  173.8 0.7 copy-done.6
  174.5 0.0 copy-start.10
  174.5 87.7 %shard_map.291 = (f32[128,2048]{1,0:T(8,128)}, bf16[128,2048]{1,0:T(8,128)(2,1)}, bf16[8,528,2048]{2,1,0:T(8,128)(2,1)}, bf16[4,512,512]{2,1,0:T(8,128)(2,1)S(1)...) custom-call(bf16[512,2048]{1,0:T(8,128)(2,1)S(1)} %copy-done.3, f32[1,2048]{1,0:T(1,128)S(1)} %copy-done.6, ...), custom_call_target="tpu_custom_call" | custom-call | flops 4294967296 | bytes 314572800 | tf_op jit(solution)/shard_map/pallas_call | solution.py:1144
  262.2 0.0 copy-start.7
  262.2 1.3 copy-done.7
  263.5 0.0 copy-start.8
  263.5 1.0 copy-done.8
  264.5 0.1 compare_convert_fusion.hot
  264.5 0.0 copy-done.10
  264.5 62.3 %shard_map.292 = (bf16[8,544,2048]{2,1,0:T(8,128)(2,1)}, bf16[8,560,2048]{2,1,0:T(8,128)(2,1)}, f32[8,512,128]{2,1,0:T(8,128)}, bf16[2048,512]{1,0:T(8,128)(2,1)...) custom-call(bf16[8,528,2048]{2,1,0:T(8,128)(2,1)} %get-tuple-element, ...), custom_call_target="tpu_custom_call", output_to_operand_aliasing={{6}: (10, {})} | custom-call | flops 25769803776 | bytes 104857600 | tf_op jit(solution)/shard_map/pallas_call | solution.py:1519
  326.9 0.0 copy-start.9
  326.9 1.2 copy-done.9
  328.1 81.1 %shard_map.293 = (bf16[8,512,2048]{2,1,0:T(8,128)(2,1)}, bf16[8,512,2048]{2,1,0:T(8,128)(2,1)}, bf16[2048,512]{1,0:T(8,128)(2,1)}, bf16[4,256,512]{2,1,0:T(8,128...) custom-call(bf16[8,528,2048]{2,1,0:T(8,128)(2,1)} %get-tuple-element.70.x, ...), custom_call_target="tpu_custom_call" | custom-call | flops 25769803776 | bytes 104857600 | tf_op jit(solution)/shard_map/pallas_call | solution.py:1519
  409.2 0.0 copy-start
  409.2 0.0 copy-start.4
  409.2 151.2 %shard_map.294 = (f32[128,2048]{1,0:T(8,128)}, bf16[512,2048]{1,0:T(8,128)(2,1)}, bf16[4,512,512]{2,1,0:T(8,128)(2,1)}, bf16[4,256,512]{2,1,0:T(8,128)(2,1)}) custom-call(bf16[8,512,2048]{2,1,0:T(8,128)(2,1)} %get-tuple-element.84.ins, bf16[8,512,2048]{2,1,0:T(8,128)(2,1)} %get-tuple-element.85.outs, bf16[4,512,512]{2,1,0:T(8,128)(2,1)} %bitcast.23, ...), custom_call_target="tpu_custom_call" | custom-call | bytes 314572800 | tf_op jit(solution)/shard_map/pallas_call | solution.py:1630
  560.4 0.0 copy-done
  560.5 0.0 copy-done.4
  560.5 0.0 copy-start.1
  560.5 1.6 copy-done.1
  562.1 0.0 copy-start.5
  562.1 1.2 copy-done.5
  563.3 0.0 copy-start.11
  563.3 5.8 shard_map.296
  569.0 0.0 copy-done.11
  569.0 1.0 reshape.84.router
  570.0 145.2 %shard_map.295 = (bf16[128,2048]{1,0:T(8,128)(2,1)}, bf16[128,2048]{1,0:T(8,128)(2,1)}, f32[64,2048]{1,0:T(8,128)}, f32[64,2048]{1,0:T(8,128)}, f32[64,2048]{1,0...) custom-call(f32[128,2048]{1,0:T(8,128)} %get-tuple-element.69.hidden, ...), custom_call_target="tpu_custom_call" | custom-call | bytes 314572800 | tf_op jit(solution)/shard_map/pallas_call | solution.py:1886
  715.3 0.0 copy-start.15
  715.3 0.0 copy-start.14
  715.3 0.8 reshape.85
  716.1 0.7 copy.38
  716.8 1.3 fusion.16
  718.0 1.2 fusion.14
  719.3 1.3 fusion.17
  720.5 0.0 copy-start.13
  720.5 1.9 copy.46
  722.5 1.9 copy.47
  724.4 0.0 copy-done.15
  724.4 0.8 copy.48
  725.2 0.0 copy-done.14
  725.2 0.8 copy.49
  726.0 0.0 copy-done.13
  726.0 0.8 copy.50
  726.8 0.0 copy-done.12
  726.8 0.8 copy.51
  (4 shorter events, 0.0 us)
Async XLA Ops:
  170.6 1.6 copy-start.2
  172.2 1.6 copy-start.3
  173.8 0.7 copy-start.6
  174.5 90.1 %copy-start.10 = (bf16[32,64,128]{2,1,0:T(8,128)(2,1)S(1)}, bf16[32,64,128]{2,1,0:T(8,128)(2,1)}, u32[]{:S(2)}) copy-start(bf16[32,64,128]{2,1,0:T(8,128)(2,1)} %get-tuple-element.74) | copy-start | bytes 1572868
  262.2 1.3 copy-start.7
  263.5 1.0 copy-start.8
  326.9 1.2 copy-start.9
  409.2 151.3 %copy-start = (bf16[4,512,512]{2,1,0:T(8,128)(2,1)S(1)}, bf16[4,512,512]{2,1,0:T(8,128)(2,1)}, u32[]{:S(2)}) copy-start(bf16[4,512,512]{2,1,0:T(8,128)(2,1)} %get-tuple-element.109.gate0.up0) | copy-start | bytes 6291460
  409.2 151.3 %copy-start.4 = (bf16[4,256,512]{2,1,0:T(8,128)(2,1)S(1)}, bf16[4,256,512]{2,1,0:T(8,128)(2,1)}, u32[]{:S(2)}) copy-start(bf16[4,256,512]{2,1,0:T(8,128)(2,1)} %get-tuple-element.111.down0) | copy-start | bytes 3145732
  560.5 1.6 copy-start.1
  562.1 1.2 copy-start.5
  563.3 5.8 copy-start.11
  715.3 9.2 %copy-start.15 = (f32[64,2048]{1,0:T(8,128)S(1)}, f32[64,2048]{1,0:T(8,128)}, u32[]{:S(2)}) copy-start(f32[64,2048]{1,0:T(8,128)} %get-tuple-element.167) | copy-start | bytes 1572868
  715.3 10.0 %copy-start.14 = (f32[64,2048]{1,0:T(8,128)S(1)}, f32[64,2048]{1,0:T(8,128)}, u32[]{:S(2)}) copy-start(f32[64,2048]{1,0:T(8,128)} %get-tuple-element.168) | copy-start | bytes 1572868
  720.5 5.5 copy-start.13
  722.5 4.3 copy-start.12
